TPU v7x, 32 devices: a whole 2x2x4 slice. The times are simulated.
32 devices in a mesh: obs: 8 (over z, x), sub: 4 (over y, core).
Axes of the slice: x: 2, y: 2, z: 4, core: 2. Of those that a mesh axis runs over, the one named last changes fastest.
Arguments:
- jacobian: bfloat16 [32768, 2048], P(('obs', 'sub')), may hold values from -0.09375 to 0.09375
- obs_weight: float32 [32768], P(('obs', 'sub')), may hold values from 0.2 to 5
- row_counts: int32 [8], P('obs'), may hold values from 1 to 4096, 24576 in all
- tile_lists: int32 [8, 8], replicated, may hold values from 0 to 15, all different within a row
- tile_slot: int32 [16], replicated, may hold values from 0 to 15, each once
- probe_block: bfloat16 [4096, 256], P('obs'), may hold values from -6 to 6
Outputs:
- owned_product: bfloat16 [4096, 256], P('obs', 'sub')
Inputs may be any that keep to these rules, and one draw needn't show every extreme that they name: `row_counts`: the live counts of one block; some block is full (4096) in every draw. `tile_lists`: each row lists 8 different tiles; every tile is listed by some block. `tile_slot`: a permutation of the tiles.
All inputs are finite; a program needn't handle non-finite values.
Results may differ from a plain program's by a relative error of at most 0.0034.
Values may be sent and summed in bfloat16 or wider, within the bound.
No kernel may reach another device: no remote copies, remote signals or barrier semaphores. Data moves between devices by JAX's collectives and lax.ppermute only.
A program may use at most 64 MiB of HBM per device.

v0:
```python
import jax
import jax.numpy as jnp
from jax import lax
from jax.sharding import PartitionSpec as P


def local(jacobian, obs_weight, row_counts, tile_lists, tile_slot, probe_block):
    rows = jacobian.shape[0]
    width = jacobian.shape[1]
    tiles_listed = tile_lists.shape[1]
    tile_count = tile_slot.shape[0]
    tile_rows = width // tiles_listed
    probe_width = probe_block.shape[1]
    sub_count = lax.axis_size("sub")
    obs_count = lax.axis_size("obs")
    quarter = probe_width // sub_count
    own_rows = tile_count * tile_rows // obs_count
    block_id = lax.axis_index("obs")
    sub_id = lax.axis_index("sub")
    offset = sub_id * rows
    live = (offset + jnp.arange(rows, dtype=jnp.int32) < row_counts[0]).astype(jnp.float32)
    weighted = (jacobian.astype(jnp.float32) * (obs_weight * live)[:, None]).astype(jnp.bfloat16)
    my_tiles = lax.dynamic_slice_in_dim(tile_lists, block_id, 1, 0)[0]
    contract_rows = (((0,), (0,)), ((), ()))
    within = jnp.arange(tile_rows, dtype=jnp.int32)
    wanted_rows = (my_tiles[:, None] * tile_rows + within[None, :]).reshape(width)
    my_part = lax.dynamic_slice_in_dim(probe_block, sub_id * quarter, quarter, 1)
    piece = lax.all_gather(my_part, "obs", axis=0, tiled=True)
    global_rows = jnp.arange(piece.shape[0], dtype=jnp.int32)
    selector = (wanted_rows[:, None] == global_rows[None, :]).astype(jnp.bfloat16)
    picked_part = jnp.dot(selector, piece, preferred_element_type=jnp.float32).astype(jnp.bfloat16)
    probe_cols = lax.all_gather(picked_part, "sub", axis=1, tiled=True)
    image = jnp.dot(jacobian, probe_cols, preferred_element_type=jnp.float32).astype(jnp.bfloat16)
    partial_prod = lax.dot_general(
        weighted, image, contract_rows, preferred_element_type=jnp.float32
    )
    tile_ids = jnp.arange(tile_count, dtype=jnp.int32)
    slots = jnp.sum(
        (my_tiles[:, None] == tile_ids[None, :]).astype(jnp.int32) * tile_slot[None, :], axis=1
    )
    positions = jnp.arange(tiles_listed, dtype=jnp.int32)
    block_sum = lax.psum_scatter(partial_prod, "sub", scatter_dimension=1, tiled=True)
    targets = jnp.arange(own_rows * lax.axis_size("obs"), dtype=jnp.int32)
    target_slot = targets // tile_rows
    match = (slots[None, :] == target_slot[:, None]).astype(jnp.int32)
    found = jnp.sum(match, axis=1)
    where_at = jnp.sum(match * positions[None, :], axis=1)
    source_rows = where_at * tile_rows + targets % tile_rows
    taken = jnp.take(block_sum, source_rows, axis=0)
    summed = lax.psum_scatter(
        taken * found[:, None].astype(jnp.float32), "obs", scatter_dimension=0, tiled=True
    )
    return summed.astype(jnp.bfloat16)


def solution(mesh):
    placed = (P(("obs", "sub"), None), P(("obs", "sub")), P("obs"), P(), P(), P("obs", None))
    return jax.shard_map(
        local, mesh=mesh, in_specs=placed, out_specs=P("obs", "sub"), check_vma=False
    )
```

profile of v0, /device:TPU:0, one launch (start us, length us, event | category | flops | bytes accessed | tf_op | source)
XLA Modules:
  0.0 192.2 jit_solution(13383141539766666536)
XLA Ops:
  6.5 0.0 copy-start
  6.5 0.0 all-gather.2.cloned.1.call-start
  6.5 0.7 broadcast_multiply_fusion.1
  7.3 0.1 add_bitcast_fusion
  7.4 0.1 copy-done
  7.5 0.1 constant_dynamic-slice_fusion
  7.6 34.7 %all_gather.6 = bf16[4096,64]{1,0:T(8,128)(2,1)S(1)} all-gather(bf16[512,64]{1,0:T(8,128)(2,1)S(1)} %constant_dynamic-slice_fusion), channel_id=1, replica_groups=mesh['obs'=8,'sub'=4] {'obs'}, dimensions={0}, use_global_device_ids=true | all-gather | bytes 589824 | tf_op jit(solution)/shard_map/all_gather | solution.py:28
  42.3 0.0 copy-start.1
  42.3 7.5 %fusion.4 = bf16[2048,64]{0,1:T(8,128)(2,1)} fusion(bf16[4096,64]{1,0:T(8,128)(2,1)S(1)} %all_gather.6, s32[2048]{0:T(1024)S(1)} %bitcast.15), kind=kOutput, calls=%fused_computation.7 | convolution fusion | flops 1082261504 | bytes 794624 | tf_op jit(solution)/shard_map/dot_general | solution.py:31
  49.8 0.0 all-gather.2.cloned.1.call-update
  49.8 0.0 reduce-scatter.3.cloned.1.call-start
  50.5 0.0 copy-done.1
  50.5 0.0 copy-start.2
  50.5 16.9 %all-gather.2.cloned.1.call-done = bf16[2048,256]{0,1:T(8,128)(2,1)} async-done(((bf16[2048,64]{0,1:T(8,128)(2,1)}), bf16[2048,256]{0,1:T(8,128)(2,1)}) %all-gather.2.cloned.1.call-update) | async-done | bytes 1048592 | tf_op jit(solution)/shard_map/all_gather | solution.py:32
  67.5 7.5 %fusion.2 = f32[2048,256]{0,1:T(8,128)} fusion(bf16[1024,2048]{1,0:T(8,128)(2,1)} %param.6, f32[1024]{0:T(1024)S(1)} %fusion.16, bf16[2048,256]{0,1:T(8,128)(2,1)} %all-gather.2.cloned.1.call-done), kind=kOutput, calls=%fused_computation.5 | convolution fusion | flops 2154037248 | bytes 7344128 | tf_op jit(solution)/shard_map/dot_general | solution.py:34
  75.0 0.0 reduce-scatter.3.cloned.1.call-update
  75.0 0.0 reduce-scatter.5.cloned.1.call-start
  75.1 0.0 copy-done.2
  75.1 0.2 select_reduce_fusion
  75.3 0.1 fusion.6
  75.5 31.1 %reduce-scatter.3.cloned.1.call-done = f32[2048,64]{0,1:T(8,128)} async-done(((f32[2048,256]{0,1:T(8,128)}), f32[2048,64]{0,1:T(8,128)}) %reduce-scatter.3.cloned.1.call-update) | async-done | bytes 524304 | tf_op jit(solution)/shard_map/reduce_scatter | solution.py:42
  106.6 1.4 copy.15
  108.0 10.8 %gather_fusion = f32[4096,64]{1,0:T(8,128)S(1)} fusion(f32[2048,64]{1,0:T(8,128)S(1)} %copy.15, s32[4096]{0:T(1024)S(1)} %broadcast_clamp_fusion), kind=kCustom, calls=%fused_computation | custom fusion | bytes 2113536 | tf_op jit(solution)/shard_map/jit(_take)/gather | solution.py:49
  118.8 0.6 copy.16
  119.4 1.1 select_multiply_fusion
  120.5 0.0 reduce-scatter.5.cloned.1.call-update
  120.5 63.6 %reduce-scatter.5.cloned.1.call-done = f32[512,64]{0,1:T(8,128)} async-done(((f32[4096,64]{0,1:T(8,128)}), f32[512,64]{0,1:T(8,128)}) %reduce-scatter.5.cloned.1.call-update) | async-done | bytes 131088 | tf_op jit(solution)/shard_map/reduce_scatter | solution.py:50
  184.1 1.5 convert_element_type.36
  (8 shorter events, 0.1 us)
Async XLA Ops:
  6.5 1.0 copy-start
  6.5 60.9 %all-gather.2.cloned.1.call-start = ((), (), s32[]{:S(2)}) async-start(), calls=%async_computation.2 | async-start | bytes 1310720 | tf_op jit(solution)/shard_map/all_gather | solution.py:32
  42.3 8.2 %copy-start.1 = (f32[1024]{0:T(1024)S(1)}, f32[1024]{0:T(1024)}, u32[]{:S(2)}) copy-start(f32[1024]{0:T(1024)} %param.7) | copy-start | bytes 12292
  49.8 56.8 %reduce-scatter.3.cloned.1.call-start = ((), (), s32[]{:S(2)}) async-start(), calls=%async_computation.3 | async-start | bytes 2621440 | tf_op jit(solution)/shard_map/reduce_scatter | solution.py:42
  50.5 24.6 %copy-start.2 = (s32[16]{0:T(128)S(1)}, s32[16]{0:T(128)}, u32[]{:S(2)}) copy-start(s32[16]{0:T(128)} %param.10) | copy-start | bytes 196
  75.0 109.1 %reduce-scatter.5.cloned.1.call-start = ((), (), s32[]{:S(2)}) async-start(), calls=%async_computation.4 | async-start | bytes 1179648 | tf_op jit(solution)/shard_map/reduce_scatter | solution.py:50
Sparse Core Ops, SparseCore 0:
  49.9 17.5 all-gather.1
  75.1 31.4 reduce-scatter.2
  120.6 63.4 reduce-scatter.4
where the time goes:
time: 192 us
  waiting for transfers between devices  112 us (58%)
  blocking collectives  34.7 us (18%)
  matrix products  15 us (8%)
  between operations  13.9 us (7%)
  local copies, waits for them, and re-layouts  13 us (7%)
  other arithmetic  3.84 us (2%)
    reduce_scatter x1, waiting for transfers between devices, local(): lax.psum_scatter(taken * found[:, None].astype(jnp.float32), 'obs', scatt...  63.6 us
    all_gather x1, blocking collectives, local(): piece = lax.all_gather(my_part, 'obs', axis=0, tiled=True)  34.7 us
    reduce_scatter x1, waiting for transfers between devices, local(): lax.psum_scatter(partial_prod, 'sub', scatter_dimension=1, tiled=True)  31.1 us
    all_gather x1, waiting for transfers between devices, local(): probe_cols = lax.all_gather(picked_part, 'sub', axis=1, tiled=True)  16.9 us
    gather x2, local copies, waits for them, and re-layouts, local(): taken = jnp.take(block_sum, source_rows, axis=0)  11.3 us
    dot_general x1, matrix products, local(): lax.dot_general(weighted, image, contract_rows, preferred_element_type=jn...  7.51 us
    dot_general x1, matrix products, local(): jnp.dot(selector, piece, preferred_element_type=jnp.float32)  7.47 us
  transfers between devices with their start and end apart: 3, of which 3 were waited for; matrix products, arithmetic and copies ran while one was open for 0% of the time, Pallas kernels for 0%

commit v1 on v0

v1 whole, which is shorter than its diff:
```python
import functools

import jax
import jax.numpy as jnp
from jax import lax
from jax.experimental import pallas as pl
from jax.experimental.pallas import tpu as pltpu
from jax.sharding import PartitionSpec as P

VMEM_LIMIT = 40 * 1024 * 1024


def swap(value, axis, count, step):
    return lax.ppermute(value, axis, [(i, i ^ step) for i in range(count)])


def pick_kernel(unit, tile, subs, obs_count, ids, lists, *refs):
    pieces, out, position = refs[:obs_count], refs[obs_count], refs[obs_count + 1]
    block = ids[0]
    listed = lists.shape[1]
    part = unit // subs
    units = pieces[0].shape[0] // part
    for a in range(position.shape[0]):
        position[a] = -1
    for k in range(listed):
        position[lists[block, k]] = k
    for step in range(obs_count):
        owner = block ^ step
        for u in range(units):
            row = (owner * units + u) * unit
            at = position[row // tile]
            inside = (row % tile) // subs

            @pl.when(at >= 0)
            def _():
                first = pl.multiple_of(at * (tile // subs) + inside, part)
                out[pl.ds(first, part), :] = pieces[step][u * part:(u + 1) * part, :]


def product_kernel(unit, tile, subs, ids, weight, jac, *refs):
    pieces, outs = refs[:subs], refs[subs:2 * subs]
    probe, image_t, weighted, product, held, sems = refs[2 * subs:]
    sub, count = ids[1], ids[2]
    rows, width = held.shape
    chunk = rows // sems.shape[0]
    copies = [
        pltpu.make_async_copy(jac.at[pl.ds(i * chunk, chunk)], held.at[pl.ds(i * chunk, chunk)], sems.at[i])
        for i in range(sems.shape[0])
    ]
    for copy in copies:
        copy.start()
    part = unit // subs
    for j in range(subs):
        other = sub ^ j
        for g in range(width // unit):
            first = pl.multiple_of(g * unit + other * part, part)
            probe[pl.ds(first, part), :] = pieces[j][g * part:(g + 1) * part, :]
    lanes = weight.shape[1]
    for i, copy in enumerate(copies):
        copy.wait()
        for r in range(i * chunk, (i + 1) * chunk, lanes):
            at = sub * rows + r + lax.broadcasted_iota(jnp.int32, (lanes, lanes), 0)
            scale = jnp.broadcast_to(weight[r // lanes:r // lanes + 1, :], (lanes, lanes)).T
            scale = scale * (at < count).astype(jnp.float32)
            scale = jnp.concatenate([scale] * (width // lanes), axis=1)
            weighted[r:r + lanes, :] = (held[r:r + lanes, :].astype(jnp.float32) * scale).astype(jnp.bfloat16)
        image = jnp.dot(held[i * chunk:(i + 1) * chunk, :], probe[...], preferred_element_type=jnp.float32)
        image_t[:, i * chunk:(i + 1) * chunk] = image.astype(jnp.bfloat16).T
    columns = 2 * tile

    @pl.loop(0, width // columns)
    def _(n):
        span = pl.ds(pl.multiple_of(n * columns, columns), columns)
        product[:, span] = jnp.dot(image_t[...], weighted[:, span], preferred_element_type=jnp.float32)

    high = product.shape[0] // subs
    for j in range(subs):
        first = pl.multiple_of((sub ^ j) * high, high)
        outs[j][...] = product[pl.ds(first, high), :].astype(outs[j].dtype)


def place_kernel(unit, tile, ids, lists, slots, *refs):
    parts, out, position, total = refs[:-3], refs[-3], refs[-2], refs[-1]
    block = ids[0]
    for a in range(position.shape[0]):
        position[a] = -1
    for k in range(lists.shape[1]):
        position[slots[lists[block, k]]] = k
    value = parts[0][...].astype(jnp.float32)
    for part in parts[1:]:
        value = value + part[...].astype(jnp.float32)
    total[...] = value
    units = out.shape[2] // unit
    for owner in range(out.shape[0]):
        for u in range(units):
            row = (owner * units + u) * unit
            at = position[row // tile]
            first = pl.multiple_of(jnp.maximum(at, 0) * tile, tile)
            taken = total[:, pl.ds(first, tile)]
            taken = jnp.where(at >= 0, taken, 0.0).astype(out.dtype)
            out[owner, :, u * unit:(u + 1) * unit] = taken[:, row % tile:row % tile + unit]


def local(obs_count, subs, jacobian, obs_weight, row_counts, tile_lists, tile_slot, probe_block):
    rows, width = jacobian.shape
    tiles = tile_slot.shape[0]
    tile = width // tile_lists.shape[1]
    own_rows, probe_width = probe_block.shape
    unit = min(own_rows, tile)
    part = unit // subs
    block, sub = lax.axis_index("obs"), lax.axis_index("sub")
    ids = jnp.stack([block, sub, row_counts[0]])
    smem, vmem = pl.BlockSpec(memory_space=pltpu.SMEM), pl.BlockSpec(memory_space=pltpu.VMEM)
    params = pltpu.CompilerParams(vmem_limit_bytes=VMEM_LIMIT)

    mine = probe_block.reshape(own_rows // unit, subs, part, probe_width)
    mine = lax.dynamic_index_in_dim(mine, sub, 1, keepdims=False).reshape(own_rows // subs, probe_width)
    pieces = [mine] + [swap(mine, "obs", obs_count, step) for step in range(1, obs_count)]
    picked = pl.pallas_call(
        functools.partial(pick_kernel, unit, tile, subs, obs_count),
        out_shape=jax.ShapeDtypeStruct((width // subs, probe_width), jnp.bfloat16),
        in_specs=[smem, smem] + [vmem] * obs_count,
        out_specs=vmem,
        scratch_shapes=[pltpu.SMEM((tiles,), jnp.int32)],
        compiler_params=params,
        name="pick_listed",
    )(ids, tile_lists, *pieces)

    columns = {0: picked}
    step = subs // 2
    while step:
        have = sorted(columns)
        got = swap(jnp.stack([columns[j] for j in have]), "sub", subs, step)
        for i, j in enumerate(have):
            columns[j ^ step] = got[i]
        step //= 2

    lanes = min(128, rows)
    high = probe_width // subs
    partial = pl.pallas_call(
        functools.partial(product_kernel, unit, tile, subs),
        out_shape=[jax.ShapeDtypeStruct((high, width), jnp.float32 if j == 0 else jnp.bfloat16) for j in range(subs)],
        in_specs=[smem, vmem, pl.BlockSpec(memory_space=pl.ANY)] + [vmem] * subs,
        out_specs=[vmem] * subs,
        scratch_shapes=[
            pltpu.VMEM((width, probe_width), jnp.bfloat16),
            pltpu.VMEM((probe_width, rows), jnp.bfloat16),
            pltpu.VMEM((rows, width), jnp.bfloat16),
            pltpu.VMEM((probe_width, width), jnp.float32),
            pltpu.VMEM((rows, width), jnp.bfloat16),
            pltpu.SemaphoreType.DMA((4,)),
        ],
        compiler_params=params,
        name="product",
    )(ids, obs_weight.reshape(rows // lanes, lanes), jacobian, *[columns[j] for j in range(subs)])

    arrived = [partial[0]] + [swap(partial[j], "sub", subs, j) for j in range(1, subs)]
    placed = pl.pallas_call(
        functools.partial(place_kernel, unit, tile),
        out_shape=jax.ShapeDtypeStruct((obs_count, high, own_rows), jnp.bfloat16),
        in_specs=[smem] * 3 + [vmem] * subs,
        out_specs=vmem,
        scratch_shapes=[pltpu.SMEM((tiles,), jnp.int32), pltpu.VMEM((high, width), jnp.float32)],
        compiler_params=params,
        name="place",
    )(ids, tile_lists, tile_slot, *arrived)
    shares = lax.all_to_all(placed, "obs", 0, 0, tiled=True)
    summed = jnp.sum(shares.astype(jnp.float32), axis=0)
    return summed.T.astype(jnp.bfloat16)


def solution(mesh):
    placed = (P(("obs", "sub"), None), P(("obs", "sub")), P("obs"), P(), P(), P("obs", None))
    return jax.shard_map(
        functools.partial(local, mesh.shape["obs"], mesh.shape["sub"]),
        mesh=mesh, in_specs=placed, out_specs=P("obs", "sub"), check_vma=False,
    )
```

time: 192 us -> 73.3 us (0.38)
  waiting for transfers between devices: 112 us -> 23.8 us
  starting transfers between devices: 0.09 us -> 16.1 us
  blocking collectives: 34.7 us -> 19.1 us
  matrix products: 15 us -> 0 us
  between operations: 13.9 us -> 0.72 us
  local copies, waits for them, and re-layouts: 13 us -> 4.55 us
  Pallas kernels: 0 us -> 7.84 us
  other arithmetic: 3.84 us -> 0.83 us
    reduce_scatter x2 -> x0, waiting for transfers between devices: 94.7 us -> none  [the longest x1 63.6 us: local(): lax.psum_scatter(taken * found[:, None].astype(jnp.float32), 'obs', scatt...]
    all_gather x1 -> x0, blocking collectives: 34.7 us -> none  [local(): piece = lax.all_gather(my_part, 'obs', axis=0, tiled=True)]
    ppermute x0 -> x12, waiting for transfers between devices: none -> 23.8 us  [swap(): return lax.ppermute(value, axis, [(i, i ^ step) for i in range(count)])]
    all_to_all x0 -> x1, blocking collectives: none -> 19.1 us  [local(): shares = lax.all_to_all(placed, 'obs', 0, 0, tiled=True)]
    all_gather x1 -> x0, waiting for transfers between devices: 16.9 us -> none  [local(): probe_cols = lax.all_gather(picked_part, 'sub', axis=1, tiled=True)]
    ppermute x0 -> x12, starting transfers between devices: none -> 16.1 us  [swap(): return lax.ppermute(value, axis, [(i, i ^ step) for i in range(count)])]
    dot_general x2 -> x0, matrix products: 15 us -> none  [the longest x1 7.51 us: local(): lax.dot_general(weighted, image, contract_rows, preferred_element_type=jn...]
    gather x2 -> x0, local copies, waits for them, and re-layouts: 11.3 us -> none  [local(): taken = jnp.take(block_sum, source_rows, axis=0)]
  transfers between devices with their start and end apart: 3 -> 12, of which waited for: 3 -> 8; matrix products, arithmetic and copies ran while one was open for 0% -> 0% of each run, Pallas kernels for 0% -> 0%
where the time goes in v1:
time: 73.3 us; the launch traced here: 73 us
  waiting for transfers between devices  23.8 us (32%)
  blocking collectives  19.1 us (26%)
  starting transfers between devices  16.1 us (22%)
  Pallas kernels  7.84 us (11%)
  local copies, waits for them, and re-layouts  4.55 us (6%)
  other arithmetic  0.83 us (1%)
    ppermute x12, waiting for transfers between devices, swap(): return lax.ppermute(value, axis, [(i, i ^ step) for i in range(count)])  23.8 us
    all_to_all x1, blocking collectives, local(): shares = lax.all_to_all(placed, 'obs', 0, 0, tiled=True)  19.1 us
    ppermute x12, starting transfers between devices, swap(): return lax.ppermute(value, axis, [(i, i ^ step) for i in range(count)])  16.1 us
    pallas_call x1, Pallas kernels, local(): pl.pallas_call(functools.partial(product_kernel, unit, tile, subs), out_s...  6.07 us
    unnamed x12, local copies, waits for them, and re-layouts  4.51 us
  transfers between devices with their start and end apart: 12, of which 8 were waited for; matrix products, arithmetic and copies ran while one was open for 0% of the time, Pallas kernels for 0%

profile of v1, /device:TPU:0, one launch (start us, length us, event | category | flops | bytes accessed | tf_op | source)
XLA Modules:
  0.0 73.0 jit_solution(6142990081326551479)
XLA Ops:
  0.0 0.0 copy-start
  0.0 0.0 copy-start.3
  0.0 0.0 copy-start.5
  0.0 0.9 %copy-done = bf16[512,256]{1,0:T(8,128)(2,1)S(1)} copy-done((bf16[512,256]{1,0:T(8,128)(2,1)S(1)}, bf16[512,256]{1,0:T(8,128)(2,1)}, u32[]{:S(2)}) %copy-start) | copy-done | bytes 262168
  1.0 6.0 %collective-permute-start.6 = (bf16[128,256]{1,0:T(8,128)(2,1)S(1)}, bf16[128,256]{1,0:T(8,128)(2,1)S(1)}, u32[]{:S(2)}, u32[]{:S(2)}) collective-permute-start(bf16[128,256]{1,0:T(8,128)(2,1)S(1)} %bitcast.18), channel_id=1, source_target_pairs={{0,28},{4,24},{8,20},{12,16},{16,12},{20,8},{24,4},{28,0},{1,29},{... | collective-permute-start | bytes 196616 | tf_op jit(solution)/shard_map/ppermute | solution.py:14
  6.9 0.2 collective-permute-start.5
  7.2 0.8 %collective-permute-start.4 = (bf16[128,256]{1,0:T(8,128)(2,1)S(1)}, bf16[128,256]{1,0:T(8,128)(2,1)S(1)}, u32[]{:S(2)}, u32[]{:S(2)}) collective-permute-start(bf16[128,256]{1,0:T(8,128)(2,1)S(1)} %bitcast.20), channel_id=1, source_target_pairs={{0,20},{4,16},{8,28},{12,24},{16,4},{20,0},{24,12},{28,8},{1,21},{... | collective-permute-start | bytes 196616 | tf_op jit(solution)/shard_map/ppermute | solution.py:14
  7.9 2.0 %collective-permute-start.3 = (bf16[128,256]{1,0:T(8,128)(2,1)S(1)}, bf16[128,256]{1,0:T(8,128)(2,1)S(1)}, u32[]{:S(2)}, u32[]{:S(2)}) collective-permute-start(bf16[128,256]{1,0:T(8,128)(2,1)S(1)} %bitcast.21), channel_id=1, source_target_pairs={{0,16},{4,20},{8,24},{12,28},{16,0},{20,4},{24,8},{28,12},{1,17},{... | collective-permute-start | bytes 196616 | tf_op jit(solution)/shard_map/ppermute | solution.py:14
  9.9 2.3 %collective-permute-start.2 = (bf16[128,256]{1,0:T(8,128)(2,1)S(1)}, bf16[128,256]{1,0:T(8,128)(2,1)S(1)}, u32[]{:S(2)}, u32[]{:S(2)}) collective-permute-start(bf16[128,256]{1,0:T(8,128)(2,1)S(1)} %bitcast.22), channel_id=1, source_target_pairs={{0,12},{4,8},{8,4},{12,0},{16,28},{20,24},{24,20},{28,16},{1,13},{... | collective-permute-start | bytes 196616 | tf_op jit(solution)/shard_map/ppermute | solution.py:14
  12.9 0.0 collective-permute-done.6.refs_7_
  12.9 0.8 %collective-permute-start.1 = (bf16[128,256]{1,0:T(8,128)(2,1)S(1)}, bf16[128,256]{1,0:T(8,128)(2,1)S(1)}, u32[]{:S(2)}, u32[]{:S(2)}) collective-permute-start(bf16[128,256]{1,0:T(8,128)(2,1)S(1)} %bitcast.23), channel_id=1, source_target_pairs={{0,8},{4,12},{8,0},{12,4},{16,24},{20,28},{24,16},{28,20},{1,9},{5... | collective-permute-start | bytes 196616 | tf_op jit(solution)/shard_map/ppermute | solution.py:14
  13.7 0.0 collective-permute-done.5.refs_6_
  13.7 0.4 collective-permute-start
  14.2 0.1 pad_add_fusion.ids
  14.2 2.4 %collective-permute-done.4.refs_5_ = bf16[128,256]{1,0:T(8,128)(2,1)S(1)} collective-permute-done((bf16[128,256]{1,0:T(8,128)(2,1)S(1)}, bf16[128,256]{1,0:T(8,128)(2,1)S(1)}, u32[]{:S(2)}, u32[]{:S(2)}) %collective-permute-start.4) | collective-permute-done | bytes 65568 | tf_op jit(solution)/shard_map/ppermute | solution.py:14
  16.6 1.6 %collective-permute-done.3.refs_4_ = bf16[128,256]{1,0:T(8,128)(2,1)S(1)} collective-permute-done((bf16[128,256]{1,0:T(8,128)(2,1)S(1)}, bf16[128,256]{1,0:T(8,128)(2,1)S(1)}, u32[]{:S(2)}, u32[]{:S(2)}) %collective-permute-start.3) | collective-permute-done | bytes 65568 | tf_op jit(solution)/shard_map/ppermute | solution.py:14
  18.2 0.1 collective-permute-done.2.refs_3_
  18.3 0.6 collective-permute-done.1.refs_2_
  18.9 0.0 collective-permute-done.refs_1_
  18.9 0.0 copy-start.2
  18.9 0.7 copy-done.2
  19.6 0.9 %pick_listed.1.refs_0_ = bf16[512,256]{1,0:T(8,128)(2,1)S(1)} custom-call(s32[3]{0:T(128)S(1)} %pad_add_fusion.ids, s32[8,8]{1,0:T(8,128)S(1)} %copy-done.2, bf16[128,256]{1,0:T(8,128)(2,1)S(1)} %bitcast.25, bf16[128,256]{1,0:T(8,128)(2,1)S(1)} %collective-permute-done.refs_1_, bf16[128,256]{1,0:T(8,128)(2,1)S(1)} %collective-permute-done.1.refs_2_, ...), custom_call_target="tpu_custom_call" | custom-call | tf_op jit(solution)/shard_map/pick_listed/pallas_call | solution.py:119
  20.5 1.6 %collective-permute-start.7 = (bf16[1,512,256]{2,1,0:T(8,128)(2,1)S(1)}, bf16[1,512,256]{2,1,0:T(8,128)(2,1)S(1)}, u32[]{:S(2)}, u32[]{:S(2)}) collective-permute-start(bf16[1,512,256]{2,1,0:T(8,128)(2,1)S(1)} %bitcast.15), channel_id=1, source_target_pairs={{0,2},{1,3},{2,0},{3,1},{4,6},{5,7},{6,4},{7,5},{8,10},{9,11},{10,... | collective-permute-start | bytes 786440 | tf_op jit(solution)/shard_map/ppermute | solution.py:14
  22.0 5.4 %collective-permute-done.7 = bf16[1,512,256]{2,1,0:T(8,128)(2,1)S(1)} collective-permute-done((bf16[1,512,256]{2,1,0:T(8,128)(2,1)S(1)}, bf16[1,512,256]{2,1,0:T(8,128)(2,1)S(1)}, u32[]{:S(2)}, u32[]{:S(2)}) %collective-permute-start.7) | collective-permute-done | bytes 262176 | tf_op jit(solution)/shard_map/ppermute | solution.py:14
  27.4 0.1 pad_maximum_fusion
  27.5 0.1 collective-permute-start.8
  27.5 1.9 %collective-permute-done.8 = bf16[2,512,256]{2,1,0:T(8,128)(2,1)S(1)} collective-permute-done((bf16[2,512,256]{2,1,0:T(8,128)(2,1)S(1)}, bf16[2,512,256]{2,1,0:T(8,128)(2,1)S(1)}, u32[]{:S(2)}, u32[]{:S(2)}) %collective-permute-start.8) | collective-permute-done | bytes 524320 | tf_op jit(solution)/shard_map/ppermute | solution.py:14
  29.5 0.0 copy-start.1
  29.5 2.2 %copy-done.1 = bf16[1024,2048]{1,0:T(8,128)(2,1)S(1)} copy-done((bf16[1024,2048]{1,0:T(8,128)(2,1)S(1)}, bf16[1024,2048]{1,0:T(8,128)(2,1)}, u32[]{:S(2)}) %copy-start.1) | copy-done | bytes 4194328
  31.7 0.0 copy-start.4
  31.7 0.7 copy-done.4
  32.4 6.1 %product.1 = (f32[64,2048]{1,0:T(8,128)S(1)}, bf16[64,2048]{1,0:T(8,128)(2,1)S(1)}, bf16[64,2048]{1,0:T(8,128)(2,1)S(1)}, bf16[64,2048]{1,0:T(8,128)(2,1)S(1)}) custom-call(s32[3]{0:T(128)S(1)} %pad_add_fusion.ids, f32[8,128]{1,0:T(8,128)S(1)} %bitcast.26, bf16[1024,2048]{1,0:T(8,128)(2,1)S(1)} %copy-done.1, bf16[512,256]{1,0:T(8,128)(2,1)S(1)} %pick_listed.1.refs_0_, ...), custom_call_target="tpu_custom_call" | custom-call | tf_op jit(solution)/shard_map/product/pallas_call | solution.py:140
  38.4 0.2 collective-permute-start.9
  38.6 1.5 %collective-permute-start.10 = (bf16[64,2048]{1,0:T(8,128)(2,1)S(1)}, bf16[64,2048]{1,0:T(8,128)(2,1)S(1)}, u32[]{:S(2)}, u32[]{:S(2)}) collective-permute-start(bf16[64,2048]{1,0:T(8,128)(2,1)S(1)} %get-tuple-element.11), channel_id=1, source_target_pairs={{0,2},{1,3},{2,0},{3,1},{4,6},{5,7},{6,4},{7,5},{8,10},{9,11},{10,... | collective-permute-start | bytes 786440 | tf_op jit(solution)/shard_map/ppermute | solution.py:14
  40.2 0.2 collective-permute-start.11
  40.4 0.0 collective-permute-done.9.refs_1_
  40.4 7.4 %collective-permute-done.10.refs_2_ = bf16[64,2048]{1,0:T(8,128)(2,1)S(1)} collective-permute-done((bf16[64,2048]{1,0:T(8,128)(2,1)S(1)}, bf16[64,2048]{1,0:T(8,128)(2,1)S(1)}, u32[]{:S(2)}, u32[]{:S(2)}) %collective-permute-start.10) | collective-permute-done | bytes 262176 | tf_op jit(solution)/shard_map/ppermute | solution.py:14
  47.8 4.5 %collective-permute-done.11.refs_3_ = bf16[64,2048]{1,0:T(8,128)(2,1)S(1)} collective-permute-done((bf16[64,2048]{1,0:T(8,128)(2,1)S(1)}, bf16[64,2048]{1,0:T(8,128)(2,1)S(1)}, u32[]{:S(2)}, u32[]{:S(2)}) %collective-permute-start.11) | collective-permute-done | bytes 262176 | tf_op jit(solution)/shard_map/ppermute | solution.py:14
  52.3 0.0 copy-done.3
  52.3 0.0 copy-done.5
  52.3 0.9 %place.1 = bf16[8,64,512]{2,1,0:T(8,128)(2,1)S(1)} custom-call(s32[3]{0:T(128)S(1)} %pad_add_fusion.ids, s32[8,8]{1,0:T(8,128)S(1)} %copy-done.3, s32[16]{0:T(128)S(1)} %copy-done.5, f32[64,2048]{1,0:T(8,128)S(1)} %get-tuple-element.9.refs_0_, bf16[64,2048]{1,0:T(8,128)(2,1)S(1)} %collective-permute-done.9.refs_1_, ...), custom_call_target="tpu_custom_call" | custom-call | tf_op jit(solution)/shard_map/place/pallas_call | solution.py:158
  53.2 19.1 %all_to_all.5 = bf16[8,64,512]{2,1,0:T(8,128)(2,1)S(1)} all-to-all(bf16[8,64,512]{2,1,0:T(8,128)(2,1)S(1)} %place.1), channel_id=1, replica_groups=mesh['obs'=8,'sub'=4] {'obs'}, dimensions={0} | all-to-all | bytes 1048576 | tf_op jit(solution)/shard_map/all_to_all | solution.py:167
  72.3 0.7 reduce_sum.12
  (2 shorter events, 0.0 us)
Async XLA Ops:
  0.0 1.0 %copy-start = (bf16[512,256]{1,0:T(8,128)(2,1)S(1)}, bf16[512,256]{1,0:T(8,128)(2,1)}, u32[]{:S(2)}) copy-start(bf16[512,256]{1,0:T(8,128)(2,1)} %param.11) | copy-start | bytes 786436
  0.0 52.3 %copy-start.3 = (s32[8,8]{1,0:T(8,128)S(1)}, s32[8,8]{1,0:T(8,128)}, u32[]{:S(2)}) copy-start(s32[8,8]{1,0:T(8,128)} %lists.3) | copy-start | bytes 772
  0.0 52.3 %copy-start.5 = (s32[16]{0:T(128)S(1)}, s32[16]{0:T(128)}, u32[]{:S(2)}) copy-start(s32[16]{0:T(128)} %slots.1) | copy-start | bytes 196
  1.0 11.9 %collective-permute-start.6 = (bf16[128,256]{1,0:T(8,128)(2,1)S(1)}, bf16[128,256]{1,0:T(8,128)(2,1)S(1)}, u32[]{:S(2)}, u32[]{:S(2)}) collective-permute-start(bf16[128,256]{1,0:T(8,128)(2,1)S(1)} %bitcast.18), channel_id=1, source_target_pairs={{0,28},{4,24},{8,20},{12,16},{16,12},{20,8},{24,4},{28,0},{1,29},{... | collective-permute-start | bytes 196616 | tf_op jit(solution)/shard_map/ppermute | solution.py:14
  6.9 6.8 %collective-permute-start.5 = (bf16[128,256]{1,0:T(8,128)(2,1)S(1)}, bf16[128,256]{1,0:T(8,128)(2,1)S(1)}, u32[]{:S(2)}, u32[]{:S(2)}) collective-permute-start(bf16[128,256]{1,0:T(8,128)(2,1)S(1)} %bitcast.19), channel_id=1, source_target_pairs={{0,24},{4,28},{8,16},{12,20},{16,8},{20,12},{24,0},{28,4},{1,25},{... | collective-permute-start | bytes 196616 | tf_op jit(solution)/shard_map/ppermute | solution.py:14
  7.2 9.5 %collective-permute-start.4 = (bf16[128,256]{1,0:T(8,128)(2,1)S(1)}, bf16[128,256]{1,0:T(8,128)(2,1)S(1)}, u32[]{:S(2)}, u32[]{:S(2)}) collective-permute-start(bf16[128,256]{1,0:T(8,128)(2,1)S(1)} %bitcast.20), channel_id=1, source_target_pairs={{0,20},{4,16},{8,28},{12,24},{16,4},{20,0},{24,12},{28,8},{1,21},{... | collective-permute-start | bytes 196616 | tf_op jit(solution)/shard_map/ppermute | solution.py:14
  7.9 10.3 %collective-permute-start.3 = (bf16[128,256]{1,0:T(8,128)(2,1)S(1)}, bf16[128,256]{1,0:T(8,128)(2,1)S(1)}, u32[]{:S(2)}, u32[]{:S(2)}) collective-permute-start(bf16[128,256]{1,0:T(8,128)(2,1)S(1)} %bitcast.21), channel_id=1, source_target_pairs={{0,16},{4,20},{8,24},{12,28},{16,0},{20,4},{24,8},{28,12},{1,17},{... | collective-permute-start | bytes 196616 | tf_op jit(solution)/shard_map/ppermute | solution.py:14
  9.9 8.3 %collective-permute-start.2 = (bf16[128,256]{1,0:T(8,128)(2,1)S(1)}, bf16[128,256]{1,0:T(8,128)(2,1)S(1)}, u32[]{:S(2)}, u32[]{:S(2)}) collective-permute-start(bf16[128,256]{1,0:T(8,128)(2,1)S(1)} %bitcast.22), channel_id=1, source_target_pairs={{0,12},{4,8},{8,4},{12,0},{16,28},{20,24},{24,20},{28,16},{1,13},{... | collective-permute-start | bytes 196616 | tf_op jit(solution)/shard_map/ppermute | solution.py:14
  12.9 6.0 %collective-permute-start.1 = (bf16[128,256]{1,0:T(8,128)(2,1)S(1)}, bf16[128,256]{1,0:T(8,128)(2,1)S(1)}, u32[]{:S(2)}, u32[]{:S(2)}) collective-permute-start(bf16[128,256]{1,0:T(8,128)(2,1)S(1)} %bitcast.23), channel_id=1, source_target_pairs={{0,8},{4,12},{8,0},{12,4},{16,24},{20,28},{24,16},{28,20},{1,9},{5... | collective-permute-start | bytes 196616 | tf_op jit(solution)/shard_map/ppermute | solution.py:14
  13.7 5.1 %collective-permute-start = (bf16[128,256]{1,0:T(8,128)(2,1)S(1)}, bf16[128,256]{1,0:T(8,128)(2,1)S(1)}, u32[]{:S(2)}, u32[]{:S(2)}) collective-permute-start(bf16[128,256]{1,0:T(8,128)(2,1)S(1)} %bitcast.24), channel_id=1, source_target_pairs={{0,4},{4,0},{8,12},{12,8},{16,20},{20,16},{24,28},{28,24},{1,5},{5... | collective-permute-start | bytes 196616 | tf_op jit(solution)/shard_map/ppermute | solution.py:14
  18.9 0.7 copy-start.2
  20.5 6.9 %collective-permute-start.7 = (bf16[1,512,256]{2,1,0:T(8,128)(2,1)S(1)}, bf16[1,512,256]{2,1,0:T(8,128)(2,1)S(1)}, u32[]{:S(2)}, u32[]{:S(2)}) collective-permute-start(bf16[1,512,256]{2,1,0:T(8,128)(2,1)S(1)} %bitcast.15), channel_id=1, source_target_pairs={{0,2},{1,3},{2,0},{3,1},{4,6},{5,7},{6,4},{7,5},{8,10},{9,11},{10,... | collective-permute-start | bytes 786440 | tf_op jit(solution)/shard_map/ppermute | solution.py:14
  27.5 2.0 %collective-permute-start.8 = (bf16[2,512,256]{2,1,0:T(8,128)(2,1)S(1)}, bf16[2,512,256]{2,1,0:T(8,128)(2,1)S(1)}, u32[]{:S(2)}, u32[]{:S(2)}) collective-permute-start(bf16[2,512,256]{2,1,0:T(8,128)(2,1)S(1)} %pad_maximum_fusion), channel_id=1, source_target_pairs={{0,1},{1,0},{2,3},{3,2},{4,5},{5,4},{6,7},{7,6},{8,9},{9,8},{10,11... | collective-permute-start | bytes 1572872 | tf_op jit(solution)/shard_map/ppermute | solution.py:14
  29.5 2.2 %copy-start.1 = (bf16[1024,2048]{1,0:T(8,128)(2,1)S(1)}, bf16[1024,2048]{1,0:T(8,128)(2,1)}, u32[]{:S(2)}) copy-start(bf16[1024,2048]{1,0:T(8,128)(2,1)} %jac.1) | copy-start | bytes 12582916
  31.7 0.7 copy-start.4
  38.4 1.9 %collective-permute-start.9 = (bf16[64,2048]{1,0:T(8,128)(2,1)S(1)}, bf16[64,2048]{1,0:T(8,128)(2,1)S(1)}, u32[]{:S(2)}, u32[]{:S(2)}) collective-permute-start(bf16[64,2048]{1,0:T(8,128)(2,1)S(1)} %get-tuple-element.10), channel_id=1, source_target_pairs={{0,1},{1,0},{2,3},{3,2},{4,5},{5,4},{6,7},{7,6},{8,9},{9,8},{10,11... | collective-permute-start | bytes 786440 | tf_op jit(solution)/shard_map/ppermute | solution.py:14
  38.6 9.1 %collective-permute-start.10 = (bf16[64,2048]{1,0:T(8,128)(2,1)S(1)}, bf16[64,2048]{1,0:T(8,128)(2,1)S(1)}, u32[]{:S(2)}, u32[]{:S(2)}) collective-permute-start(bf16[64,2048]{1,0:T(8,128)(2,1)S(1)} %get-tuple-element.11), channel_id=1, source_target_pairs={{0,2},{1,3},{2,0},{3,1},{4,6},{5,7},{6,4},{7,5},{8,10},{9,11},{10,... | collective-permute-start | bytes 786440 | tf_op jit(solution)/shard_map/ppermute | solution.py:14
  40.2 12.1 %collective-permute-start.11 = (bf16[64,2048]{1,0:T(8,128)(2,1)S(1)}, bf16[64,2048]{1,0:T(8,128)(2,1)S(1)}, u32[]{:S(2)}, u32[]{:S(2)}) collective-permute-start(bf16[64,2048]{1,0:T(8,128)(2,1)S(1)} %get-tuple-element.12), channel_id=1, source_target_pairs={{0,3},{1,2},{2,1},{3,0},{4,7},{5,6},{6,5},{7,4},{8,11},{9,10},{10,... | collective-permute-start | bytes 786440 | tf_op jit(solution)/shard_map/ppermute | solution.py:14

commit v2 on v0

v2 whole, which is shorter than its diff:
```python
import functools

import jax
import jax.numpy as jnp
from jax import lax
from jax.experimental import pallas as pl
from jax.experimental.pallas import tpu as pltpu
from jax.sharding import PartitionSpec as P

CHUNKS = 2
MIB = 1024 * 1024
SMEM = pl.BlockSpec(memory_space=pltpu.SMEM)
VMEM = pl.BlockSpec(memory_space=pltpu.VMEM)
HBM = pl.BlockSpec(memory_space=pltpu.HBM)


def swap(value, axis, count, step):
    return lax.ppermute(value, axis, [(i, i ^ step) for i in range(count)])


def far_steps(count):
    return [2 * high for high in range(count // 2 - 1, 0, -1)]


def spread(value, axis, count):
    held = {0: value}
    for step in far_steps(count):
        held[step] = swap(value, axis, count, step)
    held[1] = swap(value, axis, count, 1)
    for step in far_steps(count):
        held[step + 1] = swap(held[step], axis, count, 1)
    return [held[step] for step in range(count)]


def collect(terms, axis, count):
    parts = [terms[0]]
    for step in far_steps(count):
        passed = swap(terms[step + 1], axis, count, 1)
        both = (terms[step] + passed.astype(jnp.float32)).astype(jnp.bfloat16)
        parts.append(swap(both, axis, count, step))
    parts.append(swap(terms[1], axis, count, 1))
    return parts


def split_kernel(unit, subs, probe, *refs):
    outs, rows, sems = refs[:-2], refs[-2], refs[-1]
    sub = lax.axis_index("sub")
    part = unit // subs
    copies = [
        pltpu.make_async_copy(
            probe.at[pl.ds(pl.multiple_of(u * unit + sub * part, part), part)],
            rows.at[pl.ds(u * part, part)], sems.at[u])
        for u in range(sems.shape[0])
    ]
    for copy in copies:
        copy.start()
    width = rows.shape[1]
    lanes = width // len(outs)
    high, low = width // subs, lanes // subs
    source = lax.broadcasted_iota(jnp.int32, (width, lanes), 0)
    target = lax.broadcasted_iota(jnp.int32, (width, lanes), 1)
    wanted = (target // low) * high + target % low
    chosen = [(source == wanted + c * low).astype(jnp.bfloat16) for c in range(len(outs))]
    for copy in copies:
        copy.wait()
    for c, out in enumerate(outs):
        out[...] = jnp.dot(rows[...], chosen[c], preferred_element_type=jnp.float32).astype(out.dtype)


def weigh_kernel(count, weight, jac, held, weighted, sems):
    rows, width = held.shape
    chunk = rows // sems.shape[0]
    copies = [
        pltpu.make_async_copy(jac.at[pl.ds(i * chunk, chunk)], held.at[pl.ds(i * chunk, chunk)], sems.at[i])
        for i in range(sems.shape[0])
    ]
    for copy in copies:
        copy.start()
    sub = lax.axis_index("sub")
    lanes = weight.shape[1]
    for i, copy in enumerate(copies):
        copy.wait()
        for r in range(i * chunk, (i + 1) * chunk, lanes):
            at = sub * rows + r + lax.broadcasted_iota(jnp.int32, (lanes, lanes), 0)
            scale = jnp.broadcast_to(weight[r // lanes:r // lanes + 1, :], (lanes, lanes)).T
            scale = scale * (at < count[0]).astype(jnp.float32)
            scale = jnp.concatenate([scale] * (width // lanes), axis=1)
            weighted[r:r + lanes, :] = (held[r:r + lanes, :].astype(jnp.float32) * scale).astype(jnp.bfloat16)


def pick_kernel(unit, tile, subs, listed, info, *refs):
    pieces, out, position = refs[:-2], refs[-2], refs[-1]
    block = lax.axis_index("obs")
    part = unit // subs
    units = pieces[0].shape[0] // part
    for a in range(position.shape[0]):
        position[a] = -1
    for k in range(listed):
        position[info[k]] = k
    for step, piece in enumerate(pieces):
        for u in range(units):
            row = ((block ^ step) * units + u) * unit
            at = position[row // tile]

            @pl.when(at >= 0)
            def _():
                first = pl.multiple_of(at * (tile // subs) + (row % tile) // subs, part)
                out[pl.ds(first, part), :] = piece[u * part:(u + 1) * part, :]


def product_kernel(unit, subs, held, weighted, *refs):
    pieces, outs = refs[:subs], refs[subs:2 * subs]
    probe, product = refs[2 * subs:]
    sub = lax.axis_index("sub")
    width = held.shape[1]
    part = unit // subs
    for j in range(subs):
        for g in range(width // unit):
            first = pl.multiple_of(g * unit + (sub ^ j) * part, part)
            probe[pl.ds(first, part), :] = pieces[j][g * part:(g + 1) * part, :]
    image = jnp.dot(held[...], probe[...], preferred_element_type=jnp.float32)
    image_t = image.astype(jnp.bfloat16).T
    product[...] = jnp.dot(image_t, weighted[...], preferred_element_type=jnp.float32)
    high = product.shape[0] // subs
    for j in range(subs):
        first = pl.multiple_of((sub ^ j) * high, high)
        outs[j][...] = product[pl.ds(first, high), :].astype(outs[j].dtype)


def place_kernel(unit, tile, listed, parts_count, info, *refs):
    parts, outs = refs[:parts_count], refs[parts_count:-2]
    position, total = refs[-2:]
    block = lax.axis_index("obs")
    for a in range(position.shape[0]):
        position[a] = -1
    for k in range(listed):
        position[info[listed + info[k]]] = k
    value = parts[0][...]
    for term in parts[1:]:
        value = value + term[...].astype(jnp.float32)
    total[...] = value
    units = outs[0].shape[1] // unit
    for step, out in enumerate(outs):
        for u in range(units):
            row = ((block ^ step) * units + u) * unit
            at = position[row // tile]
            first = pl.multiple_of(jnp.maximum(at, 0) * tile, tile)
            whole = jnp.where(at >= 0, total[:, pl.ds(first, tile)], 0.0)
            taken = whole[:, :unit]
            for q in range(1, tile // unit):
                taken = jnp.where(row % tile == q * unit, whole[:, q * unit:(q + 1) * unit], taken)
            out[:, u * unit:(u + 1) * unit] = taken.astype(out.dtype)


def kept(step):
    return jnp.float32 if step % 2 == 0 else jnp.bfloat16


def local(obs_count, subs, jacobian, obs_weight, row_counts, tile_lists, tile_slot, probe_block):
    rows, width = jacobian.shape
    tiles = tile_slot.shape[0]
    listed = tile_lists.shape[1]
    tile = width // listed
    own_rows, probe_width = probe_block.shape
    unit = min(own_rows, tile)
    lanes = probe_width // CHUNKS
    high = lanes // subs
    my_list = lax.dynamic_index_in_dim(tile_lists, lax.axis_index("obs"), 0, keepdims=False)
    info = jnp.concatenate([my_list, tile_slot])

    def params(mib):
        return pltpu.CompilerParams(vmem_limit_bytes=mib * MIB)

    shares = pl.pallas_call(
        functools.partial(split_kernel, unit, subs),
        out_shape=[jax.ShapeDtypeStruct((own_rows // subs, lanes), jnp.bfloat16)] * CHUNKS,
        in_specs=[HBM],
        out_specs=[VMEM] * CHUNKS,
        scratch_shapes=[
            pltpu.VMEM((own_rows // subs, probe_width), jnp.bfloat16),
            pltpu.SemaphoreType.DMA((own_rows // unit,)),
        ],
        compiler_params=params(8),
        name="split_probe",
    )(probe_block)
    weight_lanes = min(128, rows)
    held, weighted = pl.pallas_call(
        weigh_kernel,
        out_shape=[jax.ShapeDtypeStruct((rows, width), jnp.bfloat16)] * 2,
        in_specs=[SMEM, VMEM, HBM],
        out_specs=[VMEM, VMEM],
        scratch_shapes=[pltpu.SemaphoreType.DMA((4,))],
        compiler_params=params(16),
        cost_estimate=pl.CostEstimate(flops=2 * rows * width, bytes_accessed=6 * rows * width, transcendentals=0),
        name="weigh",
    )(row_counts, obs_weight.reshape(rows // weight_lanes, weight_lanes), jacobian)

    pick = pl.pallas_call(
        functools.partial(pick_kernel, unit, tile, subs, listed),
        out_shape=jax.ShapeDtypeStruct((width // subs, lanes), jnp.bfloat16),
        in_specs=[SMEM] + [VMEM] * obs_count,
        out_specs=VMEM,
        scratch_shapes=[pltpu.SMEM((tiles,), jnp.int32)],
        compiler_params=params(8),
        name="pick_listed",
    )
    product = pl.pallas_call(
        functools.partial(product_kernel, unit, subs),
        out_shape=[jax.ShapeDtypeStruct((high, width), kept(j)) for j in range(subs)],
        in_specs=[VMEM] * (2 + subs),
        out_specs=[VMEM] * subs,
        scratch_shapes=[
            pltpu.VMEM((width, lanes), jnp.bfloat16),
            pltpu.VMEM((lanes, width), jnp.float32),
        ],
        compiler_params=params(24),
        cost_estimate=pl.CostEstimate(
            flops=4 * rows * width * lanes, bytes_accessed=4 * rows * width, transcendentals=0),
        name="product",
    )
    place = pl.pallas_call(
        functools.partial(place_kernel, unit, tile, listed, subs // 2 + 1),
        out_shape=[jax.ShapeDtypeStruct((high, own_rows), kept(step)) for step in range(obs_count)],
        in_specs=[SMEM] + [VMEM] * (subs // 2 + 1),
        out_specs=[VMEM] * obs_count,
        scratch_shapes=[pltpu.SMEM((tiles,), jnp.int32), pltpu.VMEM((high, width), jnp.float32)],
        compiler_params=params(8),
        name="place",
    )

    pieces = [spread(share, "obs", obs_count) for share in shares]
    columns = [spread(pick(info, *piece), "sub", subs) for piece in pieces]
    partial = [product(held, weighted, *column) for column in columns]
    blocks = [collect(terms, "sub", subs) for terms in partial]
    placed = [collect(place(info, *terms), "obs", obs_count) for terms in blocks]
    sums = [sum(term.astype(jnp.float32) for term in terms).astype(jnp.bfloat16) for terms in placed]
    return jnp.concatenate(sums, axis=0).T


def solution(mesh):
    placed = (P(("obs", "sub"), None), P(("obs", "sub")), P("obs"), P(), P(), P("obs", None))
    return jax.shard_map(
        functools.partial(local, mesh.shape["obs"], mesh.shape["sub"]),
        mesh=mesh, in_specs=placed, out_specs=P("obs", "sub"), check_vma=False,
    )
```

time: 192 us -> 74.4 us (0.39)
  waiting for transfers between devices: 112 us -> 14 us
  starting transfers between devices: 0.09 us -> 43.1 us
  blocking collectives: 34.7 us -> 0 us
  matrix products: 15 us -> 0 us
  between operations: 13.9 us -> 0.89 us
  Pallas kernels: 0 us -> 10.8 us
  local copies, waits for them, and re-layouts: 13 us -> 3.84 us
  other arithmetic: 3.84 us -> 1.52 us
    reduce_scatter x2 -> x0, waiting for transfers between devices: 94.7 us -> none  [the longest x1 63.6 us: local(): lax.psum_scatter(taken * found[:, None].astype(jnp.float32), 'obs', scatt...]
    ppermute x0 -> x40, starting transfers between devices: none -> 43.1 us  [swap(): return lax.ppermute(value, axis, [(i, i ^ step) for i in range(count)])]
    all_gather x1 -> x0, blocking collectives: 34.7 us -> none  [local(): piece = lax.all_gather(my_part, 'obs', axis=0, tiled=True)]
    all_gather x1 -> x0, waiting for transfers between devices: 16.9 us -> none  [local(): probe_cols = lax.all_gather(picked_part, 'sub', axis=1, tiled=True)]
    dot_general x2 -> x0, matrix products: 15 us -> none  [the longest x1 7.51 us: local(): lax.dot_general(weighted, image, contract_rows, preferred_element_type=jn...]
    ppermute x0 -> x40, waiting for transfers between devices: none -> 14 us  [swap(): return lax.ppermute(value, axis, [(i, i ^ step) for i in range(count)])]
    gather x2 -> x0, local copies, waits for them, and re-layouts: 11.3 us -> none  [local(): taken = jnp.take(block_sum, source_rows, axis=0)]
    pallas_call x0 -> x8, Pallas kernels: none -> 10.8 us  [the longest x2 6.07 us: local(): partial = [product(held, weighted, *column) for column in columns]]
  transfers between devices with their start and end apart: 3 -> 40, of which waited for: 3 -> 11; matrix products, arithmetic and copies ran while one was open for 0% -> 1% of each run, Pallas kernels for 0% -> 13%
where the time goes in v2:
time: 74.4 us; the launch traced here: 74.1 us
  starting transfers between devices  43.1 us (58%)
  waiting for transfers between devices  14 us (19%)
  Pallas kernels  10.8 us (15%)
  local copies, waits for them, and re-layouts  3.84 us (5%)
  other arithmetic  1.52 us (2%)
  between operations  0.89 us (1%)
    ppermute x40, starting transfers between devices, swap(): return lax.ppermute(value, axis, [(i, i ^ step) for i in range(count)])  43.1 us
    ppermute x40, waiting for transfers between devices, swap(): return lax.ppermute(value, axis, [(i, i ^ step) for i in range(count)])  14 us
    pallas_call x2, Pallas kernels, local(): partial = [product(held, weighted, *column) for column in columns]  6.07 us
    unnamed x8, local copies, waits for them, and re-layouts  3.84 us
    pallas_call x2, Pallas kernels, local(): columns = [spread(pick(info, *piece), 'sub', subs) for piece in pieces]  1.7 us
  transfers between devices with their start and end apart: 40, of which 11 were waited for; matrix products, arithmetic and copies ran while one was open for 1% of the time, Pallas kernels for 13%

profile of v2, /device:TPU:0, one launch (start us, length us, event | category | flops | bytes accessed | tf_op | source)
XLA Modules:
  0.0 74.1 jit_solution(18371605233572649030)
XLA Ops:
  0.0 1.0 %copy-done.2 = bf16[512,256]{1,0:T(8,128)(2,1)S(1)} copy-done((bf16[512,256]{1,0:T(8,128)(2,1)S(1)}, bf16[512,256]{1,0:T(8,128)(2,1)}, u32[]{:S(2)}) %copy-start.2) | copy-done | bytes 262168
  1.3 3.1 %collective-permute-start.1 = (bf16[128,128]{1,0:T(8,128)(2,1)S(1)}, bf16[128,128]{1,0:T(8,128)(2,1)S(1)}, u32[]{:S(2)}, u32[]{:S(2)}) collective-permute-start(bf16[128,128]{1,0:T(8,128)(2,1)S(1)} %get-tuple-element.35.refs_0_), channel_id=1, source_target_pairs={{0,8},{4,12},{8,0},{12,4},{16,24},{20,28},{24,16},{28,20},{1,9},{5... | collective-permute-start | bytes 98312 | tf_op jit(solution)/shard_map/ppermute | solution.py:18
  4.3 2.6 %collective-permute-start.3 = (bf16[128,128]{1,0:T(8,128)(2,1)S(1)}, bf16[128,128]{1,0:T(8,128)(2,1)S(1)}, u32[]{:S(2)}, u32[]{:S(2)}) collective-permute-start(bf16[128,128]{1,0:T(8,128)(2,1)S(1)} %get-tuple-element.35.refs_0_), channel_id=1, source_target_pairs={{0,16},{4,20},{8,24},{12,28},{16,0},{20,4},{24,8},{28,12},{1,17},{... | collective-permute-start | bytes 98312 | tf_op jit(solution)/shard_map/ppermute | solution.py:18
  6.9 1.7 %collective-permute-start = (bf16[128,128]{1,0:T(8,128)(2,1)S(1)}, bf16[128,128]{1,0:T(8,128)(2,1)S(1)}, u32[]{:S(2)}, u32[]{:S(2)}) collective-permute-start(bf16[128,128]{1,0:T(8,128)(2,1)S(1)} %get-tuple-element.35.refs_0_), channel_id=1, source_target_pairs={{0,4},{4,0},{8,12},{12,8},{16,20},{20,16},{24,28},{28,24},{1,5},{5... | collective-permute-start | bytes 98312 | tf_op jit(solution)/shard_map/ppermute | solution.py:18
  9.1 0.7 collective-permute-done.3.refs_4_
  9.7 1.5 %collective-permute-start.4 = (bf16[128,128]{1,0:T(8,128)(2,1)S(1)}, bf16[128,128]{1,0:T(8,128)(2,1)S(1)}, u32[]{:S(2)}, u32[]{:S(2)}) collective-permute-start(bf16[128,128]{1,0:T(8,128)(2,1)S(1)} %collective-permute-done.3.refs_4_), channel_id=1, source_target_pairs={{0,4},{4,0},{8,12},{12,8},{16,20},{20,16},{24,28},{28,24},{1,5},{5... | collective-permute-start | bytes 98312 | tf_op jit(solution)/shard_map/ppermute | solution.py:18
  11.2 1.4 %collective-permute-done.5.refs_6_ = bf16[128,128]{1,0:T(8,128)(2,1)S(1)} collective-permute-done((bf16[128,128]{1,0:T(8,128)(2,1)S(1)}, bf16[128,128]{1,0:T(8,128)(2,1)S(1)}, u32[]{:S(2)}, u32[]{:S(2)}) %collective-permute-start.5) | collective-permute-done | bytes 32800 | tf_op jit(solution)/shard_map/ppermute | solution.py:18
  12.6 1.5 %collective-permute-start.6 = (bf16[128,128]{1,0:T(8,128)(2,1)S(1)}, bf16[128,128]{1,0:T(8,128)(2,1)S(1)}, u32[]{:S(2)}, u32[]{:S(2)}) collective-permute-start(bf16[128,128]{1,0:T(8,128)(2,1)S(1)} %collective-permute-done.5.refs_6_), channel_id=1, source_target_pairs={{0,4},{4,0},{8,12},{12,8},{16,20},{20,16},{24,28},{28,24},{1,5},{5... | collective-permute-start | bytes 98312 | tf_op jit(solution)/shard_map/ppermute | solution.py:18
  14.1 0.7 pad_add_fusion.info
  14.9 1.7 %collective-permute-done.6.refs_7_ = bf16[128,128]{1,0:T(8,128)(2,1)S(1)} collective-permute-done((bf16[128,128]{1,0:T(8,128)(2,1)S(1)}, bf16[128,128]{1,0:T(8,128)(2,1)S(1)}, u32[]{:S(2)}, u32[]{:S(2)}) %collective-permute-start.6) | collective-permute-done | bytes 32800 | tf_op jit(solution)/shard_map/ppermute | solution.py:18
  16.6 0.9 %pick_listed.2.refs_0_ = bf16[512,128]{1,0:T(8,128)(2,1)S(1)} custom-call(s32[24]{0:T(128)S(1)} %pad_add_fusion.info, bf16[128,128]{1,0:T(8,128)(2,1)S(1)} %get-tuple-element.35.refs_0_, bf16[128,128]{1,0:T(8,128)(2,1)S(1)} %collective-permute-done.refs_1_, bf16[128,128]{1,0:T(8,128)(2,1)S(1)} %collective-permute-done.1.refs_2_, ...), custom_call_target="tpu_custom_call" | custom-call | tf_op jit(solution)/shard_map/pick_listed/pallas_call | solution.py:232
  17.4 1.6 %collective-permute-start.8 = (bf16[512,128]{1,0:T(8,128)(2,1)S(1)}, bf16[512,128]{1,0:T(8,128)(2,1)S(1)}, u32[]{:S(2)}, u32[]{:S(2)}) collective-permute-start(bf16[512,128]{1,0:T(8,128)(2,1)S(1)} %pick_listed.2.refs_0_), channel_id=1, source_target_pairs={{0,2},{1,3},{2,0},{3,1},{4,6},{5,7},{6,4},{7,5},{8,10},{9,11},{10,... | collective-permute-start | bytes 393224 | tf_op jit(solution)/shard_map/ppermute | solution.py:18
  19.0 2.3 %collective-permute-start.23 = (bf16[128,128]{1,0:T(8,128)(2,1)S(1)}, bf16[128,128]{1,0:T(8,128)(2,1)S(1)}, u32[]{:S(2)}, u32[]{:S(2)}) collective-permute-start(bf16[128,128]{1,0:T(8,128)(2,1)S(1)} %get-tuple-element.48.refs_0_), channel_id=1, source_target_pairs={{0,16},{4,20},{8,24},{12,28},{16,0},{20,4},{24,8},{28,12},{1,17},{... | collective-permute-start | bytes 98312 | tf_op jit(solution)/shard_map/ppermute | solution.py:18
  21.3 2.1 %collective-permute-start.25 = (bf16[128,128]{1,0:T(8,128)(2,1)S(1)}, bf16[128,128]{1,0:T(8,128)(2,1)S(1)}, u32[]{:S(2)}, u32[]{:S(2)}) collective-permute-start(bf16[128,128]{1,0:T(8,128)(2,1)S(1)} %get-tuple-element.48.refs_0_), channel_id=1, source_target_pairs={{0,24},{4,28},{8,16},{12,20},{16,8},{20,12},{24,0},{28,4},{1,25},{... | collective-permute-start | bytes 98312 | tf_op jit(solution)/shard_map/ppermute | solution.py:18
  23.4 1.5 %collective-permute-start.20 = (bf16[128,128]{1,0:T(8,128)(2,1)S(1)}, bf16[128,128]{1,0:T(8,128)(2,1)S(1)}, u32[]{:S(2)}, u32[]{:S(2)}) collective-permute-start(bf16[128,128]{1,0:T(8,128)(2,1)S(1)} %get-tuple-element.48.refs_0_), channel_id=1, source_target_pairs={{0,4},{4,0},{8,12},{12,8},{16,20},{20,16},{24,28},{28,24},{1,5},{5... | collective-permute-start | bytes 98312 | tf_op jit(solution)/shard_map/ppermute | solution.py:18
  24.9 0.5 collective-permute-start.22
  25.4 1.5 %collective-permute-start.24 = (bf16[128,128]{1,0:T(8,128)(2,1)S(1)}, bf16[128,128]{1,0:T(8,128)(2,1)S(1)}, u32[]{:S(2)}, u32[]{:S(2)}) collective-permute-start(bf16[128,128]{1,0:T(8,128)(2,1)S(1)} %collective-permute-done.23.refs_4_), channel_id=1, source_target_pairs={{0,4},{4,0},{8,12},{12,8},{16,20},{20,16},{24,28},{28,24},{1,5},{5... | collective-permute-start | bytes 98312 | tf_op jit(solution)/shard_map/ppermute | solution.py:18
  27.0 0.5 collective-permute-start.26
  27.5 1.3 %collective-permute-done.22.refs_3_ = bf16[128,128]{1,0:T(8,128)(2,1)S(1)} collective-permute-done((bf16[128,128]{1,0:T(8,128)(2,1)S(1)}, bf16[128,128]{1,0:T(8,128)(2,1)S(1)}, u32[]{:S(2)}, u32[]{:S(2)}) %collective-permute-start.22) | collective-permute-done | bytes 32800 | tf_op jit(solution)/shard_map/ppermute | solution.py:18
  28.8 0.5 collective-permute-done.24.refs_5_
  29.3 1.6 %collective-permute-done.26.refs_7_ = bf16[128,128]{1,0:T(8,128)(2,1)S(1)} collective-permute-done((bf16[128,128]{1,0:T(8,128)(2,1)S(1)}, bf16[128,128]{1,0:T(8,128)(2,1)S(1)}, u32[]{:S(2)}, u32[]{:S(2)}) %collective-permute-start.26) | collective-permute-done | bytes 32800 | tf_op jit(solution)/shard_map/ppermute | solution.py:18
  30.9 0.9 %pick_listed.3.refs_0_ = bf16[512,128]{1,0:T(8,128)(2,1)S(1)} custom-call(s32[24]{0:T(128)S(1)} %pad_add_fusion.info, bf16[128,128]{1,0:T(8,128)(2,1)S(1)} %get-tuple-element.48.refs_0_, bf16[128,128]{1,0:T(8,128)(2,1)S(1)} %collective-permute-done.20.refs_1_, bf16[128,128]{1,0:T(8,128)(2,1)S(1)} %collective-permute-done.21.refs_2_, ...), custom_call_target="tpu_custom_call" | custom-call | tf_op jit(solution)/shard_map/pick_listed/pallas_call | solution.py:232
  31.8 0.6 collective-permute-start.28
  33.5 2.2 %copy-done.1 = bf16[1024,2048]{1,0:T(8,128)(2,1)S(1)} copy-done((bf16[1024,2048]{1,0:T(8,128)(2,1)S(1)}, bf16[1024,2048]{1,0:T(8,128)(2,1)}, u32[]{:S(2)}) %copy-start.1) | copy-done | bytes 4194328
  35.7 0.7 copy-done.3
  36.4 1.3 %weigh.1 = (bf16[1024,2048]{1,0:T(8,128)(2,1)S(1)}, bf16[1024,2048]{1,0:T(8,128)(2,1)S(1)}) custom-call(s32[1]{0:T(128)S(6)} %copy.7.count, f32[8,128]{1,0:T(8,128)S(1)} %bitcast.5, bf16[1024,2048]{1,0:T(8,128)(2,1)S(1)} %copy-done.1), custom_call_target="tpu_custom_call" | custom-call | flops 4194304 | bytes 12582912 | tf_op jit(solution)/shard_map/weigh/pallas_call | solution.py:187
  38.3 3.0 %product.2 = (f32[32,2048]{1,0:T(8,128)S(1)}, bf16[32,2048]{1,0:T(8,128)(2,1)S(1)}, f32[32,2048]{1,0:T(8,128)S(1)}, bf16[32,2048]{1,0:T(8,128)(2,1)S(1)}) custom-call(bf16[1024,2048]{1,0:T(8,128)(2,1)S(1)} %get-tuple-element.33.held, bf16[1024,2048]{1,0:T(8,128)(2,1)S(1)} %get-tuple-element.34.weighted, bf16[512,128]{1,0:T(8,128)(2,1)S(1)} %pick_listed.2.refs_0_, ...), custom_call_target="tpu_custom_call" | custom-call | flops 1073741824 | bytes 8388608 | tf_op jit(solution)/shard_map/product/pallas_call | solution.py:233
  41.9 3.0 %product.3 = (f32[32,2048]{1,0:T(8,128)S(1)}, bf16[32,2048]{1,0:T(8,128)(2,1)S(1)}, f32[32,2048]{1,0:T(8,128)S(1)}, bf16[32,2048]{1,0:T(8,128)(2,1)S(1)}) custom-call(bf16[1024,2048]{1,0:T(8,128)(2,1)S(1)} %get-tuple-element.33.held, bf16[1024,2048]{1,0:T(8,128)(2,1)S(1)} %get-tuple-element.34.weighted, bf16[512,128]{1,0:T(8,128)(2,1)S(1)} %pick_listed.3.refs_0_, ...), custom_call_target="tpu_custom_call" | custom-call | flops 1073741824 | bytes 8388608 | tf_op jit(solution)/shard_map/product/pallas_call | solution.py:233
  45.6 1.6 %collective-permute-start.11 = (bf16[32,2048]{1,0:T(8,128)(2,1)S(1)}, bf16[32,2048]{1,0:T(8,128)(2,1)S(1)}, u32[]{:S(2)}, u32[]{:S(2)}) collective-permute-start(bf16[32,2048]{1,0:T(8,128)(2,1)S(1)} %add_convert_fusion.1), channel_id=1, source_target_pairs={{0,2},{1,3},{2,0},{3,1},{4,6},{5,7},{6,4},{7,5},{8,10},{9,11},{10,... | collective-permute-start | bytes 393224 | tf_op jit(solution)/shard_map/ppermute | solution.py:18
  47.2 0.8 %collective-permute-start.31 = (bf16[32,2048]{1,0:T(8,128)(2,1)S(1)}, bf16[32,2048]{1,0:T(8,128)(2,1)S(1)}, u32[]{:S(2)}, u32[]{:S(2)}) collective-permute-start(bf16[32,2048]{1,0:T(8,128)(2,1)S(1)} %add_convert_fusion), channel_id=1, source_target_pairs={{0,2},{1,3},{2,0},{3,1},{4,6},{5,7},{6,4},{7,5},{8,10},{9,11},{10,... | collective-permute-start | bytes 393224 | tf_op jit(solution)/shard_map/ppermute | solution.py:18
  48.0 4.0 %collective-permute-done.11.refs_1_ = bf16[32,2048]{1,0:T(8,128)(2,1)S(1)} collective-permute-done((bf16[32,2048]{1,0:T(8,128)(2,1)S(1)}, bf16[32,2048]{1,0:T(8,128)(2,1)S(1)}, u32[]{:S(2)}, u32[]{:S(2)}) %collective-permute-start.11) | collective-permute-done | bytes 131104 | tf_op jit(solution)/shard_map/ppermute | solution.py:18
  52.0 0.7 place.2
  52.7 0.6 collective-permute-start.13
  53.3 1.5 %collective-permute-start.15 = (bf16[32,512]{1,0:T(8,128)(2,1)S(1)}, bf16[32,512]{1,0:T(8,128)(2,1)S(1)}, u32[]{:S(2)}, u32[]{:S(2)}) collective-permute-start(bf16[32,512]{1,0:T(8,128)(2,1)S(1)} %get-tuple-element.44), channel_id=1, source_target_pairs={{0,4},{4,0},{8,12},{12,8},{16,20},{20,16},{24,28},{28,24},{1,5},{5... | collective-permute-start | bytes 98312 | tf_op jit(solution)/shard_map/ppermute | solution.py:18
  54.8 0.5 collective-permute-start.17
  55.3 1.5 %collective-permute-start.19 = (bf16[32,512]{1,0:T(8,128)(2,1)S(1)}, bf16[32,512]{1,0:T(8,128)(2,1)S(1)}, u32[]{:S(2)}, u32[]{:S(2)}) collective-permute-start(bf16[32,512]{1,0:T(8,128)(2,1)S(1)} %get-tuple-element.47), channel_id=1, source_target_pairs={{0,4},{4,0},{8,12},{12,8},{16,20},{20,16},{24,28},{28,24},{1,5},{5... | collective-permute-start | bytes 98312 | tf_op jit(solution)/shard_map/ppermute | solution.py:18
  56.8 0.7 place.3
  57.5 0.6 collective-permute-start.33
  58.1 1.5 %collective-permute-start.35 = (bf16[32,512]{1,0:T(8,128)(2,1)S(1)}, bf16[32,512]{1,0:T(8,128)(2,1)S(1)}, u32[]{:S(2)}, u32[]{:S(2)}) collective-permute-start(bf16[32,512]{1,0:T(8,128)(2,1)S(1)} %get-tuple-element.57), channel_id=1, source_target_pairs={{0,4},{4,0},{8,12},{12,8},{16,20},{20,16},{24,28},{28,24},{1,5},{5... | collective-permute-start | bytes 98312 | tf_op jit(solution)/shard_map/ppermute | solution.py:18
  59.6 0.6 collective-permute-start.37
  60.3 1.6 %collective-permute-start.39 = (bf16[32,512]{1,0:T(8,128)(2,1)S(1)}, bf16[32,512]{1,0:T(8,128)(2,1)S(1)}, u32[]{:S(2)}, u32[]{:S(2)}) collective-permute-start(bf16[32,512]{1,0:T(8,128)(2,1)S(1)} %get-tuple-element.60), channel_id=1, source_target_pairs={{0,4},{4,0},{8,12},{12,8},{16,20},{20,16},{24,28},{28,24},{1,5},{5... | collective-permute-start | bytes 98312 | tf_op jit(solution)/shard_map/ppermute | solution.py:18
  61.8 2.2 %collective-permute-start.14 = (bf16[32,512]{1,0:T(8,128)(2,1)S(1)}, bf16[32,512]{1,0:T(8,128)(2,1)S(1)}, u32[]{:S(2)}, u32[]{:S(2)}) collective-permute-start(bf16[32,512]{1,0:T(8,128)(2,1)S(1)} %add_convert_fusion.9), channel_id=1, source_target_pairs={{0,24},{4,28},{8,16},{12,20},{16,8},{20,12},{24,0},{28,4},{1,25},{... | collective-permute-start | bytes 98312 | tf_op jit(solution)/shard_map/ppermute | solution.py:18
  64.1 2.3 %collective-permute-start.18 = (bf16[32,512]{1,0:T(8,128)(2,1)S(1)}, bf16[32,512]{1,0:T(8,128)(2,1)S(1)}, u32[]{:S(2)}, u32[]{:S(2)}) collective-permute-start(bf16[32,512]{1,0:T(8,128)(2,1)S(1)} %add_convert_fusion.7), channel_id=1, source_target_pairs={{0,8},{4,12},{8,0},{12,4},{16,24},{20,28},{24,16},{28,20},{1,9},{5... | collective-permute-start | bytes 98312 | tf_op jit(solution)/shard_map/ppermute | solution.py:18
  66.5 2.2 %collective-permute-start.34 = (bf16[32,512]{1,0:T(8,128)(2,1)S(1)}, bf16[32,512]{1,0:T(8,128)(2,1)S(1)}, u32[]{:S(2)}, u32[]{:S(2)}) collective-permute-start(bf16[32,512]{1,0:T(8,128)(2,1)S(1)} %add_convert_fusion.5), channel_id=1, source_target_pairs={{0,24},{4,28},{8,16},{12,20},{16,8},{20,12},{24,0},{28,4},{1,25},{... | collective-permute-start | bytes 98312 | tf_op jit(solution)/shard_map/ppermute | solution.py:18
  68.9 2.0 %collective-permute-start.38 = (bf16[32,512]{1,0:T(8,128)(2,1)S(1)}, bf16[32,512]{1,0:T(8,128)(2,1)S(1)}, u32[]{:S(2)}, u32[]{:S(2)}) collective-permute-start(bf16[32,512]{1,0:T(8,128)(2,1)S(1)} %add_convert_fusion.3), channel_id=1, source_target_pairs={{0,8},{4,12},{8,0},{12,4},{16,24},{20,28},{24,16},{28,20},{1,9},{5... | collective-permute-start | bytes 98312 | tf_op jit(solution)/shard_map/ppermute | solution.py:18
  71.0 1.3 %collective-permute-done.34 = bf16[32,512]{1,0:T(8,128)(2,1)S(1)} collective-permute-done((bf16[32,512]{1,0:T(8,128)(2,1)S(1)}, bf16[32,512]{1,0:T(8,128)(2,1)S(1)}, u32[]{:S(2)}, u32[]{:S(2)}) %collective-permute-start.34) | collective-permute-done | bytes 32800 | tf_op jit(solution)/shard_map/ppermute | solution.py:18
  72.3 1.2 %collective-permute-done.36 = bf16[32,512]{1,0:T(8,128)(2,1)S(1)} collective-permute-done((bf16[32,512]{1,0:T(8,128)(2,1)S(1)}, bf16[32,512]{1,0:T(8,128)(2,1)S(1)}, u32[]{:S(2)}, u32[]{:S(2)}) %collective-permute-start.36) | collective-permute-done | bytes 32800 | tf_op jit(solution)/shard_map/ppermute | solution.py:18
  73.5 0.6 maximum_bitcast_fusion
  (61 shorter events, 3.5 us)
Async XLA Ops:
  0.0 8.6 %copy-start = (s32[8,8]{1,0:T(8,128)S(1)}, s32[8,8]{1,0:T(8,128)}, u32[]{:S(2)}) copy-start(s32[8,8]{1,0:T(8,128)} %param.9) | copy-start | bytes 772
  0.0 1.0 %copy-start.2 = (bf16[512,256]{1,0:T(8,128)(2,1)S(1)}, bf16[512,256]{1,0:T(8,128)(2,1)}, u32[]{:S(2)}) copy-start(bf16[512,256]{1,0:T(8,128)(2,1)} %probe.1) | copy-start | bytes 786436
  1.3 7.4 %collective-permute-start.1 = (bf16[128,128]{1,0:T(8,128)(2,1)S(1)}, bf16[128,128]{1,0:T(8,128)(2,1)S(1)}, u32[]{:S(2)}, u32[]{:S(2)}) collective-permute-start(bf16[128,128]{1,0:T(8,128)(2,1)S(1)} %get-tuple-element.35.refs_0_), channel_id=1, source_target_pairs={{0,8},{4,12},{8,0},{12,4},{16,24},{20,28},{24,16},{28,20},{1,9},{5... | collective-permute-start | bytes 98312 | tf_op jit(solution)/shard_map/ppermute | solution.py:18
  4.3 5.4 %collective-permute-start.3 = (bf16[128,128]{1,0:T(8,128)(2,1)S(1)}, bf16[128,128]{1,0:T(8,128)(2,1)S(1)}, u32[]{:S(2)}, u32[]{:S(2)}) collective-permute-start(bf16[128,128]{1,0:T(8,128)(2,1)S(1)} %get-tuple-element.35.refs_0_), channel_id=1, source_target_pairs={{0,16},{4,20},{8,24},{12,28},{16,0},{20,4},{24,8},{28,12},{1,17},{... | collective-permute-start | bytes 98312 | tf_op jit(solution)/shard_map/ppermute | solution.py:18
  6.9 5.7 %collective-permute-start.5 = (bf16[128,128]{1,0:T(8,128)(2,1)S(1)}, bf16[128,128]{1,0:T(8,128)(2,1)S(1)}, u32[]{:S(2)}, u32[]{:S(2)}) collective-permute-start(bf16[128,128]{1,0:T(8,128)(2,1)S(1)} %get-tuple-element.35.refs_0_), channel_id=1, source_target_pairs={{0,24},{4,28},{8,16},{12,20},{16,8},{20,12},{24,0},{28,4},{1,25},{... | collective-permute-start | bytes 98312 | tf_op jit(solution)/shard_map/ppermute | solution.py:18
  6.9 7.9 %collective-permute-start = (bf16[128,128]{1,0:T(8,128)(2,1)S(1)}, bf16[128,128]{1,0:T(8,128)(2,1)S(1)}, u32[]{:S(2)}, u32[]{:S(2)}) collective-permute-start(bf16[128,128]{1,0:T(8,128)(2,1)S(1)} %get-tuple-element.35.refs_0_), channel_id=1, source_target_pairs={{0,4},{4,0},{8,12},{12,8},{16,20},{20,16},{24,28},{28,24},{1,5},{5... | collective-permute-start | bytes 98312 | tf_op jit(solution)/shard_map/ppermute | solution.py:18
  8.7 6.2 %collective-permute-start.2 = (bf16[128,128]{1,0:T(8,128)(2,1)S(1)}, bf16[128,128]{1,0:T(8,128)(2,1)S(1)}, u32[]{:S(2)}, u32[]{:S(2)}) collective-permute-start(bf16[128,128]{1,0:T(8,128)(2,1)S(1)} %collective-permute-done.1.refs_2_), channel_id=1, source_target_pairs={{0,4},{4,0},{8,12},{12,8},{16,20},{20,16},{24,28},{28,24},{1,5},{5... | collective-permute-start | bytes 98312 | tf_op jit(solution)/shard_map/ppermute | solution.py:18
  9.7 5.1 %collective-permute-start.4 = (bf16[128,128]{1,0:T(8,128)(2,1)S(1)}, bf16[128,128]{1,0:T(8,128)(2,1)S(1)}, u32[]{:S(2)}, u32[]{:S(2)}) collective-permute-start(bf16[128,128]{1,0:T(8,128)(2,1)S(1)} %collective-permute-done.3.refs_4_), channel_id=1, source_target_pairs={{0,4},{4,0},{8,12},{12,8},{16,20},{20,16},{24,28},{28,24},{1,5},{5... | collective-permute-start | bytes 98312 | tf_op jit(solution)/shard_map/ppermute | solution.py:18
  12.6 3.9 %collective-permute-start.6 = (bf16[128,128]{1,0:T(8,128)(2,1)S(1)}, bf16[128,128]{1,0:T(8,128)(2,1)S(1)}, u32[]{:S(2)}, u32[]{:S(2)}) collective-permute-start(bf16[128,128]{1,0:T(8,128)(2,1)S(1)} %collective-permute-done.5.refs_6_), channel_id=1, source_target_pairs={{0,4},{4,0},{8,12},{12,8},{16,20},{20,16},{24,28},{28,24},{1,5},{5... | collective-permute-start | bytes 98312 | tf_op jit(solution)/shard_map/ppermute | solution.py:18
  17.4 14.9 %collective-permute-start.8 = (bf16[512,128]{1,0:T(8,128)(2,1)S(1)}, bf16[512,128]{1,0:T(8,128)(2,1)S(1)}, u32[]{:S(2)}, u32[]{:S(2)}) collective-permute-start(bf16[512,128]{1,0:T(8,128)(2,1)S(1)} %pick_listed.2.refs_0_), channel_id=1, source_target_pairs={{0,2},{1,3},{2,0},{3,1},{4,6},{5,7},{6,4},{7,5},{8,10},{9,11},{10,... | collective-permute-start | bytes 393224 | tf_op jit(solution)/shard_map/ppermute | solution.py:18
  19.0 5.9 %collective-permute-start.21 = (bf16[128,128]{1,0:T(8,128)(2,1)S(1)}, bf16[128,128]{1,0:T(8,128)(2,1)S(1)}, u32[]{:S(2)}, u32[]{:S(2)}) collective-permute-start(bf16[128,128]{1,0:T(8,128)(2,1)S(1)} %get-tuple-element.48.refs_0_), channel_id=1, source_target_pairs={{0,8},{4,12},{8,0},{12,4},{16,24},{20,28},{24,16},{28,20},{1,9},{5... | collective-permute-start | bytes 98312 | tf_op jit(solution)/shard_map/ppermute | solution.py:18
  19.0 6.4 %collective-permute-start.23 = (bf16[128,128]{1,0:T(8,128)(2,1)S(1)}, bf16[128,128]{1,0:T(8,128)(2,1)S(1)}, u32[]{:S(2)}, u32[]{:S(2)}) collective-permute-start(bf16[128,128]{1,0:T(8,128)(2,1)S(1)} %get-tuple-element.48.refs_0_), channel_id=1, source_target_pairs={{0,16},{4,20},{8,24},{12,28},{16,0},{20,4},{24,8},{28,12},{1,17},{... | collective-permute-start | bytes 98312 | tf_op jit(solution)/shard_map/ppermute | solution.py:18
  21.3 5.7 %collective-permute-start.25 = (bf16[128,128]{1,0:T(8,128)(2,1)S(1)}, bf16[128,128]{1,0:T(8,128)(2,1)S(1)}, u32[]{:S(2)}, u32[]{:S(2)}) collective-permute-start(bf16[128,128]{1,0:T(8,128)(2,1)S(1)} %get-tuple-element.48.refs_0_), channel_id=1, source_target_pairs={{0,24},{4,28},{8,16},{12,20},{16,8},{20,12},{24,0},{28,4},{1,25},{... | collective-permute-start | bytes 98312 | tf_op jit(solution)/shard_map/ppermute | solution.py:18
  23.4 4.1 %collective-permute-start.20 = (bf16[128,128]{1,0:T(8,128)(2,1)S(1)}, bf16[128,128]{1,0:T(8,128)(2,1)S(1)}, u32[]{:S(2)}, u32[]{:S(2)}) collective-permute-start(bf16[128,128]{1,0:T(8,128)(2,1)S(1)} %get-tuple-element.48.refs_0_), channel_id=1, source_target_pairs={{0,4},{4,0},{8,12},{12,8},{16,20},{20,16},{24,28},{28,24},{1,5},{5... | collective-permute-start | bytes 98312 | tf_op jit(solution)/shard_map/ppermute | solution.py:18
  24.9 3.9 %collective-permute-start.22 = (bf16[128,128]{1,0:T(8,128)(2,1)S(1)}, bf16[128,128]{1,0:T(8,128)(2,1)S(1)}, u32[]{:S(2)}, u32[]{:S(2)}) collective-permute-start(bf16[128,128]{1,0:T(8,128)(2,1)S(1)} %collective-permute-done.21.refs_2_), channel_id=1, source_target_pairs={{0,4},{4,0},{8,12},{12,8},{16,20},{20,16},{24,28},{28,24},{1,5},{5... | collective-permute-start | bytes 98312 | tf_op jit(solution)/shard_map/ppermute | solution.py:18
  25.4 3.9 %collective-permute-start.24 = (bf16[128,128]{1,0:T(8,128)(2,1)S(1)}, bf16[128,128]{1,0:T(8,128)(2,1)S(1)}, u32[]{:S(2)}, u32[]{:S(2)}) collective-permute-start(bf16[128,128]{1,0:T(8,128)(2,1)S(1)} %collective-permute-done.23.refs_4_), channel_id=1, source_target_pairs={{0,4},{4,0},{8,12},{12,8},{16,20},{20,16},{24,28},{28,24},{1,5},{5... | collective-permute-start | bytes 98312 | tf_op jit(solution)/shard_map/ppermute | solution.py:18
  27.0 3.9 %collective-permute-start.26 = (bf16[128,128]{1,0:T(8,128)(2,1)S(1)}, bf16[128,128]{1,0:T(8,128)(2,1)S(1)}, u32[]{:S(2)}, u32[]{:S(2)}) collective-permute-start(bf16[128,128]{1,0:T(8,128)(2,1)S(1)} %collective-permute-done.25.refs_6_), channel_id=1, source_target_pairs={{0,4},{4,0},{8,12},{12,8},{16,20},{20,16},{24,28},{28,24},{1,5},{5... | collective-permute-start | bytes 98312 | tf_op jit(solution)/shard_map/ppermute | solution.py:18
  31.8 6.0 %collective-permute-start.28 = (bf16[512,128]{1,0:T(8,128)(2,1)S(1)}, bf16[512,128]{1,0:T(8,128)(2,1)S(1)}, u32[]{:S(2)}, u32[]{:S(2)}) collective-permute-start(bf16[512,128]{1,0:T(8,128)(2,1)S(1)} %pick_listed.3.refs_0_), channel_id=1, source_target_pairs={{0,2},{1,3},{2,0},{3,1},{4,6},{5,7},{6,4},{7,5},{8,10},{9,11},{10,... | collective-permute-start | bytes 393224 | tf_op jit(solution)/shard_map/ppermute | solution.py:18
  32.3 6.0 %collective-permute-start.7 = (bf16[512,128]{1,0:T(8,128)(2,1)S(1)}, bf16[512,128]{1,0:T(8,128)(2,1)S(1)}, u32[]{:S(2)}, u32[]{:S(2)}) collective-permute-start(bf16[512,128]{1,0:T(8,128)(2,1)S(1)} %pick_listed.2.refs_0_), channel_id=1, source_target_pairs={{0,1},{1,0},{2,3},{3,2},{4,5},{5,4},{6,7},{7,6},{8,9},{9,8},{10,11... | collective-permute-start | bytes 393224 | tf_op jit(solution)/shard_map/ppermute | solution.py:18
  32.3 5.9 %collective-permute-start.9 = (bf16[512,128]{1,0:T(8,128)(2,1)S(1)}, bf16[512,128]{1,0:T(8,128)(2,1)S(1)}, u32[]{:S(2)}, u32[]{:S(2)}) collective-permute-start(bf16[512,128]{1,0:T(8,128)(2,1)S(1)} %collective-permute-done.8.refs_2_), channel_id=1, source_target_pairs={{0,1},{1,0},{2,3},{3,2},{4,5},{5,4},{6,7},{7,6},{8,9},{9,8},{10,11... | collective-permute-start | bytes 393224 | tf_op jit(solution)/shard_map/ppermute | solution.py:18
  33.5 2.2 %copy-start.1 = (bf16[1024,2048]{1,0:T(8,128)(2,1)S(1)}, bf16[1024,2048]{1,0:T(8,128)(2,1)}, u32[]{:S(2)}) copy-start(bf16[1024,2048]{1,0:T(8,128)(2,1)} %jac.1) | copy-start | bytes 12582916
  35.7 0.7 copy-start.3
  37.7 4.2 %collective-permute-start.27 = (bf16[512,128]{1,0:T(8,128)(2,1)S(1)}, bf16[512,128]{1,0:T(8,128)(2,1)S(1)}, u32[]{:S(2)}, u32[]{:S(2)}) collective-permute-start(bf16[512,128]{1,0:T(8,128)(2,1)S(1)} %pick_listed.3.refs_0_), channel_id=1, source_target_pairs={{0,1},{1,0},{2,3},{3,2},{4,5},{5,4},{6,7},{7,6},{8,9},{9,8},{10,11... | collective-permute-start | bytes 393224 | tf_op jit(solution)/shard_map/ppermute | solution.py:18
  37.8 4.1 %collective-permute-start.29 = (bf16[512,128]{1,0:T(8,128)(2,1)S(1)}, bf16[512,128]{1,0:T(8,128)(2,1)S(1)}, u32[]{:S(2)}, u32[]{:S(2)}) collective-permute-start(bf16[512,128]{1,0:T(8,128)(2,1)S(1)} %collective-permute-done.28.refs_2_), channel_id=1, source_target_pairs={{0,1},{1,0},{2,3},{3,2},{4,5},{5,4},{6,7},{7,6},{8,9},{9,8},{10,11... | collective-permute-start | bytes 393224 | tf_op jit(solution)/shard_map/ppermute | solution.py:18
  41.3 4.2 %collective-permute-start.10 = (bf16[32,2048]{1,0:T(8,128)(2,1)S(1)}, bf16[32,2048]{1,0:T(8,128)(2,1)S(1)}, u32[]{:S(2)}, u32[]{:S(2)}) collective-permute-start(bf16[32,2048]{1,0:T(8,128)(2,1)S(1)} %get-tuple-element.38), channel_id=1, source_target_pairs={{0,1},{1,0},{2,3},{3,2},{4,5},{5,4},{6,7},{7,6},{8,9},{9,8},{10,11... | collective-permute-start | bytes 393224 | tf_op jit(solution)/shard_map/ppermute | solution.py:18
  41.5 6.5 %collective-permute-start.12 = (bf16[32,2048]{1,0:T(8,128)(2,1)S(1)}, bf16[32,2048]{1,0:T(8,128)(2,1)S(1)}, u32[]{:S(2)}, u32[]{:S(2)}) collective-permute-start(bf16[32,2048]{1,0:T(8,128)(2,1)S(1)} %get-tuple-element.39), channel_id=1, source_target_pairs={{0,1},{1,0},{2,3},{3,2},{4,5},{5,4},{6,7},{7,6},{8,9},{9,8},{10,11... | collective-permute-start | bytes 393224 | tf_op jit(solution)/shard_map/ppermute | solution.py:18
  45.0 2.2 %collective-permute-start.30 = (bf16[32,2048]{1,0:T(8,128)(2,1)S(1)}, bf16[32,2048]{1,0:T(8,128)(2,1)S(1)}, u32[]{:S(2)}, u32[]{:S(2)}) collective-permute-start(bf16[32,2048]{1,0:T(8,128)(2,1)S(1)} %get-tuple-element.51), channel_id=1, source_target_pairs={{0,1},{1,0},{2,3},{3,2},{4,5},{5,4},{6,7},{7,6},{8,9},{9,8},{10,11... | collective-permute-start | bytes 393224 | tf_op jit(solution)/shard_map/ppermute | solution.py:18
  45.1 10.2 %collective-permute-start.32 = (bf16[32,2048]{1,0:T(8,128)(2,1)S(1)}, bf16[32,2048]{1,0:T(8,128)(2,1)S(1)}, u32[]{:S(2)}, u32[]{:S(2)}) collective-permute-start(bf16[32,2048]{1,0:T(8,128)(2,1)S(1)} %get-tuple-element.52), channel_id=1, source_target_pairs={{0,1},{1,0},{2,3},{3,2},{4,5},{5,4},{6,7},{7,6},{8,9},{9,8},{10,11... | collective-permute-start | bytes 393224 | tf_op jit(solution)/shard_map/ppermute | solution.py:18
  45.6 6.4 %collective-permute-start.11 = (bf16[32,2048]{1,0:T(8,128)(2,1)S(1)}, bf16[32,2048]{1,0:T(8,128)(2,1)S(1)}, u32[]{:S(2)}, u32[]{:S(2)}) collective-permute-start(bf16[32,2048]{1,0:T(8,128)(2,1)S(1)} %add_convert_fusion.1), channel_id=1, source_target_pairs={{0,2},{1,3},{2,0},{3,1},{4,6},{5,7},{6,4},{7,5},{8,10},{9,11},{10,... | collective-permute-start | bytes 393224 | tf_op jit(solution)/shard_map/ppermute | solution.py:18
  47.2 9.6 %collective-permute-start.31 = (bf16[32,2048]{1,0:T(8,128)(2,1)S(1)}, bf16[32,2048]{1,0:T(8,128)(2,1)S(1)}, u32[]{:S(2)}, u32[]{:S(2)}) collective-permute-start(bf16[32,2048]{1,0:T(8,128)(2,1)S(1)} %add_convert_fusion), channel_id=1, source_target_pairs={{0,2},{1,3},{2,0},{3,1},{4,6},{5,7},{6,4},{7,5},{8,10},{9,11},{10,... | collective-permute-start | bytes 393224 | tf_op jit(solution)/shard_map/ppermute | solution.py:18
  52.7 5.4 %collective-permute-start.13 = (bf16[32,512]{1,0:T(8,128)(2,1)S(1)}, bf16[32,512]{1,0:T(8,128)(2,1)S(1)}, u32[]{:S(2)}, u32[]{:S(2)}) collective-permute-start(bf16[32,512]{1,0:T(8,128)(2,1)S(1)} %get-tuple-element.42), channel_id=1, source_target_pairs={{0,4},{4,0},{8,12},{12,8},{16,20},{20,16},{24,28},{28,24},{1,5},{5... | collective-permute-start | bytes 98312 | tf_op jit(solution)/shard_map/ppermute | solution.py:18
  53.3 6.3 %collective-permute-start.15 = (bf16[32,512]{1,0:T(8,128)(2,1)S(1)}, bf16[32,512]{1,0:T(8,128)(2,1)S(1)}, u32[]{:S(2)}, u32[]{:S(2)}) collective-permute-start(bf16[32,512]{1,0:T(8,128)(2,1)S(1)} %get-tuple-element.44), channel_id=1, source_target_pairs={{0,4},{4,0},{8,12},{12,8},{16,20},{20,16},{24,28},{28,24},{1,5},{5... | collective-permute-start | bytes 98312 | tf_op jit(solution)/shard_map/ppermute | solution.py:18
  54.8 5.5 %collective-permute-start.17 = (bf16[32,512]{1,0:T(8,128)(2,1)S(1)}, bf16[32,512]{1,0:T(8,128)(2,1)S(1)}, u32[]{:S(2)}, u32[]{:S(2)}) collective-permute-start(bf16[32,512]{1,0:T(8,128)(2,1)S(1)} %get-tuple-element.46), channel_id=1, source_target_pairs={{0,4},{4,0},{8,12},{12,8},{16,20},{20,16},{24,28},{28,24},{1,5},{5... | collective-permute-start | bytes 98312 | tf_op jit(solution)/shard_map/ppermute | solution.py:18
  55.3 11.2 %collective-permute-start.19 = (bf16[32,512]{1,0:T(8,128)(2,1)S(1)}, bf16[32,512]{1,0:T(8,128)(2,1)S(1)}, u32[]{:S(2)}, u32[]{:S(2)}) collective-permute-start(bf16[32,512]{1,0:T(8,128)(2,1)S(1)} %get-tuple-element.47), channel_id=1, source_target_pairs={{0,4},{4,0},{8,12},{12,8},{16,20},{20,16},{24,28},{28,24},{1,5},{5... | collective-permute-start | bytes 98312 | tf_op jit(solution)/shard_map/ppermute | solution.py:18
  57.5 4.3 %collective-permute-start.33 = (bf16[32,512]{1,0:T(8,128)(2,1)S(1)}, bf16[32,512]{1,0:T(8,128)(2,1)S(1)}, u32[]{:S(2)}, u32[]{:S(2)}) collective-permute-start(bf16[32,512]{1,0:T(8,128)(2,1)S(1)} %get-tuple-element.55), channel_id=1, source_target_pairs={{0,4},{4,0},{8,12},{12,8},{16,20},{20,16},{24,28},{28,24},{1,5},{5... | collective-permute-start | bytes 98312 | tf_op jit(solution)/shard_map/ppermute | solution.py:18
  58.1 5.9 %collective-permute-start.35 = (bf16[32,512]{1,0:T(8,128)(2,1)S(1)}, bf16[32,512]{1,0:T(8,128)(2,1)S(1)}, u32[]{:S(2)}, u32[]{:S(2)}) collective-permute-start(bf16[32,512]{1,0:T(8,128)(2,1)S(1)} %get-tuple-element.57), channel_id=1, source_target_pairs={{0,4},{4,0},{8,12},{12,8},{16,20},{20,16},{24,28},{28,24},{1,5},{5... | collective-permute-start | bytes 98312 | tf_op jit(solution)/shard_map/ppermute | solution.py:18
  59.6 4.5 %collective-permute-start.37 = (bf16[32,512]{1,0:T(8,128)(2,1)S(1)}, bf16[32,512]{1,0:T(8,128)(2,1)S(1)}, u32[]{:S(2)}, u32[]{:S(2)}) collective-permute-start(bf16[32,512]{1,0:T(8,128)(2,1)S(1)} %get-tuple-element.59), channel_id=1, source_target_pairs={{0,4},{4,0},{8,12},{12,8},{16,20},{20,16},{24,28},{28,24},{1,5},{5... | collective-permute-start | bytes 98312 | tf_op jit(solution)/shard_map/ppermute | solution.py:18
  60.3 10.7 %collective-permute-start.39 = (bf16[32,512]{1,0:T(8,128)(2,1)S(1)}, bf16[32,512]{1,0:T(8,128)(2,1)S(1)}, u32[]{:S(2)}, u32[]{:S(2)}) collective-permute-start(bf16[32,512]{1,0:T(8,128)(2,1)S(1)} %get-tuple-element.60), channel_id=1, source_target_pairs={{0,4},{4,0},{8,12},{12,8},{16,20},{20,16},{24,28},{28,24},{1,5},{5... | collective-permute-start | bytes 98312 | tf_op jit(solution)/shard_map/ppermute | solution.py:18
  61.8 6.8 %collective-permute-start.14 = (bf16[32,512]{1,0:T(8,128)(2,1)S(1)}, bf16[32,512]{1,0:T(8,128)(2,1)S(1)}, u32[]{:S(2)}, u32[]{:S(2)}) collective-permute-start(bf16[32,512]{1,0:T(8,128)(2,1)S(1)} %add_convert_fusion.9), channel_id=1, source_target_pairs={{0,24},{4,28},{8,16},{12,20},{16,8},{20,12},{24,0},{28,4},{1,25},{... | collective-permute-start | bytes 98312 | tf_op jit(solution)/shard_map/ppermute | solution.py:18
  64.0 4.9 %collective-permute-start.16 = (bf16[32,512]{1,0:T(8,128)(2,1)S(1)}, bf16[32,512]{1,0:T(8,128)(2,1)S(1)}, u32[]{:S(2)}, u32[]{:S(2)}) collective-permute-start(bf16[32,512]{1,0:T(8,128)(2,1)S(1)} %add_convert_fusion.8), channel_id=1, source_target_pairs={{0,16},{4,20},{8,24},{12,28},{16,0},{20,4},{24,8},{28,12},{1,17},{... | collective-permute-start | bytes 98312 | tf_op jit(solution)/shard_map/ppermute | solution.py:18
  64.1 6.8 %collective-permute-start.18 = (bf16[32,512]{1,0:T(8,128)(2,1)S(1)}, bf16[32,512]{1,0:T(8,128)(2,1)S(1)}, u32[]{:S(2)}, u32[]{:S(2)}) collective-permute-start(bf16[32,512]{1,0:T(8,128)(2,1)S(1)} %add_convert_fusion.7), channel_id=1, source_target_pairs={{0,8},{4,12},{8,0},{12,4},{16,24},{20,28},{24,16},{28,20},{1,9},{5... | collective-permute-start | bytes 98312 | tf_op jit(solution)/shard_map/ppermute | solution.py:18
  66.5 5.8 %collective-permute-start.34 = (bf16[32,512]{1,0:T(8,128)(2,1)S(1)}, bf16[32,512]{1,0:T(8,128)(2,1)S(1)}, u32[]{:S(2)}, u32[]{:S(2)}) collective-permute-start(bf16[32,512]{1,0:T(8,128)(2,1)S(1)} %add_convert_fusion.5), channel_id=1, source_target_pairs={{0,24},{4,28},{8,16},{12,20},{16,8},{20,12},{24,0},{28,4},{1,25},{... | collective-permute-start | bytes 98312 | tf_op jit(solution)/shard_map/ppermute | solution.py:18
  68.7 4.8 %collective-permute-start.36 = (bf16[32,512]{1,0:T(8,128)(2,1)S(1)}, bf16[32,512]{1,0:T(8,128)(2,1)S(1)}, u32[]{:S(2)}, u32[]{:S(2)}) collective-permute-start(bf16[32,512]{1,0:T(8,128)(2,1)S(1)} %add_convert_fusion.4), channel_id=1, source_target_pairs={{0,16},{4,20},{8,24},{12,28},{16,0},{20,4},{24,8},{28,12},{1,17},{... | collective-permute-start | bytes 98312 | tf_op jit(solution)/shard_map/ppermute | solution.py:18
  68.9 4.6 %collective-permute-start.38 = (bf16[32,512]{1,0:T(8,128)(2,1)S(1)}, bf16[32,512]{1,0:T(8,128)(2,1)S(1)}, u32[]{:S(2)}, u32[]{:S(2)}) collective-permute-start(bf16[32,512]{1,0:T(8,128)(2,1)S(1)} %add_convert_fusion.3), channel_id=1, source_target_pairs={{0,8},{4,12},{8,0},{12,4},{16,24},{20,28},{24,16},{28,20},{1,9},{5... | collective-permute-start | bytes 98312 | tf_op jit(solution)/shard_map/ppermute | solution.py:18

commit v3 on v2

--- a/solution.py
+++ b/solution.py
@@ -7,7 +7,6 @@
 from jax.experimental.pallas import tpu as pltpu
 from jax.sharding import PartitionSpec as P
 
-CHUNKS = 2
 MIB = 1024 * 1024
 SMEM = pl.BlockSpec(memory_space=pltpu.SMEM)
 VMEM = pl.BlockSpec(memory_space=pltpu.VMEM)
@@ -42,29 +41,19 @@
     return parts
 
 
-def split_kernel(unit, subs, probe, *refs):
-    outs, rows, sems = refs[:-2], refs[-2], refs[-1]
+def share_kernel(unit, subs, probe, out, sems):
     sub = lax.axis_index("sub")
     part = unit // subs
     copies = [
         pltpu.make_async_copy(
             probe.at[pl.ds(pl.multiple_of(u * unit + sub * part, part), part)],
-            rows.at[pl.ds(u * part, part)], sems.at[u])
+            out.at[pl.ds(u * part, part)], sems.at[u])
         for u in range(sems.shape[0])
     ]
     for copy in copies:
         copy.start()
-    width = rows.shape[1]
-    lanes = width // len(outs)
-    high, low = width // subs, lanes // subs
-    source = lax.broadcasted_iota(jnp.int32, (width, lanes), 0)
-    target = lax.broadcasted_iota(jnp.int32, (width, lanes), 1)
-    wanted = (target // low) * high + target % low
-    chosen = [(source == wanted + c * low).astype(jnp.bfloat16) for c in range(len(outs))]
     for copy in copies:
         copy.wait()
-    for c, out in enumerate(outs):
-        out[...] = jnp.dot(rows[...], chosen[c], preferred_element_type=jnp.float32).astype(out.dtype)
 
 
 def weigh_kernel(count, weight, jac, held, weighted, sems):
@@ -88,7 +77,7 @@
             weighted[r:r + lanes, :] = (held[r:r + lanes, :].astype(jnp.float32) * scale).astype(jnp.bfloat16)
 
 
-def pick_kernel(unit, tile, subs, listed, info, *refs):
+def pick_kernel(unit, tile, subs, listed, info, ready, *refs):
     pieces, out, position = refs[:-2], refs[-2], refs[-1]
     block = lax.axis_index("obs")
     part = unit // subs
@@ -163,25 +152,21 @@
     tile = width // listed
     own_rows, probe_width = probe_block.shape
     unit = min(own_rows, tile)
-    lanes = probe_width // CHUNKS
-    high = lanes // subs
+    high = probe_width // subs
     my_list = lax.dynamic_index_in_dim(tile_lists, lax.axis_index("obs"), 0, keepdims=False)
     info = jnp.concatenate([my_list, tile_slot])
 
     def params(mib):
         return pltpu.CompilerParams(vmem_limit_bytes=mib * MIB)
 
-    shares = pl.pallas_call(
-        functools.partial(split_kernel, unit, subs),
-        out_shape=[jax.ShapeDtypeStruct((own_rows // subs, lanes), jnp.bfloat16)] * CHUNKS,
+    share = pl.pallas_call(
+        functools.partial(share_kernel, unit, subs),
+        out_shape=jax.ShapeDtypeStruct((own_rows // subs, probe_width), jnp.bfloat16),
         in_specs=[HBM],
-        out_specs=[VMEM] * CHUNKS,
-        scratch_shapes=[
-            pltpu.VMEM((own_rows // subs, probe_width), jnp.bfloat16),
-            pltpu.SemaphoreType.DMA((own_rows // unit,)),
-        ],
-        compiler_params=params(8),
-        name="split_probe",
+        out_specs=VMEM,
+        scratch_shapes=[pltpu.SemaphoreType.DMA((own_rows // unit,))],
+        compiler_params=params(60),
+        name="share_probe",
     )(probe_block)
     weight_lanes = min(128, rows)
     held, weighted = pl.pallas_call(
@@ -197,8 +182,8 @@
 
     pick = pl.pallas_call(
         functools.partial(pick_kernel, unit, tile, subs, listed),
-        out_shape=jax.ShapeDtypeStruct((width // subs, lanes), jnp.bfloat16),
-        in_specs=[SMEM] + [VMEM] * obs_count,
+        out_shape=jax.ShapeDtypeStruct((width // subs, probe_width), jnp.bfloat16),
+        in_specs=[SMEM, pl.BlockSpec(memory_space=pl.ANY)] + [VMEM] * obs_count,
         out_specs=VMEM,
         scratch_shapes=[pltpu.SMEM((tiles,), jnp.int32)],
         compiler_params=params(8),
@@ -210,12 +195,12 @@
         in_specs=[VMEM] * (2 + subs),
         out_specs=[VMEM] * subs,
         scratch_shapes=[
-            pltpu.VMEM((width, lanes), jnp.bfloat16),
-            pltpu.VMEM((lanes, width), jnp.float32),
+            pltpu.VMEM((width, probe_width), jnp.bfloat16),
+            pltpu.VMEM((probe_width, width), jnp.float32),
         ],
         compiler_params=params(24),
         cost_estimate=pl.CostEstimate(
-            flops=4 * rows * width * lanes, bytes_accessed=4 * rows * width, transcendentals=0),
+            flops=4 * rows * width * probe_width, bytes_accessed=4 * rows * width, transcendentals=0),
         name="product",
     )
     place = pl.pallas_call(
@@ -228,13 +213,11 @@
         name="place",
     )
 
-    pieces = [spread(share, "obs", obs_count) for share in shares]
-    columns = [spread(pick(info, *piece), "sub", subs) for piece in pieces]
-    partial = [product(held, weighted, *column) for column in columns]
-    blocks = [collect(terms, "sub", subs) for terms in partial]
-    placed = [collect(place(info, *terms), "obs", obs_count) for terms in blocks]
-    sums = [sum(term.astype(jnp.float32) for term in terms).astype(jnp.bfloat16) for terms in placed]
-    return jnp.concatenate(sums, axis=0).T
+    pieces = spread(share, "obs", obs_count)
+    columns = spread(pick(info, weighted, *pieces), "sub", subs)
+    terms = collect(product(held, weighted, *columns), "sub", subs)
+    terms = collect(place(info, *terms), "obs", obs_count)
+    return sum(term.astype(jnp.float32) for term in terms).T.astype(jnp.bfloat16)
 
 
 def solution(mesh):

time: 74.4 us -> 59.3 us (0.80)
  starting transfers between devices: 43.1 us -> 23.2 us
  waiting for transfers between devices: 14 us -> 22.3 us
  Pallas kernels: 10.8 us -> 9.01 us
  local copies, waits for them, and re-layouts: 3.84 us -> 2.89 us
    ppermute x40 -> x20, starting transfers between devices: 43.1 us -> 23.2 us  [swap(): return lax.ppermute(value, axis, [(i, i ^ step) for i in range(count)])]
    ppermute x40 -> x20, waiting for transfers between devices: 14 us -> 22.3 us  [swap(): return lax.ppermute(value, axis, [(i, i ^ step) for i in range(count)])]
    pallas_call x7 -> x4, Pallas kernels: 9.43 us -> 7.69 us  [the longest x1 4.6 us: local(): terms = collect(product(held, weighted, *columns), 'sub', subs)]
    unnamed x8 -> x10, local copies, waits for them, and re-layouts: 3.84 us -> 2.88 us
  transfers between devices with their start and end apart: 40 -> 20, of which waited for: 11 -> 10; matrix products, arithmetic and copies ran while one was open for 1% -> 0% of each run, Pallas kernels for 13% -> 2%
where the time goes in v3:
time: 59.3 us; the launch traced here: 59.1 us
  starting transfers between devices  23.2 us (39%)
  waiting for transfers between devices  22.3 us (38%)
  Pallas kernels  9.01 us (15%)
  local copies, waits for them, and re-layouts  2.89 us (5%)
  other arithmetic  0.84 us (1%)
  between operations  0.78 us (1%)
    ppermute x20, starting transfers between devices, swap(): return lax.ppermute(value, axis, [(i, i ^ step) for i in range(count)])  23.2 us
    ppermute x20, waiting for transfers between devices, swap(): return lax.ppermute(value, axis, [(i, i ^ step) for i in range(count)])  22.3 us
    pallas_call x1, Pallas kernels, local(): terms = collect(product(held, weighted, *columns), 'sub', subs)  4.6 us
    unnamed x10, local copies, waits for them, and re-layouts  2.88 us
    pallas_call x1, Pallas kernels, local(): pl.pallas_call(functools.partial(share_kernel, unit, subs), out_shape=jax...  1.45 us
    pallas_call x1, Pallas kernels, local(): pl.pallas_call(weigh_kernel, out_shape=[jax.ShapeDtypeStruct((rows, width...  1.32 us
  transfers between devices with their start and end apart: 20, of which 10 were waited for; matrix products, arithmetic and copies ran while one was open for 0% of the time, Pallas kernels for 2%

profile of v3, /device:TPU:0, one launch (start us, length us, event | category | flops | bytes accessed | tf_op | source)
XLA Modules:
  0.0 59.1 jit_solution(13498632202293547704)
XLA Ops:
  0.0 1.4 %share_probe.1.refs_0_ = bf16[128,256]{1,0:T(8,128)(2,1)} custom-call(bf16[512,256]{1,0:T(8,128)(2,1)} %probe.1), custom_call_target="tpu_custom_call" | custom-call | tf_op jit(solution)/shard_map/share_probe/pallas_call | solution.py:162
  1.5 5.1 %collective-permute-start.5 = (bf16[128,256]{1,0:T(8,128)(2,1)}, bf16[128,256]{1,0:T(8,128)(2,1)S(1)}, u32[]{:S(2)}, u32[]{:S(2)}) collective-permute-start(bf16[128,256]{1,0:T(8,128)(2,1)} %share_probe.1.refs_0_), channel_id=1, source_target_pairs={{0,24},{4,28},{8,16},{12,20},{16,8},{20,12},{24,0},{28,4},{1,25},{... | collective-permute-start | bytes 196616 | tf_op jit(solution)/shard_map/ppermute | solution.py:17
  6.6 0.0 collective-permute-start.3
  6.6 0.6 %collective-permute-start.1 = (bf16[128,256]{1,0:T(8,128)(2,1)}, bf16[128,256]{1,0:T(8,128)(2,1)S(1)}, u32[]{:S(2)}, u32[]{:S(2)}) collective-permute-start(bf16[128,256]{1,0:T(8,128)(2,1)} %share_probe.1.refs_0_), channel_id=1, source_target_pairs={{0,8},{4,12},{8,0},{12,4},{16,24},{20,28},{24,16},{28,20},{1,9},{5... | collective-permute-start | bytes 196616 | tf_op jit(solution)/shard_map/ppermute | solution.py:17
  7.2 1.6 %collective-permute-start = (bf16[128,256]{1,0:T(8,128)(2,1)}, bf16[128,256]{1,0:T(8,128)(2,1)S(1)}, u32[]{:S(2)}, u32[]{:S(2)}) collective-permute-start(bf16[128,256]{1,0:T(8,128)(2,1)} %share_probe.1.refs_0_), channel_id=1, source_target_pairs={{0,4},{4,0},{8,12},{12,8},{16,20},{20,16},{24,28},{28,24},{1,5},{5... | collective-permute-start | bytes 196616 | tf_op jit(solution)/shard_map/ppermute | solution.py:17
  9.5 0.0 copy-start.1
  9.5 2.2 %copy-done.1 = bf16[1024,2048]{1,0:T(8,128)(2,1)S(1)} copy-done((bf16[1024,2048]{1,0:T(8,128)(2,1)S(1)}, bf16[1024,2048]{1,0:T(8,128)(2,1)}, u32[]{:S(2)}) %copy-start.1) | copy-done | bytes 4194328
  11.7 0.7 %copy-done.3 = f32[1024]{0:T(1024)S(1)} copy-done((f32[1024]{0:T(1024)S(1)}, f32[1024]{0:T(1024)}, u32[]{:S(2)}) %copy-start.3) | copy-done | bytes 4120
  12.4 1.3 %weigh.1 = (bf16[1024,2048]{1,0:T(8,128)(2,1)S(1)}, bf16[1024,2048]{1,0:T(8,128)(2,1)S(1)}) custom-call(s32[1]{0:T(128)S(6)} %copy.7.count, f32[8,128]{1,0:T(8,128)S(1)} %bitcast.5, bf16[1024,2048]{1,0:T(8,128)(2,1)S(1)} %copy-done.1), custom_call_target="tpu_custom_call" | custom-call | flops 4194304 | bytes 12582912 | tf_op jit(solution)/shard_map/weigh/pallas_call | solution.py:172
  13.7 0.0 collective-permute-done.5.refs_6_
  13.8 0.5 collective-permute-start.6
  14.2 0.0 collective-permute-done.3.refs_4_
  14.2 1.6 %collective-permute-start.4 = (bf16[128,256]{1,0:T(8,128)(2,1)S(1)}, bf16[128,256]{1,0:T(8,128)(2,1)S(1)}, u32[]{:S(2)}, u32[]{:S(2)}) collective-permute-start(bf16[128,256]{1,0:T(8,128)(2,1)S(1)} %collective-permute-done.3.refs_4_), channel_id=1, source_target_pairs={{0,4},{4,0},{8,12},{12,8},{16,20},{20,16},{24,28},{28,24},{1,5},{5... | collective-permute-start | bytes 196616 | tf_op jit(solution)/shard_map/ppermute | solution.py:17
  15.8 0.0 collective-permute-done.1.refs_2_
  15.8 0.4 collective-permute-start.2
  16.2 0.1 pad_add_fusion.info
  16.3 0.0 collective-permute-done.refs_1_
  16.3 1.8 %collective-permute-done.6.refs_7_ = bf16[128,256]{1,0:T(8,128)(2,1)S(1)} collective-permute-done((bf16[128,256]{1,0:T(8,128)(2,1)S(1)}, bf16[128,256]{1,0:T(8,128)(2,1)S(1)}, u32[]{:S(2)}, u32[]{:S(2)}) %collective-permute-start.6) | collective-permute-done | bytes 65568 | tf_op jit(solution)/shard_map/ppermute | solution.py:17
  18.1 0.7 %collective-permute-done.4.refs_5_ = bf16[128,256]{1,0:T(8,128)(2,1)S(1)} collective-permute-done((bf16[128,256]{1,0:T(8,128)(2,1)S(1)}, bf16[128,256]{1,0:T(8,128)(2,1)S(1)}, u32[]{:S(2)}, u32[]{:S(2)}) %collective-permute-start.4) | collective-permute-done | bytes 65568 | tf_op jit(solution)/shard_map/ppermute | solution.py:17
  18.8 1.3 %collective-permute-done.2.refs_3_ = bf16[128,256]{1,0:T(8,128)(2,1)S(1)} collective-permute-done((bf16[128,256]{1,0:T(8,128)(2,1)S(1)}, bf16[128,256]{1,0:T(8,128)(2,1)S(1)}, u32[]{:S(2)}, u32[]{:S(2)}) %collective-permute-start.2) | collective-permute-done | bytes 65568 | tf_op jit(solution)/shard_map/ppermute | solution.py:17
  20.1 0.9 %pick_listed.1.refs_0_ = bf16[512,256]{1,0:T(8,128)(2,1)S(1)} custom-call(s32[24]{0:T(128)S(1)} %pad_add_fusion.info, bf16[1024,2048]{1,0:T(8,128)(2,1)S(1)} %get-tuple-element.20.ready.weighted, bf16[128,256]{1,0:T(8,128)(2,1)S(1)} %copy-done.2, bf16[128,256]{1,0:T(8,128)(2,1)S(1)} %collective-permute-done.refs_1_, ...), custom_call_target="tpu_custom_call" | custom-call | tf_op jit(solution)/shard_map/pick_listed/pallas_call | solution.py:217
  21.0 1.6 %collective-permute-start.8 = (bf16[512,256]{1,0:T(8,128)(2,1)S(1)}, bf16[512,256]{1,0:T(8,128)(2,1)S(1)}, u32[]{:S(2)}, u32[]{:S(2)}) collective-permute-start(bf16[512,256]{1,0:T(8,128)(2,1)S(1)} %pick_listed.1.refs_0_), channel_id=1, source_target_pairs={{0,2},{1,3},{2,0},{3,1},{4,6},{5,7},{6,4},{7,5},{8,10},{9,11},{10,... | collective-permute-start | bytes 786440 | tf_op jit(solution)/shard_map/ppermute | solution.py:17
  22.6 0.0 collective-permute-start.7
  22.6 4.8 %collective-permute-done.8.refs_2_ = bf16[512,256]{1,0:T(8,128)(2,1)S(1)} collective-permute-done((bf16[512,256]{1,0:T(8,128)(2,1)S(1)}, bf16[512,256]{1,0:T(8,128)(2,1)S(1)}, u32[]{:S(2)}, u32[]{:S(2)}) %collective-permute-start.8) | collective-permute-done | bytes 262176 | tf_op jit(solution)/shard_map/ppermute | solution.py:17
  27.4 0.0 collective-permute-start.9
  27.4 0.0 collective-permute-done.7.refs_1_
  27.4 1.5 %collective-permute-done.9.refs_3_ = bf16[512,256]{1,0:T(8,128)(2,1)S(1)} collective-permute-done((bf16[512,256]{1,0:T(8,128)(2,1)S(1)}, bf16[512,256]{1,0:T(8,128)(2,1)S(1)}, u32[]{:S(2)}, u32[]{:S(2)}) %collective-permute-start.9) | collective-permute-done | bytes 262176 | tf_op jit(solution)/shard_map/ppermute | solution.py:17
  29.0 4.6 %product.1 = (f32[64,2048]{1,0:T(8,128)S(1)}, bf16[64,2048]{1,0:T(8,128)(2,1)S(1)}, f32[64,2048]{1,0:T(8,128)S(1)}, bf16[64,2048]{1,0:T(8,128)(2,1)S(1)}) custom-call(bf16[1024,2048]{1,0:T(8,128)(2,1)S(1)} %get-tuple-element.19.held, bf16[1024,2048]{1,0:T(8,128)(2,1)S(1)} %get-tuple-element.20.ready.weighted, bf16[512,256]{1,0:T(8,128)(2,1)S(1)} %pick_listed.1.refs_0_, ...), custom_call_target="tpu_custom_call" | custom-call | flops 2147483648 | bytes 8388608 | tf_op jit(solution)/shard_map/product/pallas_call | solution.py:218
  33.6 0.2 collective-permute-start.10
  33.8 0.4 collective-permute-start.12
  34.2 1.0 %collective-permute-done.10 = bf16[64,2048]{1,0:T(8,128)(2,1)S(1)} collective-permute-done((bf16[64,2048]{1,0:T(8,128)(2,1)S(1)}, bf16[64,2048]{1,0:T(8,128)(2,1)S(1)}, u32[]{:S(2)}, u32[]{:S(2)}) %collective-permute-start.10) | collective-permute-done | bytes 262176 | tf_op jit(solution)/shard_map/ppermute | solution.py:17
  35.2 1.6 %collective-permute-start.11 = (bf16[64,2048]{1,0:T(8,128)(2,1)S(1)}, bf16[64,2048]{1,0:T(8,128)(2,1)S(1)}, u32[]{:S(2)}, u32[]{:S(2)}) collective-permute-start(bf16[64,2048]{1,0:T(8,128)(2,1)S(1)} %add_convert_fusion), channel_id=1, source_target_pairs={{0,2},{1,3},{2,0},{3,1},{4,6},{5,7},{6,4},{7,5},{8,10},{9,11},{10,... | collective-permute-start | bytes 786440 | tf_op jit(solution)/shard_map/ppermute | solution.py:17
  36.8 0.0 collective-permute-done.12.refs_2_
  36.8 6.8 %collective-permute-done.11.refs_1_ = bf16[64,2048]{1,0:T(8,128)(2,1)S(1)} collective-permute-done((bf16[64,2048]{1,0:T(8,128)(2,1)S(1)}, bf16[64,2048]{1,0:T(8,128)(2,1)S(1)}, u32[]{:S(2)}, u32[]{:S(2)}) %collective-permute-start.11) | collective-permute-done | bytes 262176 | tf_op jit(solution)/shard_map/ppermute | solution.py:17
  43.6 0.8 %place.1 = (f32[64,512]{1,0:T(8,128)S(1)}, bf16[64,512]{1,0:T(8,128)(2,1)S(1)}, f32[64,512]{1,0:T(8,128)S(1)}, bf16[64,512]{1,0:T(8,128)(2,1)S(1)}, f32[64,512]{...) custom-call(s32[24]{0:T(128)S(1)} %pad_add_fusion.info, ...), custom_call_target="tpu_custom_call" | custom-call | tf_op jit(solution)/shard_map/place/pallas_call | solution.py:219
  44.4 1.0 %collective-permute-start.13 = (bf16[64,512]{1,0:T(8,128)(2,1)S(1)}, bf16[64,512]{1,0:T(8,128)(2,1)S(1)}, u32[]{:S(2)}, u32[]{:S(2)}) collective-permute-start(bf16[64,512]{1,0:T(8,128)(2,1)S(1)} %get-tuple-element.27), channel_id=1, source_target_pairs={{0,4},{4,0},{8,12},{12,8},{16,20},{20,16},{24,28},{28,24},{1,5},{5... | collective-permute-start | bytes 196616 | tf_op jit(solution)/shard_map/ppermute | solution.py:17
  45.4 1.1 %collective-permute-start.15 = (bf16[64,512]{1,0:T(8,128)(2,1)S(1)}, bf16[64,512]{1,0:T(8,128)(2,1)S(1)}, u32[]{:S(2)}, u32[]{:S(2)}) collective-permute-start(bf16[64,512]{1,0:T(8,128)(2,1)S(1)} %get-tuple-element.29), channel_id=1, source_target_pairs={{0,4},{4,0},{8,12},{12,8},{16,20},{20,16},{24,28},{28,24},{1,5},{5... | collective-permute-start | bytes 196616 | tf_op jit(solution)/shard_map/ppermute | solution.py:17
  46.5 0.9 %collective-permute-start.17 = (bf16[64,512]{1,0:T(8,128)(2,1)S(1)}, bf16[64,512]{1,0:T(8,128)(2,1)S(1)}, u32[]{:S(2)}, u32[]{:S(2)}) collective-permute-start(bf16[64,512]{1,0:T(8,128)(2,1)S(1)} %get-tuple-element.31), channel_id=1, source_target_pairs={{0,4},{4,0},{8,12},{12,8},{16,20},{20,16},{24,28},{28,24},{1,5},{5... | collective-permute-start | bytes 196616 | tf_op jit(solution)/shard_map/ppermute | solution.py:17
  47.5 1.1 %collective-permute-start.19 = (bf16[64,512]{1,0:T(8,128)(2,1)S(1)}, bf16[64,512]{1,0:T(8,128)(2,1)S(1)}, u32[]{:S(2)}, u32[]{:S(2)}) collective-permute-start(bf16[64,512]{1,0:T(8,128)(2,1)S(1)} %get-tuple-element.32), channel_id=1, source_target_pairs={{0,4},{4,0},{8,12},{12,8},{16,20},{20,16},{24,28},{28,24},{1,5},{5... | collective-permute-start | bytes 196616 | tf_op jit(solution)/shard_map/ppermute | solution.py:17
  48.5 0.9 %collective-permute-done.13 = bf16[64,512]{1,0:T(8,128)(2,1)S(1)} collective-permute-done((bf16[64,512]{1,0:T(8,128)(2,1)S(1)}, bf16[64,512]{1,0:T(8,128)(2,1)S(1)}, u32[]{:S(2)}, u32[]{:S(2)}) %collective-permute-start.13) | collective-permute-done | bytes 65568 | tf_op jit(solution)/shard_map/ppermute | solution.py:17
  49.5 3.7 %collective-permute-start.14 = (bf16[64,512]{1,0:T(8,128)(2,1)S(1)}, bf16[64,512]{1,0:T(8,128)(2,1)S(1)}, u32[]{:S(2)}, u32[]{:S(2)}) collective-permute-start(bf16[64,512]{1,0:T(8,128)(2,1)S(1)} %add_convert_fusion.4), channel_id=1, source_target_pairs={{0,24},{4,28},{8,16},{12,20},{16,8},{20,12},{24,0},{28,4},{1,25},{... | collective-permute-start | bytes 196616 | tf_op jit(solution)/shard_map/ppermute | solution.py:17
  53.2 0.1 collective-permute-start.16
  53.2 0.0 collective-permute-done.17
  53.3 1.7 %collective-permute-start.18 = (bf16[64,512]{1,0:T(8,128)(2,1)S(1)}, bf16[64,512]{1,0:T(8,128)(2,1)S(1)}, u32[]{:S(2)}, u32[]{:S(2)}) collective-permute-start(bf16[64,512]{1,0:T(8,128)(2,1)S(1)} %add_convert_fusion.2), channel_id=1, source_target_pairs={{0,8},{4,12},{8,0},{12,4},{16,24},{20,28},{24,16},{28,20},{1,9},{5... | collective-permute-start | bytes 196616 | tf_op jit(solution)/shard_map/ppermute | solution.py:17
  55.0 1.0 %collective-permute-done.14 = bf16[64,512]{1,0:T(8,128)(2,1)S(1)} collective-permute-done((bf16[64,512]{1,0:T(8,128)(2,1)S(1)}, bf16[64,512]{1,0:T(8,128)(2,1)S(1)}, u32[]{:S(2)}, u32[]{:S(2)}) %collective-permute-start.14) | collective-permute-done | bytes 65568 | tf_op jit(solution)/shard_map/ppermute | solution.py:17
  56.0 2.4 %collective-permute-done.16 = bf16[64,512]{1,0:T(8,128)(2,1)S(1)} collective-permute-done((bf16[64,512]{1,0:T(8,128)(2,1)S(1)}, bf16[64,512]{1,0:T(8,128)(2,1)S(1)}, u32[]{:S(2)}, u32[]{:S(2)}) %collective-permute-start.16) | collective-permute-done | bytes 65568 | tf_op jit(solution)/shard_map/ppermute | solution.py:17
  58.4 0.0 collective-permute-done.18
  58.4 0.7 %fusion = bf16[512,64]{0,1:T(8,128)(2,1)} fusion(bf16[64,512]{1,0:T(8,128)(2,1)S(1)} %collective-permute-done.19, bf16[64,512]{1,0:T(8,128)(2,1)S(1)} %collective-permute-done.18, bf16[64,512]{1,0:T(8,128)(2,1)S(1)} %collective-permute-done.16, f32[64,512]{1,0:T(8,128)S(1)} %get-tuple-element.25, bf16[64,512]{1,0:T(8,128)(2,1)S(1)} %collective-permute-done.14), kind=kLoop, calls=%fused_computation.5 | loop fusion | flops 294912 | bytes 458752 | tf_op jit(solution)/shard_map/convert_element_type | solution.py:220
  (14 shorter events, 0.1 us)
Async XLA Ops:
  0.0 13.7 %copy-start = (s32[8,8]{1,0:T(8,128)S(1)}, s32[8,8]{1,0:T(8,128)}, u32[]{:S(2)}) copy-start(s32[8,8]{1,0:T(8,128)} %param.9) | copy-start | bytes 772
  0.0 16.2 %copy-start.4 = (s32[16]{0:T(128)S(1)}, s32[16]{0:T(128)}, u32[]{:S(2)}) copy-start(s32[16]{0:T(128)} %param.10) | copy-start | bytes 196
  1.5 12.3 %collective-permute-start.5 = (bf16[128,256]{1,0:T(8,128)(2,1)}, bf16[128,256]{1,0:T(8,128)(2,1)S(1)}, u32[]{:S(2)}, u32[]{:S(2)}) collective-permute-start(bf16[128,256]{1,0:T(8,128)(2,1)} %share_probe.1.refs_0_), channel_id=1, source_target_pairs={{0,24},{4,28},{8,16},{12,20},{16,8},{20,12},{24,0},{28,4},{1,25},{... | collective-permute-start | bytes 196616 | tf_op jit(solution)/shard_map/ppermute | solution.py:17
  6.6 7.6 %collective-permute-start.3 = (bf16[128,256]{1,0:T(8,128)(2,1)}, bf16[128,256]{1,0:T(8,128)(2,1)S(1)}, u32[]{:S(2)}, u32[]{:S(2)}) collective-permute-start(bf16[128,256]{1,0:T(8,128)(2,1)} %share_probe.1.refs_0_), channel_id=1, source_target_pairs={{0,16},{4,20},{8,24},{12,28},{16,0},{20,4},{24,8},{28,12},{1,17},{... | collective-permute-start | bytes 196616 | tf_op jit(solution)/shard_map/ppermute | solution.py:17
  6.6 9.3 %collective-permute-start.1 = (bf16[128,256]{1,0:T(8,128)(2,1)}, bf16[128,256]{1,0:T(8,128)(2,1)S(1)}, u32[]{:S(2)}, u32[]{:S(2)}) collective-permute-start(bf16[128,256]{1,0:T(8,128)(2,1)} %share_probe.1.refs_0_), channel_id=1, source_target_pairs={{0,8},{4,12},{8,0},{12,4},{16,24},{20,28},{24,16},{28,20},{1,9},{5... | collective-permute-start | bytes 196616 | tf_op jit(solution)/shard_map/ppermute | solution.py:17
  7.2 9.1 %collective-permute-start = (bf16[128,256]{1,0:T(8,128)(2,1)}, bf16[128,256]{1,0:T(8,128)(2,1)S(1)}, u32[]{:S(2)}, u32[]{:S(2)}) collective-permute-start(bf16[128,256]{1,0:T(8,128)(2,1)} %share_probe.1.refs_0_), channel_id=1, source_target_pairs={{0,4},{4,0},{8,12},{12,8},{16,20},{20,16},{24,28},{28,24},{1,5},{5... | collective-permute-start | bytes 196616 | tf_op jit(solution)/shard_map/ppermute | solution.py:17
  9.5 2.2 %copy-start.1 = (bf16[1024,2048]{1,0:T(8,128)(2,1)S(1)}, bf16[1024,2048]{1,0:T(8,128)(2,1)}, u32[]{:S(2)}) copy-start(bf16[1024,2048]{1,0:T(8,128)(2,1)} %jac.1) | copy-start | bytes 12582916
  11.7 0.7 %copy-start.3 = (f32[1024]{0:T(1024)S(1)}, f32[1024]{0:T(1024)}, u32[]{:S(2)}) copy-start(f32[1024]{0:T(1024)} %param.7) | copy-start | bytes 12292
  12.4 7.7 %copy-start.2 = (bf16[128,256]{1,0:T(8,128)(2,1)S(1)}, bf16[128,256]{1,0:T(8,128)(2,1)}, u32[]{:S(2)}) copy-start(bf16[128,256]{1,0:T(8,128)(2,1)} %share_probe.1.refs_0_) | copy-start | bytes 196612
  13.8 4.4 %collective-permute-start.6 = (bf16[128,256]{1,0:T(8,128)(2,1)S(1)}, bf16[128,256]{1,0:T(8,128)(2,1)S(1)}, u32[]{:S(2)}, u32[]{:S(2)}) collective-permute-start(bf16[128,256]{1,0:T(8,128)(2,1)S(1)} %collective-permute-done.5.refs_6_), channel_id=1, source_target_pairs={{0,4},{4,0},{8,12},{12,8},{16,20},{20,16},{24,28},{28,24},{1,5},{5... | collective-permute-start | bytes 196616 | tf_op jit(solution)/shard_map/ppermute | solution.py:17
  14.2 4.6 %collective-permute-start.4 = (bf16[128,256]{1,0:T(8,128)(2,1)S(1)}, bf16[128,256]{1,0:T(8,128)(2,1)S(1)}, u32[]{:S(2)}, u32[]{:S(2)}) collective-permute-start(bf16[128,256]{1,0:T(8,128)(2,1)S(1)} %collective-permute-done.3.refs_4_), channel_id=1, source_target_pairs={{0,4},{4,0},{8,12},{12,8},{16,20},{20,16},{24,28},{28,24},{1,5},{5... | collective-permute-start | bytes 196616 | tf_op jit(solution)/shard_map/ppermute | solution.py:17
  15.8 4.3 %collective-permute-start.2 = (bf16[128,256]{1,0:T(8,128)(2,1)S(1)}, bf16[128,256]{1,0:T(8,128)(2,1)S(1)}, u32[]{:S(2)}, u32[]{:S(2)}) collective-permute-start(bf16[128,256]{1,0:T(8,128)(2,1)S(1)} %collective-permute-done.1.refs_2_), channel_id=1, source_target_pairs={{0,4},{4,0},{8,12},{12,8},{16,20},{20,16},{24,28},{28,24},{1,5},{5... | collective-permute-start | bytes 196616 | tf_op jit(solution)/shard_map/ppermute | solution.py:17
  21.0 6.4 %collective-permute-start.8 = (bf16[512,256]{1,0:T(8,128)(2,1)S(1)}, bf16[512,256]{1,0:T(8,128)(2,1)S(1)}, u32[]{:S(2)}, u32[]{:S(2)}) collective-permute-start(bf16[512,256]{1,0:T(8,128)(2,1)S(1)} %pick_listed.1.refs_0_), channel_id=1, source_target_pairs={{0,2},{1,3},{2,0},{3,1},{4,6},{5,7},{6,4},{7,5},{8,10},{9,11},{10,... | collective-permute-start | bytes 786440 | tf_op jit(solution)/shard_map/ppermute | solution.py:17
  22.6 4.9 %collective-permute-start.7 = (bf16[512,256]{1,0:T(8,128)(2,1)S(1)}, bf16[512,256]{1,0:T(8,128)(2,1)S(1)}, u32[]{:S(2)}, u32[]{:S(2)}) collective-permute-start(bf16[512,256]{1,0:T(8,128)(2,1)S(1)} %pick_listed.1.refs_0_), channel_id=1, source_target_pairs={{0,1},{1,0},{2,3},{3,2},{4,5},{5,4},{6,7},{7,6},{8,9},{9,8},{10,11... | collective-permute-start | bytes 786440 | tf_op jit(solution)/shard_map/ppermute | solution.py:17
  27.4 1.5 %collective-permute-start.9 = (bf16[512,256]{1,0:T(8,128)(2,1)S(1)}, bf16[512,256]{1,0:T(8,128)(2,1)S(1)}, u32[]{:S(2)}, u32[]{:S(2)}) collective-permute-start(bf16[512,256]{1,0:T(8,128)(2,1)S(1)} %collective-permute-done.8.refs_2_), channel_id=1, source_target_pairs={{0,1},{1,0},{2,3},{3,2},{4,5},{5,4},{6,7},{7,6},{8,9},{9,8},{10,11... | collective-permute-start | bytes 786440 | tf_op jit(solution)/shard_map/ppermute | solution.py:17
  33.6 1.6 %collective-permute-start.10 = (bf16[64,2048]{1,0:T(8,128)(2,1)S(1)}, bf16[64,2048]{1,0:T(8,128)(2,1)S(1)}, u32[]{:S(2)}, u32[]{:S(2)}) collective-permute-start(bf16[64,2048]{1,0:T(8,128)(2,1)S(1)} %get-tuple-element.23), channel_id=1, source_target_pairs={{0,1},{1,0},{2,3},{3,2},{4,5},{5,4},{6,7},{7,6},{8,9},{9,8},{10,11... | collective-permute-start | bytes 786440 | tf_op jit(solution)/shard_map/ppermute | solution.py:17
  33.8 3.0 %collective-permute-start.12 = (bf16[64,2048]{1,0:T(8,128)(2,1)S(1)}, bf16[64,2048]{1,0:T(8,128)(2,1)S(1)}, u32[]{:S(2)}, u32[]{:S(2)}) collective-permute-start(bf16[64,2048]{1,0:T(8,128)(2,1)S(1)} %get-tuple-element.24), channel_id=1, source_target_pairs={{0,1},{1,0},{2,3},{3,2},{4,5},{5,4},{6,7},{7,6},{8,9},{9,8},{10,11... | collective-permute-start | bytes 786440 | tf_op jit(solution)/shard_map/ppermute | solution.py:17
  35.2 8.4 %collective-permute-start.11 = (bf16[64,2048]{1,0:T(8,128)(2,1)S(1)}, bf16[64,2048]{1,0:T(8,128)(2,1)S(1)}, u32[]{:S(2)}, u32[]{:S(2)}) collective-permute-start(bf16[64,2048]{1,0:T(8,128)(2,1)S(1)} %add_convert_fusion), channel_id=1, source_target_pairs={{0,2},{1,3},{2,0},{3,1},{4,6},{5,7},{6,4},{7,5},{8,10},{9,11},{10,... | collective-permute-start | bytes 786440 | tf_op jit(solution)/shard_map/ppermute | solution.py:17
  44.4 5.0 %collective-permute-start.13 = (bf16[64,512]{1,0:T(8,128)(2,1)S(1)}, bf16[64,512]{1,0:T(8,128)(2,1)S(1)}, u32[]{:S(2)}, u32[]{:S(2)}) collective-permute-start(bf16[64,512]{1,0:T(8,128)(2,1)S(1)} %get-tuple-element.27), channel_id=1, source_target_pairs={{0,4},{4,0},{8,12},{12,8},{16,20},{20,16},{24,28},{28,24},{1,5},{5... | collective-permute-start | bytes 196616 | tf_op jit(solution)/shard_map/ppermute | solution.py:17
  45.4 7.7 %collective-permute-start.15 = (bf16[64,512]{1,0:T(8,128)(2,1)S(1)}, bf16[64,512]{1,0:T(8,128)(2,1)S(1)}, u32[]{:S(2)}, u32[]{:S(2)}) collective-permute-start(bf16[64,512]{1,0:T(8,128)(2,1)S(1)} %get-tuple-element.29), channel_id=1, source_target_pairs={{0,4},{4,0},{8,12},{12,8},{16,20},{20,16},{24,28},{28,24},{1,5},{5... | collective-permute-start | bytes 196616 | tf_op jit(solution)/shard_map/ppermute | solution.py:17
  46.5 6.7 %collective-permute-start.17 = (bf16[64,512]{1,0:T(8,128)(2,1)S(1)}, bf16[64,512]{1,0:T(8,128)(2,1)S(1)}, u32[]{:S(2)}, u32[]{:S(2)}) collective-permute-start(bf16[64,512]{1,0:T(8,128)(2,1)S(1)} %get-tuple-element.31), channel_id=1, source_target_pairs={{0,4},{4,0},{8,12},{12,8},{16,20},{20,16},{24,28},{28,24},{1,5},{5... | collective-permute-start | bytes 196616 | tf_op jit(solution)/shard_map/ppermute | solution.py:17
  47.5 7.6 %collective-permute-start.19 = (bf16[64,512]{1,0:T(8,128)(2,1)S(1)}, bf16[64,512]{1,0:T(8,128)(2,1)S(1)}, u32[]{:S(2)}, u32[]{:S(2)}) collective-permute-start(bf16[64,512]{1,0:T(8,128)(2,1)S(1)} %get-tuple-element.32), channel_id=1, source_target_pairs={{0,4},{4,0},{8,12},{12,8},{16,20},{20,16},{24,28},{28,24},{1,5},{5... | collective-permute-start | bytes 196616 | tf_op jit(solution)/shard_map/ppermute | solution.py:17
  49.5 6.6 %collective-permute-start.14 = (bf16[64,512]{1,0:T(8,128)(2,1)S(1)}, bf16[64,512]{1,0:T(8,128)(2,1)S(1)}, u32[]{:S(2)}, u32[]{:S(2)}) collective-permute-start(bf16[64,512]{1,0:T(8,128)(2,1)S(1)} %add_convert_fusion.4), channel_id=1, source_target_pairs={{0,24},{4,28},{8,16},{12,20},{16,8},{20,12},{24,0},{28,4},{1,25},{... | collective-permute-start | bytes 196616 | tf_op jit(solution)/shard_map/ppermute | solution.py:17
  53.2 5.2 %collective-permute-start.16 = (bf16[64,512]{1,0:T(8,128)(2,1)S(1)}, bf16[64,512]{1,0:T(8,128)(2,1)S(1)}, u32[]{:S(2)}, u32[]{:S(2)}) collective-permute-start(bf16[64,512]{1,0:T(8,128)(2,1)S(1)} %add_convert_fusion.3), channel_id=1, source_target_pairs={{0,16},{4,20},{8,24},{12,28},{16,0},{20,4},{24,8},{28,12},{1,17},{... | collective-permute-start | bytes 196616 | tf_op jit(solution)/shard_map/ppermute | solution.py:17
  53.3 5.1 %collective-permute-start.18 = (bf16[64,512]{1,0:T(8,128)(2,1)S(1)}, bf16[64,512]{1,0:T(8,128)(2,1)S(1)}, u32[]{:S(2)}, u32[]{:S(2)}) collective-permute-start(bf16[64,512]{1,0:T(8,128)(2,1)S(1)} %add_convert_fusion.2), channel_id=1, source_target_pairs={{0,8},{4,12},{8,0},{12,4},{16,24},{20,28},{24,16},{28,20},{1,9},{5... | collective-permute-start | bytes 196616 | tf_op jit(solution)/shard_map/ppermute | solution.py:17

commit v4 on v3

--- a/solution.py
+++ b/solution.py
@@ -8,6 +8,9 @@
 from jax.sharding import PartitionSpec as P
 
 MIB = 1024 * 1024
+SUB_DIRECT = 2
+OBS_DIRECT = 4
+COLUMNS = 512
 SMEM = pl.BlockSpec(memory_space=pltpu.SMEM)
 VMEM = pl.BlockSpec(memory_space=pltpu.VMEM)
 HBM = pl.BlockSpec(memory_space=pltpu.HBM)
@@ -21,42 +24,29 @@
     return [2 * high for high in range(count // 2 - 1, 0, -1)]
 
 
-def spread(value, axis, count):
+def spread(value, axis, count, before=None):
     held = {0: value}
     for step in far_steps(count):
         held[step] = swap(value, axis, count, step)
     held[1] = swap(value, axis, count, 1)
     for step in far_steps(count):
-        held[step + 1] = swap(held[step], axis, count, 1)
+        passed = held[step] if before is None else lax.optimization_barrier((held[step], before))[0]
+        held[step + 1] = swap(passed, axis, count, 1)
     return [held[step] for step in range(count)]
 
 
-def collect(terms, axis, count):
+def collect(terms, axis, count, direct):
     parts = [terms[0]]
-    for step in far_steps(count):
+    for step in range(count - 2, direct - 1, -2):
         passed = swap(terms[step + 1], axis, count, 1)
         both = (terms[step] + passed.astype(jnp.float32)).astype(jnp.bfloat16)
         parts.append(swap(both, axis, count, step))
-    parts.append(swap(terms[1], axis, count, 1))
+    for step in range(min(direct, count) - 1, 0, -1):
+        parts.append(swap(terms[step], axis, count, step))
     return parts
 
 
-def share_kernel(unit, subs, probe, out, sems):
-    sub = lax.axis_index("sub")
-    part = unit // subs
-    copies = [
-        pltpu.make_async_copy(
-            probe.at[pl.ds(pl.multiple_of(u * unit + sub * part, part), part)],
-            out.at[pl.ds(u * part, part)], sems.at[u])
-        for u in range(sems.shape[0])
-    ]
-    for copy in copies:
-        copy.start()
-    for copy in copies:
-        copy.wait()
-
-
-def weigh_kernel(count, weight, jac, held, weighted, sems):
+def weigh_kernel(count, weight, jac, after, held, weighted, sems):
     rows, width = held.shape
     chunk = rows // sems.shape[0]
     copies = [
@@ -77,7 +67,7 @@
             weighted[r:r + lanes, :] = (held[r:r + lanes, :].astype(jnp.float32) * scale).astype(jnp.bfloat16)
 
 
-def pick_kernel(unit, tile, subs, listed, info, ready, *refs):
+def pick_kernel(unit, tile, subs, listed, info, *refs):
     pieces, out, position = refs[:-2], refs[-2], refs[-1]
     block = lax.axis_index("obs")
     part = unit // subs
@@ -99,7 +89,7 @@
 
 def product_kernel(unit, subs, held, weighted, *refs):
     pieces, outs = refs[:subs], refs[subs:2 * subs]
-    probe, product = refs[2 * subs:]
+    probe, image_t = refs[2 * subs:]
     sub = lax.axis_index("sub")
     width = held.shape[1]
     part = unit // subs
@@ -108,12 +98,14 @@
             first = pl.multiple_of(g * unit + (sub ^ j) * part, part)
             probe[pl.ds(first, part), :] = pieces[j][g * part:(g + 1) * part, :]
     image = jnp.dot(held[...], probe[...], preferred_element_type=jnp.float32)
-    image_t = image.astype(jnp.bfloat16).T
-    product[...] = jnp.dot(image_t, weighted[...], preferred_element_type=jnp.float32)
-    high = product.shape[0] // subs
-    for j in range(subs):
-        first = pl.multiple_of((sub ^ j) * high, high)
-        outs[j][...] = product[pl.ds(first, high), :].astype(outs[j].dtype)
+    image_t[...] = image.astype(jnp.bfloat16).T
+    high = image_t.shape[0] // subs
+    by_step = [image_t[pl.ds(pl.multiple_of((sub ^ j) * high, high), high), :] for j in range(subs)]
+    by_step = jnp.concatenate(by_step, axis=0)
+    for n in range(0, width, COLUMNS):
+        product = jnp.dot(by_step, weighted[:, n:n + COLUMNS], preferred_element_type=jnp.float32)
+        for j in range(subs):
+            outs[j][:, n:n + COLUMNS] = product[j * high:(j + 1) * high, :].astype(outs[j].dtype)
 
 
 def place_kernel(unit, tile, listed, parts_count, info, *refs):
@@ -141,8 +133,8 @@
             out[:, u * unit:(u + 1) * unit] = taken.astype(out.dtype)
 
 
-def kept(step):
-    return jnp.float32 if step % 2 == 0 else jnp.bfloat16
+def kept(step, direct):
+    return jnp.float32 if step == 0 or step >= direct and step % 2 == 0 else jnp.bfloat16
 
 
 def local(obs_count, subs, jacobian, obs_weight, row_counts, tile_lists, tile_slot, probe_block):
@@ -159,44 +151,39 @@
     def params(mib):
         return pltpu.CompilerParams(vmem_limit_bytes=mib * MIB)
 
-    share = pl.pallas_call(
-        functools.partial(share_kernel, unit, subs),
-        out_shape=jax.ShapeDtypeStruct((own_rows // subs, probe_width), jnp.bfloat16),
-        in_specs=[HBM],
+    share = probe_block.reshape(own_rows // unit, subs, unit // subs, probe_width)
+    share = lax.dynamic_index_in_dim(share, lax.axis_index("sub"), 1, keepdims=False)
+    share = share.reshape(own_rows // subs, probe_width)
+    pick = pl.pallas_call(
+        functools.partial(pick_kernel, unit, tile, subs, listed),
+        out_shape=jax.ShapeDtypeStruct((width // subs, probe_width), jnp.bfloat16),
+        in_specs=[SMEM] + [VMEM] * obs_count,
         out_specs=VMEM,
-        scratch_shapes=[pltpu.SemaphoreType.DMA((own_rows // unit,))],
-        compiler_params=params(60),
-        name="share_probe",
-    )(probe_block)
+        scratch_shapes=[pltpu.SMEM((tiles,), jnp.int32)],
+        compiler_params=params(8),
+        name="pick_listed",
+    )
+    picked = pick(info, *spread(share, "obs", obs_count))
     weight_lanes = min(128, rows)
     held, weighted = pl.pallas_call(
         weigh_kernel,
         out_shape=[jax.ShapeDtypeStruct((rows, width), jnp.bfloat16)] * 2,
-        in_specs=[SMEM, VMEM, HBM],
+        in_specs=[SMEM, VMEM, HBM, pl.BlockSpec(memory_space=pl.ANY)],
         out_specs=[VMEM, VMEM],
         scratch_shapes=[pltpu.SemaphoreType.DMA((4,))],
         compiler_params=params(16),
         cost_estimate=pl.CostEstimate(flops=2 * rows * width, bytes_accessed=6 * rows * width, transcendentals=0),
         name="weigh",
-    )(row_counts, obs_weight.reshape(rows // weight_lanes, weight_lanes), jacobian)
-
-    pick = pl.pallas_call(
-        functools.partial(pick_kernel, unit, tile, subs, listed),
-        out_shape=jax.ShapeDtypeStruct((width // subs, probe_width), jnp.bfloat16),
-        in_specs=[SMEM, pl.BlockSpec(memory_space=pl.ANY)] + [VMEM] * obs_count,
-        out_specs=VMEM,
-        scratch_shapes=[pltpu.SMEM((tiles,), jnp.int32)],
-        compiler_params=params(8),
-        name="pick_listed",
-    )
+    )(row_counts, obs_weight.reshape(rows // weight_lanes, weight_lanes), jacobian, picked)
+
     product = pl.pallas_call(
         functools.partial(product_kernel, unit, subs),
-        out_shape=[jax.ShapeDtypeStruct((high, width), kept(j)) for j in range(subs)],
+        out_shape=[jax.ShapeDtypeStruct((high, width), kept(j, SUB_DIRECT)) for j in range(subs)],
         in_specs=[VMEM] * (2 + subs),
         out_specs=[VMEM] * subs,
         scratch_shapes=[
             pltpu.VMEM((width, probe_width), jnp.bfloat16),
-            pltpu.VMEM((probe_width, width), jnp.float32),
+            pltpu.VMEM((probe_width, rows), jnp.bfloat16),
         ],
         compiler_params=params(24),
         cost_estimate=pl.CostEstimate(
@@ -205,7 +192,7 @@
     )
     place = pl.pallas_call(
         functools.partial(place_kernel, unit, tile, listed, subs // 2 + 1),
-        out_shape=[jax.ShapeDtypeStruct((high, own_rows), kept(step)) for step in range(obs_count)],
+        out_shape=[jax.ShapeDtypeStruct((high, own_rows), kept(step, OBS_DIRECT)) for step in range(obs_count)],
         in_specs=[SMEM] + [VMEM] * (subs // 2 + 1),
         out_specs=[VMEM] * obs_count,
         scratch_shapes=[pltpu.SMEM((tiles,), jnp.int32), pltpu.VMEM((high, width), jnp.float32)],
@@ -213,10 +200,9 @@
         name="place",
     )
 
-    pieces = spread(share, "obs", obs_count)
-    columns = spread(pick(info, weighted, *pieces), "sub", subs)
-    terms = collect(product(held, weighted, *columns), "sub", subs)
-    terms = collect(place(info, *terms), "obs", obs_count)
+    columns = spread(picked, "sub", subs, weighted)
+    terms = collect(product(held, weighted, *columns), "sub", subs, SUB_DIRECT)
+    terms = collect(place(info, *terms), "obs", obs_count, OBS_DIRECT)
     return sum(term.astype(jnp.float32) for term in terms).T.astype(jnp.bfloat16)
 
 

time: 59.3 us -> 57 us (0.961)
  waiting for transfers between devices: 22.3 us -> 19.8 us
  local copies, waits for them, and re-layouts: 2.89 us -> 4.52 us
  Pallas kernels: 9.01 us -> 7.66 us
  starting transfers between devices: 23.2 us -> 22.5 us
  other arithmetic: 0.84 us -> 1.48 us
    ppermute x20, waiting for transfers between devices: 22.3 us -> 19.8 us  [swap(): return lax.ppermute(value, axis, [(i, i ^ step) for i in range(count)])]
    pallas_call x4 -> x3, Pallas kernels: 7.69 us -> 6.34 us  [the longest x1 4.7 us: local(): terms = collect(product(held, weighted, *columns), 'sub', subs, SUB_DIRECT)]
    unnamed x10 -> x6, local copies, waits for them, and re-layouts: 2.88 us -> 3.82 us
    ppermute x20, starting transfers between devices: 23.2 us -> 22.5 us  [swap(): return lax.ppermute(value, axis, [(i, i ^ step) for i in range(count)])]
    squeeze x1, local copies, waits for them, and re-layouts: 0.01 us -> 0.69 us  [local(): lax.dynamic_index_in_dim(tile_lists, lax.axis_index('obs'), 0, keepdims=F...]
    concatenate x1, other arithmetic: 0.07 us -> 0.73 us  [local(): info = jnp.concatenate([my_list, tile_slot])]
  transfers between devices with their start and end apart: 20 -> 20, of which waited for: 10 -> 10; matrix products, arithmetic and copies ran while one was open for 0% -> 3% of each run, Pallas kernels for 2% -> 2%
where the time goes in v4:
time: 57 us; the launch traced here: 56.8 us
  starting transfers between devices  22.5 us (39%)
  waiting for transfers between devices  19.8 us (35%)
  Pallas kernels  7.66 us (13%)
  local copies, waits for them, and re-layouts  4.52 us (8%)
  other arithmetic  1.48 us (3%)
  between operations  0.76 us (1%)
    ppermute x20, starting transfers between devices, swap(): return lax.ppermute(value, axis, [(i, i ^ step) for i in range(count)])  22.5 us
    ppermute x20, waiting for transfers between devices, swap(): return lax.ppermute(value, axis, [(i, i ^ step) for i in range(count)])  19.8 us
    pallas_call x1, Pallas kernels, local(): terms = collect(product(held, weighted, *columns), 'sub', subs, SUB_DIRECT)  4.7 us
    unnamed x6, local copies, waits for them, and re-layouts  3.82 us
    pallas_call x1, Pallas kernels, local(): pl.pallas_call(weigh_kernel, out_shape=[jax.ShapeDtypeStruct((rows, width...  1.32 us
  transfers between devices with their start and end apart: 20, of which 10 were waited for; matrix products, arithmetic and copies ran while one was open for 3% of the time, Pallas kernels for 2%

profile of v4, /device:TPU:0, one launch (start us, length us, event | category | flops | bytes accessed | tf_op | source)
XLA Modules:
  0.0 56.8 jit_solution(7198490618502261192)
XLA Ops:
  0.0 0.9 %copy-done = bf16[512,256]{1,0:T(8,128)(2,1)S(1)} copy-done((bf16[512,256]{1,0:T(8,128)(2,1)S(1)}, bf16[512,256]{1,0:T(8,128)(2,1)}, u32[]{:S(2)}) %copy-start) | copy-done | bytes 262168
  1.0 5.0 %collective-permute-start.5 = (bf16[128,256]{1,0:T(8,128)(2,1)S(1)}, bf16[128,256]{1,0:T(8,128)(2,1)S(1)}, u32[]{:S(2)}, u32[]{:S(2)}) collective-permute-start(bf16[128,256]{1,0:T(8,128)(2,1)S(1)} %bitcast.10), channel_id=1, source_target_pairs={{0,24},{4,28},{8,16},{12,20},{16,8},{20,12},{24,0},{28,4},{1,25},{... | collective-permute-start | bytes 196616 | tf_op jit(solution)/shard_map/ppermute | solution.py:20
  6.0 0.0 collective-permute-start.3
  6.0 0.6 %collective-permute-start.1 = (bf16[128,256]{1,0:T(8,128)(2,1)S(1)}, bf16[128,256]{1,0:T(8,128)(2,1)S(1)}, u32[]{:S(2)}, u32[]{:S(2)}) collective-permute-start(bf16[128,256]{1,0:T(8,128)(2,1)S(1)} %bitcast.12), channel_id=1, source_target_pairs={{0,8},{4,12},{8,0},{12,4},{16,24},{20,28},{24,16},{28,20},{1,9},{5... | collective-permute-start | bytes 196616 | tf_op jit(solution)/shard_map/ppermute | solution.py:20
  6.6 1.6 %collective-permute-start = (bf16[128,256]{1,0:T(8,128)(2,1)S(1)}, bf16[128,256]{1,0:T(8,128)(2,1)S(1)}, u32[]{:S(2)}, u32[]{:S(2)}) collective-permute-start(bf16[128,256]{1,0:T(8,128)(2,1)S(1)} %bitcast.13), channel_id=1, source_target_pairs={{0,4},{4,0},{8,12},{12,8},{16,20},{20,16},{24,28},{28,24},{1,5},{5... | collective-permute-start | bytes 196616 | tf_op jit(solution)/shard_map/ppermute | solution.py:20
  8.3 0.7 %dynamic-slice_bitcast_fusion = s32[8]{0:T(128)S(1)} fusion(s32[8,8]{1,0:T(8,128)} %param.9, s32[]{:T(128)S(6)} %select_n.8), kind=kLoop, calls=%fused_computation.6 | loop fusion | bytes 68 | tf_op jit(solution)/shard_map/jit(dynamic_index_in_dim)/squeeze | solution.py:148
  9.0 0.0 collective-permute-done.5.refs_6_
  9.0 1.5 %collective-permute-start.6 = (bf16[128,256]{1,0:T(8,128)(2,1)S(1)}, bf16[128,256]{1,0:T(8,128)(2,1)S(1)}, u32[]{:S(2)}, u32[]{:S(2)}) collective-permute-start(bf16[128,256]{1,0:T(8,128)(2,1)S(1)} %collective-permute-done.5.refs_6_), channel_id=1, source_target_pairs={{0,4},{4,0},{8,12},{12,8},{16,20},{20,16},{24,28},{28,24},{1,5},{5... | collective-permute-start | bytes 196616 | tf_op jit(solution)/shard_map/ppermute | solution.py:20
  10.4 1.2 %collective-permute-done.3.refs_4_ = bf16[128,256]{1,0:T(8,128)(2,1)S(1)} collective-permute-done((bf16[128,256]{1,0:T(8,128)(2,1)S(1)}, bf16[128,256]{1,0:T(8,128)(2,1)S(1)}, u32[]{:S(2)}, u32[]{:S(2)}) %collective-permute-start.3) | collective-permute-done | bytes 65568 | tf_op jit(solution)/shard_map/ppermute | solution.py:20
  11.6 1.5 %collective-permute-start.4 = (bf16[128,256]{1,0:T(8,128)(2,1)S(1)}, bf16[128,256]{1,0:T(8,128)(2,1)S(1)}, u32[]{:S(2)}, u32[]{:S(2)}) collective-permute-start(bf16[128,256]{1,0:T(8,128)(2,1)S(1)} %collective-permute-done.3.refs_4_), channel_id=1, source_target_pairs={{0,4},{4,0},{8,12},{12,8},{16,20},{20,16},{24,28},{28,24},{1,5},{5... | collective-permute-start | bytes 196616 | tf_op jit(solution)/shard_map/ppermute | solution.py:20
  13.1 0.0 collective-permute-done.1.refs_2_
  13.1 0.5 collective-permute-start.2
  13.6 0.7 %pad_add_fusion.info = s32[24]{0:T(128)S(1)} fusion(s32[16]{0:T(128)} %param.10, s32[8]{0:T(128)S(1)} %dynamic-slice_bitcast_fusion), kind=kLoop, calls=%fused_computation.5 | loop fusion | flops 24 | bytes 192 | tf_op jit(solution)/shard_map/concatenate | solution.py:149
  14.4 0.0 collective-permute-done.refs_1_
  14.4 2.1 %collective-permute-done.4.refs_5_ = bf16[128,256]{1,0:T(8,128)(2,1)S(1)} collective-permute-done((bf16[128,256]{1,0:T(8,128)(2,1)S(1)}, bf16[128,256]{1,0:T(8,128)(2,1)S(1)}, u32[]{:S(2)}, u32[]{:S(2)}) %collective-permute-start.4) | collective-permute-done | bytes 65568 | tf_op jit(solution)/shard_map/ppermute | solution.py:20
  16.5 0.9 %collective-permute-done.2.refs_3_ = bf16[128,256]{1,0:T(8,128)(2,1)S(1)} collective-permute-done((bf16[128,256]{1,0:T(8,128)(2,1)S(1)}, bf16[128,256]{1,0:T(8,128)(2,1)S(1)}, u32[]{:S(2)}, u32[]{:S(2)}) %collective-permute-start.2) | collective-permute-done | bytes 65568 | tf_op jit(solution)/shard_map/ppermute | solution.py:20
  17.4 0.9 %pick_listed.1.after.refs_0_ = bf16[512,256]{1,0:T(8,128)(2,1)S(1)} custom-call(s32[24]{0:T(128)S(1)} %pad_add_fusion.info, bf16[128,256]{1,0:T(8,128)(2,1)S(1)} %bitcast.14, bf16[128,256]{1,0:T(8,128)(2,1)S(1)} %collective-permute-done.refs_1_, bf16[128,256]{1,0:T(8,128)(2,1)S(1)} %collective-permute-done.1.refs_2_, ...), custom_call_target="tpu_custom_call" | custom-call | tf_op jit(solution)/shard_map/pick_listed/pallas_call | solution.py:166
  18.2 1.6 %collective-permute-start.8 = (bf16[512,256]{1,0:T(8,128)(2,1)S(1)}, bf16[512,256]{1,0:T(8,128)(2,1)S(1)}, u32[]{:S(2)}, u32[]{:S(2)}) collective-permute-start(bf16[512,256]{1,0:T(8,128)(2,1)S(1)} %pick_listed.1.after.refs_0_), channel_id=1, source_target_pairs={{0,2},{1,3},{2,0},{3,1},{4,6},{5,7},{6,4},{7,5},{8,10},{9,11},{10,... | collective-permute-start | bytes 786440 | tf_op jit(solution)/shard_map/ppermute | solution.py:20
  20.5 0.1 collective-permute-start.7
  20.6 0.0 copy-start.1
  20.6 2.2 %copy-done.1 = bf16[1024,2048]{1,0:T(8,128)(2,1)S(1)} copy-done((bf16[1024,2048]{1,0:T(8,128)(2,1)S(1)}, bf16[1024,2048]{1,0:T(8,128)(2,1)}, u32[]{:S(2)}) %copy-start.1) | copy-done | bytes 4194328
  22.7 0.7 %copy-done.2 = f32[1024]{0:T(1024)S(1)} copy-done((f32[1024]{0:T(1024)S(1)}, f32[1024]{0:T(1024)}, u32[]{:S(2)}) %copy-start.2) | copy-done | bytes 4120
  23.4 1.3 %weigh.1 = (bf16[1024,2048]{1,0:T(8,128)(2,1)S(1)}, bf16[1024,2048]{1,0:T(8,128)(2,1)S(1)}) custom-call(s32[1]{0:T(128)S(6)} %copy.9.count, f32[8,128]{1,0:T(8,128)S(1)} %bitcast.15, bf16[1024,2048]{1,0:T(8,128)(2,1)S(1)} %copy-done.1, bf16[512,256]{1,0:T(8,128)(2,1)S(1)} %pick_listed.1.after.refs_0_), custom_call_target="tpu_custom_call" | custom-call | flops 4194304 | bytes 12582912 | tf_op jit(solution)/shard_map/weigh/pallas_call | solution.py:168
  24.8 1.0 %collective-permute-done.8.refs_2_ = bf16[512,256]{1,0:T(8,128)(2,1)S(1)} collective-permute-done((bf16[512,256]{1,0:T(8,128)(2,1)S(1)}, bf16[512,256]{1,0:T(8,128)(2,1)S(1)}, u32[]{:S(2)}, u32[]{:S(2)}) %collective-permute-start.8) | collective-permute-done | bytes 262176 | tf_op jit(solution)/shard_map/ppermute | solution.py:20
  25.7 0.0 collective-permute-start.9
  25.7 0.0 collective-permute-done.7.refs_1_
  25.8 1.5 %collective-permute-done.9.refs_3_ = bf16[512,256]{1,0:T(8,128)(2,1)S(1)} collective-permute-done((bf16[512,256]{1,0:T(8,128)(2,1)S(1)}, bf16[512,256]{1,0:T(8,128)(2,1)S(1)}, u32[]{:S(2)}, u32[]{:S(2)}) %collective-permute-start.9) | collective-permute-done | bytes 262176 | tf_op jit(solution)/shard_map/ppermute | solution.py:20
  27.3 4.7 %product.1 = (f32[64,2048]{1,0:T(8,128)S(1)}, bf16[64,2048]{1,0:T(8,128)(2,1)S(1)}, f32[64,2048]{1,0:T(8,128)S(1)}, bf16[64,2048]{1,0:T(8,128)(2,1)S(1)}) custom-call(bf16[1024,2048]{1,0:T(8,128)(2,1)S(1)} %get-tuple-element.20.held, bf16[1024,2048]{1,0:T(8,128)(2,1)S(1)} %get-tuple-element.21.weighted, bf16[512,256]{1,0:T(8,128)(2,1)S(1)} %pick_listed.1.after.refs_0_, ...), custom_call_target="tpu_custom_call" | custom-call | flops 2147483648 | bytes 8388608 | tf_op jit(solution)/shard_map/product/pallas_call | solution.py:204
  32.0 0.2 collective-permute-start.10
  32.2 0.4 collective-permute-start.12
  32.6 1.0 %collective-permute-done.10 = bf16[64,2048]{1,0:T(8,128)(2,1)S(1)} collective-permute-done((bf16[64,2048]{1,0:T(8,128)(2,1)S(1)}, bf16[64,2048]{1,0:T(8,128)(2,1)S(1)}, u32[]{:S(2)}, u32[]{:S(2)}) %collective-permute-start.10) | collective-permute-done | bytes 262176 | tf_op jit(solution)/shard_map/ppermute | solution.py:20
  33.6 1.6 %collective-permute-start.11 = (bf16[64,2048]{1,0:T(8,128)(2,1)S(1)}, bf16[64,2048]{1,0:T(8,128)(2,1)S(1)}, u32[]{:S(2)}, u32[]{:S(2)}) collective-permute-start(bf16[64,2048]{1,0:T(8,128)(2,1)S(1)} %add_convert_fusion), channel_id=1, source_target_pairs={{0,2},{1,3},{2,0},{3,1},{4,6},{5,7},{6,4},{7,5},{8,10},{9,11},{10,... | collective-permute-start | bytes 786440 | tf_op jit(solution)/shard_map/ppermute | solution.py:20
  35.2 0.0 collective-permute-done.12.refs_2_
  35.2 6.8 %collective-permute-done.11.refs_1_ = bf16[64,2048]{1,0:T(8,128)(2,1)S(1)} collective-permute-done((bf16[64,2048]{1,0:T(8,128)(2,1)S(1)}, bf16[64,2048]{1,0:T(8,128)(2,1)S(1)}, u32[]{:S(2)}, u32[]{:S(2)}) %collective-permute-start.11) | collective-permute-done | bytes 262176 | tf_op jit(solution)/shard_map/ppermute | solution.py:20
  42.1 0.8 %place.1 = (f32[64,512]{1,0:T(8,128)S(1)}, bf16[64,512]{1,0:T(8,128)(2,1)S(1)}, bf16[64,512]{1,0:T(8,128)(2,1)S(1)}, bf16[64,512]{1,0:T(8,128)(2,1)S(1)}, f32[64...) custom-call(s32[24]{0:T(128)S(1)} %pad_add_fusion.info, ...), custom_call_target="tpu_custom_call" | custom-call | tf_op jit(solution)/shard_map/place/pallas_call | solution.py:205
  42.8 0.8 %collective-permute-start.13 = (bf16[64,512]{1,0:T(8,128)(2,1)S(1)}, bf16[64,512]{1,0:T(8,128)(2,1)S(1)}, u32[]{:S(2)}, u32[]{:S(2)}) collective-permute-start(bf16[64,512]{1,0:T(8,128)(2,1)S(1)} %get-tuple-element.29), channel_id=1, source_target_pairs={{0,4},{4,0},{8,12},{12,8},{16,20},{20,16},{24,28},{28,24},{1,5},{5... | collective-permute-start | bytes 196616 | tf_op jit(solution)/shard_map/ppermute | solution.py:20
  43.6 1.3 %collective-permute-start.15 = (bf16[64,512]{1,0:T(8,128)(2,1)S(1)}, bf16[64,512]{1,0:T(8,128)(2,1)S(1)}, u32[]{:S(2)}, u32[]{:S(2)}) collective-permute-start(bf16[64,512]{1,0:T(8,128)(2,1)S(1)} %get-tuple-element.31), channel_id=1, source_target_pairs={{0,4},{4,0},{8,12},{12,8},{16,20},{20,16},{24,28},{28,24},{1,5},{5... | collective-permute-start | bytes 196616 | tf_op jit(solution)/shard_map/ppermute | solution.py:20
  44.9 0.3 collective-permute-start.17
  45.2 1.9 %collective-permute-start.18 = (bf16[64,512]{1,0:T(8,128)(2,1)S(1)}, bf16[64,512]{1,0:T(8,128)(2,1)S(1)}, u32[]{:S(2)}, u32[]{:S(2)}) collective-permute-start(bf16[64,512]{1,0:T(8,128)(2,1)S(1)} %get-tuple-element.33), channel_id=1, source_target_pairs={{0,8},{4,12},{8,0},{12,4},{16,24},{20,28},{24,16},{28,20},{1,9},{5... | collective-permute-start | bytes 196616 | tf_op jit(solution)/shard_map/ppermute | solution.py:20
  47.1 1.3 %collective-permute-start.19 = (bf16[64,512]{1,0:T(8,128)(2,1)S(1)}, bf16[64,512]{1,0:T(8,128)(2,1)S(1)}, u32[]{:S(2)}, u32[]{:S(2)}) collective-permute-start(bf16[64,512]{1,0:T(8,128)(2,1)S(1)} %get-tuple-element.34), channel_id=1, source_target_pairs={{0,4},{4,0},{8,12},{12,8},{16,20},{20,16},{24,28},{28,24},{1,5},{5... | collective-permute-start | bytes 196616 | tf_op jit(solution)/shard_map/ppermute | solution.py:20
  48.4 0.0 collective-permute-done.13
  48.4 2.2 %collective-permute-start.14 = (bf16[64,512]{1,0:T(8,128)(2,1)S(1)}, bf16[64,512]{1,0:T(8,128)(2,1)S(1)}, u32[]{:S(2)}, u32[]{:S(2)}) collective-permute-start(bf16[64,512]{1,0:T(8,128)(2,1)S(1)} %add_convert_fusion.3), channel_id=1, source_target_pairs={{0,24},{4,28},{8,16},{12,20},{16,8},{20,12},{24,0},{28,4},{1,25},{... | collective-permute-start | bytes 196616 | tf_op jit(solution)/shard_map/ppermute | solution.py:20
  50.7 0.1 collective-permute-start.16
  50.8 0.0 collective-permute-done.17
  50.8 0.6 %collective-permute-done.19 = bf16[64,512]{1,0:T(8,128)(2,1)S(1)} collective-permute-done((bf16[64,512]{1,0:T(8,128)(2,1)S(1)}, bf16[64,512]{1,0:T(8,128)(2,1)S(1)}, u32[]{:S(2)}, u32[]{:S(2)}) %collective-permute-start.19) | collective-permute-done | bytes 65568 | tf_op jit(solution)/shard_map/ppermute | solution.py:20
  51.4 3.3 %collective-permute-done.14 = bf16[64,512]{1,0:T(8,128)(2,1)S(1)} collective-permute-done((bf16[64,512]{1,0:T(8,128)(2,1)S(1)}, bf16[64,512]{1,0:T(8,128)(2,1)S(1)}, u32[]{:S(2)}, u32[]{:S(2)}) %collective-permute-start.14) | collective-permute-done | bytes 65568 | tf_op jit(solution)/shard_map/ppermute | solution.py:20
  54.7 1.4 %collective-permute-done.16 = bf16[64,512]{1,0:T(8,128)(2,1)S(1)} collective-permute-done((bf16[64,512]{1,0:T(8,128)(2,1)S(1)}, bf16[64,512]{1,0:T(8,128)(2,1)S(1)}, u32[]{:S(2)}, u32[]{:S(2)}) %collective-permute-start.16) | collective-permute-done | bytes 65568 | tf_op jit(solution)/shard_map/ppermute | solution.py:20
  56.1 0.7 %fusion = bf16[512,64]{0,1:T(8,128)(2,1)} fusion(bf16[64,512]{1,0:T(8,128)(2,1)S(1)} %collective-permute-done.19, bf16[64,512]{1,0:T(8,128)(2,1)S(1)} %collective-permute-done.18, bf16[64,512]{1,0:T(8,128)(2,1)S(1)} %collective-permute-done.17, bf16[64,512]{1,0:T(8,128)(2,1)S(1)} %collective-permute-done.16, f32[64,512]{1,0:T(8,128)S(1)} %get-tuple-element.27, ...), kind=kLoop, calls=%fused_computation.4 | loop fusion | flops 360448 | bytes 524288 | tf_op jit(solution)/shard_map/convert_element_type | solution.py:206
  (9 shorter events, 0.1 us)
Async XLA Ops:
  0.0 1.0 %copy-start = (bf16[512,256]{1,0:T(8,128)(2,1)S(1)}, bf16[512,256]{1,0:T(8,128)(2,1)}, u32[]{:S(2)}) copy-start(bf16[512,256]{1,0:T(8,128)(2,1)} %param.11) | copy-start | bytes 786436
  1.0 8.0 %collective-permute-start.5 = (bf16[128,256]{1,0:T(8,128)(2,1)S(1)}, bf16[128,256]{1,0:T(8,128)(2,1)S(1)}, u32[]{:S(2)}, u32[]{:S(2)}) collective-permute-start(bf16[128,256]{1,0:T(8,128)(2,1)S(1)} %bitcast.10), channel_id=1, source_target_pairs={{0,24},{4,28},{8,16},{12,20},{16,8},{20,12},{24,0},{28,4},{1,25},{... | collective-permute-start | bytes 196616 | tf_op jit(solution)/shard_map/ppermute | solution.py:20
  6.0 5.6 %collective-permute-start.3 = (bf16[128,256]{1,0:T(8,128)(2,1)S(1)}, bf16[128,256]{1,0:T(8,128)(2,1)S(1)}, u32[]{:S(2)}, u32[]{:S(2)}) collective-permute-start(bf16[128,256]{1,0:T(8,128)(2,1)S(1)} %bitcast.11), channel_id=1, source_target_pairs={{0,16},{4,20},{8,24},{12,28},{16,0},{20,4},{24,8},{28,12},{1,17},{... | collective-permute-start | bytes 196616 | tf_op jit(solution)/shard_map/ppermute | solution.py:20
  6.0 7.1 %collective-permute-start.1 = (bf16[128,256]{1,0:T(8,128)(2,1)S(1)}, bf16[128,256]{1,0:T(8,128)(2,1)S(1)}, u32[]{:S(2)}, u32[]{:S(2)}) collective-permute-start(bf16[128,256]{1,0:T(8,128)(2,1)S(1)} %bitcast.12), channel_id=1, source_target_pairs={{0,8},{4,12},{8,0},{12,4},{16,24},{20,28},{24,16},{28,20},{1,9},{5... | collective-permute-start | bytes 196616 | tf_op jit(solution)/shard_map/ppermute | solution.py:20
  6.6 7.7 %collective-permute-start = (bf16[128,256]{1,0:T(8,128)(2,1)S(1)}, bf16[128,256]{1,0:T(8,128)(2,1)S(1)}, u32[]{:S(2)}, u32[]{:S(2)}) collective-permute-start(bf16[128,256]{1,0:T(8,128)(2,1)S(1)} %bitcast.13), channel_id=1, source_target_pairs={{0,4},{4,0},{8,12},{12,8},{16,20},{20,16},{24,28},{28,24},{1,5},{5... | collective-permute-start | bytes 196616 | tf_op jit(solution)/shard_map/ppermute | solution.py:20
  9.0 5.4 %collective-permute-start.6 = (bf16[128,256]{1,0:T(8,128)(2,1)S(1)}, bf16[128,256]{1,0:T(8,128)(2,1)S(1)}, u32[]{:S(2)}, u32[]{:S(2)}) collective-permute-start(bf16[128,256]{1,0:T(8,128)(2,1)S(1)} %collective-permute-done.5.refs_6_), channel_id=1, source_target_pairs={{0,4},{4,0},{8,12},{12,8},{16,20},{20,16},{24,28},{28,24},{1,5},{5... | collective-permute-start | bytes 196616 | tf_op jit(solution)/shard_map/ppermute | solution.py:20
  11.6 4.9 %collective-permute-start.4 = (bf16[128,256]{1,0:T(8,128)(2,1)S(1)}, bf16[128,256]{1,0:T(8,128)(2,1)S(1)}, u32[]{:S(2)}, u32[]{:S(2)}) collective-permute-start(bf16[128,256]{1,0:T(8,128)(2,1)S(1)} %collective-permute-done.3.refs_4_), channel_id=1, source_target_pairs={{0,4},{4,0},{8,12},{12,8},{16,20},{20,16},{24,28},{28,24},{1,5},{5... | collective-permute-start | bytes 196616 | tf_op jit(solution)/shard_map/ppermute | solution.py:20
  13.1 4.3 %collective-permute-start.2 = (bf16[128,256]{1,0:T(8,128)(2,1)S(1)}, bf16[128,256]{1,0:T(8,128)(2,1)S(1)}, u32[]{:S(2)}, u32[]{:S(2)}) collective-permute-start(bf16[128,256]{1,0:T(8,128)(2,1)S(1)} %collective-permute-done.1.refs_2_), channel_id=1, source_target_pairs={{0,4},{4,0},{8,12},{12,8},{16,20},{20,16},{24,28},{28,24},{1,5},{5... | collective-permute-start | bytes 196616 | tf_op jit(solution)/shard_map/ppermute | solution.py:20
  18.2 7.5 %collective-permute-start.8 = (bf16[512,256]{1,0:T(8,128)(2,1)S(1)}, bf16[512,256]{1,0:T(8,128)(2,1)S(1)}, u32[]{:S(2)}, u32[]{:S(2)}) collective-permute-start(bf16[512,256]{1,0:T(8,128)(2,1)S(1)} %pick_listed.1.after.refs_0_), channel_id=1, source_target_pairs={{0,2},{1,3},{2,0},{3,1},{4,6},{5,7},{6,4},{7,5},{8,10},{9,11},{10,... | collective-permute-start | bytes 786440 | tf_op jit(solution)/shard_map/ppermute | solution.py:20
  20.5 5.3 %collective-permute-start.7 = (bf16[512,256]{1,0:T(8,128)(2,1)S(1)}, bf16[512,256]{1,0:T(8,128)(2,1)S(1)}, u32[]{:S(2)}, u32[]{:S(2)}) collective-permute-start(bf16[512,256]{1,0:T(8,128)(2,1)S(1)} %pick_listed.1.after.refs_0_), channel_id=1, source_target_pairs={{0,1},{1,0},{2,3},{3,2},{4,5},{5,4},{6,7},{7,6},{8,9},{9,8},{10,11... | collective-permute-start | bytes 786440 | tf_op jit(solution)/shard_map/ppermute | solution.py:20
  20.6 2.2 %copy-start.1 = (bf16[1024,2048]{1,0:T(8,128)(2,1)S(1)}, bf16[1024,2048]{1,0:T(8,128)(2,1)}, u32[]{:S(2)}) copy-start(bf16[1024,2048]{1,0:T(8,128)(2,1)} %jac.1) | copy-start | bytes 12582916
  22.7 0.7 %copy-start.2 = (f32[1024]{0:T(1024)S(1)}, f32[1024]{0:T(1024)}, u32[]{:S(2)}) copy-start(f32[1024]{0:T(1024)} %param.7) | copy-start | bytes 12292
  25.7 1.5 %collective-permute-start.9 = (bf16[512,256]{1,0:T(8,128)(2,1)S(1)}, bf16[512,256]{1,0:T(8,128)(2,1)S(1)}, u32[]{:S(2)}, u32[]{:S(2)}) collective-permute-start(bf16[512,256]{1,0:T(8,128)(2,1)S(1)} %collective-permute-done.8.refs_2_), channel_id=1, source_target_pairs={{0,1},{1,0},{2,3},{3,2},{4,5},{5,4},{6,7},{7,6},{8,9},{9,8},{10,11... | collective-permute-start | bytes 786440 | tf_op jit(solution)/shard_map/ppermute | solution.py:20
  32.0 1.6 %collective-permute-start.10 = (bf16[64,2048]{1,0:T(8,128)(2,1)S(1)}, bf16[64,2048]{1,0:T(8,128)(2,1)S(1)}, u32[]{:S(2)}, u32[]{:S(2)}) collective-permute-start(bf16[64,2048]{1,0:T(8,128)(2,1)S(1)} %get-tuple-element.25), channel_id=1, source_target_pairs={{0,1},{1,0},{2,3},{3,2},{4,5},{5,4},{6,7},{7,6},{8,9},{9,8},{10,11... | collective-permute-start | bytes 786440 | tf_op jit(solution)/shard_map/ppermute | solution.py:20
  32.2 3.0 %collective-permute-start.12 = (bf16[64,2048]{1,0:T(8,128)(2,1)S(1)}, bf16[64,2048]{1,0:T(8,128)(2,1)S(1)}, u32[]{:S(2)}, u32[]{:S(2)}) collective-permute-start(bf16[64,2048]{1,0:T(8,128)(2,1)S(1)} %get-tuple-element.26), channel_id=1, source_target_pairs={{0,1},{1,0},{2,3},{3,2},{4,5},{5,4},{6,7},{7,6},{8,9},{9,8},{10,11... | collective-permute-start | bytes 786440 | tf_op jit(solution)/shard_map/ppermute | solution.py:20
  33.6 8.4 %collective-permute-start.11 = (bf16[64,2048]{1,0:T(8,128)(2,1)S(1)}, bf16[64,2048]{1,0:T(8,128)(2,1)S(1)}, u32[]{:S(2)}, u32[]{:S(2)}) collective-permute-start(bf16[64,2048]{1,0:T(8,128)(2,1)S(1)} %add_convert_fusion), channel_id=1, source_target_pairs={{0,2},{1,3},{2,0},{3,1},{4,6},{5,7},{6,4},{7,5},{8,10},{9,11},{10,... | collective-permute-start | bytes 786440 | tf_op jit(solution)/shard_map/ppermute | solution.py:20
  42.8 5.6 %collective-permute-start.13 = (bf16[64,512]{1,0:T(8,128)(2,1)S(1)}, bf16[64,512]{1,0:T(8,128)(2,1)S(1)}, u32[]{:S(2)}, u32[]{:S(2)}) collective-permute-start(bf16[64,512]{1,0:T(8,128)(2,1)S(1)} %get-tuple-element.29), channel_id=1, source_target_pairs={{0,4},{4,0},{8,12},{12,8},{16,20},{20,16},{24,28},{28,24},{1,5},{5... | collective-permute-start | bytes 196616 | tf_op jit(solution)/shard_map/ppermute | solution.py:20
  43.6 7.0 %collective-permute-start.15 = (bf16[64,512]{1,0:T(8,128)(2,1)S(1)}, bf16[64,512]{1,0:T(8,128)(2,1)S(1)}, u32[]{:S(2)}, u32[]{:S(2)}) collective-permute-start(bf16[64,512]{1,0:T(8,128)(2,1)S(1)} %get-tuple-element.31), channel_id=1, source_target_pairs={{0,4},{4,0},{8,12},{12,8},{16,20},{20,16},{24,28},{28,24},{1,5},{5... | collective-permute-start | bytes 196616 | tf_op jit(solution)/shard_map/ppermute | solution.py:20
  44.9 5.8 %collective-permute-start.17 = (bf16[64,512]{1,0:T(8,128)(2,1)S(1)}, bf16[64,512]{1,0:T(8,128)(2,1)S(1)}, u32[]{:S(2)}, u32[]{:S(2)}) collective-permute-start(bf16[64,512]{1,0:T(8,128)(2,1)S(1)} %get-tuple-element.32), channel_id=1, source_target_pairs={{0,12},{4,8},{8,4},{12,0},{16,28},{20,24},{24,20},{28,16},{1,13},{... | collective-permute-start | bytes 196616 | tf_op jit(solution)/shard_map/ppermute | solution.py:20
  45.2 5.6 %collective-permute-start.18 = (bf16[64,512]{1,0:T(8,128)(2,1)S(1)}, bf16[64,512]{1,0:T(8,128)(2,1)S(1)}, u32[]{:S(2)}, u32[]{:S(2)}) collective-permute-start(bf16[64,512]{1,0:T(8,128)(2,1)S(1)} %get-tuple-element.33), channel_id=1, source_target_pairs={{0,8},{4,12},{8,0},{12,4},{16,24},{20,28},{24,16},{28,20},{1,9},{5... | collective-permute-start | bytes 196616 | tf_op jit(solution)/shard_map/ppermute | solution.py:20
  47.1 4.3 %collective-permute-start.19 = (bf16[64,512]{1,0:T(8,128)(2,1)S(1)}, bf16[64,512]{1,0:T(8,128)(2,1)S(1)}, u32[]{:S(2)}, u32[]{:S(2)}) collective-permute-start(bf16[64,512]{1,0:T(8,128)(2,1)S(1)} %get-tuple-element.34), channel_id=1, source_target_pairs={{0,4},{4,0},{8,12},{12,8},{16,20},{20,16},{24,28},{28,24},{1,5},{5... | collective-permute-start | bytes 196616 | tf_op jit(solution)/shard_map/ppermute | solution.py:20
  48.4 6.2 %collective-permute-start.14 = (bf16[64,512]{1,0:T(8,128)(2,1)S(1)}, bf16[64,512]{1,0:T(8,128)(2,1)S(1)}, u32[]{:S(2)}, u32[]{:S(2)}) collective-permute-start(bf16[64,512]{1,0:T(8,128)(2,1)S(1)} %add_convert_fusion.3), channel_id=1, source_target_pairs={{0,24},{4,28},{8,16},{12,20},{16,8},{20,12},{24,0},{28,4},{1,25},{... | collective-permute-start | bytes 196616 | tf_op jit(solution)/shard_map/ppermute | solution.py:20
  50.7 5.4 %collective-permute-start.16 = (bf16[64,512]{1,0:T(8,128)(2,1)S(1)}, bf16[64,512]{1,0:T(8,128)(2,1)S(1)}, u32[]{:S(2)}, u32[]{:S(2)}) collective-permute-start(bf16[64,512]{1,0:T(8,128)(2,1)S(1)} %add_convert_fusion.2), channel_id=1, source_target_pairs={{0,16},{4,20},{8,24},{12,28},{16,0},{20,4},{24,8},{28,12},{1,17},{... | collective-permute-start | bytes 196616 | tf_op jit(solution)/shard_map/ppermute | solution.py:20

commit v5 on v4

--- a/solution.py
+++ b/solution.py
@@ -11,6 +11,7 @@
 SUB_DIRECT = 2
 OBS_DIRECT = 4
 COLUMNS = 512
+CONTRACT_LAST = (((1,), (1,)), ((), ()))
 SMEM = pl.BlockSpec(memory_space=pltpu.SMEM)
 VMEM = pl.BlockSpec(memory_space=pltpu.VMEM)
 HBM = pl.BlockSpec(memory_space=pltpu.HBM)
@@ -20,30 +21,40 @@
     return lax.ppermute(value, axis, [(i, i ^ step) for i in range(count)])
 
 
-def far_steps(count):
-    return [2 * high for high in range(count // 2 - 1, 0, -1)]
-
-
-def spread(value, axis, count, before=None):
+def after(value, *before):
+    return lax.optimization_barrier((value, *before))[0]
+
+
+def spread(value, axis, count, direct, before=()):
     held = {0: value}
-    for step in far_steps(count):
+    far = range(count - 2, direct - 1, -2)
+    for step in (*far, *range(min(direct, count) - 1, 0, -1)):
         held[step] = swap(value, axis, count, step)
-    held[1] = swap(value, axis, count, 1)
-    for step in far_steps(count):
-        passed = held[step] if before is None else lax.optimization_barrier((held[step], before))[0]
-        held[step + 1] = swap(passed, axis, count, 1)
+    for step in far:
+        held[step + 1] = swap(after(held[step], *before), axis, count, 1)
     return [held[step] for step in range(count)]
 
 
 def collect(terms, axis, count, direct):
-    parts = [terms[0]]
-    for step in range(count - 2, direct - 1, -2):
-        passed = swap(terms[step + 1], axis, count, 1)
-        both = (terms[step] + passed.astype(jnp.float32)).astype(jnp.bfloat16)
-        parts.append(swap(both, axis, count, step))
-    for step in range(min(direct, count) - 1, 0, -1):
-        parts.append(swap(terms[step], axis, count, step))
+    parts, both = [terms[0]], []
+    far = range(count - 2, direct - 1, -2)
+    passed = [swap(terms[step + 1], axis, count, 1) for step in far]
+    parts.append(swap(terms[1], axis, count, 1))
+    for step, part in zip(far, passed):
+        both.append((terms[step] + part.astype(jnp.float32)).astype(jnp.bfloat16))
+        parts.append(swap(both[-1], axis, count, step))
+    for step in range(min(direct, count) - 1, 1, -1):
+        parts.append(swap(after(terms[step], *both), axis, count, step))
     return parts
+
+
+def share_kernel(probe, out):
+    high, width = out.shape[0], probe.shape[1]
+    first = lax.axis_index("sub") * high
+    row = lax.broadcasted_iota(jnp.int32, (high, width), 0)
+    column = lax.broadcasted_iota(jnp.int32, (high, width), 1)
+    wanted = (column == row + first).astype(jnp.bfloat16)
+    out[...] = lax.dot_general(wanted, probe[...], CONTRACT_LAST, preferred_element_type=jnp.float32).astype(out.dtype)
 
 
 def weigh_kernel(count, weight, jac, after, held, weighted, sems):
@@ -67,11 +78,11 @@
             weighted[r:r + lanes, :] = (held[r:r + lanes, :].astype(jnp.float32) * scale).astype(jnp.bfloat16)
 
 
-def pick_kernel(unit, tile, subs, listed, info, *refs):
+def pick_kernel(unit, info, *refs):
     pieces, out, position = refs[:-2], refs[-2], refs[-1]
+    listed, _, tile = out.shape
     block = lax.axis_index("obs")
-    part = unit // subs
-    units = pieces[0].shape[0] // part
+    units = pieces[0].shape[1] // unit
     for a in range(position.shape[0]):
         position[a] = -1
     for k in range(listed):
@@ -80,32 +91,25 @@
         for u in range(units):
             row = ((block ^ step) * units + u) * unit
             at = position[row // tile]
-
-            @pl.when(at >= 0)
-            def _():
-                first = pl.multiple_of(at * (tile // subs) + (row % tile) // subs, part)
-                out[pl.ds(first, part), :] = piece[u * part:(u + 1) * part, :]
-
-
-def product_kernel(unit, subs, held, weighted, *refs):
-    pieces, outs = refs[:subs], refs[subs:2 * subs]
-    probe, image_t = refs[2 * subs:]
-    sub = lax.axis_index("sub")
-    width = held.shape[1]
-    part = unit // subs
-    for j in range(subs):
-        for g in range(width // unit):
-            first = pl.multiple_of(g * unit + (sub ^ j) * part, part)
-            probe[pl.ds(first, part), :] = pieces[j][g * part:(g + 1) * part, :]
-    image = jnp.dot(held[...], probe[...], preferred_element_type=jnp.float32)
-    image_t[...] = image.astype(jnp.bfloat16).T
-    high = image_t.shape[0] // subs
-    by_step = [image_t[pl.ds(pl.multiple_of((sub ^ j) * high, high), high), :] for j in range(subs)]
-    by_step = jnp.concatenate(by_step, axis=0)
-    for n in range(0, width, COLUMNS):
-        product = jnp.dot(by_step, weighted[:, n:n + COLUMNS], preferred_element_type=jnp.float32)
-        for j in range(subs):
-            outs[j][:, n:n + COLUMNS] = product[j * high:(j + 1) * high, :].astype(outs[j].dtype)
+            for q in range(tile // unit):
+
+                @pl.when((at >= 0) & (row % tile == q * unit))
+                def _():
+                    out[at, :, q * unit:(q + 1) * unit] = piece[:, u * unit:(u + 1) * unit]
+
+
+def product_kernel(held, weighted, *refs):
+    pieces, outs, probe = refs[:len(refs) // 2], refs[len(refs) // 2:-1], refs[-1]
+    listed, high, tile = pieces[0].shape
+    for j, piece in enumerate(pieces):
+        for k in range(listed):
+            probe[j * high:(j + 1) * high, k * tile:(k + 1) * tile] = piece[k]
+    image = lax.dot_general(probe[...], held[...], CONTRACT_LAST, preferred_element_type=jnp.float32)
+    image = image.astype(jnp.bfloat16)
+    for n in range(0, held.shape[1], COLUMNS):
+        product = jnp.dot(image, weighted[:, n:n + COLUMNS], preferred_element_type=jnp.float32)
+        for j, out in enumerate(outs):
+            out[:, n:n + COLUMNS] = product[j * high:(j + 1) * high, :].astype(out.dtype)
 
 
 def place_kernel(unit, tile, listed, parts_count, info, *refs):
@@ -151,19 +155,24 @@
     def params(mib):
         return pltpu.CompilerParams(vmem_limit_bytes=mib * MIB)
 
-    share = probe_block.reshape(own_rows // unit, subs, unit // subs, probe_width)
-    share = lax.dynamic_index_in_dim(share, lax.axis_index("sub"), 1, keepdims=False)
-    share = share.reshape(own_rows // subs, probe_width)
+    share = pl.pallas_call(
+        share_kernel,
+        out_shape=jax.ShapeDtypeStruct((high, own_rows), jnp.bfloat16),
+        in_specs=[VMEM],
+        out_specs=VMEM,
+        compiler_params=params(8),
+        name="share_probe",
+    )(probe_block)
     pick = pl.pallas_call(
-        functools.partial(pick_kernel, unit, tile, subs, listed),
-        out_shape=jax.ShapeDtypeStruct((width // subs, probe_width), jnp.bfloat16),
+        functools.partial(pick_kernel, unit),
+        out_shape=jax.ShapeDtypeStruct((listed, high, tile), jnp.bfloat16),
         in_specs=[SMEM] + [VMEM] * obs_count,
         out_specs=VMEM,
         scratch_shapes=[pltpu.SMEM((tiles,), jnp.int32)],
         compiler_params=params(8),
         name="pick_listed",
     )
-    picked = pick(info, *spread(share, "obs", obs_count))
+    picked = pick(info, *spread(share, "obs", obs_count, OBS_DIRECT))
     weight_lanes = min(128, rows)
     held, weighted = pl.pallas_call(
         weigh_kernel,
@@ -177,13 +186,12 @@
     )(row_counts, obs_weight.reshape(rows // weight_lanes, weight_lanes), jacobian, picked)
 
     product = pl.pallas_call(
-        functools.partial(product_kernel, unit, subs),
+        product_kernel,
         out_shape=[jax.ShapeDtypeStruct((high, width), kept(j, SUB_DIRECT)) for j in range(subs)],
         in_specs=[VMEM] * (2 + subs),
         out_specs=[VMEM] * subs,
         scratch_shapes=[
-            pltpu.VMEM((width, probe_width), jnp.bfloat16),
-            pltpu.VMEM((probe_width, rows), jnp.bfloat16),
+            pltpu.VMEM((probe_width, width), jnp.bfloat16),
         ],
         compiler_params=params(24),
         cost_estimate=pl.CostEstimate(
@@ -200,7 +208,7 @@
         name="place",
     )
 
-    columns = spread(picked, "sub", subs, weighted)
+    columns = spread(picked, "sub", subs, SUB_DIRECT, (weighted,))
     terms = collect(product(held, weighted, *columns), "sub", subs, SUB_DIRECT)
     terms = collect(place(info, *terms), "obs", obs_count, OBS_DIRECT)
     return sum(term.astype(jnp.float32) for term in terms).T.astype(jnp.bfloat16)

time: 57 us -> 55.7 us (0.977)
  starting transfers between devices: 22.5 us -> 25.2 us
  Pallas kernels: 7.66 us -> 5.47 us
  waiting for transfers between devices: 19.8 us -> 18.8 us
  local copies, waits for them, and re-layouts: 4.52 us -> 3.84 us
    ppermute x20, starting transfers between devices: 22.5 us -> 25.2 us  [swap(): return lax.ppermute(value, axis, [(i, i ^ step) for i in range(count)])]
    pallas_call x1, Pallas kernels: 4.7 us -> 2.37 us  [local(): terms = collect(product(held, weighted, *columns), 'sub', subs, SUB_DIRECT)]
    ppermute x20, waiting for transfers between devices: 19.8 us -> 18.8 us  [swap(): return lax.ppermute(value, axis, [(i, i ^ step) for i in range(count)])]
    squeeze x1, local copies, waits for them, and re-layouts: 0.69 us -> 0.01 us  [local(): lax.dynamic_index_in_dim(tile_lists, lax.axis_index('obs'), 0, keepdims=F...]
    unnamed x6 -> x8, local copies, waits for them, and re-layouts: 3.82 us -> 3.84 us
  transfers between devices with their start and end apart: 20 -> 20, of which waited for: 10 -> 12; matrix products, arithmetic and copies ran while one was open for 3% -> 1% of each run, Pallas kernels for 2% -> 2%
where the time goes in v5:
time: 55.7 us; the launch traced here: 55.5 us
  starting transfers between devices  25.2 us (45%)
  waiting for transfers between devices  18.8 us (34%)
  Pallas kernels  5.47 us (10%)
  local copies, waits for them, and re-layouts  3.84 us (7%)
  other arithmetic  1.48 us (3%)
  between operations  0.74 us (1%)
    ppermute x20, starting transfers between devices, swap(): return lax.ppermute(value, axis, [(i, i ^ step) for i in range(count)])  25.2 us
    ppermute x20, waiting for transfers between devices, swap(): return lax.ppermute(value, axis, [(i, i ^ step) for i in range(count)])  18.8 us
    unnamed x8, local copies, waits for them, and re-layouts  3.84 us
    pallas_call x1, Pallas kernels, local(): terms = collect(product(held, weighted, *columns), 'sub', subs, SUB_DIRECT)  2.37 us
    pallas_call x1, Pallas kernels, local(): pl.pallas_call(weigh_kernel, out_shape=[jax.ShapeDtypeStruct((rows, width...  1.32 us
  transfers between devices with their start and end apart: 20, of which 12 were waited for; matrix products, arithmetic and copies ran while one was open for 1% of the time, Pallas kernels for 2%

profile of v5, /device:TPU:0, one launch (start us, length us, event | category | flops | bytes accessed | tf_op | source)
XLA Modules:
  0.0 55.5 jit_solution(4635758520247078704)
XLA Ops:
  0.0 1.0 %copy-done.2 = bf16[512,256]{1,0:T(8,128)(2,1)S(1)} copy-done((bf16[512,256]{1,0:T(8,128)(2,1)S(1)}, bf16[512,256]{1,0:T(8,128)(2,1)}, u32[]{:S(2)}) %copy-start.2) | copy-done | bytes 262168
  1.0 0.2 share_probe.1.refs_0_
  1.2 5.1 %collective-permute-start.5 = (bf16[64,512]{1,0:T(8,128)(2,1)S(1)}, bf16[64,512]{1,0:T(8,128)(2,1)S(1)}, u32[]{:S(2)}, u32[]{:S(2)}) collective-permute-start(bf16[64,512]{1,0:T(8,128)(2,1)S(1)} %share_probe.1.refs_0_), channel_id=1, source_target_pairs={{0,24},{4,28},{8,16},{12,20},{16,8},{20,12},{24,0},{28,4},{1,25},{... | collective-permute-start | bytes 196616 | tf_op jit(solution)/shard_map/ppermute | solution.py:21
  6.3 0.0 collective-permute-start.3
  6.3 1.7 %collective-permute-start.2 = (bf16[64,512]{1,0:T(8,128)(2,1)S(1)}, bf16[64,512]{1,0:T(8,128)(2,1)S(1)}, u32[]{:S(2)}, u32[]{:S(2)}) collective-permute-start(bf16[64,512]{1,0:T(8,128)(2,1)S(1)} %share_probe.1.refs_0_), channel_id=1, source_target_pairs={{0,12},{4,8},{8,4},{12,0},{16,28},{20,24},{24,20},{28,16},{1,13},{... | collective-permute-start | bytes 196616 | tf_op jit(solution)/shard_map/ppermute | solution.py:21
  8.0 1.2 %collective-permute-start.1 = (bf16[64,512]{1,0:T(8,128)(2,1)S(1)}, bf16[64,512]{1,0:T(8,128)(2,1)S(1)}, u32[]{:S(2)}, u32[]{:S(2)}) collective-permute-start(bf16[64,512]{1,0:T(8,128)(2,1)S(1)} %share_probe.1.refs_0_), channel_id=1, source_target_pairs={{0,8},{4,12},{8,0},{12,4},{16,24},{20,28},{24,16},{28,20},{1,9},{5... | collective-permute-start | bytes 196616 | tf_op jit(solution)/shard_map/ppermute | solution.py:21
  9.2 0.5 collective-permute-start
  9.8 0.0 collective-permute-done.5.refs_6_
  9.8 1.6 %collective-permute-start.6 = (bf16[64,512]{1,0:T(8,128)(2,1)S(1)}, bf16[64,512]{1,0:T(8,128)(2,1)S(1)}, u32[]{:S(2)}, u32[]{:S(2)}) collective-permute-start(bf16[64,512]{1,0:T(8,128)(2,1)S(1)} %collective-permute-done.5.refs_6_), channel_id=1, source_target_pairs={{0,4},{4,0},{8,12},{12,8},{16,20},{20,16},{24,28},{28,24},{1,5},{5... | collective-permute-start | bytes 196616 | tf_op jit(solution)/shard_map/ppermute | solution.py:21
  11.3 0.6 %collective-permute-done.3.refs_4_ = bf16[64,512]{1,0:T(8,128)(2,1)S(1)} collective-permute-done((bf16[64,512]{1,0:T(8,128)(2,1)S(1)}, bf16[64,512]{1,0:T(8,128)(2,1)S(1)}, u32[]{:S(2)}, u32[]{:S(2)}) %collective-permute-start.3) | collective-permute-done | bytes 65568 | tf_op jit(solution)/shard_map/ppermute | solution.py:21
  12.0 1.5 %collective-permute-start.4 = (bf16[64,512]{1,0:T(8,128)(2,1)S(1)}, bf16[64,512]{1,0:T(8,128)(2,1)S(1)}, u32[]{:S(2)}, u32[]{:S(2)}) collective-permute-start(bf16[64,512]{1,0:T(8,128)(2,1)S(1)} %collective-permute-done.3.refs_4_), channel_id=1, source_target_pairs={{0,4},{4,0},{8,12},{12,8},{16,20},{20,16},{24,28},{28,24},{1,5},{5... | collective-permute-start | bytes 196616 | tf_op jit(solution)/shard_map/ppermute | solution.py:21
  13.5 0.7 %pad_add_fusion.info = s32[24]{0:T(128)S(1)} fusion(s32[16]{0:T(128)} %param.10, s32[8]{0:T(128)S(1)} %dynamic-slice_bitcast_fusion), kind=kLoop, calls=%fused_computation.5 | loop fusion | flops 24 | bytes 192 | tf_op jit(solution)/shard_map/concatenate | solution.py:153
  14.2 0.0 collective-permute-done.2.refs_3_
  14.2 0.0 collective-permute-done.1.refs_2_
  14.2 0.0 collective-permute-done.refs_1_
  14.2 0.6 %collective-permute-done.6.refs_7_ = bf16[64,512]{1,0:T(8,128)(2,1)S(1)} collective-permute-done((bf16[64,512]{1,0:T(8,128)(2,1)S(1)}, bf16[64,512]{1,0:T(8,128)(2,1)S(1)}, u32[]{:S(2)}, u32[]{:S(2)}) %collective-permute-start.6) | collective-permute-done | bytes 65568 | tf_op jit(solution)/shard_map/ppermute | solution.py:21
  14.8 1.4 %collective-permute-done.4.refs_5_ = bf16[64,512]{1,0:T(8,128)(2,1)S(1)} collective-permute-done((bf16[64,512]{1,0:T(8,128)(2,1)S(1)}, bf16[64,512]{1,0:T(8,128)(2,1)S(1)}, u32[]{:S(2)}, u32[]{:S(2)}) %collective-permute-start.4) | collective-permute-done | bytes 65568 | tf_op jit(solution)/shard_map/ppermute | solution.py:21
  16.3 0.8 %pick_listed.1.after.refs_0_ = bf16[8,64,256]{2,1,0:T(8,128)(2,1)S(1)} custom-call(s32[24]{0:T(128)S(1)} %pad_add_fusion.info, bf16[64,512]{1,0:T(8,128)(2,1)S(1)} %share_probe.1.refs_0_, bf16[64,512]{1,0:T(8,128)(2,1)S(1)} %collective-permute-done.refs_1_, bf16[64,512]{1,0:T(8,128)(2,1)S(1)} %collective-permute-done.1.refs_2_, ...), custom_call_target="tpu_custom_call" | custom-call | tf_op jit(solution)/shard_map/pick_listed/pallas_call | solution.py:175
  17.1 1.6 %collective-permute-start.8 = (bf16[8,64,256]{2,1,0:T(8,128)(2,1)S(1)}, bf16[8,64,256]{2,1,0:T(8,128)(2,1)S(1)}, u32[]{:S(2)}, u32[]{:S(2)}) collective-permute-start(bf16[8,64,256]{2,1,0:T(8,128)(2,1)S(1)} %pick_listed.1.after.refs_0_), channel_id=1, source_target_pairs={{0,2},{1,3},{2,0},{3,1},{4,6},{5,7},{6,4},{7,5},{8,10},{9,11},{10,... | collective-permute-start | bytes 786440 | tf_op jit(solution)/shard_map/ppermute | solution.py:21
  19.3 0.1 collective-permute-start.7
  19.4 0.0 copy-start.1
  19.4 2.2 %copy-done.1 = bf16[1024,2048]{1,0:T(8,128)(2,1)S(1)} copy-done((bf16[1024,2048]{1,0:T(8,128)(2,1)S(1)}, bf16[1024,2048]{1,0:T(8,128)(2,1)}, u32[]{:S(2)}) %copy-start.1) | copy-done | bytes 4194328
  21.6 0.7 %copy-done.3 = f32[1024]{0:T(1024)S(1)} copy-done((f32[1024]{0:T(1024)S(1)}, f32[1024]{0:T(1024)}, u32[]{:S(2)}) %copy-start.3) | copy-done | bytes 4120
  22.3 1.3 %weigh.1 = (bf16[1024,2048]{1,0:T(8,128)(2,1)S(1)}, bf16[1024,2048]{1,0:T(8,128)(2,1)S(1)}) custom-call(s32[1]{0:T(128)S(6)} %copy.7.count, f32[8,128]{1,0:T(8,128)S(1)} %bitcast.5, bf16[1024,2048]{1,0:T(8,128)(2,1)S(1)} %copy-done.1, bf16[8,64,256]{2,1,0:T(8,128)(2,1)S(1)} %pick_listed.1.after.refs_0_), custom_call_target="tpu_custom_call" | custom-call | flops 4194304 | bytes 12582912 | tf_op jit(solution)/shard_map/weigh/pallas_call | solution.py:177
  23.6 0.5 collective-permute-done.8.refs_2_
  24.1 0.0 collective-permute-start.9
  24.2 0.0 collective-permute-done.7.refs_1_
  24.2 1.5 %collective-permute-done.9.refs_3_ = bf16[8,64,256]{2,1,0:T(8,128)(2,1)S(1)} collective-permute-done((bf16[8,64,256]{2,1,0:T(8,128)(2,1)S(1)}, bf16[8,64,256]{2,1,0:T(8,128)(2,1)S(1)}, u32[]{:S(2)}, u32[]{:S(2)}) %collective-permute-start.9) | collective-permute-done | bytes 262176 | tf_op jit(solution)/shard_map/ppermute | solution.py:21
  25.7 2.4 %product.1 = (f32[64,2048]{1,0:T(8,128)S(1)}, bf16[64,2048]{1,0:T(8,128)(2,1)S(1)}, f32[64,2048]{1,0:T(8,128)S(1)}, bf16[64,2048]{1,0:T(8,128)(2,1)S(1)}) custom-call(bf16[1024,2048]{1,0:T(8,128)(2,1)S(1)} %get-tuple-element.22.held, bf16[1024,2048]{1,0:T(8,128)(2,1)S(1)} %get-tuple-element.23.weighted, bf16[8,64,256]{2,1,0:T(8,128)(2,1)S(1)} %pick_listed.1.after.refs_0_, ...), custom_call_target="tpu_custom_call" | custom-call | flops 2147483648 | bytes 8388608 | tf_op jit(solution)/shard_map/product/pallas_call | solution.py:212
  28.0 0.2 collective-permute-start.11
  28.2 0.4 collective-permute-start.10
  28.6 1.0 %collective-permute-done.11 = bf16[64,2048]{1,0:T(8,128)(2,1)S(1)} collective-permute-done((bf16[64,2048]{1,0:T(8,128)(2,1)S(1)}, bf16[64,2048]{1,0:T(8,128)(2,1)S(1)}, u32[]{:S(2)}, u32[]{:S(2)}) %collective-permute-start.11) | collective-permute-done | bytes 262176 | tf_op jit(solution)/shard_map/ppermute | solution.py:21
  29.7 1.6 %collective-permute-start.12 = (bf16[64,2048]{1,0:T(8,128)(2,1)S(1)}, bf16[64,2048]{1,0:T(8,128)(2,1)S(1)}, u32[]{:S(2)}, u32[]{:S(2)}) collective-permute-start(bf16[64,2048]{1,0:T(8,128)(2,1)S(1)} %add_convert_fusion), channel_id=1, source_target_pairs={{0,2},{1,3},{2,0},{3,1},{4,6},{5,7},{6,4},{7,5},{8,10},{9,11},{10,... | collective-permute-start | bytes 786440 | tf_op jit(solution)/shard_map/ppermute | solution.py:21
  31.3 6.8 %collective-permute-done.12.refs_2_ = bf16[64,2048]{1,0:T(8,128)(2,1)S(1)} collective-permute-done((bf16[64,2048]{1,0:T(8,128)(2,1)S(1)}, bf16[64,2048]{1,0:T(8,128)(2,1)S(1)}, u32[]{:S(2)}, u32[]{:S(2)}) %collective-permute-start.12) | collective-permute-done | bytes 262176 | tf_op jit(solution)/shard_map/ppermute | solution.py:21
  38.1 0.8 %place.1 = (f32[64,512]{1,0:T(8,128)S(1)}, bf16[64,512]{1,0:T(8,128)(2,1)S(1)}, bf16[64,512]{1,0:T(8,128)(2,1)S(1)}, bf16[64,512]{1,0:T(8,128)(2,1)S(1)}, f32[64...) custom-call(s32[24]{0:T(128)S(1)} %pad_add_fusion.info, ...), custom_call_target="tpu_custom_call" | custom-call | tf_op jit(solution)/shard_map/place/pallas_call | solution.py:213
  38.9 1.4 %collective-permute-start.14 = (bf16[64,512]{1,0:T(8,128)(2,1)S(1)}, bf16[64,512]{1,0:T(8,128)(2,1)S(1)}, u32[]{:S(2)}, u32[]{:S(2)}) collective-permute-start(bf16[64,512]{1,0:T(8,128)(2,1)S(1)} %get-tuple-element.32), channel_id=1, source_target_pairs={{0,4},{4,0},{8,12},{12,8},{16,20},{20,16},{24,28},{28,24},{1,5},{5... | collective-permute-start | bytes 196616 | tf_op jit(solution)/shard_map/ppermute | solution.py:21
  40.3 0.6 %collective-permute-start.13 = (bf16[64,512]{1,0:T(8,128)(2,1)S(1)}, bf16[64,512]{1,0:T(8,128)(2,1)S(1)}, u32[]{:S(2)}, u32[]{:S(2)}) collective-permute-start(bf16[64,512]{1,0:T(8,128)(2,1)S(1)} %get-tuple-element.30), channel_id=1, source_target_pairs={{0,4},{4,0},{8,12},{12,8},{16,20},{20,16},{24,28},{28,24},{1,5},{5... | collective-permute-start | bytes 196616 | tf_op jit(solution)/shard_map/ppermute | solution.py:21
  41.0 1.4 %collective-permute-start.16 = (bf16[64,512]{1,0:T(8,128)(2,1)S(1)}, bf16[64,512]{1,0:T(8,128)(2,1)S(1)}, u32[]{:S(2)}, u32[]{:S(2)}) collective-permute-start(bf16[64,512]{1,0:T(8,128)(2,1)S(1)} %get-tuple-element.34), channel_id=1, source_target_pairs={{0,4},{4,0},{8,12},{12,8},{16,20},{20,16},{24,28},{28,24},{1,5},{5... | collective-permute-start | bytes 196616 | tf_op jit(solution)/shard_map/ppermute | solution.py:21
  42.4 1.5 %collective-permute-done.14 = bf16[64,512]{1,0:T(8,128)(2,1)S(1)} collective-permute-done((bf16[64,512]{1,0:T(8,128)(2,1)S(1)}, bf16[64,512]{1,0:T(8,128)(2,1)S(1)}, u32[]{:S(2)}, u32[]{:S(2)}) %collective-permute-start.14) | collective-permute-done | bytes 65568 | tf_op jit(solution)/shard_map/ppermute | solution.py:21
  43.9 2.7 %collective-permute-start.15 = (bf16[64,512]{1,0:T(8,128)(2,1)S(1)}, bf16[64,512]{1,0:T(8,128)(2,1)S(1)}, u32[]{:S(2)}, u32[]{:S(2)}) collective-permute-start(bf16[64,512]{1,0:T(8,128)(2,1)S(1)} %add_convert_fusion.3), channel_id=1, source_target_pairs={{0,24},{4,28},{8,16},{12,20},{16,8},{20,12},{24,0},{28,4},{1,25},{... | collective-permute-start | bytes 196616 | tf_op jit(solution)/shard_map/ppermute | solution.py:21
  46.5 0.6 %collective-permute-start.18 = (bf16[64,512]{1,0:T(8,128)(2,1)S(1)}, bf16[64,512]{1,0:T(8,128)(2,1)S(1)}, u32[]{:S(2)}, u32[]{:S(2)}) collective-permute-start(bf16[64,512]{1,0:T(8,128)(2,1)S(1)} %get-tuple-element.36), channel_id=1, source_target_pairs={{0,12},{4,8},{8,4},{12,0},{16,28},{20,24},{24,20},{28,16},{1,13},{... | collective-permute-start | bytes 196616 | tf_op jit(solution)/shard_map/ppermute | solution.py:21
  47.2 2.3 %collective-permute-start.19 = (bf16[64,512]{1,0:T(8,128)(2,1)S(1)}, bf16[64,512]{1,0:T(8,128)(2,1)S(1)}, u32[]{:S(2)}, u32[]{:S(2)}) collective-permute-start(bf16[64,512]{1,0:T(8,128)(2,1)S(1)} %get-tuple-element.38), channel_id=1, source_target_pairs={{0,8},{4,12},{8,0},{12,4},{16,24},{20,28},{24,16},{28,20},{1,9},{5... | collective-permute-start | bytes 196616 | tf_op jit(solution)/shard_map/ppermute | solution.py:21
  49.5 0.6 %collective-permute-start.17 = (bf16[64,512]{1,0:T(8,128)(2,1)S(1)}, bf16[64,512]{1,0:T(8,128)(2,1)S(1)}, u32[]{:S(2)}, u32[]{:S(2)}) collective-permute-start(bf16[64,512]{1,0:T(8,128)(2,1)S(1)} %add_convert_fusion.2), channel_id=1, source_target_pairs={{0,16},{4,20},{8,24},{12,28},{16,0},{20,4},{24,8},{28,12},{1,17},{... | collective-permute-start | bytes 196616 | tf_op jit(solution)/shard_map/ppermute | solution.py:21
  50.1 0.5 collective-permute-done.15
  50.6 1.6 %collective-permute-done.18 = bf16[64,512]{1,0:T(8,128)(2,1)S(1)} collective-permute-done((bf16[64,512]{1,0:T(8,128)(2,1)S(1)}, bf16[64,512]{1,0:T(8,128)(2,1)S(1)}, u32[]{:S(2)}, u32[]{:S(2)}) %collective-permute-start.18) | collective-permute-done | bytes 65568 | tf_op jit(solution)/shard_map/ppermute | solution.py:21
  52.2 0.3 collective-permute-done.19
  52.4 2.4 %collective-permute-done.17 = bf16[64,512]{1,0:T(8,128)(2,1)S(1)} collective-permute-done((bf16[64,512]{1,0:T(8,128)(2,1)S(1)}, bf16[64,512]{1,0:T(8,128)(2,1)S(1)}, u32[]{:S(2)}, u32[]{:S(2)}) %collective-permute-start.17) | collective-permute-done | bytes 65568 | tf_op jit(solution)/shard_map/ppermute | solution.py:21
  54.8 0.7 %fusion = bf16[512,64]{0,1:T(8,128)(2,1)} fusion(bf16[64,512]{1,0:T(8,128)(2,1)S(1)} %collective-permute-done.19, bf16[64,512]{1,0:T(8,128)(2,1)S(1)} %collective-permute-done.18, bf16[64,512]{1,0:T(8,128)(2,1)S(1)} %collective-permute-done.17, bf16[64,512]{1,0:T(8,128)(2,1)S(1)} %collective-permute-done.15, f32[64,512]{1,0:T(8,128)S(1)} %get-tuple-element.29, ...), kind=kLoop, calls=%fused_computation.4 | loop fusion | flops 360448 | bytes 524288 | tf_op jit(solution)/shard_map/convert_element_type | solution.py:214
  (11 shorter events, 0.1 us)
Async XLA Ops:
  0.0 9.8 %copy-start = (s32[8,8]{1,0:T(8,128)S(1)}, s32[8,8]{1,0:T(8,128)}, u32[]{:S(2)}) copy-start(s32[8,8]{1,0:T(8,128)} %param.9) | copy-start | bytes 772
  0.0 1.0 %copy-start.2 = (bf16[512,256]{1,0:T(8,128)(2,1)S(1)}, bf16[512,256]{1,0:T(8,128)(2,1)}, u32[]{:S(2)}) copy-start(bf16[512,256]{1,0:T(8,128)(2,1)} %probe.1) | copy-start | bytes 786436
  1.2 8.6 %collective-permute-start.5 = (bf16[64,512]{1,0:T(8,128)(2,1)S(1)}, bf16[64,512]{1,0:T(8,128)(2,1)S(1)}, u32[]{:S(2)}, u32[]{:S(2)}) collective-permute-start(bf16[64,512]{1,0:T(8,128)(2,1)S(1)} %share_probe.1.refs_0_), channel_id=1, source_target_pairs={{0,24},{4,28},{8,16},{12,20},{16,8},{20,12},{24,0},{28,4},{1,25},{... | collective-permute-start | bytes 196616 | tf_op jit(solution)/shard_map/ppermute | solution.py:21
  6.3 5.7 %collective-permute-start.3 = (bf16[64,512]{1,0:T(8,128)(2,1)S(1)}, bf16[64,512]{1,0:T(8,128)(2,1)S(1)}, u32[]{:S(2)}, u32[]{:S(2)}) collective-permute-start(bf16[64,512]{1,0:T(8,128)(2,1)S(1)} %share_probe.1.refs_0_), channel_id=1, source_target_pairs={{0,16},{4,20},{8,24},{12,28},{16,0},{20,4},{24,8},{28,12},{1,17},{... | collective-permute-start | bytes 196616 | tf_op jit(solution)/shard_map/ppermute | solution.py:21
  6.3 7.9 %collective-permute-start.2 = (bf16[64,512]{1,0:T(8,128)(2,1)S(1)}, bf16[64,512]{1,0:T(8,128)(2,1)S(1)}, u32[]{:S(2)}, u32[]{:S(2)}) collective-permute-start(bf16[64,512]{1,0:T(8,128)(2,1)S(1)} %share_probe.1.refs_0_), channel_id=1, source_target_pairs={{0,12},{4,8},{8,4},{12,0},{16,28},{20,24},{24,20},{28,16},{1,13},{... | collective-permute-start | bytes 196616 | tf_op jit(solution)/shard_map/ppermute | solution.py:21
  8.0 6.2 %collective-permute-start.1 = (bf16[64,512]{1,0:T(8,128)(2,1)S(1)}, bf16[64,512]{1,0:T(8,128)(2,1)S(1)}, u32[]{:S(2)}, u32[]{:S(2)}) collective-permute-start(bf16[64,512]{1,0:T(8,128)(2,1)S(1)} %share_probe.1.refs_0_), channel_id=1, source_target_pairs={{0,8},{4,12},{8,0},{12,4},{16,24},{20,28},{24,16},{28,20},{1,9},{5... | collective-permute-start | bytes 196616 | tf_op jit(solution)/shard_map/ppermute | solution.py:21
  9.2 5.0 %collective-permute-start = (bf16[64,512]{1,0:T(8,128)(2,1)S(1)}, bf16[64,512]{1,0:T(8,128)(2,1)S(1)}, u32[]{:S(2)}, u32[]{:S(2)}) collective-permute-start(bf16[64,512]{1,0:T(8,128)(2,1)S(1)} %share_probe.1.refs_0_), channel_id=1, source_target_pairs={{0,4},{4,0},{8,12},{12,8},{16,20},{20,16},{24,28},{28,24},{1,5},{5... | collective-permute-start | bytes 196616 | tf_op jit(solution)/shard_map/ppermute | solution.py:21
  9.8 5.0 %collective-permute-start.6 = (bf16[64,512]{1,0:T(8,128)(2,1)S(1)}, bf16[64,512]{1,0:T(8,128)(2,1)S(1)}, u32[]{:S(2)}, u32[]{:S(2)}) collective-permute-start(bf16[64,512]{1,0:T(8,128)(2,1)S(1)} %collective-permute-done.5.refs_6_), channel_id=1, source_target_pairs={{0,4},{4,0},{8,12},{12,8},{16,20},{20,16},{24,28},{28,24},{1,5},{5... | collective-permute-start | bytes 196616 | tf_op jit(solution)/shard_map/ppermute | solution.py:21
  12.0 4.3 %collective-permute-start.4 = (bf16[64,512]{1,0:T(8,128)(2,1)S(1)}, bf16[64,512]{1,0:T(8,128)(2,1)S(1)}, u32[]{:S(2)}, u32[]{:S(2)}) collective-permute-start(bf16[64,512]{1,0:T(8,128)(2,1)S(1)} %collective-permute-done.3.refs_4_), channel_id=1, source_target_pairs={{0,4},{4,0},{8,12},{12,8},{16,20},{20,16},{24,28},{28,24},{1,5},{5... | collective-permute-start | bytes 196616 | tf_op jit(solution)/shard_map/ppermute | solution.py:21
  17.1 7.1 %collective-permute-start.8 = (bf16[8,64,256]{2,1,0:T(8,128)(2,1)S(1)}, bf16[8,64,256]{2,1,0:T(8,128)(2,1)S(1)}, u32[]{:S(2)}, u32[]{:S(2)}) collective-permute-start(bf16[8,64,256]{2,1,0:T(8,128)(2,1)S(1)} %pick_listed.1.after.refs_0_), channel_id=1, source_target_pairs={{0,2},{1,3},{2,0},{3,1},{4,6},{5,7},{6,4},{7,5},{8,10},{9,11},{10,... | collective-permute-start | bytes 786440 | tf_op jit(solution)/shard_map/ppermute | solution.py:21
  19.3 4.9 %collective-permute-start.7 = (bf16[8,64,256]{2,1,0:T(8,128)(2,1)S(1)}, bf16[8,64,256]{2,1,0:T(8,128)(2,1)S(1)}, u32[]{:S(2)}, u32[]{:S(2)}) collective-permute-start(bf16[8,64,256]{2,1,0:T(8,128)(2,1)S(1)} %pick_listed.1.after.refs_0_), channel_id=1, source_target_pairs={{0,1},{1,0},{2,3},{3,2},{4,5},{5,4},{6,7},{7,6},{8,9},{9,8},{10,11... | collective-permute-start | bytes 786440 | tf_op jit(solution)/shard_map/ppermute | solution.py:21
  19.4 2.2 %copy-start.1 = (bf16[1024,2048]{1,0:T(8,128)(2,1)S(1)}, bf16[1024,2048]{1,0:T(8,128)(2,1)}, u32[]{:S(2)}) copy-start(bf16[1024,2048]{1,0:T(8,128)(2,1)} %jac.1) | copy-start | bytes 12582916
  21.6 0.7 %copy-start.3 = (f32[1024]{0:T(1024)S(1)}, f32[1024]{0:T(1024)}, u32[]{:S(2)}) copy-start(f32[1024]{0:T(1024)} %param.7) | copy-start | bytes 12292
  24.1 1.5 %collective-permute-start.9 = (bf16[8,64,256]{2,1,0:T(8,128)(2,1)S(1)}, bf16[8,64,256]{2,1,0:T(8,128)(2,1)S(1)}, u32[]{:S(2)}, u32[]{:S(2)}) collective-permute-start(bf16[8,64,256]{2,1,0:T(8,128)(2,1)S(1)} %collective-permute-done.8.refs_2_), channel_id=1, source_target_pairs={{0,1},{1,0},{2,3},{3,2},{4,5},{5,4},{6,7},{7,6},{8,9},{9,8},{10,11... | collective-permute-start | bytes 786440 | tf_op jit(solution)/shard_map/ppermute | solution.py:21
  28.0 1.6 %collective-permute-start.11 = (bf16[64,2048]{1,0:T(8,128)(2,1)S(1)}, bf16[64,2048]{1,0:T(8,128)(2,1)S(1)}, u32[]{:S(2)}, u32[]{:S(2)}) collective-permute-start(bf16[64,2048]{1,0:T(8,128)(2,1)S(1)} %get-tuple-element.28), channel_id=1, source_target_pairs={{0,1},{1,0},{2,3},{3,2},{4,5},{5,4},{6,7},{7,6},{8,9},{9,8},{10,11... | collective-permute-start | bytes 786440 | tf_op jit(solution)/shard_map/ppermute | solution.py:21
  28.2 3.0 %collective-permute-start.10 = (bf16[64,2048]{1,0:T(8,128)(2,1)S(1)}, bf16[64,2048]{1,0:T(8,128)(2,1)S(1)}, u32[]{:S(2)}, u32[]{:S(2)}) collective-permute-start(bf16[64,2048]{1,0:T(8,128)(2,1)S(1)} %get-tuple-element.26), channel_id=1, source_target_pairs={{0,1},{1,0},{2,3},{3,2},{4,5},{5,4},{6,7},{7,6},{8,9},{9,8},{10,11... | collective-permute-start | bytes 786440 | tf_op jit(solution)/shard_map/ppermute | solution.py:21
  29.7 8.4 %collective-permute-start.12 = (bf16[64,2048]{1,0:T(8,128)(2,1)S(1)}, bf16[64,2048]{1,0:T(8,128)(2,1)S(1)}, u32[]{:S(2)}, u32[]{:S(2)}) collective-permute-start(bf16[64,2048]{1,0:T(8,128)(2,1)S(1)} %add_convert_fusion), channel_id=1, source_target_pairs={{0,2},{1,3},{2,0},{3,1},{4,6},{5,7},{6,4},{7,5},{8,10},{9,11},{10,... | collective-permute-start | bytes 786440 | tf_op jit(solution)/shard_map/ppermute | solution.py:21
  38.9 5.0 %collective-permute-start.14 = (bf16[64,512]{1,0:T(8,128)(2,1)S(1)}, bf16[64,512]{1,0:T(8,128)(2,1)S(1)}, u32[]{:S(2)}, u32[]{:S(2)}) collective-permute-start(bf16[64,512]{1,0:T(8,128)(2,1)S(1)} %get-tuple-element.32), channel_id=1, source_target_pairs={{0,4},{4,0},{8,12},{12,8},{16,20},{20,16},{24,28},{28,24},{1,5},{5... | collective-permute-start | bytes 196616 | tf_op jit(solution)/shard_map/ppermute | solution.py:21
  40.3 9.8 %collective-permute-start.13 = (bf16[64,512]{1,0:T(8,128)(2,1)S(1)}, bf16[64,512]{1,0:T(8,128)(2,1)S(1)}, u32[]{:S(2)}, u32[]{:S(2)}) collective-permute-start(bf16[64,512]{1,0:T(8,128)(2,1)S(1)} %get-tuple-element.30), channel_id=1, source_target_pairs={{0,4},{4,0},{8,12},{12,8},{16,20},{20,16},{24,28},{28,24},{1,5},{5... | collective-permute-start | bytes 196616 | tf_op jit(solution)/shard_map/ppermute | solution.py:21
  41.0 5.5 %collective-permute-start.16 = (bf16[64,512]{1,0:T(8,128)(2,1)S(1)}, bf16[64,512]{1,0:T(8,128)(2,1)S(1)}, u32[]{:S(2)}, u32[]{:S(2)}) collective-permute-start(bf16[64,512]{1,0:T(8,128)(2,1)S(1)} %get-tuple-element.34), channel_id=1, source_target_pairs={{0,4},{4,0},{8,12},{12,8},{16,20},{20,16},{24,28},{28,24},{1,5},{5... | collective-permute-start | bytes 196616 | tf_op jit(solution)/shard_map/ppermute | solution.py:21
  43.9 6.7 %collective-permute-start.15 = (bf16[64,512]{1,0:T(8,128)(2,1)S(1)}, bf16[64,512]{1,0:T(8,128)(2,1)S(1)}, u32[]{:S(2)}, u32[]{:S(2)}) collective-permute-start(bf16[64,512]{1,0:T(8,128)(2,1)S(1)} %add_convert_fusion.3), channel_id=1, source_target_pairs={{0,24},{4,28},{8,16},{12,20},{16,8},{20,12},{24,0},{28,4},{1,25},{... | collective-permute-start | bytes 196616 | tf_op jit(solution)/shard_map/ppermute | solution.py:21
  46.5 5.6 %collective-permute-start.18 = (bf16[64,512]{1,0:T(8,128)(2,1)S(1)}, bf16[64,512]{1,0:T(8,128)(2,1)S(1)}, u32[]{:S(2)}, u32[]{:S(2)}) collective-permute-start(bf16[64,512]{1,0:T(8,128)(2,1)S(1)} %get-tuple-element.36), channel_id=1, source_target_pairs={{0,12},{4,8},{8,4},{12,0},{16,28},{20,24},{24,20},{28,16},{1,13},{... | collective-permute-start | bytes 196616 | tf_op jit(solution)/shard_map/ppermute | solution.py:21
  47.2 5.3 %collective-permute-start.19 = (bf16[64,512]{1,0:T(8,128)(2,1)S(1)}, bf16[64,512]{1,0:T(8,128)(2,1)S(1)}, u32[]{:S(2)}, u32[]{:S(2)}) collective-permute-start(bf16[64,512]{1,0:T(8,128)(2,1)S(1)} %get-tuple-element.38), channel_id=1, source_target_pairs={{0,8},{4,12},{8,0},{12,4},{16,24},{20,28},{24,16},{28,20},{1,9},{5... | collective-permute-start | bytes 196616 | tf_op jit(solution)/shard_map/ppermute | solution.py:21
  49.5 5.3 %collective-permute-start.17 = (bf16[64,512]{1,0:T(8,128)(2,1)S(1)}, bf16[64,512]{1,0:T(8,128)(2,1)S(1)}, u32[]{:S(2)}, u32[]{:S(2)}) collective-permute-start(bf16[64,512]{1,0:T(8,128)(2,1)S(1)} %add_convert_fusion.2), channel_id=1, source_target_pairs={{0,16},{4,20},{8,24},{12,28},{16,0},{20,4},{24,8},{28,12},{1,17},{... | collective-permute-start | bytes 196616 | tf_op jit(solution)/shard_map/ppermute | solution.py:21

commit v6 on v5

--- a/solution.py
+++ b/solution.py
@@ -8,6 +8,7 @@
 from jax.sharding import PartitionSpec as P
 
 MIB = 1024 * 1024
+SPREAD_DIRECT = 2
 SUB_DIRECT = 2
 OBS_DIRECT = 4
 COLUMNS = 512
@@ -36,15 +37,13 @@
 
 
 def collect(terms, axis, count, direct):
-    parts, both = [terms[0]], []
-    far = range(count - 2, direct - 1, -2)
-    passed = [swap(terms[step + 1], axis, count, 1) for step in far]
-    parts.append(swap(terms[1], axis, count, 1))
-    for step, part in zip(far, passed):
-        both.append((terms[step] + part.astype(jnp.float32)).astype(jnp.bfloat16))
-        parts.append(swap(both[-1], axis, count, step))
-    for step in range(min(direct, count) - 1, 1, -1):
-        parts.append(swap(after(terms[step], *both), axis, count, step))
+    parts = [terms[0]]
+    for step in range(count - 2, direct - 1, -2):
+        passed = swap(terms[step + 1], axis, count, 1)
+        both = (terms[step] + passed.astype(jnp.float32)).astype(jnp.bfloat16)
+        parts.append(swap(both, axis, count, step))
+    for step in range(min(direct, count) - 1, 0, -1):
+        parts.append(swap(terms[step], axis, count, step))
     return parts
 
 
@@ -172,7 +171,7 @@
         compiler_params=params(8),
         name="pick_listed",
     )
-    picked = pick(info, *spread(share, "obs", obs_count, OBS_DIRECT))
+    picked = pick(info, *spread(share, "obs", obs_count, SPREAD_DIRECT))
     weight_lanes = min(128, rows)
     held, weighted = pl.pallas_call(
         weigh_kernel,
@@ -208,7 +207,7 @@
         name="place",
     )
 
-    columns = spread(picked, "sub", subs, SUB_DIRECT, (weighted,))
+    columns = spread(picked, "sub", subs, SPREAD_DIRECT, (weighted,))
     terms = collect(product(held, weighted, *columns), "sub", subs, SUB_DIRECT)
     terms = collect(place(info, *terms), "obs", obs_count, OBS_DIRECT)
     return sum(term.astype(jnp.float32) for term in terms).T.astype(jnp.bfloat16)

time: 55.7 us -> 54.9 us (0.986)
  starting transfers between devices: 25.2 us -> 23 us
  waiting for transfers between devices: 18.8 us -> 20.1 us
    ppermute x20, starting transfers between devices: 25.2 us -> 23 us  [swap(): return lax.ppermute(value, axis, [(i, i ^ step) for i in range(count)])]
    ppermute x20, waiting for transfers between devices: 18.8 us -> 20.1 us  [swap(): return lax.ppermute(value, axis, [(i, i ^ step) for i in range(count)])]
  transfers between devices with their start and end apart: 20 -> 20, of which waited for: 12 -> 11; matrix products, arithmetic and copies ran while one was open for 1% -> 1% of each run, Pallas kernels for 2% -> 2%
where the time goes in v6:
time: 54.9 us; the launch traced here: 54.6 us
  starting transfers between devices  23 us (42%)
  waiting for transfers between devices  20.1 us (37%)
  Pallas kernels  5.46 us (10%)
  local copies, waits for them, and re-layouts  3.84 us (7%)
  other arithmetic  1.48 us (3%)
  between operations  0.76 us (1%)
    ppermute x20, starting transfers between devices, swap(): return lax.ppermute(value, axis, [(i, i ^ step) for i in range(count)])  23 us
    ppermute x20, waiting for transfers between devices, swap(): return lax.ppermute(value, axis, [(i, i ^ step) for i in range(count)])  20.1 us
    unnamed x8, local copies, waits for them, and re-layouts  3.84 us
    pallas_call x1, Pallas kernels, local(): terms = collect(product(held, weighted, *columns), 'sub', subs, SUB_DIRECT)  2.37 us
    pallas_call x1, Pallas kernels, local(): pl.pallas_call(weigh_kernel, out_shape=[jax.ShapeDtypeStruct((rows, width...  1.32 us
  transfers between devices with their start and end apart: 20, of which 11 were waited for; matrix products, arithmetic and copies ran while one was open for 1% of the time, Pallas kernels for 2%

profile of v6, /device:TPU:0, one launch (start us, length us, event | category | flops | bytes accessed | tf_op | source)
XLA Modules:
  0.0 54.6 jit_solution(7132094630172942435)
XLA Ops:
  0.0 1.0 %copy-done.2 = bf16[512,256]{1,0:T(8,128)(2,1)S(1)} copy-done((bf16[512,256]{1,0:T(8,128)(2,1)S(1)}, bf16[512,256]{1,0:T(8,128)(2,1)}, u32[]{:S(2)}) %copy-start.2) | copy-done | bytes 262168
  1.0 0.2 share_probe.1.refs_0_
  1.2 5.1 %collective-permute-start.5 = (bf16[64,512]{1,0:T(8,128)(2,1)S(1)}, bf16[64,512]{1,0:T(8,128)(2,1)S(1)}, u32[]{:S(2)}, u32[]{:S(2)}) collective-permute-start(bf16[64,512]{1,0:T(8,128)(2,1)S(1)} %share_probe.1.refs_0_), channel_id=1, source_target_pairs={{0,24},{4,28},{8,16},{12,20},{16,8},{20,12},{24,0},{28,4},{1,25},{... | collective-permute-start | bytes 196616 | tf_op jit(solution)/shard_map/ppermute | solution.py:22
  6.3 0.0 collective-permute-start.3
  6.3 0.6 %collective-permute-start.1 = (bf16[64,512]{1,0:T(8,128)(2,1)S(1)}, bf16[64,512]{1,0:T(8,128)(2,1)S(1)}, u32[]{:S(2)}, u32[]{:S(2)}) collective-permute-start(bf16[64,512]{1,0:T(8,128)(2,1)S(1)} %share_probe.1.refs_0_), channel_id=1, source_target_pairs={{0,8},{4,12},{8,0},{12,4},{16,24},{20,28},{24,16},{28,20},{1,9},{5... | collective-permute-start | bytes 196616 | tf_op jit(solution)/shard_map/ppermute | solution.py:22
  6.9 1.6 %collective-permute-start = (bf16[64,512]{1,0:T(8,128)(2,1)S(1)}, bf16[64,512]{1,0:T(8,128)(2,1)S(1)}, u32[]{:S(2)}, u32[]{:S(2)}) collective-permute-start(bf16[64,512]{1,0:T(8,128)(2,1)S(1)} %share_probe.1.refs_0_), channel_id=1, source_target_pairs={{0,4},{4,0},{8,12},{12,8},{16,20},{20,16},{24,28},{28,24},{1,5},{5... | collective-permute-start | bytes 196616 | tf_op jit(solution)/shard_map/ppermute | solution.py:22
  8.6 0.3 collective-permute-done.5.refs_6_
  8.9 1.9 %collective-permute-start.6 = (bf16[64,512]{1,0:T(8,128)(2,1)S(1)}, bf16[64,512]{1,0:T(8,128)(2,1)S(1)}, u32[]{:S(2)}, u32[]{:S(2)}) collective-permute-start(bf16[64,512]{1,0:T(8,128)(2,1)S(1)} %collective-permute-done.5.refs_6_), channel_id=1, source_target_pairs={{0,4},{4,0},{8,12},{12,8},{16,20},{20,16},{24,28},{28,24},{1,5},{5... | collective-permute-start | bytes 196616 | tf_op jit(solution)/shard_map/ppermute | solution.py:22
  10.7 1.2 %collective-permute-done.3.refs_4_ = bf16[64,512]{1,0:T(8,128)(2,1)S(1)} collective-permute-done((bf16[64,512]{1,0:T(8,128)(2,1)S(1)}, bf16[64,512]{1,0:T(8,128)(2,1)S(1)}, u32[]{:S(2)}, u32[]{:S(2)}) %collective-permute-start.3) | collective-permute-done | bytes 65568 | tf_op jit(solution)/shard_map/ppermute | solution.py:22
  11.9 1.5 %collective-permute-start.4 = (bf16[64,512]{1,0:T(8,128)(2,1)S(1)}, bf16[64,512]{1,0:T(8,128)(2,1)S(1)}, u32[]{:S(2)}, u32[]{:S(2)}) collective-permute-start(bf16[64,512]{1,0:T(8,128)(2,1)S(1)} %collective-permute-done.3.refs_4_), channel_id=1, source_target_pairs={{0,4},{4,0},{8,12},{12,8},{16,20},{20,16},{24,28},{28,24},{1,5},{5... | collective-permute-start | bytes 196616 | tf_op jit(solution)/shard_map/ppermute | solution.py:22
  13.4 0.0 collective-permute-done.1.refs_2_
  13.4 0.5 collective-permute-start.2
  13.9 0.7 %pad_add_fusion.info = s32[24]{0:T(128)S(1)} fusion(s32[16]{0:T(128)} %param.10, s32[8]{0:T(128)S(1)} %dynamic-slice_bitcast_fusion), kind=kLoop, calls=%fused_computation.5 | loop fusion | flops 24 | bytes 192 | tf_op jit(solution)/shard_map/concatenate | solution.py:152
  14.6 0.0 collective-permute-done.refs_1_
  14.7 0.0 collective-permute-done.6.refs_7_
  14.7 2.1 %collective-permute-done.4.refs_5_ = bf16[64,512]{1,0:T(8,128)(2,1)S(1)} collective-permute-done((bf16[64,512]{1,0:T(8,128)(2,1)S(1)}, bf16[64,512]{1,0:T(8,128)(2,1)S(1)}, u32[]{:S(2)}, u32[]{:S(2)}) %collective-permute-start.4) | collective-permute-done | bytes 65568 | tf_op jit(solution)/shard_map/ppermute | solution.py:22
  16.8 0.9 %collective-permute-done.2.refs_3_ = bf16[64,512]{1,0:T(8,128)(2,1)S(1)} collective-permute-done((bf16[64,512]{1,0:T(8,128)(2,1)S(1)}, bf16[64,512]{1,0:T(8,128)(2,1)S(1)}, u32[]{:S(2)}, u32[]{:S(2)}) %collective-permute-start.2) | collective-permute-done | bytes 65568 | tf_op jit(solution)/shard_map/ppermute | solution.py:22
  17.6 0.8 %pick_listed.1.after.refs_0_ = bf16[8,64,256]{2,1,0:T(8,128)(2,1)S(1)} custom-call(s32[24]{0:T(128)S(1)} %pad_add_fusion.info, bf16[64,512]{1,0:T(8,128)(2,1)S(1)} %share_probe.1.refs_0_, bf16[64,512]{1,0:T(8,128)(2,1)S(1)} %collective-permute-done.refs_1_, bf16[64,512]{1,0:T(8,128)(2,1)S(1)} %collective-permute-done.1.refs_2_, ...), custom_call_target="tpu_custom_call" | custom-call | tf_op jit(solution)/shard_map/pick_listed/pallas_call | solution.py:174
  18.5 1.6 %collective-permute-start.8 = (bf16[8,64,256]{2,1,0:T(8,128)(2,1)S(1)}, bf16[8,64,256]{2,1,0:T(8,128)(2,1)S(1)}, u32[]{:S(2)}, u32[]{:S(2)}) collective-permute-start(bf16[8,64,256]{2,1,0:T(8,128)(2,1)S(1)} %pick_listed.1.after.refs_0_), channel_id=1, source_target_pairs={{0,2},{1,3},{2,0},{3,1},{4,6},{5,7},{6,4},{7,5},{8,10},{9,11},{10,... | collective-permute-start | bytes 786440 | tf_op jit(solution)/shard_map/ppermute | solution.py:22
  20.7 0.1 collective-permute-start.7
  20.8 0.0 copy-start.1
  20.8 2.2 %copy-done.1 = bf16[1024,2048]{1,0:T(8,128)(2,1)S(1)} copy-done((bf16[1024,2048]{1,0:T(8,128)(2,1)S(1)}, bf16[1024,2048]{1,0:T(8,128)(2,1)}, u32[]{:S(2)}) %copy-start.1) | copy-done | bytes 4194328
  23.0 0.7 %copy-done.3 = f32[1024]{0:T(1024)S(1)} copy-done((f32[1024]{0:T(1024)S(1)}, f32[1024]{0:T(1024)}, u32[]{:S(2)}) %copy-start.3) | copy-done | bytes 4120
  23.7 1.3 %weigh.1 = (bf16[1024,2048]{1,0:T(8,128)(2,1)S(1)}, bf16[1024,2048]{1,0:T(8,128)(2,1)S(1)}) custom-call(s32[1]{0:T(128)S(6)} %copy.7.count, f32[8,128]{1,0:T(8,128)S(1)} %bitcast.5, bf16[1024,2048]{1,0:T(8,128)(2,1)S(1)} %copy-done.1, bf16[8,64,256]{2,1,0:T(8,128)(2,1)S(1)} %pick_listed.1.after.refs_0_), custom_call_target="tpu_custom_call" | custom-call | flops 4194304 | bytes 12582912 | tf_op jit(solution)/shard_map/weigh/pallas_call | solution.py:176
  25.0 1.0 %collective-permute-done.8.refs_2_ = bf16[8,64,256]{2,1,0:T(8,128)(2,1)S(1)} collective-permute-done((bf16[8,64,256]{2,1,0:T(8,128)(2,1)S(1)}, bf16[8,64,256]{2,1,0:T(8,128)(2,1)S(1)}, u32[]{:S(2)}, u32[]{:S(2)}) %collective-permute-start.8) | collective-permute-done | bytes 262176 | tf_op jit(solution)/shard_map/ppermute | solution.py:22
  26.0 0.0 collective-permute-start.9
  26.0 1.5 %collective-permute-done.9.refs_3_ = bf16[8,64,256]{2,1,0:T(8,128)(2,1)S(1)} collective-permute-done((bf16[8,64,256]{2,1,0:T(8,128)(2,1)S(1)}, bf16[8,64,256]{2,1,0:T(8,128)(2,1)S(1)}, u32[]{:S(2)}, u32[]{:S(2)}) %collective-permute-start.9) | collective-permute-done | bytes 262176 | tf_op jit(solution)/shard_map/ppermute | solution.py:22
  27.5 2.4 %product.1 = (f32[64,2048]{1,0:T(8,128)S(1)}, bf16[64,2048]{1,0:T(8,128)(2,1)S(1)}, f32[64,2048]{1,0:T(8,128)S(1)}, bf16[64,2048]{1,0:T(8,128)(2,1)S(1)}) custom-call(bf16[1024,2048]{1,0:T(8,128)(2,1)S(1)} %get-tuple-element.20.held, bf16[1024,2048]{1,0:T(8,128)(2,1)S(1)} %get-tuple-element.21.weighted, bf16[8,64,256]{2,1,0:T(8,128)(2,1)S(1)} %pick_listed.1.after.refs_0_, ...), custom_call_target="tpu_custom_call" | custom-call | flops 2147483648 | bytes 8388608 | tf_op jit(solution)/shard_map/product/pallas_call | solution.py:211
  29.9 0.2 collective-permute-start.10
  30.1 0.4 collective-permute-start.12
  30.5 1.0 %collective-permute-done.10 = bf16[64,2048]{1,0:T(8,128)(2,1)S(1)} collective-permute-done((bf16[64,2048]{1,0:T(8,128)(2,1)S(1)}, bf16[64,2048]{1,0:T(8,128)(2,1)S(1)}, u32[]{:S(2)}, u32[]{:S(2)}) %collective-permute-start.10) | collective-permute-done | bytes 262176 | tf_op jit(solution)/shard_map/ppermute | solution.py:22
  31.5 1.6 %collective-permute-start.11 = (bf16[64,2048]{1,0:T(8,128)(2,1)S(1)}, bf16[64,2048]{1,0:T(8,128)(2,1)S(1)}, u32[]{:S(2)}, u32[]{:S(2)}) collective-permute-start(bf16[64,2048]{1,0:T(8,128)(2,1)S(1)} %add_convert_fusion), channel_id=1, source_target_pairs={{0,2},{1,3},{2,0},{3,1},{4,6},{5,7},{6,4},{7,5},{8,10},{9,11},{10,... | collective-permute-start | bytes 786440 | tf_op jit(solution)/shard_map/ppermute | solution.py:22
  33.1 6.8 %collective-permute-done.11.refs_1_ = bf16[64,2048]{1,0:T(8,128)(2,1)S(1)} collective-permute-done((bf16[64,2048]{1,0:T(8,128)(2,1)S(1)}, bf16[64,2048]{1,0:T(8,128)(2,1)S(1)}, u32[]{:S(2)}, u32[]{:S(2)}) %collective-permute-start.11) | collective-permute-done | bytes 262176 | tf_op jit(solution)/shard_map/ppermute | solution.py:22
  39.9 0.8 %place.1 = (f32[64,512]{1,0:T(8,128)S(1)}, bf16[64,512]{1,0:T(8,128)(2,1)S(1)}, bf16[64,512]{1,0:T(8,128)(2,1)S(1)}, bf16[64,512]{1,0:T(8,128)(2,1)S(1)}, f32[64...) custom-call(s32[24]{0:T(128)S(1)} %pad_add_fusion.info, ...), custom_call_target="tpu_custom_call" | custom-call | tf_op jit(solution)/shard_map/place/pallas_call | solution.py:212
  40.7 0.8 %collective-permute-start.13 = (bf16[64,512]{1,0:T(8,128)(2,1)S(1)}, bf16[64,512]{1,0:T(8,128)(2,1)S(1)}, u32[]{:S(2)}, u32[]{:S(2)}) collective-permute-start(bf16[64,512]{1,0:T(8,128)(2,1)S(1)} %get-tuple-element.29), channel_id=1, source_target_pairs={{0,4},{4,0},{8,12},{12,8},{16,20},{20,16},{24,28},{28,24},{1,5},{5... | collective-permute-start | bytes 196616 | tf_op jit(solution)/shard_map/ppermute | solution.py:22
  41.5 1.3 %collective-permute-start.15 = (bf16[64,512]{1,0:T(8,128)(2,1)S(1)}, bf16[64,512]{1,0:T(8,128)(2,1)S(1)}, u32[]{:S(2)}, u32[]{:S(2)}) collective-permute-start(bf16[64,512]{1,0:T(8,128)(2,1)S(1)} %get-tuple-element.31), channel_id=1, source_target_pairs={{0,4},{4,0},{8,12},{12,8},{16,20},{20,16},{24,28},{28,24},{1,5},{5... | collective-permute-start | bytes 196616 | tf_op jit(solution)/shard_map/ppermute | solution.py:22
  42.8 0.3 collective-permute-start.17
  43.1 1.9 %collective-permute-start.18 = (bf16[64,512]{1,0:T(8,128)(2,1)S(1)}, bf16[64,512]{1,0:T(8,128)(2,1)S(1)}, u32[]{:S(2)}, u32[]{:S(2)}) collective-permute-start(bf16[64,512]{1,0:T(8,128)(2,1)S(1)} %get-tuple-element.33), channel_id=1, source_target_pairs={{0,8},{4,12},{8,0},{12,4},{16,24},{20,28},{24,16},{28,20},{1,9},{5... | collective-permute-start | bytes 196616 | tf_op jit(solution)/shard_map/ppermute | solution.py:22
  45.0 1.3 %collective-permute-start.19 = (bf16[64,512]{1,0:T(8,128)(2,1)S(1)}, bf16[64,512]{1,0:T(8,128)(2,1)S(1)}, u32[]{:S(2)}, u32[]{:S(2)}) collective-permute-start(bf16[64,512]{1,0:T(8,128)(2,1)S(1)} %get-tuple-element.34), channel_id=1, source_target_pairs={{0,4},{4,0},{8,12},{12,8},{16,20},{20,16},{24,28},{28,24},{1,5},{5... | collective-permute-start | bytes 196616 | tf_op jit(solution)/shard_map/ppermute | solution.py:22
  46.3 0.0 collective-permute-done.13
  46.3 2.2 %collective-permute-start.14 = (bf16[64,512]{1,0:T(8,128)(2,1)S(1)}, bf16[64,512]{1,0:T(8,128)(2,1)S(1)}, u32[]{:S(2)}, u32[]{:S(2)}) collective-permute-start(bf16[64,512]{1,0:T(8,128)(2,1)S(1)} %add_convert_fusion.3), channel_id=1, source_target_pairs={{0,24},{4,28},{8,16},{12,20},{16,8},{20,12},{24,0},{28,4},{1,25},{... | collective-permute-start | bytes 196616 | tf_op jit(solution)/shard_map/ppermute | solution.py:22
  48.6 0.1 collective-permute-start.16
  48.7 0.0 collective-permute-done.17
  48.7 0.0 collective-permute-done.18
  48.7 0.6 %collective-permute-done.19 = bf16[64,512]{1,0:T(8,128)(2,1)S(1)} collective-permute-done((bf16[64,512]{1,0:T(8,128)(2,1)S(1)}, bf16[64,512]{1,0:T(8,128)(2,1)S(1)}, u32[]{:S(2)}, u32[]{:S(2)}) %collective-permute-start.19) | collective-permute-done | bytes 65568 | tf_op jit(solution)/shard_map/ppermute | solution.py:22
  49.3 3.3 %collective-permute-done.14 = bf16[64,512]{1,0:T(8,128)(2,1)S(1)} collective-permute-done((bf16[64,512]{1,0:T(8,128)(2,1)S(1)}, bf16[64,512]{1,0:T(8,128)(2,1)S(1)}, u32[]{:S(2)}, u32[]{:S(2)}) %collective-permute-start.14) | collective-permute-done | bytes 65568 | tf_op jit(solution)/shard_map/ppermute | solution.py:22
  52.6 1.4 %collective-permute-done.16 = bf16[64,512]{1,0:T(8,128)(2,1)S(1)} collective-permute-done((bf16[64,512]{1,0:T(8,128)(2,1)S(1)}, bf16[64,512]{1,0:T(8,128)(2,1)S(1)}, u32[]{:S(2)}, u32[]{:S(2)}) %collective-permute-start.16) | collective-permute-done | bytes 65568 | tf_op jit(solution)/shard_map/ppermute | solution.py:22
  54.0 0.7 %fusion = bf16[512,64]{0,1:T(8,128)(2,1)} fusion(bf16[64,512]{1,0:T(8,128)(2,1)S(1)} %collective-permute-done.19, bf16[64,512]{1,0:T(8,128)(2,1)S(1)} %collective-permute-done.18, bf16[64,512]{1,0:T(8,128)(2,1)S(1)} %collective-permute-done.17, bf16[64,512]{1,0:T(8,128)(2,1)S(1)} %collective-permute-done.16, f32[64,512]{1,0:T(8,128)S(1)} %get-tuple-element.27, ...), kind=kLoop, calls=%fused_computation.4 | loop fusion | flops 360448 | bytes 524288 | tf_op jit(solution)/shard_map/convert_element_type | solution.py:213
  (11 shorter events, 0.1 us)
Async XLA Ops:
  0.0 8.6 %copy-start = (s32[8,8]{1,0:T(8,128)S(1)}, s32[8,8]{1,0:T(8,128)}, u32[]{:S(2)}) copy-start(s32[8,8]{1,0:T(8,128)} %param.9) | copy-start | bytes 772
  0.0 1.0 %copy-start.2 = (bf16[512,256]{1,0:T(8,128)(2,1)S(1)}, bf16[512,256]{1,0:T(8,128)(2,1)}, u32[]{:S(2)}) copy-start(bf16[512,256]{1,0:T(8,128)(2,1)} %probe.1) | copy-start | bytes 786436
  1.2 7.7 %collective-permute-start.5 = (bf16[64,512]{1,0:T(8,128)(2,1)S(1)}, bf16[64,512]{1,0:T(8,128)(2,1)S(1)}, u32[]{:S(2)}, u32[]{:S(2)}) collective-permute-start(bf16[64,512]{1,0:T(8,128)(2,1)S(1)} %share_probe.1.refs_0_), channel_id=1, source_target_pairs={{0,24},{4,28},{8,16},{12,20},{16,8},{20,12},{24,0},{28,4},{1,25},{... | collective-permute-start | bytes 196616 | tf_op jit(solution)/shard_map/ppermute | solution.py:22
  6.3 5.6 %collective-permute-start.3 = (bf16[64,512]{1,0:T(8,128)(2,1)S(1)}, bf16[64,512]{1,0:T(8,128)(2,1)S(1)}, u32[]{:S(2)}, u32[]{:S(2)}) collective-permute-start(bf16[64,512]{1,0:T(8,128)(2,1)S(1)} %share_probe.1.refs_0_), channel_id=1, source_target_pairs={{0,16},{4,20},{8,24},{12,28},{16,0},{20,4},{24,8},{28,12},{1,17},{... | collective-permute-start | bytes 196616 | tf_op jit(solution)/shard_map/ppermute | solution.py:22
  6.3 7.1 %collective-permute-start.1 = (bf16[64,512]{1,0:T(8,128)(2,1)S(1)}, bf16[64,512]{1,0:T(8,128)(2,1)S(1)}, u32[]{:S(2)}, u32[]{:S(2)}) collective-permute-start(bf16[64,512]{1,0:T(8,128)(2,1)S(1)} %share_probe.1.refs_0_), channel_id=1, source_target_pairs={{0,8},{4,12},{8,0},{12,4},{16,24},{20,28},{24,16},{28,20},{1,9},{5... | collective-permute-start | bytes 196616 | tf_op jit(solution)/shard_map/ppermute | solution.py:22
  6.9 7.7 %collective-permute-start = (bf16[64,512]{1,0:T(8,128)(2,1)S(1)}, bf16[64,512]{1,0:T(8,128)(2,1)S(1)}, u32[]{:S(2)}, u32[]{:S(2)}) collective-permute-start(bf16[64,512]{1,0:T(8,128)(2,1)S(1)} %share_probe.1.refs_0_), channel_id=1, source_target_pairs={{0,4},{4,0},{8,12},{12,8},{16,20},{20,16},{24,28},{28,24},{1,5},{5... | collective-permute-start | bytes 196616 | tf_op jit(solution)/shard_map/ppermute | solution.py:22
  8.9 5.8 %collective-permute-start.6 = (bf16[64,512]{1,0:T(8,128)(2,1)S(1)}, bf16[64,512]{1,0:T(8,128)(2,1)S(1)}, u32[]{:S(2)}, u32[]{:S(2)}) collective-permute-start(bf16[64,512]{1,0:T(8,128)(2,1)S(1)} %collective-permute-done.5.refs_6_), channel_id=1, source_target_pairs={{0,4},{4,0},{8,12},{12,8},{16,20},{20,16},{24,28},{28,24},{1,5},{5... | collective-permute-start | bytes 196616 | tf_op jit(solution)/shard_map/ppermute | solution.py:22
  11.9 4.9 %collective-permute-start.4 = (bf16[64,512]{1,0:T(8,128)(2,1)S(1)}, bf16[64,512]{1,0:T(8,128)(2,1)S(1)}, u32[]{:S(2)}, u32[]{:S(2)}) collective-permute-start(bf16[64,512]{1,0:T(8,128)(2,1)S(1)} %collective-permute-done.3.refs_4_), channel_id=1, source_target_pairs={{0,4},{4,0},{8,12},{12,8},{16,20},{20,16},{24,28},{28,24},{1,5},{5... | collective-permute-start | bytes 196616 | tf_op jit(solution)/shard_map/ppermute | solution.py:22
  13.4 4.3 %collective-permute-start.2 = (bf16[64,512]{1,0:T(8,128)(2,1)S(1)}, bf16[64,512]{1,0:T(8,128)(2,1)S(1)}, u32[]{:S(2)}, u32[]{:S(2)}) collective-permute-start(bf16[64,512]{1,0:T(8,128)(2,1)S(1)} %collective-permute-done.1.refs_2_), channel_id=1, source_target_pairs={{0,4},{4,0},{8,12},{12,8},{16,20},{20,16},{24,28},{28,24},{1,5},{5... | collective-permute-start | bytes 196616 | tf_op jit(solution)/shard_map/ppermute | solution.py:22
  18.5 7.5 %collective-permute-start.8 = (bf16[8,64,256]{2,1,0:T(8,128)(2,1)S(1)}, bf16[8,64,256]{2,1,0:T(8,128)(2,1)S(1)}, u32[]{:S(2)}, u32[]{:S(2)}) collective-permute-start(bf16[8,64,256]{2,1,0:T(8,128)(2,1)S(1)} %pick_listed.1.after.refs_0_), channel_id=1, source_target_pairs={{0,2},{1,3},{2,0},{3,1},{4,6},{5,7},{6,4},{7,5},{8,10},{9,11},{10,... | collective-permute-start | bytes 786440 | tf_op jit(solution)/shard_map/ppermute | solution.py:22
  20.7 5.3 %collective-permute-start.7 = (bf16[8,64,256]{2,1,0:T(8,128)(2,1)S(1)}, bf16[8,64,256]{2,1,0:T(8,128)(2,1)S(1)}, u32[]{:S(2)}, u32[]{:S(2)}) collective-permute-start(bf16[8,64,256]{2,1,0:T(8,128)(2,1)S(1)} %pick_listed.1.after.refs_0_), channel_id=1, source_target_pairs={{0,1},{1,0},{2,3},{3,2},{4,5},{5,4},{6,7},{7,6},{8,9},{9,8},{10,11... | collective-permute-start | bytes 786440 | tf_op jit(solution)/shard_map/ppermute | solution.py:22
  20.8 2.2 %copy-start.1 = (bf16[1024,2048]{1,0:T(8,128)(2,1)S(1)}, bf16[1024,2048]{1,0:T(8,128)(2,1)}, u32[]{:S(2)}) copy-start(bf16[1024,2048]{1,0:T(8,128)(2,1)} %jac.1) | copy-start | bytes 12582916
  23.0 0.7 %copy-start.3 = (f32[1024]{0:T(1024)S(1)}, f32[1024]{0:T(1024)}, u32[]{:S(2)}) copy-start(f32[1024]{0:T(1024)} %param.7) | copy-start | bytes 12292
  26.0 1.5 %collective-permute-start.9 = (bf16[8,64,256]{2,1,0:T(8,128)(2,1)S(1)}, bf16[8,64,256]{2,1,0:T(8,128)(2,1)S(1)}, u32[]{:S(2)}, u32[]{:S(2)}) collective-permute-start(bf16[8,64,256]{2,1,0:T(8,128)(2,1)S(1)} %collective-permute-done.8.refs_2_), channel_id=1, source_target_pairs={{0,1},{1,0},{2,3},{3,2},{4,5},{5,4},{6,7},{7,6},{8,9},{9,8},{10,11... | collective-permute-start | bytes 786440 | tf_op jit(solution)/shard_map/ppermute | solution.py:22
  29.9 1.6 %collective-permute-start.10 = (bf16[64,2048]{1,0:T(8,128)(2,1)S(1)}, bf16[64,2048]{1,0:T(8,128)(2,1)S(1)}, u32[]{:S(2)}, u32[]{:S(2)}) collective-permute-start(bf16[64,2048]{1,0:T(8,128)(2,1)S(1)} %get-tuple-element.25), channel_id=1, source_target_pairs={{0,1},{1,0},{2,3},{3,2},{4,5},{5,4},{6,7},{7,6},{8,9},{9,8},{10,11... | collective-permute-start | bytes 786440 | tf_op jit(solution)/shard_map/ppermute | solution.py:22
  30.1 3.0 %collective-permute-start.12 = (bf16[64,2048]{1,0:T(8,128)(2,1)S(1)}, bf16[64,2048]{1,0:T(8,128)(2,1)S(1)}, u32[]{:S(2)}, u32[]{:S(2)}) collective-permute-start(bf16[64,2048]{1,0:T(8,128)(2,1)S(1)} %get-tuple-element.26), channel_id=1, source_target_pairs={{0,1},{1,0},{2,3},{3,2},{4,5},{5,4},{6,7},{7,6},{8,9},{9,8},{10,11... | collective-permute-start | bytes 786440 | tf_op jit(solution)/shard_map/ppermute | solution.py:22
  31.5 8.4 %collective-permute-start.11 = (bf16[64,2048]{1,0:T(8,128)(2,1)S(1)}, bf16[64,2048]{1,0:T(8,128)(2,1)S(1)}, u32[]{:S(2)}, u32[]{:S(2)}) collective-permute-start(bf16[64,2048]{1,0:T(8,128)(2,1)S(1)} %add_convert_fusion), channel_id=1, source_target_pairs={{0,2},{1,3},{2,0},{3,1},{4,6},{5,7},{6,4},{7,5},{8,10},{9,11},{10,... | collective-permute-start | bytes 786440 | tf_op jit(solution)/shard_map/ppermute | solution.py:22
  40.7 5.6 %collective-permute-start.13 = (bf16[64,512]{1,0:T(8,128)(2,1)S(1)}, bf16[64,512]{1,0:T(8,128)(2,1)S(1)}, u32[]{:S(2)}, u32[]{:S(2)}) collective-permute-start(bf16[64,512]{1,0:T(8,128)(2,1)S(1)} %get-tuple-element.29), channel_id=1, source_target_pairs={{0,4},{4,0},{8,12},{12,8},{16,20},{20,16},{24,28},{28,24},{1,5},{5... | collective-permute-start | bytes 196616 | tf_op jit(solution)/shard_map/ppermute | solution.py:22
  41.5 7.0 %collective-permute-start.15 = (bf16[64,512]{1,0:T(8,128)(2,1)S(1)}, bf16[64,512]{1,0:T(8,128)(2,1)S(1)}, u32[]{:S(2)}, u32[]{:S(2)}) collective-permute-start(bf16[64,512]{1,0:T(8,128)(2,1)S(1)} %get-tuple-element.31), channel_id=1, source_target_pairs={{0,4},{4,0},{8,12},{12,8},{16,20},{20,16},{24,28},{28,24},{1,5},{5... | collective-permute-start | bytes 196616 | tf_op jit(solution)/shard_map/ppermute | solution.py:22
  42.8 5.8 %collective-permute-start.17 = (bf16[64,512]{1,0:T(8,128)(2,1)S(1)}, bf16[64,512]{1,0:T(8,128)(2,1)S(1)}, u32[]{:S(2)}, u32[]{:S(2)}) collective-permute-start(bf16[64,512]{1,0:T(8,128)(2,1)S(1)} %get-tuple-element.32), channel_id=1, source_target_pairs={{0,12},{4,8},{8,4},{12,0},{16,28},{20,24},{24,20},{28,16},{1,13},{... | collective-permute-start | bytes 196616 | tf_op jit(solution)/shard_map/ppermute | solution.py:22
  43.1 5.6 %collective-permute-start.18 = (bf16[64,512]{1,0:T(8,128)(2,1)S(1)}, bf16[64,512]{1,0:T(8,128)(2,1)S(1)}, u32[]{:S(2)}, u32[]{:S(2)}) collective-permute-start(bf16[64,512]{1,0:T(8,128)(2,1)S(1)} %get-tuple-element.33), channel_id=1, source_target_pairs={{0,8},{4,12},{8,0},{12,4},{16,24},{20,28},{24,16},{28,20},{1,9},{5... | collective-permute-start | bytes 196616 | tf_op jit(solution)/shard_map/ppermute | solution.py:22
  45.0 4.3 %collective-permute-start.19 = (bf16[64,512]{1,0:T(8,128)(2,1)S(1)}, bf16[64,512]{1,0:T(8,128)(2,1)S(1)}, u32[]{:S(2)}, u32[]{:S(2)}) collective-permute-start(bf16[64,512]{1,0:T(8,128)(2,1)S(1)} %get-tuple-element.34), channel_id=1, source_target_pairs={{0,4},{4,0},{8,12},{12,8},{16,20},{20,16},{24,28},{28,24},{1,5},{5... | collective-permute-start | bytes 196616 | tf_op jit(solution)/shard_map/ppermute | solution.py:22
  46.3 6.2 %collective-permute-start.14 = (bf16[64,512]{1,0:T(8,128)(2,1)S(1)}, bf16[64,512]{1,0:T(8,128)(2,1)S(1)}, u32[]{:S(2)}, u32[]{:S(2)}) collective-permute-start(bf16[64,512]{1,0:T(8,128)(2,1)S(1)} %add_convert_fusion.3), channel_id=1, source_target_pairs={{0,24},{4,28},{8,16},{12,20},{16,8},{20,12},{24,0},{28,4},{1,25},{... | collective-permute-start | bytes 196616 | tf_op jit(solution)/shard_map/ppermute | solution.py:22
  48.6 5.4 %collective-permute-start.16 = (bf16[64,512]{1,0:T(8,128)(2,1)S(1)}, bf16[64,512]{1,0:T(8,128)(2,1)S(1)}, u32[]{:S(2)}, u32[]{:S(2)}) collective-permute-start(bf16[64,512]{1,0:T(8,128)(2,1)S(1)} %add_convert_fusion.2), channel_id=1, source_target_pairs={{0,16},{4,20},{8,24},{12,28},{16,0},{20,4},{24,8},{28,12},{1,17},{... | collective-permute-start | bytes 196616 | tf_op jit(solution)/shard_map/ppermute | solution.py:22

commit v7 on v6

--- a/solution.py
+++ b/solution.py
@@ -37,14 +37,15 @@
 
 
 def collect(terms, axis, count, direct):
-    parts = [terms[0]]
+    first, later, ready = [terms[0]], [], ()
     for step in range(count - 2, direct - 1, -2):
         passed = swap(terms[step + 1], axis, count, 1)
-        both = (terms[step] + passed.astype(jnp.float32)).astype(jnp.bfloat16)
-        parts.append(swap(both, axis, count, step))
-    for step in range(min(direct, count) - 1, 0, -1):
-        parts.append(swap(terms[step], axis, count, step))
-    return parts
+        ready = (terms[step] + passed.astype(jnp.float32)).astype(jnp.bfloat16),
+        first.append(swap(*ready, axis, count, step))
+    first.append(swap(terms[1], axis, count, 1))
+    for step in range(min(direct, count) - 1, 1, -1):
+        later.append(swap(after(terms[step], *ready), axis, count, step))
+    return first, later
 
 
 def share_kernel(probe, out):
@@ -208,9 +209,10 @@
     )
 
     columns = spread(picked, "sub", subs, SPREAD_DIRECT, (weighted,))
-    terms = collect(product(held, weighted, *columns), "sub", subs, SUB_DIRECT)
-    terms = collect(place(info, *terms), "obs", obs_count, OBS_DIRECT)
-    return sum(term.astype(jnp.float32) for term in terms).T.astype(jnp.bfloat16)
+    first, later = collect(product(held, weighted, *columns), "sub", subs, SUB_DIRECT)
+    first, later = collect(place(info, *first, *later), "obs", obs_count, OBS_DIRECT)
+    total = after(sum(term.astype(jnp.float32) for term in first))
+    return sum((term.astype(jnp.float32) for term in later), total).T.astype(jnp.bfloat16)
 
 
 def solution(mesh):

time: 54.9 us -> 55.6 us (1.013)
  waiting for transfers between devices: 20.1 us -> 21.1 us
    ppermute x20, waiting for transfers between devices: 20.1 us -> 21.1 us  [swap(): return lax.ppermute(value, axis, [(i, i ^ step) for i in range(count)])]
  transfers between devices with their start and end apart: 20 -> 20, of which waited for: 11 -> 13; matrix products, arithmetic and copies ran while one was open for 1% -> 2% of each run, Pallas kernels for 2% -> 2%
where the time goes in v7:
time: 55.6 us; the launch traced here: 55.3 us
  starting transfers between devices  22.7 us (41%)
  waiting for transfers between devices  21.1 us (38%)
  Pallas kernels  5.46 us (10%)
  local copies, waits for them, and re-layouts  3.84 us (7%)
  other arithmetic  1.49 us (3%)
  between operations  0.75 us (1%)
    ppermute x20, starting transfers between devices, swap(): return lax.ppermute(value, axis, [(i, i ^ step) for i in range(count)])  22.7 us
    ppermute x20, waiting for transfers between devices, swap(): return lax.ppermute(value, axis, [(i, i ^ step) for i in range(count)])  21.1 us
    unnamed x8, local copies, waits for them, and re-layouts  3.84 us
    pallas_call x1, Pallas kernels, local(): product(held, weighted, *columns)  2.37 us
    pallas_call x1, Pallas kernels, local(): pl.pallas_call(weigh_kernel, out_shape=[jax.ShapeDtypeStruct((rows, width...  1.32 us
  transfers between devices with their start and end apart: 20, of which 13 were waited for; matrix products, arithmetic and copies ran while one was open for 2% of the time, Pallas kernels for 2%

profile of v7, /device:TPU:0, one launch (start us, length us, event | category | flops | bytes accessed | tf_op | source)
XLA Modules:
  0.0 55.3 jit_solution(291089895823165509)
XLA Ops:
  0.0 1.0 %copy-done.2 = bf16[512,256]{1,0:T(8,128)(2,1)S(1)} copy-done((bf16[512,256]{1,0:T(8,128)(2,1)S(1)}, bf16[512,256]{1,0:T(8,128)(2,1)}, u32[]{:S(2)}) %copy-start.2) | copy-done | bytes 262168
  1.0 0.2 share_probe.1.refs_0_
  1.2 5.1 %collective-permute-start.5 = (bf16[64,512]{1,0:T(8,128)(2,1)S(1)}, bf16[64,512]{1,0:T(8,128)(2,1)S(1)}, u32[]{:S(2)}, u32[]{:S(2)}) collective-permute-start(bf16[64,512]{1,0:T(8,128)(2,1)S(1)} %share_probe.1.refs_0_), channel_id=1, source_target_pairs={{0,24},{4,28},{8,16},{12,20},{16,8},{20,12},{24,0},{28,4},{1,25},{... | collective-permute-start | bytes 196616 | tf_op jit(solution)/shard_map/ppermute | solution.py:22
  6.3 0.0 collective-permute-start.3
  6.3 0.6 %collective-permute-start.1 = (bf16[64,512]{1,0:T(8,128)(2,1)S(1)}, bf16[64,512]{1,0:T(8,128)(2,1)S(1)}, u32[]{:S(2)}, u32[]{:S(2)}) collective-permute-start(bf16[64,512]{1,0:T(8,128)(2,1)S(1)} %share_probe.1.refs_0_), channel_id=1, source_target_pairs={{0,8},{4,12},{8,0},{12,4},{16,24},{20,28},{24,16},{28,20},{1,9},{5... | collective-permute-start | bytes 196616 | tf_op jit(solution)/shard_map/ppermute | solution.py:22
  6.9 1.6 %collective-permute-start = (bf16[64,512]{1,0:T(8,128)(2,1)S(1)}, bf16[64,512]{1,0:T(8,128)(2,1)S(1)}, u32[]{:S(2)}, u32[]{:S(2)}) collective-permute-start(bf16[64,512]{1,0:T(8,128)(2,1)S(1)} %share_probe.1.refs_0_), channel_id=1, source_target_pairs={{0,4},{4,0},{8,12},{12,8},{16,20},{20,16},{24,28},{28,24},{1,5},{5... | collective-permute-start | bytes 196616 | tf_op jit(solution)/shard_map/ppermute | solution.py:22
  8.6 0.3 collective-permute-done.5.refs_6_
  8.9 1.9 %collective-permute-start.6 = (bf16[64,512]{1,0:T(8,128)(2,1)S(1)}, bf16[64,512]{1,0:T(8,128)(2,1)S(1)}, u32[]{:S(2)}, u32[]{:S(2)}) collective-permute-start(bf16[64,512]{1,0:T(8,128)(2,1)S(1)} %collective-permute-done.5.refs_6_), channel_id=1, source_target_pairs={{0,4},{4,0},{8,12},{12,8},{16,20},{20,16},{24,28},{28,24},{1,5},{5... | collective-permute-start | bytes 196616 | tf_op jit(solution)/shard_map/ppermute | solution.py:22
  10.7 1.2 %collective-permute-done.3.refs_4_ = bf16[64,512]{1,0:T(8,128)(2,1)S(1)} collective-permute-done((bf16[64,512]{1,0:T(8,128)(2,1)S(1)}, bf16[64,512]{1,0:T(8,128)(2,1)S(1)}, u32[]{:S(2)}, u32[]{:S(2)}) %collective-permute-start.3) | collective-permute-done | bytes 65568 | tf_op jit(solution)/shard_map/ppermute | solution.py:22
  11.9 1.5 %collective-permute-start.4 = (bf16[64,512]{1,0:T(8,128)(2,1)S(1)}, bf16[64,512]{1,0:T(8,128)(2,1)S(1)}, u32[]{:S(2)}, u32[]{:S(2)}) collective-permute-start(bf16[64,512]{1,0:T(8,128)(2,1)S(1)} %collective-permute-done.3.refs_4_), channel_id=1, source_target_pairs={{0,4},{4,0},{8,12},{12,8},{16,20},{20,16},{24,28},{28,24},{1,5},{5... | collective-permute-start | bytes 196616 | tf_op jit(solution)/shard_map/ppermute | solution.py:22
  13.4 0.0 collective-permute-done.1.refs_2_
  13.4 0.5 collective-permute-start.2
  13.9 0.7 %pad_add_fusion.info = s32[24]{0:T(128)S(1)} fusion(s32[16]{0:T(128)} %param.10, s32[8]{0:T(128)S(1)} %dynamic-slice_bitcast_fusion), kind=kLoop, calls=%fused_computation.6 | loop fusion | flops 24 | bytes 192 | tf_op jit(solution)/shard_map/concatenate | solution.py:153
  14.7 2.1 %collective-permute-done.4.refs_5_ = bf16[64,512]{1,0:T(8,128)(2,1)S(1)} collective-permute-done((bf16[64,512]{1,0:T(8,128)(2,1)S(1)}, bf16[64,512]{1,0:T(8,128)(2,1)S(1)}, u32[]{:S(2)}, u32[]{:S(2)}) %collective-permute-start.4) | collective-permute-done | bytes 65568 | tf_op jit(solution)/shard_map/ppermute | solution.py:22
  16.8 0.9 %collective-permute-done.2.refs_3_ = bf16[64,512]{1,0:T(8,128)(2,1)S(1)} collective-permute-done((bf16[64,512]{1,0:T(8,128)(2,1)S(1)}, bf16[64,512]{1,0:T(8,128)(2,1)S(1)}, u32[]{:S(2)}, u32[]{:S(2)}) %collective-permute-start.2) | collective-permute-done | bytes 65568 | tf_op jit(solution)/shard_map/ppermute | solution.py:22
  17.6 0.8 %pick_listed.1.after.refs_0_ = bf16[8,64,256]{2,1,0:T(8,128)(2,1)S(1)} custom-call(s32[24]{0:T(128)S(1)} %pad_add_fusion.info, bf16[64,512]{1,0:T(8,128)(2,1)S(1)} %share_probe.1.refs_0_, bf16[64,512]{1,0:T(8,128)(2,1)S(1)} %collective-permute-done.refs_1_, bf16[64,512]{1,0:T(8,128)(2,1)S(1)} %collective-permute-done.1.refs_2_, ...), custom_call_target="tpu_custom_call" | custom-call | tf_op jit(solution)/shard_map/pick_listed/pallas_call | solution.py:175
  18.5 1.6 %collective-permute-start.8 = (bf16[8,64,256]{2,1,0:T(8,128)(2,1)S(1)}, bf16[8,64,256]{2,1,0:T(8,128)(2,1)S(1)}, u32[]{:S(2)}, u32[]{:S(2)}) collective-permute-start(bf16[8,64,256]{2,1,0:T(8,128)(2,1)S(1)} %pick_listed.1.after.refs_0_), channel_id=1, source_target_pairs={{0,2},{1,3},{2,0},{3,1},{4,6},{5,7},{6,4},{7,5},{8,10},{9,11},{10,... | collective-permute-start | bytes 786440 | tf_op jit(solution)/shard_map/ppermute | solution.py:22
  20.7 0.1 collective-permute-start.7
  20.8 0.0 copy-start.1
  20.8 2.2 %copy-done.1 = bf16[1024,2048]{1,0:T(8,128)(2,1)S(1)} copy-done((bf16[1024,2048]{1,0:T(8,128)(2,1)S(1)}, bf16[1024,2048]{1,0:T(8,128)(2,1)}, u32[]{:S(2)}) %copy-start.1) | copy-done | bytes 4194328
  23.0 0.7 %copy-done.3 = f32[1024]{0:T(1024)S(1)} copy-done((f32[1024]{0:T(1024)S(1)}, f32[1024]{0:T(1024)}, u32[]{:S(2)}) %copy-start.3) | copy-done | bytes 4120
  23.7 1.3 %weigh.1 = (bf16[1024,2048]{1,0:T(8,128)(2,1)S(1)}, bf16[1024,2048]{1,0:T(8,128)(2,1)S(1)}) custom-call(s32[1]{0:T(128)S(6)} %copy.7.count, f32[8,128]{1,0:T(8,128)S(1)} %bitcast.5, bf16[1024,2048]{1,0:T(8,128)(2,1)S(1)} %copy-done.1, bf16[8,64,256]{2,1,0:T(8,128)(2,1)S(1)} %pick_listed.1.after.refs_0_), custom_call_target="tpu_custom_call" | custom-call | flops 4194304 | bytes 12582912 | tf_op jit(solution)/shard_map/weigh/pallas_call | solution.py:177
  25.0 1.0 %collective-permute-done.8.refs_2_ = bf16[8,64,256]{2,1,0:T(8,128)(2,1)S(1)} collective-permute-done((bf16[8,64,256]{2,1,0:T(8,128)(2,1)S(1)}, bf16[8,64,256]{2,1,0:T(8,128)(2,1)S(1)}, u32[]{:S(2)}, u32[]{:S(2)}) %collective-permute-start.8) | collective-permute-done | bytes 262176 | tf_op jit(solution)/shard_map/ppermute | solution.py:22
  26.0 0.0 collective-permute-done.7.refs_1_
  26.0 1.5 %collective-permute-done.9.refs_3_ = bf16[8,64,256]{2,1,0:T(8,128)(2,1)S(1)} collective-permute-done((bf16[8,64,256]{2,1,0:T(8,128)(2,1)S(1)}, bf16[8,64,256]{2,1,0:T(8,128)(2,1)S(1)}, u32[]{:S(2)}, u32[]{:S(2)}) %collective-permute-start.9) | collective-permute-done | bytes 262176 | tf_op jit(solution)/shard_map/ppermute | solution.py:22
  27.5 2.4 %product.1 = (f32[64,2048]{1,0:T(8,128)S(1)}, bf16[64,2048]{1,0:T(8,128)(2,1)S(1)}, f32[64,2048]{1,0:T(8,128)S(1)}, bf16[64,2048]{1,0:T(8,128)(2,1)S(1)}) custom-call(bf16[1024,2048]{1,0:T(8,128)(2,1)S(1)} %get-tuple-element.22.held, bf16[1024,2048]{1,0:T(8,128)(2,1)S(1)} %get-tuple-element.23.weighted, bf16[8,64,256]{2,1,0:T(8,128)(2,1)S(1)} %pick_listed.1.after.refs_0_, ...), custom_call_target="tpu_custom_call" | custom-call | flops 2147483648 | bytes 8388608 | tf_op jit(solution)/shard_map/product/pallas_call | solution.py:212
  29.9 0.2 collective-permute-start.10
  30.1 0.4 collective-permute-start.12
  30.5 1.0 %collective-permute-done.10 = bf16[64,2048]{1,0:T(8,128)(2,1)S(1)} collective-permute-done((bf16[64,2048]{1,0:T(8,128)(2,1)S(1)}, bf16[64,2048]{1,0:T(8,128)(2,1)S(1)}, u32[]{:S(2)}, u32[]{:S(2)}) %collective-permute-start.10) | collective-permute-done | bytes 262176 | tf_op jit(solution)/shard_map/ppermute | solution.py:22
  31.5 1.6 %collective-permute-start.11 = (bf16[64,2048]{1,0:T(8,128)(2,1)S(1)}, bf16[64,2048]{1,0:T(8,128)(2,1)S(1)}, u32[]{:S(2)}, u32[]{:S(2)}) collective-permute-start(bf16[64,2048]{1,0:T(8,128)(2,1)S(1)} %add_convert_fusion), channel_id=1, source_target_pairs={{0,2},{1,3},{2,0},{3,1},{4,6},{5,7},{6,4},{7,5},{8,10},{9,11},{10,... | collective-permute-start | bytes 786440 | tf_op jit(solution)/shard_map/ppermute | solution.py:22
  33.1 0.0 collective-permute-done.12.refs_2_
  33.1 6.8 %collective-permute-done.11.refs_1_ = bf16[64,2048]{1,0:T(8,128)(2,1)S(1)} collective-permute-done((bf16[64,2048]{1,0:T(8,128)(2,1)S(1)}, bf16[64,2048]{1,0:T(8,128)(2,1)S(1)}, u32[]{:S(2)}, u32[]{:S(2)}) %collective-permute-start.11) | collective-permute-done | bytes 262176 | tf_op jit(solution)/shard_map/ppermute | solution.py:22
  39.9 0.8 %place.1 = (f32[64,512]{1,0:T(8,128)S(1)}, bf16[64,512]{1,0:T(8,128)(2,1)S(1)}, bf16[64,512]{1,0:T(8,128)(2,1)S(1)}, bf16[64,512]{1,0:T(8,128)(2,1)S(1)}, f32[64...) custom-call(s32[24]{0:T(128)S(1)} %pad_add_fusion.info, ...), custom_call_target="tpu_custom_call" | custom-call | tf_op jit(solution)/shard_map/place/pallas_call | solution.py:213
  40.7 0.8 %collective-permute-start.13 = (bf16[64,512]{1,0:T(8,128)(2,1)S(1)}, bf16[64,512]{1,0:T(8,128)(2,1)S(1)}, u32[]{:S(2)}, u32[]{:S(2)}) collective-permute-start(bf16[64,512]{1,0:T(8,128)(2,1)S(1)} %get-tuple-element.31), channel_id=1, source_target_pairs={{0,4},{4,0},{8,12},{12,8},{16,20},{20,16},{24,28},{28,24},{1,5},{5... | collective-permute-start | bytes 196616 | tf_op jit(solution)/shard_map/ppermute | solution.py:22
  41.5 1.3 %collective-permute-start.15 = (bf16[64,512]{1,0:T(8,128)(2,1)S(1)}, bf16[64,512]{1,0:T(8,128)(2,1)S(1)}, u32[]{:S(2)}, u32[]{:S(2)}) collective-permute-start(bf16[64,512]{1,0:T(8,128)(2,1)S(1)} %get-tuple-element.33), channel_id=1, source_target_pairs={{0,4},{4,0},{8,12},{12,8},{16,20},{20,16},{24,28},{28,24},{1,5},{5... | collective-permute-start | bytes 196616 | tf_op jit(solution)/shard_map/ppermute | solution.py:22
  42.8 0.7 %collective-permute-start.17 = (bf16[64,512]{1,0:T(8,128)(2,1)S(1)}, bf16[64,512]{1,0:T(8,128)(2,1)S(1)}, u32[]{:S(2)}, u32[]{:S(2)}) collective-permute-start(bf16[64,512]{1,0:T(8,128)(2,1)S(1)} %get-tuple-element.34), channel_id=1, source_target_pairs={{0,4},{4,0},{8,12},{12,8},{16,20},{20,16},{24,28},{28,24},{1,5},{5... | collective-permute-start | bytes 196616 | tf_op jit(solution)/shard_map/ppermute | solution.py:22
  43.5 2.0 %collective-permute-done.13 = bf16[64,512]{1,0:T(8,128)(2,1)S(1)} collective-permute-done((bf16[64,512]{1,0:T(8,128)(2,1)S(1)}, bf16[64,512]{1,0:T(8,128)(2,1)S(1)}, u32[]{:S(2)}, u32[]{:S(2)}) %collective-permute-start.13) | collective-permute-done | bytes 65568 | tf_op jit(solution)/shard_map/ppermute | solution.py:22
  45.6 2.4 %collective-permute-start.14 = (bf16[64,512]{1,0:T(8,128)(2,1)S(1)}, bf16[64,512]{1,0:T(8,128)(2,1)S(1)}, u32[]{:S(2)}, u32[]{:S(2)}) collective-permute-start(bf16[64,512]{1,0:T(8,128)(2,1)S(1)} %add_convert_fusion.3), channel_id=1, source_target_pairs={{0,24},{4,28},{8,16},{12,20},{16,8},{20,12},{24,0},{28,4},{1,25},{... | collective-permute-start | bytes 196616 | tf_op jit(solution)/shard_map/ppermute | solution.py:22
  48.0 0.0 collective-permute-done.15
  48.0 0.1 collective-permute-start.16
  48.1 2.4 %collective-permute-start.18 = (bf16[64,512]{1,0:T(8,128)(2,1)S(1)}, bf16[64,512]{1,0:T(8,128)(2,1)S(1)}, u32[]{:S(2)}, u32[]{:S(2)}) collective-permute-start(bf16[64,512]{1,0:T(8,128)(2,1)S(1)} %get-tuple-element.36), channel_id=1, source_target_pairs={{0,12},{4,8},{8,4},{12,0},{16,28},{20,24},{24,20},{28,16},{1,13},{... | collective-permute-start | bytes 196616 | tf_op jit(solution)/shard_map/ppermute | solution.py:22
  50.4 0.0 collective-permute-start.19
  50.4 0.0 collective-permute-done.17
  50.4 1.9 %collective-permute-done.14 = bf16[64,512]{1,0:T(8,128)(2,1)S(1)} collective-permute-done((bf16[64,512]{1,0:T(8,128)(2,1)S(1)}, bf16[64,512]{1,0:T(8,128)(2,1)S(1)}, u32[]{:S(2)}, u32[]{:S(2)}) %collective-permute-start.14) | collective-permute-done | bytes 65568 | tf_op jit(solution)/shard_map/ppermute | solution.py:22
  52.4 1.5 %collective-permute-done.16 = bf16[64,512]{1,0:T(8,128)(2,1)S(1)} collective-permute-done((bf16[64,512]{1,0:T(8,128)(2,1)S(1)}, bf16[64,512]{1,0:T(8,128)(2,1)S(1)}, u32[]{:S(2)}, u32[]{:S(2)}) %collective-permute-start.16) | collective-permute-done | bytes 65568 | tf_op jit(solution)/shard_map/ppermute | solution.py:22
  53.9 0.1 collective-permute-done.18
  54.0 0.7 %collective-permute-done.19 = bf16[64,512]{1,0:T(8,128)(2,1)S(1)} collective-permute-done((bf16[64,512]{1,0:T(8,128)(2,1)S(1)}, bf16[64,512]{1,0:T(8,128)(2,1)S(1)}, u32[]{:S(2)}, u32[]{:S(2)}) %collective-permute-start.19) | collective-permute-done | bytes 65568 | tf_op jit(solution)/shard_map/ppermute | solution.py:22
  54.7 0.7 %fusion = bf16[512,64]{0,1:T(8,128)(2,1)} fusion(bf16[64,512]{1,0:T(8,128)(2,1)S(1)} %collective-permute-done.19, f32[64,512]{1,0:T(8,128)S(1)} %convert_add_fusion, bf16[64,512]{1,0:T(8,128)(2,1)S(1)} %collective-permute-done.18), kind=kLoop, calls=%fused_computation.5 | loop fusion | flops 163840 | bytes 327680 | tf_op jit(solution)/shard_map/convert_element_type | solution.py:215
  (12 shorter events, 0.1 us)
Async XLA Ops:
  0.0 8.6 %copy-start = (s32[8,8]{1,0:T(8,128)S(1)}, s32[8,8]{1,0:T(8,128)}, u32[]{:S(2)}) copy-start(s32[8,8]{1,0:T(8,128)} %param.9) | copy-start | bytes 772
  0.0 1.0 %copy-start.2 = (bf16[512,256]{1,0:T(8,128)(2,1)S(1)}, bf16[512,256]{1,0:T(8,128)(2,1)}, u32[]{:S(2)}) copy-start(bf16[512,256]{1,0:T(8,128)(2,1)} %probe.1) | copy-start | bytes 786436
  1.2 7.7 %collective-permute-start.5 = (bf16[64,512]{1,0:T(8,128)(2,1)S(1)}, bf16[64,512]{1,0:T(8,128)(2,1)S(1)}, u32[]{:S(2)}, u32[]{:S(2)}) collective-permute-start(bf16[64,512]{1,0:T(8,128)(2,1)S(1)} %share_probe.1.refs_0_), channel_id=1, source_target_pairs={{0,24},{4,28},{8,16},{12,20},{16,8},{20,12},{24,0},{28,4},{1,25},{... | collective-permute-start | bytes 196616 | tf_op jit(solution)/shard_map/ppermute | solution.py:22
  6.3 5.6 %collective-permute-start.3 = (bf16[64,512]{1,0:T(8,128)(2,1)S(1)}, bf16[64,512]{1,0:T(8,128)(2,1)S(1)}, u32[]{:S(2)}, u32[]{:S(2)}) collective-permute-start(bf16[64,512]{1,0:T(8,128)(2,1)S(1)} %share_probe.1.refs_0_), channel_id=1, source_target_pairs={{0,16},{4,20},{8,24},{12,28},{16,0},{20,4},{24,8},{28,12},{1,17},{... | collective-permute-start | bytes 196616 | tf_op jit(solution)/shard_map/ppermute | solution.py:22
  6.3 7.1 %collective-permute-start.1 = (bf16[64,512]{1,0:T(8,128)(2,1)S(1)}, bf16[64,512]{1,0:T(8,128)(2,1)S(1)}, u32[]{:S(2)}, u32[]{:S(2)}) collective-permute-start(bf16[64,512]{1,0:T(8,128)(2,1)S(1)} %share_probe.1.refs_0_), channel_id=1, source_target_pairs={{0,8},{4,12},{8,0},{12,4},{16,24},{20,28},{24,16},{28,20},{1,9},{5... | collective-permute-start | bytes 196616 | tf_op jit(solution)/shard_map/ppermute | solution.py:22
  6.9 7.7 %collective-permute-start = (bf16[64,512]{1,0:T(8,128)(2,1)S(1)}, bf16[64,512]{1,0:T(8,128)(2,1)S(1)}, u32[]{:S(2)}, u32[]{:S(2)}) collective-permute-start(bf16[64,512]{1,0:T(8,128)(2,1)S(1)} %share_probe.1.refs_0_), channel_id=1, source_target_pairs={{0,4},{4,0},{8,12},{12,8},{16,20},{20,16},{24,28},{28,24},{1,5},{5... | collective-permute-start | bytes 196616 | tf_op jit(solution)/shard_map/ppermute | solution.py:22
  8.9 5.8 %collective-permute-start.6 = (bf16[64,512]{1,0:T(8,128)(2,1)S(1)}, bf16[64,512]{1,0:T(8,128)(2,1)S(1)}, u32[]{:S(2)}, u32[]{:S(2)}) collective-permute-start(bf16[64,512]{1,0:T(8,128)(2,1)S(1)} %collective-permute-done.5.refs_6_), channel_id=1, source_target_pairs={{0,4},{4,0},{8,12},{12,8},{16,20},{20,16},{24,28},{28,24},{1,5},{5... | collective-permute-start | bytes 196616 | tf_op jit(solution)/shard_map/ppermute | solution.py:22
  11.9 4.9 %collective-permute-start.4 = (bf16[64,512]{1,0:T(8,128)(2,1)S(1)}, bf16[64,512]{1,0:T(8,128)(2,1)S(1)}, u32[]{:S(2)}, u32[]{:S(2)}) collective-permute-start(bf16[64,512]{1,0:T(8,128)(2,1)S(1)} %collective-permute-done.3.refs_4_), channel_id=1, source_target_pairs={{0,4},{4,0},{8,12},{12,8},{16,20},{20,16},{24,28},{28,24},{1,5},{5... | collective-permute-start | bytes 196616 | tf_op jit(solution)/shard_map/ppermute | solution.py:22
  13.4 4.3 %collective-permute-start.2 = (bf16[64,512]{1,0:T(8,128)(2,1)S(1)}, bf16[64,512]{1,0:T(8,128)(2,1)S(1)}, u32[]{:S(2)}, u32[]{:S(2)}) collective-permute-start(bf16[64,512]{1,0:T(8,128)(2,1)S(1)} %collective-permute-done.1.refs_2_), channel_id=1, source_target_pairs={{0,4},{4,0},{8,12},{12,8},{16,20},{20,16},{24,28},{28,24},{1,5},{5... | collective-permute-start | bytes 196616 | tf_op jit(solution)/shard_map/ppermute | solution.py:22
  18.5 7.5 %collective-permute-start.8 = (bf16[8,64,256]{2,1,0:T(8,128)(2,1)S(1)}, bf16[8,64,256]{2,1,0:T(8,128)(2,1)S(1)}, u32[]{:S(2)}, u32[]{:S(2)}) collective-permute-start(bf16[8,64,256]{2,1,0:T(8,128)(2,1)S(1)} %pick_listed.1.after.refs_0_), channel_id=1, source_target_pairs={{0,2},{1,3},{2,0},{3,1},{4,6},{5,7},{6,4},{7,5},{8,10},{9,11},{10,... | collective-permute-start | bytes 786440 | tf_op jit(solution)/shard_map/ppermute | solution.py:22
  20.7 5.3 %collective-permute-start.7 = (bf16[8,64,256]{2,1,0:T(8,128)(2,1)S(1)}, bf16[8,64,256]{2,1,0:T(8,128)(2,1)S(1)}, u32[]{:S(2)}, u32[]{:S(2)}) collective-permute-start(bf16[8,64,256]{2,1,0:T(8,128)(2,1)S(1)} %pick_listed.1.after.refs_0_), channel_id=1, source_target_pairs={{0,1},{1,0},{2,3},{3,2},{4,5},{5,4},{6,7},{7,6},{8,9},{9,8},{10,11... | collective-permute-start | bytes 786440 | tf_op jit(solution)/shard_map/ppermute | solution.py:22
  20.8 2.2 %copy-start.1 = (bf16[1024,2048]{1,0:T(8,128)(2,1)S(1)}, bf16[1024,2048]{1,0:T(8,128)(2,1)}, u32[]{:S(2)}) copy-start(bf16[1024,2048]{1,0:T(8,128)(2,1)} %jac.1) | copy-start | bytes 12582916
  23.0 0.7 %copy-start.3 = (f32[1024]{0:T(1024)S(1)}, f32[1024]{0:T(1024)}, u32[]{:S(2)}) copy-start(f32[1024]{0:T(1024)} %param.7) | copy-start | bytes 12292
  26.0 1.5 %collective-permute-start.9 = (bf16[8,64,256]{2,1,0:T(8,128)(2,1)S(1)}, bf16[8,64,256]{2,1,0:T(8,128)(2,1)S(1)}, u32[]{:S(2)}, u32[]{:S(2)}) collective-permute-start(bf16[8,64,256]{2,1,0:T(8,128)(2,1)S(1)} %collective-permute-done.8.refs_2_), channel_id=1, source_target_pairs={{0,1},{1,0},{2,3},{3,2},{4,5},{5,4},{6,7},{7,6},{8,9},{9,8},{10,11... | collective-permute-start | bytes 786440 | tf_op jit(solution)/shard_map/ppermute | solution.py:22
  29.9 1.6 %collective-permute-start.10 = (bf16[64,2048]{1,0:T(8,128)(2,1)S(1)}, bf16[64,2048]{1,0:T(8,128)(2,1)S(1)}, u32[]{:S(2)}, u32[]{:S(2)}) collective-permute-start(bf16[64,2048]{1,0:T(8,128)(2,1)S(1)} %get-tuple-element.27), channel_id=1, source_target_pairs={{0,1},{1,0},{2,3},{3,2},{4,5},{5,4},{6,7},{7,6},{8,9},{9,8},{10,11... | collective-permute-start | bytes 786440 | tf_op jit(solution)/shard_map/ppermute | solution.py:22
  30.1 3.0 %collective-permute-start.12 = (bf16[64,2048]{1,0:T(8,128)(2,1)S(1)}, bf16[64,2048]{1,0:T(8,128)(2,1)S(1)}, u32[]{:S(2)}, u32[]{:S(2)}) collective-permute-start(bf16[64,2048]{1,0:T(8,128)(2,1)S(1)} %get-tuple-element.28), channel_id=1, source_target_pairs={{0,1},{1,0},{2,3},{3,2},{4,5},{5,4},{6,7},{7,6},{8,9},{9,8},{10,11... | collective-permute-start | bytes 786440 | tf_op jit(solution)/shard_map/ppermute | solution.py:22
  31.5 8.4 %collective-permute-start.11 = (bf16[64,2048]{1,0:T(8,128)(2,1)S(1)}, bf16[64,2048]{1,0:T(8,128)(2,1)S(1)}, u32[]{:S(2)}, u32[]{:S(2)}) collective-permute-start(bf16[64,2048]{1,0:T(8,128)(2,1)S(1)} %add_convert_fusion), channel_id=1, source_target_pairs={{0,2},{1,3},{2,0},{3,1},{4,6},{5,7},{6,4},{7,5},{8,10},{9,11},{10,... | collective-permute-start | bytes 786440 | tf_op jit(solution)/shard_map/ppermute | solution.py:22
  40.7 4.8 %collective-permute-start.13 = (bf16[64,512]{1,0:T(8,128)(2,1)S(1)}, bf16[64,512]{1,0:T(8,128)(2,1)S(1)}, u32[]{:S(2)}, u32[]{:S(2)}) collective-permute-start(bf16[64,512]{1,0:T(8,128)(2,1)S(1)} %get-tuple-element.31), channel_id=1, source_target_pairs={{0,4},{4,0},{8,12},{12,8},{16,20},{20,16},{24,28},{28,24},{1,5},{5... | collective-permute-start | bytes 196616 | tf_op jit(solution)/shard_map/ppermute | solution.py:22
  41.5 6.4 %collective-permute-start.15 = (bf16[64,512]{1,0:T(8,128)(2,1)S(1)}, bf16[64,512]{1,0:T(8,128)(2,1)S(1)}, u32[]{:S(2)}, u32[]{:S(2)}) collective-permute-start(bf16[64,512]{1,0:T(8,128)(2,1)S(1)} %get-tuple-element.33), channel_id=1, source_target_pairs={{0,4},{4,0},{8,12},{12,8},{16,20},{20,16},{24,28},{28,24},{1,5},{5... | collective-permute-start | bytes 196616 | tf_op jit(solution)/shard_map/ppermute | solution.py:22
  42.8 7.6 %collective-permute-start.17 = (bf16[64,512]{1,0:T(8,128)(2,1)S(1)}, bf16[64,512]{1,0:T(8,128)(2,1)S(1)}, u32[]{:S(2)}, u32[]{:S(2)}) collective-permute-start(bf16[64,512]{1,0:T(8,128)(2,1)S(1)} %get-tuple-element.34), channel_id=1, source_target_pairs={{0,4},{4,0},{8,12},{12,8},{16,20},{20,16},{24,28},{28,24},{1,5},{5... | collective-permute-start | bytes 196616 | tf_op jit(solution)/shard_map/ppermute | solution.py:22
  45.6 6.8 %collective-permute-start.14 = (bf16[64,512]{1,0:T(8,128)(2,1)S(1)}, bf16[64,512]{1,0:T(8,128)(2,1)S(1)}, u32[]{:S(2)}, u32[]{:S(2)}) collective-permute-start(bf16[64,512]{1,0:T(8,128)(2,1)S(1)} %add_convert_fusion.3), channel_id=1, source_target_pairs={{0,24},{4,28},{8,16},{12,20},{16,8},{20,12},{24,0},{28,4},{1,25},{... | collective-permute-start | bytes 196616 | tf_op jit(solution)/shard_map/ppermute | solution.py:22
  48.0 5.9 %collective-permute-start.16 = (bf16[64,512]{1,0:T(8,128)(2,1)S(1)}, bf16[64,512]{1,0:T(8,128)(2,1)S(1)}, u32[]{:S(2)}, u32[]{:S(2)}) collective-permute-start(bf16[64,512]{1,0:T(8,128)(2,1)S(1)} %add_convert_fusion.2), channel_id=1, source_target_pairs={{0,16},{4,20},{8,24},{12,28},{16,0},{20,4},{24,8},{28,12},{1,17},{... | collective-permute-start | bytes 196616 | tf_op jit(solution)/shard_map/ppermute | solution.py:22
  48.1 5.9 %collective-permute-start.18 = (bf16[64,512]{1,0:T(8,128)(2,1)S(1)}, bf16[64,512]{1,0:T(8,128)(2,1)S(1)}, u32[]{:S(2)}, u32[]{:S(2)}) collective-permute-start(bf16[64,512]{1,0:T(8,128)(2,1)S(1)} %get-tuple-element.36), channel_id=1, source_target_pairs={{0,12},{4,8},{8,4},{12,0},{16,28},{20,24},{24,20},{28,16},{1,13},{... | collective-permute-start | bytes 196616 | tf_op jit(solution)/shard_map/ppermute | solution.py:22
  50.4 4.3 %collective-permute-start.19 = (bf16[64,512]{1,0:T(8,128)(2,1)S(1)}, bf16[64,512]{1,0:T(8,128)(2,1)S(1)}, u32[]{:S(2)}, u32[]{:S(2)}) collective-permute-start(bf16[64,512]{1,0:T(8,128)(2,1)S(1)} %get-tuple-element.38), channel_id=1, source_target_pairs={{0,8},{4,12},{8,0},{12,4},{16,24},{20,28},{24,16},{28,20},{1,9},{5... | collective-permute-start | bytes 196616 | tf_op jit(solution)/shard_map/ppermute | solution.py:22

commit v8 on v7

--- a/solution.py
+++ b/solution.py
@@ -44,7 +44,10 @@
         first.append(swap(*ready, axis, count, step))
     first.append(swap(terms[1], axis, count, 1))
     for step in range(min(direct, count) - 1, 1, -1):
-        later.append(swap(after(terms[step], *ready), axis, count, step))
+        if step % 2:
+            later.append(swap(after(terms[step], *ready), axis, count, step))
+        else:
+            first.append(swap(terms[step], axis, count, step))
     return first, later
 
 
@@ -57,25 +60,14 @@
     out[...] = lax.dot_general(wanted, probe[...], CONTRACT_LAST, preferred_element_type=jnp.float32).astype(out.dtype)
 
 
-def weigh_kernel(count, weight, jac, after, held, weighted, sems):
-    rows, width = held.shape
-    chunk = rows // sems.shape[0]
-    copies = [
-        pltpu.make_async_copy(jac.at[pl.ds(i * chunk, chunk)], held.at[pl.ds(i * chunk, chunk)], sems.at[i])
-        for i in range(sems.shape[0])
-    ]
-    for copy in copies:
-        copy.start()
-    sub = lax.axis_index("sub")
+def weigh_kernel(weight, jac, after, weighted):
+    rows, width = jac.shape
     lanes = weight.shape[1]
-    for i, copy in enumerate(copies):
-        copy.wait()
-        for r in range(i * chunk, (i + 1) * chunk, lanes):
-            at = sub * rows + r + lax.broadcasted_iota(jnp.int32, (lanes, lanes), 0)
-            scale = jnp.broadcast_to(weight[r // lanes:r // lanes + 1, :], (lanes, lanes)).T
-            scale = scale * (at < count[0]).astype(jnp.float32)
-            scale = jnp.concatenate([scale] * (width // lanes), axis=1)
-            weighted[r:r + lanes, :] = (held[r:r + lanes, :].astype(jnp.float32) * scale).astype(jnp.bfloat16)
+    for i in range(rows // lanes):
+        scale = jnp.broadcast_to(weight[i:i + 1, :], (lanes, lanes)).T
+        scale = jnp.concatenate([scale] * (width // lanes), axis=1)
+        span = slice(i * lanes, (i + 1) * lanes)
+        weighted[span, :] = (jac[span, :].astype(jnp.float32) * scale).astype(jnp.bfloat16)
 
 
 def pick_kernel(unit, info, *refs):
@@ -172,27 +164,28 @@
         compiler_params=params(8),
         name="pick_listed",
     )
+    weight_lanes = min(128, rows)
+    observation = lax.axis_index("sub") * rows + jnp.arange(rows, dtype=jnp.int32)
+    weight = obs_weight * (observation < row_counts[0]).astype(jnp.float32)
+    weight = weight.reshape(rows // weight_lanes, weight_lanes)
+    info, weight = lax.optimization_barrier((info, weight))
     picked = pick(info, *spread(share, "obs", obs_count, SPREAD_DIRECT))
-    weight_lanes = min(128, rows)
-    held, weighted = pl.pallas_call(
+    weighted = pl.pallas_call(
         weigh_kernel,
-        out_shape=[jax.ShapeDtypeStruct((rows, width), jnp.bfloat16)] * 2,
-        in_specs=[SMEM, VMEM, HBM, pl.BlockSpec(memory_space=pl.ANY)],
-        out_specs=[VMEM, VMEM],
-        scratch_shapes=[pltpu.SemaphoreType.DMA((4,))],
+        out_shape=jax.ShapeDtypeStruct((rows, width), jnp.bfloat16),
+        in_specs=[VMEM, VMEM, pl.BlockSpec(memory_space=pl.ANY)],
+        out_specs=VMEM,
         compiler_params=params(16),
-        cost_estimate=pl.CostEstimate(flops=2 * rows * width, bytes_accessed=6 * rows * width, transcendentals=0),
+        cost_estimate=pl.CostEstimate(flops=2 * rows * width, bytes_accessed=4 * rows * width, transcendentals=0),
         name="weigh",
-    )(row_counts, obs_weight.reshape(rows // weight_lanes, weight_lanes), jacobian, picked)
+    )(weight, jacobian, picked)
 
     product = pl.pallas_call(
         product_kernel,
         out_shape=[jax.ShapeDtypeStruct((high, width), kept(j, SUB_DIRECT)) for j in range(subs)],
         in_specs=[VMEM] * (2 + subs),
         out_specs=[VMEM] * subs,
-        scratch_shapes=[
-            pltpu.VMEM((probe_width, width), jnp.bfloat16),
-        ],
+        scratch_shapes=[pltpu.VMEM((probe_width, width), jnp.bfloat16)],
         compiler_params=params(24),
         cost_estimate=pl.CostEstimate(
             flops=4 * rows * width * probe_width, bytes_accessed=4 * rows * width, transcendentals=0),
@@ -209,7 +202,7 @@
     )
 
     columns = spread(picked, "sub", subs, SPREAD_DIRECT, (weighted,))
-    first, later = collect(product(held, weighted, *columns), "sub", subs, SUB_DIRECT)
+    first, later = collect(product(jacobian, weighted, *columns), "sub", subs, SUB_DIRECT)
     first, later = collect(place(info, *first, *later), "obs", obs_count, OBS_DIRECT)
     total = after(sum(term.astype(jnp.float32) for term in first))
     return sum((term.astype(jnp.float32) for term in later), total).T.astype(jnp.bfloat16)

time: 55.6 us -> 54 us (0.971)
  starting transfers between devices: 22.7 us -> 21.6 us
  other arithmetic: 1.49 us -> 2.18 us
  local copies, waits for them, and re-layouts: 3.84 us -> 3.16 us
  Pallas kernels: 5.46 us -> 4.89 us
    ppermute x20, starting transfers between devices: 22.7 us -> 21.6 us  [swap(): return lax.ppermute(value, axis, [(i, i ^ step) for i in range(count)])]
    reshape x0 -> x1, other arithmetic: none -> 0.69 us  [local(): weight = weight.reshape(rows // weight_lanes, weight_lanes)]
    unnamed x8, local copies, waits for them, and re-layouts: 3.84 us -> 3.16 us
    pallas_call x2, Pallas kernels: 3.68 us -> 3.1 us  [the longest x1 2.36 us: local(): product(jacobian, weighted, *columns)]
  transfers between devices with their start and end apart: 20 -> 20, of which waited for: 13 -> 10; matrix products, arithmetic and copies ran while one was open for 2% -> 3% of each run, Pallas kernels for 2% -> 1%
where the time goes in v8:
time: 54 us; the launch traced here: 53.8 us
  starting transfers between devices  21.6 us (40%)
  waiting for transfers between devices  21.3 us (39%)
  Pallas kernels  4.89 us (9%)
  local copies, waits for them, and re-layouts  3.16 us (6%)
  other arithmetic  2.18 us (4%)
  between operations  0.75 us (1%)
    ppermute x20, starting transfers between devices, swap(): return lax.ppermute(value, axis, [(i, i ^ step) for i in range(count)])  21.6 us
    ppermute x20, waiting for transfers between devices, swap(): return lax.ppermute(value, axis, [(i, i ^ step) for i in range(count)])  21.3 us
    unnamed x8, local copies, waits for them, and re-layouts  3.16 us
    pallas_call x1, Pallas kernels, local(): product(jacobian, weighted, *columns)  2.36 us
  transfers between devices with their start and end apart: 20, of which 10 were waited for; matrix products, arithmetic and copies ran while one was open for 3% of the time, Pallas kernels for 1%

profile of v8, /device:TPU:0, one launch (start us, length us, event | category | flops | bytes accessed | tf_op | source)
XLA Modules:
  0.0 53.8 jit_solution(9453435952583348253)
XLA Ops:
  0.0 1.0 %copy-done.3 = bf16[512,256]{1,0:T(8,128)(2,1)S(1)} copy-done((bf16[512,256]{1,0:T(8,128)(2,1)S(1)}, bf16[512,256]{1,0:T(8,128)(2,1)}, u32[]{:S(2)}) %copy-start.3) | copy-done | bytes 262168
  1.0 0.2 share_probe.1.refs_0_
  1.2 5.1 %collective-permute-start.5 = (bf16[64,512]{1,0:T(8,128)(2,1)S(1)}, bf16[64,512]{1,0:T(8,128)(2,1)S(1)}, u32[]{:S(2)}, u32[]{:S(2)}) collective-permute-start(bf16[64,512]{1,0:T(8,128)(2,1)S(1)} %share_probe.1.refs_0_), channel_id=1, source_target_pairs={{0,24},{4,28},{8,16},{12,20},{16,8},{20,12},{24,0},{28,4},{1,25},{... | collective-permute-start | bytes 196616 | tf_op jit(solution)/shard_map/ppermute | solution.py:22
  6.3 0.0 collective-permute-start.3
  6.3 0.6 %collective-permute-start.1 = (bf16[64,512]{1,0:T(8,128)(2,1)S(1)}, bf16[64,512]{1,0:T(8,128)(2,1)S(1)}, u32[]{:S(2)}, u32[]{:S(2)}) collective-permute-start(bf16[64,512]{1,0:T(8,128)(2,1)S(1)} %share_probe.1.refs_0_), channel_id=1, source_target_pairs={{0,8},{4,12},{8,0},{12,4},{16,24},{20,28},{24,16},{28,20},{1,9},{5... | collective-permute-start | bytes 196616 | tf_op jit(solution)/shard_map/ppermute | solution.py:22
  6.9 1.6 %collective-permute-start = (bf16[64,512]{1,0:T(8,128)(2,1)S(1)}, bf16[64,512]{1,0:T(8,128)(2,1)S(1)}, u32[]{:S(2)}, u32[]{:S(2)}) collective-permute-start(bf16[64,512]{1,0:T(8,128)(2,1)S(1)} %share_probe.1.refs_0_), channel_id=1, source_target_pairs={{0,4},{4,0},{8,12},{12,8},{16,20},{20,16},{24,28},{28,24},{1,5},{5... | collective-permute-start | bytes 196616 | tf_op jit(solution)/shard_map/ppermute | solution.py:22
  9.2 0.7 %select_bitcast_fusion.weight = f32[8,128]{1,0:T(8,128)S(1)} fusion(f32[1024]{0:T(1024)} %param.7, s32[]{:T(128)} %bitcast.7, s32[]{:T(128)S(6)} %mul.6), kind=kLoop, calls=%fused_computation.6 | loop fusion | flops 3072 | bytes 8200 | tf_op jit(solution)/shard_map/reshape | solution.py:170
  9.9 0.0 collective-permute-done.5.refs_6_
  9.9 0.8 %collective-permute-start.6 = (bf16[64,512]{1,0:T(8,128)(2,1)S(1)}, bf16[64,512]{1,0:T(8,128)(2,1)S(1)}, u32[]{:S(2)}, u32[]{:S(2)}) collective-permute-start(bf16[64,512]{1,0:T(8,128)(2,1)S(1)} %collective-permute-done.5.refs_6_), channel_id=1, source_target_pairs={{0,4},{4,0},{8,12},{12,8},{16,20},{20,16},{24,28},{28,24},{1,5},{5... | collective-permute-start | bytes 196616 | tf_op jit(solution)/shard_map/ppermute | solution.py:22
  10.7 1.2 %collective-permute-done.3.refs_4_ = bf16[64,512]{1,0:T(8,128)(2,1)S(1)} collective-permute-done((bf16[64,512]{1,0:T(8,128)(2,1)S(1)}, bf16[64,512]{1,0:T(8,128)(2,1)S(1)}, u32[]{:S(2)}, u32[]{:S(2)}) %collective-permute-start.3) | collective-permute-done | bytes 65568 | tf_op jit(solution)/shard_map/ppermute | solution.py:22
  11.9 1.5 %collective-permute-start.4 = (bf16[64,512]{1,0:T(8,128)(2,1)S(1)}, bf16[64,512]{1,0:T(8,128)(2,1)S(1)}, u32[]{:S(2)}, u32[]{:S(2)}) collective-permute-start(bf16[64,512]{1,0:T(8,128)(2,1)S(1)} %collective-permute-done.3.refs_4_), channel_id=1, source_target_pairs={{0,4},{4,0},{8,12},{12,8},{16,20},{20,16},{24,28},{28,24},{1,5},{5... | collective-permute-start | bytes 196616 | tf_op jit(solution)/shard_map/ppermute | solution.py:22
  13.4 0.0 collective-permute-done.1.refs_2_
  13.4 0.5 collective-permute-start.2
  13.9 0.7 %pad_add_fusion.info = s32[24]{0:T(128)S(1)} fusion(s32[16]{0:T(128)} %param.10, s32[8]{0:T(128)S(1)} %dynamic-slice_bitcast_fusion), kind=kLoop, calls=%fused_computation.8 | loop fusion | flops 24 | bytes 192 | tf_op jit(solution)/shard_map/concatenate | solution.py:145
  14.7 2.1 %collective-permute-done.4.refs_5_ = bf16[64,512]{1,0:T(8,128)(2,1)S(1)} collective-permute-done((bf16[64,512]{1,0:T(8,128)(2,1)S(1)}, bf16[64,512]{1,0:T(8,128)(2,1)S(1)}, u32[]{:S(2)}, u32[]{:S(2)}) %collective-permute-start.4) | collective-permute-done | bytes 65568 | tf_op jit(solution)/shard_map/ppermute | solution.py:22
  16.8 0.9 %collective-permute-done.2.refs_3_ = bf16[64,512]{1,0:T(8,128)(2,1)S(1)} collective-permute-done((bf16[64,512]{1,0:T(8,128)(2,1)S(1)}, bf16[64,512]{1,0:T(8,128)(2,1)S(1)}, u32[]{:S(2)}, u32[]{:S(2)}) %collective-permute-start.2) | collective-permute-done | bytes 65568 | tf_op jit(solution)/shard_map/ppermute | solution.py:22
  17.6 0.8 %pick_listed.1.after.refs_0_ = bf16[8,64,256]{2,1,0:T(8,128)(2,1)S(1)} custom-call(s32[24]{0:T(128)S(1)} %pad_add_fusion.info, bf16[64,512]{1,0:T(8,128)(2,1)S(1)} %share_probe.1.refs_0_, bf16[64,512]{1,0:T(8,128)(2,1)S(1)} %collective-permute-done.refs_1_, bf16[64,512]{1,0:T(8,128)(2,1)S(1)} %collective-permute-done.1.refs_2_, ...), custom_call_target="tpu_custom_call" | custom-call | tf_op jit(solution)/shard_map/pick_listed/pallas_call | solution.py:172
  18.5 1.6 %collective-permute-start.8 = (bf16[8,64,256]{2,1,0:T(8,128)(2,1)S(1)}, bf16[8,64,256]{2,1,0:T(8,128)(2,1)S(1)}, u32[]{:S(2)}, u32[]{:S(2)}) collective-permute-start(bf16[8,64,256]{2,1,0:T(8,128)(2,1)S(1)} %pick_listed.1.after.refs_0_), channel_id=1, source_target_pairs={{0,2},{1,3},{2,0},{3,1},{4,6},{5,7},{6,4},{7,5},{8,10},{9,11},{10,... | collective-permute-start | bytes 786440 | tf_op jit(solution)/shard_map/ppermute | solution.py:22
  20.1 0.0 collective-permute-start.7
  20.1 2.2 %copy-done.1 = bf16[1024,2048]{1,0:T(8,128)(2,1)S(1)} copy-done((bf16[1024,2048]{1,0:T(8,128)(2,1)S(1)}, bf16[1024,2048]{1,0:T(8,128)(2,1)}, u32[]{:S(2)}) %copy-start.1) | copy-done | bytes 4194328
  22.2 0.7 %weigh.1.weighted = bf16[1024,2048]{1,0:T(8,128)(2,1)S(1)} custom-call(f32[8,128]{1,0:T(8,128)S(1)} %select_bitcast_fusion.weight, bf16[1024,2048]{1,0:T(8,128)(2,1)S(1)} %copy-done.1, bf16[8,64,256]{2,1,0:T(8,128)(2,1)S(1)} %pick_listed.1.after.refs_0_), custom_call_target="tpu_custom_call" | custom-call | flops 4194304 | bytes 8388608 | tf_op jit(solution)/shard_map/weigh/pallas_call | solution.py:173
  23.0 3.0 %collective-permute-done.8.refs_2_ = bf16[8,64,256]{2,1,0:T(8,128)(2,1)S(1)} collective-permute-done((bf16[8,64,256]{2,1,0:T(8,128)(2,1)S(1)}, bf16[8,64,256]{2,1,0:T(8,128)(2,1)S(1)}, u32[]{:S(2)}, u32[]{:S(2)}) %collective-permute-start.8) | collective-permute-done | bytes 262176 | tf_op jit(solution)/shard_map/ppermute | solution.py:22
  26.0 0.0 collective-permute-start.9
  26.0 0.0 collective-permute-done.7.refs_1_
  26.0 1.5 %collective-permute-done.9.refs_3_ = bf16[8,64,256]{2,1,0:T(8,128)(2,1)S(1)} collective-permute-done((bf16[8,64,256]{2,1,0:T(8,128)(2,1)S(1)}, bf16[8,64,256]{2,1,0:T(8,128)(2,1)S(1)}, u32[]{:S(2)}, u32[]{:S(2)}) %collective-permute-start.9) | collective-permute-done | bytes 262176 | tf_op jit(solution)/shard_map/ppermute | solution.py:22
  27.5 2.4 %product.1 = (f32[64,2048]{1,0:T(8,128)S(1)}, bf16[64,2048]{1,0:T(8,128)(2,1)S(1)}, f32[64,2048]{1,0:T(8,128)S(1)}, bf16[64,2048]{1,0:T(8,128)(2,1)S(1)}) custom-call(bf16[1024,2048]{1,0:T(8,128)(2,1)S(1)} %copy-done.2, bf16[1024,2048]{1,0:T(8,128)(2,1)S(1)} %weigh.1.weighted, bf16[8,64,256]{2,1,0:T(8,128)(2,1)S(1)} %pick_listed.1.after.refs_0_, ...), custom_call_target="tpu_custom_call" | custom-call | flops 2147483648 | bytes 8388608 | tf_op jit(solution)/shard_map/product/pallas_call | solution.py:205
  29.9 0.2 collective-permute-start.10
  30.1 0.4 collective-permute-start.12
  30.5 1.0 %collective-permute-done.10 = bf16[64,2048]{1,0:T(8,128)(2,1)S(1)} collective-permute-done((bf16[64,2048]{1,0:T(8,128)(2,1)S(1)}, bf16[64,2048]{1,0:T(8,128)(2,1)S(1)}, u32[]{:S(2)}, u32[]{:S(2)}) %collective-permute-start.10) | collective-permute-done | bytes 262176 | tf_op jit(solution)/shard_map/ppermute | solution.py:22
  31.5 1.6 %collective-permute-start.11 = (bf16[64,2048]{1,0:T(8,128)(2,1)S(1)}, bf16[64,2048]{1,0:T(8,128)(2,1)S(1)}, u32[]{:S(2)}, u32[]{:S(2)}) collective-permute-start(bf16[64,2048]{1,0:T(8,128)(2,1)S(1)} %add_convert_fusion), channel_id=1, source_target_pairs={{0,2},{1,3},{2,0},{3,1},{4,6},{5,7},{6,4},{7,5},{8,10},{9,11},{10,... | collective-permute-start | bytes 786440 | tf_op jit(solution)/shard_map/ppermute | solution.py:22
  33.1 0.0 collective-permute-done.12.refs_2_
  33.1 6.8 %collective-permute-done.11.refs_1_ = bf16[64,2048]{1,0:T(8,128)(2,1)S(1)} collective-permute-done((bf16[64,2048]{1,0:T(8,128)(2,1)S(1)}, bf16[64,2048]{1,0:T(8,128)(2,1)S(1)}, u32[]{:S(2)}, u32[]{:S(2)}) %collective-permute-start.11) | collective-permute-done | bytes 262176 | tf_op jit(solution)/shard_map/ppermute | solution.py:22
  40.0 0.8 %place.1 = (f32[64,512]{1,0:T(8,128)S(1)}, bf16[64,512]{1,0:T(8,128)(2,1)S(1)}, bf16[64,512]{1,0:T(8,128)(2,1)S(1)}, bf16[64,512]{1,0:T(8,128)(2,1)S(1)}, f32[64...) custom-call(s32[24]{0:T(128)S(1)} %pad_add_fusion.info, ...), custom_call_target="tpu_custom_call" | custom-call | tf_op jit(solution)/shard_map/place/pallas_call | solution.py:206
  40.7 0.8 %collective-permute-start.13 = (bf16[64,512]{1,0:T(8,128)(2,1)S(1)}, bf16[64,512]{1,0:T(8,128)(2,1)S(1)}, u32[]{:S(2)}, u32[]{:S(2)}) collective-permute-start(bf16[64,512]{1,0:T(8,128)(2,1)S(1)} %get-tuple-element.30), channel_id=1, source_target_pairs={{0,4},{4,0},{8,12},{12,8},{16,20},{20,16},{24,28},{28,24},{1,5},{5... | collective-permute-start | bytes 196616 | tf_op jit(solution)/shard_map/ppermute | solution.py:22
  41.5 1.3 %collective-permute-start.15 = (bf16[64,512]{1,0:T(8,128)(2,1)S(1)}, bf16[64,512]{1,0:T(8,128)(2,1)S(1)}, u32[]{:S(2)}, u32[]{:S(2)}) collective-permute-start(bf16[64,512]{1,0:T(8,128)(2,1)S(1)} %get-tuple-element.32), channel_id=1, source_target_pairs={{0,4},{4,0},{8,12},{12,8},{16,20},{20,16},{24,28},{28,24},{1,5},{5... | collective-permute-start | bytes 196616 | tf_op jit(solution)/shard_map/ppermute | solution.py:22
  42.8 0.7 %collective-permute-start.17 = (bf16[64,512]{1,0:T(8,128)(2,1)S(1)}, bf16[64,512]{1,0:T(8,128)(2,1)S(1)}, u32[]{:S(2)}, u32[]{:S(2)}) collective-permute-start(bf16[64,512]{1,0:T(8,128)(2,1)S(1)} %get-tuple-element.33), channel_id=1, source_target_pairs={{0,4},{4,0},{8,12},{12,8},{16,20},{20,16},{24,28},{28,24},{1,5},{5... | collective-permute-start | bytes 196616 | tf_op jit(solution)/shard_map/ppermute | solution.py:22
  43.5 0.0 collective-permute-start.18
  43.5 2.0 %collective-permute-done.13 = bf16[64,512]{1,0:T(8,128)(2,1)S(1)} collective-permute-done((bf16[64,512]{1,0:T(8,128)(2,1)S(1)}, bf16[64,512]{1,0:T(8,128)(2,1)S(1)}, u32[]{:S(2)}, u32[]{:S(2)}) %collective-permute-start.13) | collective-permute-done | bytes 65568 | tf_op jit(solution)/shard_map/ppermute | solution.py:22
  45.6 1.7 %collective-permute-start.14 = (bf16[64,512]{1,0:T(8,128)(2,1)S(1)}, bf16[64,512]{1,0:T(8,128)(2,1)S(1)}, u32[]{:S(2)}, u32[]{:S(2)}) collective-permute-start(bf16[64,512]{1,0:T(8,128)(2,1)S(1)} %add_convert_fusion.3), channel_id=1, source_target_pairs={{0,24},{4,28},{8,16},{12,20},{16,8},{20,12},{24,0},{28,4},{1,25},{... | collective-permute-start | bytes 196616 | tf_op jit(solution)/shard_map/ppermute | solution.py:22
  47.3 0.0 collective-permute-done.15
  47.3 0.1 collective-permute-start.16
  47.4 3.0 %collective-permute-start.19 = (bf16[64,512]{1,0:T(8,128)(2,1)S(1)}, bf16[64,512]{1,0:T(8,128)(2,1)S(1)}, u32[]{:S(2)}, u32[]{:S(2)}) collective-permute-start(bf16[64,512]{1,0:T(8,128)(2,1)S(1)} %get-tuple-element.36), channel_id=1, source_target_pairs={{0,12},{4,8},{8,4},{12,0},{16,28},{20,24},{24,20},{28,16},{1,13},{... | collective-permute-start | bytes 196616 | tf_op jit(solution)/shard_map/ppermute | solution.py:22
  50.4 0.0 collective-permute-done.17
  50.4 0.0 collective-permute-done.18
  50.4 1.3 %collective-permute-done.14 = bf16[64,512]{1,0:T(8,128)(2,1)S(1)} collective-permute-done((bf16[64,512]{1,0:T(8,128)(2,1)S(1)}, bf16[64,512]{1,0:T(8,128)(2,1)S(1)}, u32[]{:S(2)}, u32[]{:S(2)}) %collective-permute-start.14) | collective-permute-done | bytes 65568 | tf_op jit(solution)/shard_map/ppermute | solution.py:22
  51.7 1.4 %collective-permute-done.16 = bf16[64,512]{1,0:T(8,128)(2,1)S(1)} collective-permute-done((bf16[64,512]{1,0:T(8,128)(2,1)S(1)}, bf16[64,512]{1,0:T(8,128)(2,1)S(1)}, u32[]{:S(2)}, u32[]{:S(2)}) %collective-permute-start.16) | collective-permute-done | bytes 65568 | tf_op jit(solution)/shard_map/ppermute | solution.py:22
  53.2 0.0 collective-permute-done.19
  53.2 0.6 %fusion = bf16[512,64]{0,1:T(8,128)(2,1)} fusion(f32[64,512]{1,0:T(8,128)S(1)} %convert_add_fusion, bf16[64,512]{1,0:T(8,128)(2,1)S(1)} %collective-permute-done.19), kind=kLoop, calls=%fused_computation.5 | loop fusion | flops 98304 | bytes 262144 | tf_op jit(solution)/shard_map/convert_element_type | solution.py:208
  (13 shorter events, 0.1 us)
Async XLA Ops:
  0.0 9.9 %copy-start = (s32[8,8]{1,0:T(8,128)S(1)}, s32[8,8]{1,0:T(8,128)}, u32[]{:S(2)}) copy-start(s32[8,8]{1,0:T(8,128)} %param.9) | copy-start | bytes 772
  0.0 1.0 %copy-start.3 = (bf16[512,256]{1,0:T(8,128)(2,1)S(1)}, bf16[512,256]{1,0:T(8,128)(2,1)}, u32[]{:S(2)}) copy-start(bf16[512,256]{1,0:T(8,128)(2,1)} %probe.1) | copy-start | bytes 786436
  1.2 8.8 %collective-permute-start.5 = (bf16[64,512]{1,0:T(8,128)(2,1)S(1)}, bf16[64,512]{1,0:T(8,128)(2,1)S(1)}, u32[]{:S(2)}, u32[]{:S(2)}) collective-permute-start(bf16[64,512]{1,0:T(8,128)(2,1)S(1)} %share_probe.1.refs_0_), channel_id=1, source_target_pairs={{0,24},{4,28},{8,16},{12,20},{16,8},{20,12},{24,0},{28,4},{1,25},{... | collective-permute-start | bytes 196616 | tf_op jit(solution)/shard_map/ppermute | solution.py:22
  6.3 5.6 %collective-permute-start.3 = (bf16[64,512]{1,0:T(8,128)(2,1)S(1)}, bf16[64,512]{1,0:T(8,128)(2,1)S(1)}, u32[]{:S(2)}, u32[]{:S(2)}) collective-permute-start(bf16[64,512]{1,0:T(8,128)(2,1)S(1)} %share_probe.1.refs_0_), channel_id=1, source_target_pairs={{0,16},{4,20},{8,24},{12,28},{16,0},{20,4},{24,8},{28,12},{1,17},{... | collective-permute-start | bytes 196616 | tf_op jit(solution)/shard_map/ppermute | solution.py:22
  6.3 7.1 %collective-permute-start.1 = (bf16[64,512]{1,0:T(8,128)(2,1)S(1)}, bf16[64,512]{1,0:T(8,128)(2,1)S(1)}, u32[]{:S(2)}, u32[]{:S(2)}) collective-permute-start(bf16[64,512]{1,0:T(8,128)(2,1)S(1)} %share_probe.1.refs_0_), channel_id=1, source_target_pairs={{0,8},{4,12},{8,0},{12,4},{16,24},{20,28},{24,16},{28,20},{1,9},{5... | collective-permute-start | bytes 196616 | tf_op jit(solution)/shard_map/ppermute | solution.py:22
  6.9 7.7 %collective-permute-start = (bf16[64,512]{1,0:T(8,128)(2,1)S(1)}, bf16[64,512]{1,0:T(8,128)(2,1)S(1)}, u32[]{:S(2)}, u32[]{:S(2)}) collective-permute-start(bf16[64,512]{1,0:T(8,128)(2,1)S(1)} %share_probe.1.refs_0_), channel_id=1, source_target_pairs={{0,4},{4,0},{8,12},{12,8},{16,20},{20,16},{24,28},{28,24},{1,5},{5... | collective-permute-start | bytes 196616 | tf_op jit(solution)/shard_map/ppermute | solution.py:22
  9.9 4.7 %collective-permute-start.6 = (bf16[64,512]{1,0:T(8,128)(2,1)S(1)}, bf16[64,512]{1,0:T(8,128)(2,1)S(1)}, u32[]{:S(2)}, u32[]{:S(2)}) collective-permute-start(bf16[64,512]{1,0:T(8,128)(2,1)S(1)} %collective-permute-done.5.refs_6_), channel_id=1, source_target_pairs={{0,4},{4,0},{8,12},{12,8},{16,20},{20,16},{24,28},{28,24},{1,5},{5... | collective-permute-start | bytes 196616 | tf_op jit(solution)/shard_map/ppermute | solution.py:22
  11.9 4.9 %collective-permute-start.4 = (bf16[64,512]{1,0:T(8,128)(2,1)S(1)}, bf16[64,512]{1,0:T(8,128)(2,1)S(1)}, u32[]{:S(2)}, u32[]{:S(2)}) collective-permute-start(bf16[64,512]{1,0:T(8,128)(2,1)S(1)} %collective-permute-done.3.refs_4_), channel_id=1, source_target_pairs={{0,4},{4,0},{8,12},{12,8},{16,20},{20,16},{24,28},{28,24},{1,5},{5... | collective-permute-start | bytes 196616 | tf_op jit(solution)/shard_map/ppermute | solution.py:22
  13.4 4.3 %collective-permute-start.2 = (bf16[64,512]{1,0:T(8,128)(2,1)S(1)}, bf16[64,512]{1,0:T(8,128)(2,1)S(1)}, u32[]{:S(2)}, u32[]{:S(2)}) collective-permute-start(bf16[64,512]{1,0:T(8,128)(2,1)S(1)} %collective-permute-done.1.refs_2_), channel_id=1, source_target_pairs={{0,4},{4,0},{8,12},{12,8},{16,20},{20,16},{24,28},{28,24},{1,5},{5... | collective-permute-start | bytes 196616 | tf_op jit(solution)/shard_map/ppermute | solution.py:22
  18.5 7.5 %collective-permute-start.8 = (bf16[8,64,256]{2,1,0:T(8,128)(2,1)S(1)}, bf16[8,64,256]{2,1,0:T(8,128)(2,1)S(1)}, u32[]{:S(2)}, u32[]{:S(2)}) collective-permute-start(bf16[8,64,256]{2,1,0:T(8,128)(2,1)S(1)} %pick_listed.1.after.refs_0_), channel_id=1, source_target_pairs={{0,2},{1,3},{2,0},{3,1},{4,6},{5,7},{6,4},{7,5},{8,10},{9,11},{10,... | collective-permute-start | bytes 786440 | tf_op jit(solution)/shard_map/ppermute | solution.py:22
  20.1 5.9 %collective-permute-start.7 = (bf16[8,64,256]{2,1,0:T(8,128)(2,1)S(1)}, bf16[8,64,256]{2,1,0:T(8,128)(2,1)S(1)}, u32[]{:S(2)}, u32[]{:S(2)}) collective-permute-start(bf16[8,64,256]{2,1,0:T(8,128)(2,1)S(1)} %pick_listed.1.after.refs_0_), channel_id=1, source_target_pairs={{0,1},{1,0},{2,3},{3,2},{4,5},{5,4},{6,7},{7,6},{8,9},{9,8},{10,11... | collective-permute-start | bytes 786440 | tf_op jit(solution)/shard_map/ppermute | solution.py:22
  20.1 2.2 %copy-start.1 = (bf16[1024,2048]{1,0:T(8,128)(2,1)S(1)}, bf16[1024,2048]{1,0:T(8,128)(2,1)}, u32[]{:S(2)}) copy-start(bf16[1024,2048]{1,0:T(8,128)(2,1)} %held.1) | copy-start | bytes 12582916
  22.2 5.3 %copy-start.2 = (bf16[1024,2048]{1,0:T(8,128)(2,1)S(1)}, bf16[1024,2048]{1,0:T(8,128)(2,1)}, u32[]{:S(2)}) copy-start(bf16[1024,2048]{1,0:T(8,128)(2,1)} %held.1) | copy-start | bytes 12582916
  26.0 1.5 %collective-permute-start.9 = (bf16[8,64,256]{2,1,0:T(8,128)(2,1)S(1)}, bf16[8,64,256]{2,1,0:T(8,128)(2,1)S(1)}, u32[]{:S(2)}, u32[]{:S(2)}) collective-permute-start(bf16[8,64,256]{2,1,0:T(8,128)(2,1)S(1)} %collective-permute-done.8.refs_2_), channel_id=1, source_target_pairs={{0,1},{1,0},{2,3},{3,2},{4,5},{5,4},{6,7},{7,6},{8,9},{9,8},{10,11... | collective-permute-start | bytes 786440 | tf_op jit(solution)/shard_map/ppermute | solution.py:22
  29.9 1.6 %collective-permute-start.10 = (bf16[64,2048]{1,0:T(8,128)(2,1)S(1)}, bf16[64,2048]{1,0:T(8,128)(2,1)S(1)}, u32[]{:S(2)}, u32[]{:S(2)}) collective-permute-start(bf16[64,2048]{1,0:T(8,128)(2,1)S(1)} %get-tuple-element.26), channel_id=1, source_target_pairs={{0,1},{1,0},{2,3},{3,2},{4,5},{5,4},{6,7},{7,6},{8,9},{9,8},{10,11... | collective-permute-start | bytes 786440 | tf_op jit(solution)/shard_map/ppermute | solution.py:22
  30.1 3.0 %collective-permute-start.12 = (bf16[64,2048]{1,0:T(8,128)(2,1)S(1)}, bf16[64,2048]{1,0:T(8,128)(2,1)S(1)}, u32[]{:S(2)}, u32[]{:S(2)}) collective-permute-start(bf16[64,2048]{1,0:T(8,128)(2,1)S(1)} %get-tuple-element.27), channel_id=1, source_target_pairs={{0,1},{1,0},{2,3},{3,2},{4,5},{5,4},{6,7},{7,6},{8,9},{9,8},{10,11... | collective-permute-start | bytes 786440 | tf_op jit(solution)/shard_map/ppermute | solution.py:22
  31.5 8.4 %collective-permute-start.11 = (bf16[64,2048]{1,0:T(8,128)(2,1)S(1)}, bf16[64,2048]{1,0:T(8,128)(2,1)S(1)}, u32[]{:S(2)}, u32[]{:S(2)}) collective-permute-start(bf16[64,2048]{1,0:T(8,128)(2,1)S(1)} %add_convert_fusion), channel_id=1, source_target_pairs={{0,2},{1,3},{2,0},{3,1},{4,6},{5,7},{6,4},{7,5},{8,10},{9,11},{10,... | collective-permute-start | bytes 786440 | tf_op jit(solution)/shard_map/ppermute | solution.py:22
  40.7 4.8 %collective-permute-start.13 = (bf16[64,512]{1,0:T(8,128)(2,1)S(1)}, bf16[64,512]{1,0:T(8,128)(2,1)S(1)}, u32[]{:S(2)}, u32[]{:S(2)}) collective-permute-start(bf16[64,512]{1,0:T(8,128)(2,1)S(1)} %get-tuple-element.30), channel_id=1, source_target_pairs={{0,4},{4,0},{8,12},{12,8},{16,20},{20,16},{24,28},{28,24},{1,5},{5... | collective-permute-start | bytes 196616 | tf_op jit(solution)/shard_map/ppermute | solution.py:22
  41.5 5.8 %collective-permute-start.15 = (bf16[64,512]{1,0:T(8,128)(2,1)S(1)}, bf16[64,512]{1,0:T(8,128)(2,1)S(1)}, u32[]{:S(2)}, u32[]{:S(2)}) collective-permute-start(bf16[64,512]{1,0:T(8,128)(2,1)S(1)} %get-tuple-element.32), channel_id=1, source_target_pairs={{0,4},{4,0},{8,12},{12,8},{16,20},{20,16},{24,28},{28,24},{1,5},{5... | collective-permute-start | bytes 196616 | tf_op jit(solution)/shard_map/ppermute | solution.py:22
  42.8 7.6 %collective-permute-start.17 = (bf16[64,512]{1,0:T(8,128)(2,1)S(1)}, bf16[64,512]{1,0:T(8,128)(2,1)S(1)}, u32[]{:S(2)}, u32[]{:S(2)}) collective-permute-start(bf16[64,512]{1,0:T(8,128)(2,1)S(1)} %get-tuple-element.33), channel_id=1, source_target_pairs={{0,4},{4,0},{8,12},{12,8},{16,20},{20,16},{24,28},{28,24},{1,5},{5... | collective-permute-start | bytes 196616 | tf_op jit(solution)/shard_map/ppermute | solution.py:22
  43.5 6.9 %collective-permute-start.18 = (bf16[64,512]{1,0:T(8,128)(2,1)S(1)}, bf16[64,512]{1,0:T(8,128)(2,1)S(1)}, u32[]{:S(2)}, u32[]{:S(2)}) collective-permute-start(bf16[64,512]{1,0:T(8,128)(2,1)S(1)} %get-tuple-element.34), channel_id=1, source_target_pairs={{0,8},{4,12},{8,0},{12,4},{16,24},{20,28},{24,16},{28,20},{1,9},{5... | collective-permute-start | bytes 196616 | tf_op jit(solution)/shard_map/ppermute | solution.py:22
  45.6 6.1 %collective-permute-start.14 = (bf16[64,512]{1,0:T(8,128)(2,1)S(1)}, bf16[64,512]{1,0:T(8,128)(2,1)S(1)}, u32[]{:S(2)}, u32[]{:S(2)}) collective-permute-start(bf16[64,512]{1,0:T(8,128)(2,1)S(1)} %add_convert_fusion.3), channel_id=1, source_target_pairs={{0,24},{4,28},{8,16},{12,20},{16,8},{20,12},{24,0},{28,4},{1,25},{... | collective-permute-start | bytes 196616 | tf_op jit(solution)/shard_map/ppermute | solution.py:22
  47.3 5.8 %collective-permute-start.16 = (bf16[64,512]{1,0:T(8,128)(2,1)S(1)}, bf16[64,512]{1,0:T(8,128)(2,1)S(1)}, u32[]{:S(2)}, u32[]{:S(2)}) collective-permute-start(bf16[64,512]{1,0:T(8,128)(2,1)S(1)} %add_convert_fusion.2), channel_id=1, source_target_pairs={{0,16},{4,20},{8,24},{12,28},{16,0},{20,4},{24,8},{28,12},{1,17},{... | collective-permute-start | bytes 196616 | tf_op jit(solution)/shard_map/ppermute | solution.py:22
  47.4 5.8 %collective-permute-start.19 = (bf16[64,512]{1,0:T(8,128)(2,1)S(1)}, bf16[64,512]{1,0:T(8,128)(2,1)S(1)}, u32[]{:S(2)}, u32[]{:S(2)}) collective-permute-start(bf16[64,512]{1,0:T(8,128)(2,1)S(1)} %get-tuple-element.36), channel_id=1, source_target_pairs={{0,12},{4,8},{8,4},{12,0},{16,28},{20,24},{24,20},{28,16},{1,13},{... | collective-permute-start | bytes 196616 | tf_op jit(solution)/shard_map/ppermute | solution.py:22

commit v9 on v8

--- a/solution.py
+++ b/solution.py
@@ -36,13 +36,17 @@
     return [held[step] for step in range(count)]
 
 
-def collect(terms, axis, count, direct):
-    first, later, ready = [terms[0]], [], ()
+def collect_far(terms, axis, count, direct):
+    parts, ready = [], ()
     for step in range(count - 2, direct - 1, -2):
         passed = swap(terms[step + 1], axis, count, 1)
         ready = (terms[step] + passed.astype(jnp.float32)).astype(jnp.bfloat16),
-        first.append(swap(*ready, axis, count, step))
-    first.append(swap(terms[1], axis, count, 1))
+        parts.append(swap(*ready, axis, count, step))
+    return parts, ready
+
+
+def collect_near(terms, axis, count, direct, ready):
+    first, later = [terms[0], swap(terms[1], axis, count, 1)], []
     for step in range(min(direct, count) - 1, 1, -1):
         if step % 2:
             later.append(swap(after(terms[step], *ready), axis, count, step))
@@ -180,21 +184,24 @@
         name="weigh",
     )(weight, jacobian, picked)
 
-    product = pl.pallas_call(
-        product_kernel,
-        out_shape=[jax.ShapeDtypeStruct((high, width), kept(j, SUB_DIRECT)) for j in range(subs)],
-        in_specs=[VMEM] * (2 + subs),
-        out_specs=[VMEM] * subs,
-        scratch_shapes=[pltpu.VMEM((probe_width, width), jnp.bfloat16)],
-        compiler_params=params(24),
-        cost_estimate=pl.CostEstimate(
-            flops=4 * rows * width * probe_width, bytes_accessed=4 * rows * width, transcendentals=0),
-        name="product",
-    )
+    def product(name, steps, columns):
+        lanes = high * len(steps)
+        return pl.pallas_call(
+            product_kernel,
+            out_shape=[jax.ShapeDtypeStruct((high, width), kept(j, SUB_DIRECT)) for j in steps],
+            in_specs=[VMEM] * (2 + len(steps)),
+            out_specs=[VMEM] * len(steps),
+            scratch_shapes=[pltpu.VMEM((lanes, width), jnp.bfloat16)],
+            compiler_params=params(24),
+            cost_estimate=pl.CostEstimate(
+                flops=4 * rows * width * lanes, bytes_accessed=4 * rows * width, transcendentals=0),
+            name=name,
+        )(jacobian, weighted, *columns)
+
     place = pl.pallas_call(
-        functools.partial(place_kernel, unit, tile, listed, subs // 2 + 1),
+        functools.partial(place_kernel, unit, tile, listed, 2),
         out_shape=[jax.ShapeDtypeStruct((high, own_rows), kept(step, OBS_DIRECT)) for step in range(obs_count)],
-        in_specs=[SMEM] + [VMEM] * (subs // 2 + 1),
+        in_specs=[SMEM] + [VMEM] * 2,
         out_specs=[VMEM] * obs_count,
         scratch_shapes=[pltpu.SMEM((tiles,), jnp.int32), pltpu.VMEM((high, width), jnp.float32)],
         compiler_params=params(8),
@@ -202,8 +209,17 @@
     )
 
     columns = spread(picked, "sub", subs, SPREAD_DIRECT, (weighted,))
-    first, later = collect(product(jacobian, weighted, *columns), "sub", subs, SUB_DIRECT)
-    first, later = collect(place(info, *first, *later), "obs", obs_count, OBS_DIRECT)
+    terms = {}
+    if subs > 2:
+        terms = dict(enumerate(product("far_product", range(2, subs), columns[2:]), 2))
+    far, ready = collect_far(terms, "sub", subs, SUB_DIRECT)
+    near = product("near_product", range(2), [columns[0], after(columns[1], *ready)])
+    first, _ = collect_near(near, "sub", subs, SUB_DIRECT, ready)
+    partial = sum((term.astype(jnp.float32) for term in far), first[0])
+    terms = place(info, partial, first[1])
+    far, ready = collect_far(terms, "obs", obs_count, OBS_DIRECT)
+    first, later = collect_near(terms, "obs", obs_count, OBS_DIRECT, ready)
+    first += far
     total = after(sum(term.astype(jnp.float32) for term in first))
     return sum((term.astype(jnp.float32) for term in later), total).T.astype(jnp.bfloat16)
 

time: 54 us -> 54 us (level)
  waiting for transfers between devices: 21.3 us -> 17.8 us
  Pallas kernels: 4.89 us -> 6.6 us
  starting transfers between devices: 21.6 us -> 23.2 us
    ppermute x20, waiting for transfers between devices: 21.3 us -> 17.8 us  [swap(): return lax.ppermute(value, axis, [(i, i ^ step) for i in range(count)])]
    pallas_call x2 -> x3, Pallas kernels: 3.14 us -> 4.85 us  [the longest x2 4.12 us: product(): pl.pallas_call(product_kernel, out_shape=[jax.ShapeDtypeStruct((high, wid...]
    ppermute x20, starting transfers between devices: 21.6 us -> 23.2 us  [swap(): return lax.ppermute(value, axis, [(i, i ^ step) for i in range(count)])]
  transfers between devices with their start and end apart: 20 -> 20, of which waited for: 10 -> 11; matrix products, arithmetic and copies ran while one was open for 3% -> 3% of each run, Pallas kernels for 1% -> 5%
where the time goes in v9:
time: 54 us; the launch traced here: 53.8 us
  starting transfers between devices  23.2 us (43%)
  waiting for transfers between devices  17.8 us (33%)
  Pallas kernels  6.6 us (12%)
  local copies, waits for them, and re-layouts  3.16 us (6%)
  other arithmetic  2.23 us (4%)
  between operations  0.77 us (1%)
    ppermute x20, starting transfers between devices, swap(): return lax.ppermute(value, axis, [(i, i ^ step) for i in range(count)])  23.2 us
    ppermute x20, waiting for transfers between devices, swap(): return lax.ppermute(value, axis, [(i, i ^ step) for i in range(count)])  17.8 us
    pallas_call x2, Pallas kernels, product(): pl.pallas_call(product_kernel, out_shape=[jax.ShapeDtypeStruct((high, wid...  4.12 us
    unnamed x8, local copies, waits for them, and re-layouts  3.16 us
  transfers between devices with their start and end apart: 20, of which 11 were waited for; matrix products, arithmetic and copies ran while one was open for 3% of the time, Pallas kernels for 5%

profile of v9, /device:TPU:0, one launch (start us, length us, event | category | flops | bytes accessed | tf_op | source)
XLA Modules:
  0.0 53.8 jit_solution(10481382802498223210)
XLA Ops:
  0.0 1.0 %copy-done.3 = bf16[512,256]{1,0:T(8,128)(2,1)S(1)} copy-done((bf16[512,256]{1,0:T(8,128)(2,1)S(1)}, bf16[512,256]{1,0:T(8,128)(2,1)}, u32[]{:S(2)}) %copy-start.3) | copy-done | bytes 262168
  1.0 0.2 share_probe.1.refs_0_
  1.2 3.1 %collective-permute-start.1 = (bf16[64,512]{1,0:T(8,128)(2,1)S(1)}, bf16[64,512]{1,0:T(8,128)(2,1)S(1)}, u32[]{:S(2)}, u32[]{:S(2)}) collective-permute-start(bf16[64,512]{1,0:T(8,128)(2,1)S(1)} %share_probe.1.refs_0_), channel_id=1, source_target_pairs={{0,8},{4,12},{8,0},{12,4},{16,24},{20,28},{24,16},{28,20},{1,9},{5... | collective-permute-start | bytes 196616 | tf_op jit(solution)/shard_map/ppermute | solution.py:22
  4.3 2.6 %collective-permute-start.3 = (bf16[64,512]{1,0:T(8,128)(2,1)S(1)}, bf16[64,512]{1,0:T(8,128)(2,1)S(1)}, u32[]{:S(2)}, u32[]{:S(2)}) collective-permute-start(bf16[64,512]{1,0:T(8,128)(2,1)S(1)} %share_probe.1.refs_0_), channel_id=1, source_target_pairs={{0,16},{4,20},{8,24},{12,28},{16,0},{20,4},{24,8},{28,12},{1,17},{... | collective-permute-start | bytes 196616 | tf_op jit(solution)/shard_map/ppermute | solution.py:22
  6.8 0.0 collective-permute-start.5
  6.9 1.7 %collective-permute-start = (bf16[64,512]{1,0:T(8,128)(2,1)S(1)}, bf16[64,512]{1,0:T(8,128)(2,1)S(1)}, u32[]{:S(2)}, u32[]{:S(2)}) collective-permute-start(bf16[64,512]{1,0:T(8,128)(2,1)S(1)} %share_probe.1.refs_0_), channel_id=1, source_target_pairs={{0,4},{4,0},{8,12},{12,8},{16,20},{20,16},{24,28},{28,24},{1,5},{5... | collective-permute-start | bytes 196616 | tf_op jit(solution)/shard_map/ppermute | solution.py:22
  9.2 0.7 %select_bitcast_fusion.weight = f32[8,128]{1,0:T(8,128)S(1)} fusion(f32[1024]{0:T(1024)} %param.7, s32[]{:T(128)} %bitcast.7, s32[]{:T(128)S(6)} %mul.6), kind=kLoop, calls=%fused_computation.7 | loop fusion | flops 3072 | bytes 8200 | tf_op jit(solution)/shard_map/reshape | solution.py:174
  9.9 0.0 collective-permute-done.1.refs_2_
  9.9 0.4 collective-permute-start.2
  10.3 1.2 %collective-permute-done.3.refs_4_ = bf16[64,512]{1,0:T(8,128)(2,1)S(1)} collective-permute-done((bf16[64,512]{1,0:T(8,128)(2,1)S(1)}, bf16[64,512]{1,0:T(8,128)(2,1)S(1)}, u32[]{:S(2)}, u32[]{:S(2)}) %collective-permute-start.3) | collective-permute-done | bytes 65568 | tf_op jit(solution)/shard_map/ppermute | solution.py:22
  11.5 1.5 %collective-permute-start.4 = (bf16[64,512]{1,0:T(8,128)(2,1)S(1)}, bf16[64,512]{1,0:T(8,128)(2,1)S(1)}, u32[]{:S(2)}, u32[]{:S(2)}) collective-permute-start(bf16[64,512]{1,0:T(8,128)(2,1)S(1)} %collective-permute-done.3.refs_4_), channel_id=1, source_target_pairs={{0,4},{4,0},{8,12},{12,8},{16,20},{20,16},{24,28},{28,24},{1,5},{5... | collective-permute-start | bytes 196616 | tf_op jit(solution)/shard_map/ppermute | solution.py:22
  13.0 0.0 collective-permute-done.5.refs_6_
  13.0 1.4 %collective-permute-start.6 = (bf16[64,512]{1,0:T(8,128)(2,1)S(1)}, bf16[64,512]{1,0:T(8,128)(2,1)S(1)}, u32[]{:S(2)}, u32[]{:S(2)}) collective-permute-start(bf16[64,512]{1,0:T(8,128)(2,1)S(1)} %collective-permute-done.5.refs_6_), channel_id=1, source_target_pairs={{0,4},{4,0},{8,12},{12,8},{16,20},{20,16},{24,28},{28,24},{1,5},{5... | collective-permute-start | bytes 196616 | tf_op jit(solution)/shard_map/ppermute | solution.py:22
  14.4 0.7 %pad_add_fusion.info = s32[24]{0:T(128)S(1)} fusion(s32[16]{0:T(128)} %param.10, s32[8]{0:T(128)S(1)} %dynamic-slice_bitcast_fusion), kind=kLoop, calls=%fused_computation.9 | loop fusion | flops 24 | bytes 192 | tf_op jit(solution)/shard_map/concatenate | solution.py:149
  15.1 0.0 collective-permute-done.refs_1_
  15.1 0.0 collective-permute-done.2.refs_3_
  15.2 0.6 %collective-permute-done.4.refs_5_ = bf16[64,512]{1,0:T(8,128)(2,1)S(1)} collective-permute-done((bf16[64,512]{1,0:T(8,128)(2,1)S(1)}, bf16[64,512]{1,0:T(8,128)(2,1)S(1)}, u32[]{:S(2)}, u32[]{:S(2)}) %collective-permute-start.4) | collective-permute-done | bytes 65568 | tf_op jit(solution)/shard_map/ppermute | solution.py:22
  15.8 1.5 %collective-permute-done.6.refs_7_ = bf16[64,512]{1,0:T(8,128)(2,1)S(1)} collective-permute-done((bf16[64,512]{1,0:T(8,128)(2,1)S(1)}, bf16[64,512]{1,0:T(8,128)(2,1)S(1)}, u32[]{:S(2)}, u32[]{:S(2)}) %collective-permute-start.6) | collective-permute-done | bytes 65568 | tf_op jit(solution)/shard_map/ppermute | solution.py:22
  17.3 0.8 %pick_listed.1.after.refs_0_ = bf16[8,64,256]{2,1,0:T(8,128)(2,1)S(1)} custom-call(s32[24]{0:T(128)S(1)} %pad_add_fusion.info, bf16[64,512]{1,0:T(8,128)(2,1)S(1)} %share_probe.1.refs_0_, bf16[64,512]{1,0:T(8,128)(2,1)S(1)} %collective-permute-done.refs_1_, bf16[64,512]{1,0:T(8,128)(2,1)S(1)} %collective-permute-done.1.refs_2_, ...), custom_call_target="tpu_custom_call" | custom-call | tf_op jit(solution)/shard_map/pick_listed/pallas_call | solution.py:176
  18.1 1.6 %collective-permute-start.8 = (bf16[8,64,256]{2,1,0:T(8,128)(2,1)S(1)}, bf16[8,64,256]{2,1,0:T(8,128)(2,1)S(1)}, u32[]{:S(2)}, u32[]{:S(2)}) collective-permute-start(bf16[8,64,256]{2,1,0:T(8,128)(2,1)S(1)} %pick_listed.1.after.refs_0_), channel_id=1, source_target_pairs={{0,2},{1,3},{2,0},{3,1},{4,6},{5,7},{6,4},{7,5},{8,10},{9,11},{10,... | collective-permute-start | bytes 786440 | tf_op jit(solution)/shard_map/ppermute | solution.py:22
  19.7 2.2 %copy-done.1 = bf16[1024,2048]{1,0:T(8,128)(2,1)S(1)} copy-done((bf16[1024,2048]{1,0:T(8,128)(2,1)S(1)}, bf16[1024,2048]{1,0:T(8,128)(2,1)}, u32[]{:S(2)}) %copy-start.1) | copy-done | bytes 4194328
  21.9 0.7 %weigh.1.weighted = bf16[1024,2048]{1,0:T(8,128)(2,1)S(1)} custom-call(f32[8,128]{1,0:T(8,128)S(1)} %select_bitcast_fusion.weight, bf16[1024,2048]{1,0:T(8,128)(2,1)S(1)} %copy-done.1, bf16[8,64,256]{2,1,0:T(8,128)(2,1)S(1)} %pick_listed.1.after.refs_0_), custom_call_target="tpu_custom_call" | custom-call | flops 4194304 | bytes 8388608 | tf_op jit(solution)/shard_map/weigh/pallas_call | solution.py:177
  22.6 1.9 %collective-permute-done.8.refs_0_ = bf16[8,64,256]{2,1,0:T(8,128)(2,1)S(1)} collective-permute-done((bf16[8,64,256]{2,1,0:T(8,128)(2,1)S(1)}, bf16[8,64,256]{2,1,0:T(8,128)(2,1)S(1)}, u32[]{:S(2)}, u32[]{:S(2)}) %collective-permute-start.8) | collective-permute-done | bytes 262176 | tf_op jit(solution)/shard_map/ppermute | solution.py:22
  24.5 0.0 collective-permute-start.9
  24.5 1.5 %collective-permute-done.9.refs_1_ = bf16[8,64,256]{2,1,0:T(8,128)(2,1)S(1)} collective-permute-done((bf16[8,64,256]{2,1,0:T(8,128)(2,1)S(1)}, bf16[8,64,256]{2,1,0:T(8,128)(2,1)S(1)}, u32[]{:S(2)}, u32[]{:S(2)}) %collective-permute-start.9) | collective-permute-done | bytes 262176 | tf_op jit(solution)/shard_map/ppermute | solution.py:22
  26.1 2.1 %far_product.1 = (f32[64,2048]{1,0:T(8,128)S(1)}, bf16[64,2048]{1,0:T(8,128)(2,1)S(1)}) custom-call(bf16[1024,2048]{1,0:T(8,128)(2,1)S(1)} %copy-done.2, bf16[1024,2048]{1,0:T(8,128)(2,1)S(1)} %weigh.1.weighted, bf16[8,64,256]{2,1,0:T(8,128)(2,1)S(1)} %collective-permute-done.8.refs_0_, bf16[8,64,256]{2,1,0:T(8,128)(2,1)S(1)} %collective-permute-done.9.refs_1_), custom_call_target="tpu_custom_call" | custom-call | flops 1073741824 | bytes 8388608 | tf_op jit(solution)/shard_map/far_product/pallas_call | solution.py:189
  28.1 0.2 collective-permute-start.10
  28.3 0.4 collective-permute-start.7
  28.7 1.0 %collective-permute-done.10 = bf16[64,2048]{1,0:T(8,128)(2,1)S(1)} collective-permute-done((bf16[64,2048]{1,0:T(8,128)(2,1)S(1)}, bf16[64,2048]{1,0:T(8,128)(2,1)S(1)}, u32[]{:S(2)}, u32[]{:S(2)}) %collective-permute-start.10) | collective-permute-done | bytes 262176 | tf_op jit(solution)/shard_map/ppermute | solution.py:22
  29.8 1.6 %collective-permute-start.11 = (bf16[64,2048]{1,0:T(8,128)(2,1)S(1)}, bf16[64,2048]{1,0:T(8,128)(2,1)S(1)}, u32[]{:S(2)}, u32[]{:S(2)}) collective-permute-start(bf16[64,2048]{1,0:T(8,128)(2,1)S(1)} %add_convert_fusion), channel_id=1, source_target_pairs={{0,2},{1,3},{2,0},{3,1},{4,6},{5,7},{6,4},{7,5},{8,10},{9,11},{10,... | collective-permute-start | bytes 786440 | tf_op jit(solution)/shard_map/ppermute | solution.py:22
  31.4 0.0 collective-permute-done.7.refs_1_
  31.4 2.1 %near_product.1 = (f32[64,2048]{1,0:T(8,128)S(1)}, bf16[64,2048]{1,0:T(8,128)(2,1)S(1)}) custom-call(bf16[1024,2048]{1,0:T(8,128)(2,1)S(1)} %copy-done.2, bf16[1024,2048]{1,0:T(8,128)(2,1)S(1)} %weigh.1.weighted, bf16[8,64,256]{2,1,0:T(8,128)(2,1)S(1)} %pick_listed.1.after.refs_0_, bf16[8,64,256]{2,1,0:T(8,128)(2,1)S(1)} %collective-permute-done.7.refs_1_), custom_call_target="tpu_custom_call" | custom-call | flops 1073741824 | bytes 8388608 | tf_op jit(solution)/shard_map/near_product/pallas_call | solution.py:189
  33.5 0.1 collective-permute-start.12
  33.5 4.7 %collective-permute-done.11 = bf16[64,2048]{1,0:T(8,128)(2,1)S(1)} collective-permute-done((bf16[64,2048]{1,0:T(8,128)(2,1)S(1)}, bf16[64,2048]{1,0:T(8,128)(2,1)S(1)}, u32[]{:S(2)}, u32[]{:S(2)}) %collective-permute-start.11) | collective-permute-done | bytes 262176 | tf_op jit(solution)/shard_map/ppermute | solution.py:22
  38.3 0.7 %place.1 = (f32[64,512]{1,0:T(8,128)S(1)}, bf16[64,512]{1,0:T(8,128)(2,1)S(1)}, bf16[64,512]{1,0:T(8,128)(2,1)S(1)}, bf16[64,512]{1,0:T(8,128)(2,1)S(1)}, f32[64...) custom-call(s32[24]{0:T(128)S(1)} %pad_add_fusion.info, ...), custom_call_target="tpu_custom_call" | custom-call | tf_op jit(solution)/shard_map/place/pallas_call | solution.py:219
  39.0 1.5 %collective-permute-start.15 = (bf16[64,512]{1,0:T(8,128)(2,1)S(1)}, bf16[64,512]{1,0:T(8,128)(2,1)S(1)}, u32[]{:S(2)}, u32[]{:S(2)}) collective-permute-start(bf16[64,512]{1,0:T(8,128)(2,1)S(1)} %get-tuple-element.34), channel_id=1, source_target_pairs={{0,4},{4,0},{8,12},{12,8},{16,20},{20,16},{24,28},{28,24},{1,5},{5... | collective-permute-start | bytes 196616 | tf_op jit(solution)/shard_map/ppermute | solution.py:22
  40.5 0.6 %collective-permute-start.17 = (bf16[64,512]{1,0:T(8,128)(2,1)S(1)}, bf16[64,512]{1,0:T(8,128)(2,1)S(1)}, u32[]{:S(2)}, u32[]{:S(2)}) collective-permute-start(bf16[64,512]{1,0:T(8,128)(2,1)S(1)} %get-tuple-element.36), channel_id=1, source_target_pairs={{0,4},{4,0},{8,12},{12,8},{16,20},{20,16},{24,28},{28,24},{1,5},{5... | collective-permute-start | bytes 196616 | tf_op jit(solution)/shard_map/ppermute | solution.py:22
  41.1 1.4 %collective-permute-start.13 = (bf16[64,512]{1,0:T(8,128)(2,1)S(1)}, bf16[64,512]{1,0:T(8,128)(2,1)S(1)}, u32[]{:S(2)}, u32[]{:S(2)}) collective-permute-start(bf16[64,512]{1,0:T(8,128)(2,1)S(1)} %get-tuple-element.31), channel_id=1, source_target_pairs={{0,4},{4,0},{8,12},{12,8},{16,20},{20,16},{24,28},{28,24},{1,5},{5... | collective-permute-start | bytes 196616 | tf_op jit(solution)/shard_map/ppermute | solution.py:22
  42.5 0.0 collective-permute-start.14
  42.5 1.5 %collective-permute-done.15 = bf16[64,512]{1,0:T(8,128)(2,1)S(1)} collective-permute-done((bf16[64,512]{1,0:T(8,128)(2,1)S(1)}, bf16[64,512]{1,0:T(8,128)(2,1)S(1)}, u32[]{:S(2)}, u32[]{:S(2)}) %collective-permute-start.15) | collective-permute-done | bytes 65568 | tf_op jit(solution)/shard_map/ppermute | solution.py:22
  44.0 3.1 %collective-permute-start.16 = (bf16[64,512]{1,0:T(8,128)(2,1)S(1)}, bf16[64,512]{1,0:T(8,128)(2,1)S(1)}, u32[]{:S(2)}, u32[]{:S(2)}) collective-permute-start(bf16[64,512]{1,0:T(8,128)(2,1)S(1)} %add_convert_fusion.3), channel_id=1, source_target_pairs={{0,24},{4,28},{8,16},{12,20},{16,8},{20,12},{24,0},{28,4},{1,25},{... | collective-permute-start | bytes 196616 | tf_op jit(solution)/shard_map/ppermute | solution.py:22
  47.1 0.0 collective-permute-done.17
  47.1 0.1 collective-permute-start.18
  47.2 2.0 %collective-permute-start.19 = (bf16[64,512]{1,0:T(8,128)(2,1)S(1)}, bf16[64,512]{1,0:T(8,128)(2,1)S(1)}, u32[]{:S(2)}, u32[]{:S(2)}) collective-permute-start(bf16[64,512]{1,0:T(8,128)(2,1)S(1)} %get-tuple-element.38), channel_id=1, source_target_pairs={{0,12},{4,8},{8,4},{12,0},{16,28},{20,24},{24,20},{28,16},{1,13},{... | collective-permute-start | bytes 196616 | tf_op jit(solution)/shard_map/ppermute | solution.py:22
  49.3 1.5 %collective-permute-done.16 = bf16[64,512]{1,0:T(8,128)(2,1)S(1)} collective-permute-done((bf16[64,512]{1,0:T(8,128)(2,1)S(1)}, bf16[64,512]{1,0:T(8,128)(2,1)S(1)}, u32[]{:S(2)}, u32[]{:S(2)}) %collective-permute-start.16) | collective-permute-done | bytes 65568 | tf_op jit(solution)/shard_map/ppermute | solution.py:22
  50.8 1.7 %collective-permute-done.18 = bf16[64,512]{1,0:T(8,128)(2,1)S(1)} collective-permute-done((bf16[64,512]{1,0:T(8,128)(2,1)S(1)}, bf16[64,512]{1,0:T(8,128)(2,1)S(1)}, u32[]{:S(2)}, u32[]{:S(2)}) %collective-permute-start.18) | collective-permute-done | bytes 65568 | tf_op jit(solution)/shard_map/ppermute | solution.py:22
  52.5 0.6 %collective-permute-done.19 = bf16[64,512]{1,0:T(8,128)(2,1)S(1)} collective-permute-done((bf16[64,512]{1,0:T(8,128)(2,1)S(1)}, bf16[64,512]{1,0:T(8,128)(2,1)S(1)}, u32[]{:S(2)}, u32[]{:S(2)}) %collective-permute-start.19) | collective-permute-done | bytes 65568 | tf_op jit(solution)/shard_map/ppermute | solution.py:22
  53.1 0.6 %fusion = bf16[512,64]{0,1:T(8,128)(2,1)} fusion(f32[64,512]{1,0:T(8,128)S(1)} %convert_add_fusion.1, bf16[64,512]{1,0:T(8,128)(2,1)S(1)} %collective-permute-done.19), kind=kLoop, calls=%fused_computation.6 | loop fusion | flops 98304 | bytes 262144 | tf_op jit(solution)/shard_map/convert_element_type | solution.py:224
  (15 shorter events, 0.2 us)
Async XLA Ops:
  0.0 9.9 %copy-start = (s32[8,8]{1,0:T(8,128)S(1)}, s32[8,8]{1,0:T(8,128)}, u32[]{:S(2)}) copy-start(s32[8,8]{1,0:T(8,128)} %param.9) | copy-start | bytes 772
  0.0 1.0 %copy-start.3 = (bf16[512,256]{1,0:T(8,128)(2,1)S(1)}, bf16[512,256]{1,0:T(8,128)(2,1)}, u32[]{:S(2)}) copy-start(bf16[512,256]{1,0:T(8,128)(2,1)} %probe.1) | copy-start | bytes 786436
  1.2 8.8 %collective-permute-start.1 = (bf16[64,512]{1,0:T(8,128)(2,1)S(1)}, bf16[64,512]{1,0:T(8,128)(2,1)S(1)}, u32[]{:S(2)}, u32[]{:S(2)}) collective-permute-start(bf16[64,512]{1,0:T(8,128)(2,1)S(1)} %share_probe.1.refs_0_), channel_id=1, source_target_pairs={{0,8},{4,12},{8,0},{12,4},{16,24},{20,28},{24,16},{28,20},{1,9},{5... | collective-permute-start | bytes 196616 | tf_op jit(solution)/shard_map/ppermute | solution.py:22
  4.3 7.3 %collective-permute-start.3 = (bf16[64,512]{1,0:T(8,128)(2,1)S(1)}, bf16[64,512]{1,0:T(8,128)(2,1)S(1)}, u32[]{:S(2)}, u32[]{:S(2)}) collective-permute-start(bf16[64,512]{1,0:T(8,128)(2,1)S(1)} %share_probe.1.refs_0_), channel_id=1, source_target_pairs={{0,16},{4,20},{8,24},{12,28},{16,0},{20,4},{24,8},{28,12},{1,17},{... | collective-permute-start | bytes 196616 | tf_op jit(solution)/shard_map/ppermute | solution.py:22
  6.8 6.2 %collective-permute-start.5 = (bf16[64,512]{1,0:T(8,128)(2,1)S(1)}, bf16[64,512]{1,0:T(8,128)(2,1)S(1)}, u32[]{:S(2)}, u32[]{:S(2)}) collective-permute-start(bf16[64,512]{1,0:T(8,128)(2,1)S(1)} %share_probe.1.refs_0_), channel_id=1, source_target_pairs={{0,24},{4,28},{8,16},{12,20},{16,8},{20,12},{24,0},{28,4},{1,25},{... | collective-permute-start | bytes 196616 | tf_op jit(solution)/shard_map/ppermute | solution.py:22
  6.9 8.3 %collective-permute-start = (bf16[64,512]{1,0:T(8,128)(2,1)S(1)}, bf16[64,512]{1,0:T(8,128)(2,1)S(1)}, u32[]{:S(2)}, u32[]{:S(2)}) collective-permute-start(bf16[64,512]{1,0:T(8,128)(2,1)S(1)} %share_probe.1.refs_0_), channel_id=1, source_target_pairs={{0,4},{4,0},{8,12},{12,8},{16,20},{20,16},{24,28},{28,24},{1,5},{5... | collective-permute-start | bytes 196616 | tf_op jit(solution)/shard_map/ppermute | solution.py:22
  9.9 5.2 %collective-permute-start.2 = (bf16[64,512]{1,0:T(8,128)(2,1)S(1)}, bf16[64,512]{1,0:T(8,128)(2,1)S(1)}, u32[]{:S(2)}, u32[]{:S(2)}) collective-permute-start(bf16[64,512]{1,0:T(8,128)(2,1)S(1)} %collective-permute-done.1.refs_2_), channel_id=1, source_target_pairs={{0,4},{4,0},{8,12},{12,8},{16,20},{20,16},{24,28},{28,24},{1,5},{5... | collective-permute-start | bytes 196616 | tf_op jit(solution)/shard_map/ppermute | solution.py:22
  11.5 4.3 %collective-permute-start.4 = (bf16[64,512]{1,0:T(8,128)(2,1)S(1)}, bf16[64,512]{1,0:T(8,128)(2,1)S(1)}, u32[]{:S(2)}, u32[]{:S(2)}) collective-permute-start(bf16[64,512]{1,0:T(8,128)(2,1)S(1)} %collective-permute-done.3.refs_4_), channel_id=1, source_target_pairs={{0,4},{4,0},{8,12},{12,8},{16,20},{20,16},{24,28},{28,24},{1,5},{5... | collective-permute-start | bytes 196616 | tf_op jit(solution)/shard_map/ppermute | solution.py:22
  13.0 4.3 %collective-permute-start.6 = (bf16[64,512]{1,0:T(8,128)(2,1)S(1)}, bf16[64,512]{1,0:T(8,128)(2,1)S(1)}, u32[]{:S(2)}, u32[]{:S(2)}) collective-permute-start(bf16[64,512]{1,0:T(8,128)(2,1)S(1)} %collective-permute-done.5.refs_6_), channel_id=1, source_target_pairs={{0,4},{4,0},{8,12},{12,8},{16,20},{20,16},{24,28},{28,24},{1,5},{5... | collective-permute-start | bytes 196616 | tf_op jit(solution)/shard_map/ppermute | solution.py:22
  18.1 6.4 %collective-permute-start.8 = (bf16[8,64,256]{2,1,0:T(8,128)(2,1)S(1)}, bf16[8,64,256]{2,1,0:T(8,128)(2,1)S(1)}, u32[]{:S(2)}, u32[]{:S(2)}) collective-permute-start(bf16[8,64,256]{2,1,0:T(8,128)(2,1)S(1)} %pick_listed.1.after.refs_0_), channel_id=1, source_target_pairs={{0,2},{1,3},{2,0},{3,1},{4,6},{5,7},{6,4},{7,5},{8,10},{9,11},{10,... | collective-permute-start | bytes 786440 | tf_op jit(solution)/shard_map/ppermute | solution.py:22
  19.7 2.2 %copy-start.1 = (bf16[1024,2048]{1,0:T(8,128)(2,1)S(1)}, bf16[1024,2048]{1,0:T(8,128)(2,1)}, u32[]{:S(2)}) copy-start(bf16[1024,2048]{1,0:T(8,128)(2,1)} %held.3) | copy-start | bytes 12582916
  21.9 4.2 %copy-start.2 = (bf16[1024,2048]{1,0:T(8,128)(2,1)S(1)}, bf16[1024,2048]{1,0:T(8,128)(2,1)}, u32[]{:S(2)}) copy-start(bf16[1024,2048]{1,0:T(8,128)(2,1)} %held.3) | copy-start | bytes 12582916
  24.5 1.5 %collective-permute-start.9 = (bf16[8,64,256]{2,1,0:T(8,128)(2,1)S(1)}, bf16[8,64,256]{2,1,0:T(8,128)(2,1)S(1)}, u32[]{:S(2)}, u32[]{:S(2)}) collective-permute-start(bf16[8,64,256]{2,1,0:T(8,128)(2,1)S(1)} %collective-permute-done.8.refs_0_), channel_id=1, source_target_pairs={{0,1},{1,0},{2,3},{3,2},{4,5},{5,4},{6,7},{7,6},{8,9},{9,8},{10,11... | collective-permute-start | bytes 786440 | tf_op jit(solution)/shard_map/ppermute | solution.py:22
  28.1 1.6 %collective-permute-start.10 = (bf16[64,2048]{1,0:T(8,128)(2,1)S(1)}, bf16[64,2048]{1,0:T(8,128)(2,1)S(1)}, u32[]{:S(2)}, u32[]{:S(2)}) collective-permute-start(bf16[64,2048]{1,0:T(8,128)(2,1)S(1)} %get-tuple-element.26), channel_id=1, source_target_pairs={{0,1},{1,0},{2,3},{3,2},{4,5},{5,4},{6,7},{7,6},{8,9},{9,8},{10,11... | collective-permute-start | bytes 786440 | tf_op jit(solution)/shard_map/ppermute | solution.py:22
  28.3 3.0 %collective-permute-start.7 = (bf16[8,64,256]{2,1,0:T(8,128)(2,1)S(1)}, bf16[8,64,256]{2,1,0:T(8,128)(2,1)S(1)}, u32[]{:S(2)}, u32[]{:S(2)}) collective-permute-start(bf16[8,64,256]{2,1,0:T(8,128)(2,1)S(1)} %pick_listed.1.after.refs_0_), channel_id=1, source_target_pairs={{0,1},{1,0},{2,3},{3,2},{4,5},{5,4},{6,7},{7,6},{8,9},{9,8},{10,11... | collective-permute-start | bytes 786440 | tf_op jit(solution)/shard_map/ppermute | solution.py:22
  29.8 8.4 %collective-permute-start.11 = (bf16[64,2048]{1,0:T(8,128)(2,1)S(1)}, bf16[64,2048]{1,0:T(8,128)(2,1)S(1)}, u32[]{:S(2)}, u32[]{:S(2)}) collective-permute-start(bf16[64,2048]{1,0:T(8,128)(2,1)S(1)} %add_convert_fusion), channel_id=1, source_target_pairs={{0,2},{1,3},{2,0},{3,1},{4,6},{5,7},{6,4},{7,5},{8,10},{9,11},{10,... | collective-permute-start | bytes 786440 | tf_op jit(solution)/shard_map/ppermute | solution.py:22
  33.5 4.8 %collective-permute-start.12 = (bf16[64,2048]{1,0:T(8,128)(2,1)S(1)}, bf16[64,2048]{1,0:T(8,128)(2,1)S(1)}, u32[]{:S(2)}, u32[]{:S(2)}) collective-permute-start(bf16[64,2048]{1,0:T(8,128)(2,1)S(1)} %get-tuple-element.29), channel_id=1, source_target_pairs={{0,1},{1,0},{2,3},{3,2},{4,5},{5,4},{6,7},{7,6},{8,9},{9,8},{10,11... | collective-permute-start | bytes 786440 | tf_op jit(solution)/shard_map/ppermute | solution.py:22
  39.0 5.0 %collective-permute-start.15 = (bf16[64,512]{1,0:T(8,128)(2,1)S(1)}, bf16[64,512]{1,0:T(8,128)(2,1)S(1)}, u32[]{:S(2)}, u32[]{:S(2)}) collective-permute-start(bf16[64,512]{1,0:T(8,128)(2,1)S(1)} %get-tuple-element.34), channel_id=1, source_target_pairs={{0,4},{4,0},{8,12},{12,8},{16,20},{20,16},{24,28},{28,24},{1,5},{5... | collective-permute-start | bytes 196616 | tf_op jit(solution)/shard_map/ppermute | solution.py:22
  40.5 6.6 %collective-permute-start.17 = (bf16[64,512]{1,0:T(8,128)(2,1)S(1)}, bf16[64,512]{1,0:T(8,128)(2,1)S(1)}, u32[]{:S(2)}, u32[]{:S(2)}) collective-permute-start(bf16[64,512]{1,0:T(8,128)(2,1)S(1)} %get-tuple-element.36), channel_id=1, source_target_pairs={{0,4},{4,0},{8,12},{12,8},{16,20},{20,16},{24,28},{28,24},{1,5},{5... | collective-permute-start | bytes 196616 | tf_op jit(solution)/shard_map/ppermute | solution.py:22
  41.1 8.2 %collective-permute-start.13 = (bf16[64,512]{1,0:T(8,128)(2,1)S(1)}, bf16[64,512]{1,0:T(8,128)(2,1)S(1)}, u32[]{:S(2)}, u32[]{:S(2)}) collective-permute-start(bf16[64,512]{1,0:T(8,128)(2,1)S(1)} %get-tuple-element.31), channel_id=1, source_target_pairs={{0,4},{4,0},{8,12},{12,8},{16,20},{20,16},{24,28},{28,24},{1,5},{5... | collective-permute-start | bytes 196616 | tf_op jit(solution)/shard_map/ppermute | solution.py:22
  42.5 6.8 %collective-permute-start.14 = (bf16[64,512]{1,0:T(8,128)(2,1)S(1)}, bf16[64,512]{1,0:T(8,128)(2,1)S(1)}, u32[]{:S(2)}, u32[]{:S(2)}) collective-permute-start(bf16[64,512]{1,0:T(8,128)(2,1)S(1)} %get-tuple-element.32), channel_id=1, source_target_pairs={{0,8},{4,12},{8,0},{12,4},{16,24},{20,28},{24,16},{28,20},{1,9},{5... | collective-permute-start | bytes 196616 | tf_op jit(solution)/shard_map/ppermute | solution.py:22
  44.0 6.8 %collective-permute-start.16 = (bf16[64,512]{1,0:T(8,128)(2,1)S(1)}, bf16[64,512]{1,0:T(8,128)(2,1)S(1)}, u32[]{:S(2)}, u32[]{:S(2)}) collective-permute-start(bf16[64,512]{1,0:T(8,128)(2,1)S(1)} %add_convert_fusion.3), channel_id=1, source_target_pairs={{0,24},{4,28},{8,16},{12,20},{16,8},{20,12},{24,0},{28,4},{1,25},{... | collective-permute-start | bytes 196616 | tf_op jit(solution)/shard_map/ppermute | solution.py:22
  47.1 5.3 %collective-permute-start.18 = (bf16[64,512]{1,0:T(8,128)(2,1)S(1)}, bf16[64,512]{1,0:T(8,128)(2,1)S(1)}, u32[]{:S(2)}, u32[]{:S(2)}) collective-permute-start(bf16[64,512]{1,0:T(8,128)(2,1)S(1)} %add_convert_fusion.2), channel_id=1, source_target_pairs={{0,16},{4,20},{8,24},{12,28},{16,0},{20,4},{24,8},{28,12},{1,17},{... | collective-permute-start | bytes 196616 | tf_op jit(solution)/shard_map/ppermute | solution.py:22
  47.2 5.9 %collective-permute-start.19 = (bf16[64,512]{1,0:T(8,128)(2,1)S(1)}, bf16[64,512]{1,0:T(8,128)(2,1)S(1)}, u32[]{:S(2)}, u32[]{:S(2)}) collective-permute-start(bf16[64,512]{1,0:T(8,128)(2,1)S(1)} %get-tuple-element.38), channel_id=1, source_target_pairs={{0,12},{4,8},{8,4},{12,0},{16,28},{20,24},{24,20},{28,16},{1,13},{... | collective-permute-start | bytes 196616 | tf_op jit(solution)/shard_map/ppermute | solution.py:22

commit v10 on v9

--- a/solution.py
+++ b/solution.py
@@ -106,6 +106,20 @@
         product = jnp.dot(image, weighted[:, n:n + COLUMNS], preferred_element_type=jnp.float32)
         for j, out in enumerate(outs):
             out[:, n:n + COLUMNS] = product[j * high:(j + 1) * high, :].astype(out.dtype)
+
+
+def merge_kernel(term, passed, held, weighted, own, beside, both, first, second, probe):
+    both[...] = (term[...] + passed[...].astype(jnp.float32)).astype(both.dtype)
+
+    @pl.when(lax.axis_index("sub") % 2 == 1)
+    def _():
+        product_kernel(held, weighted, own, beside, first, second, probe)
+
+
+def near_kernel(_, __, held, weighted, own, beside, first, second, probe):
+    @pl.when(lax.axis_index("sub") % 2 == 0)
+    def _():
+        product_kernel(held, weighted, own, beside, first, second, probe)
 
 
 def place_kernel(unit, tile, listed, parts_count, info, *refs):
@@ -209,12 +223,37 @@
     )
 
     columns = spread(picked, "sub", subs, SPREAD_DIRECT, (weighted,))
-    terms = {}
-    if subs > 2:
-        terms = dict(enumerate(product("far_product", range(2, subs), columns[2:]), 2))
-    far, ready = collect_far(terms, "sub", subs, SUB_DIRECT)
-    near = product("near_product", range(2), [columns[0], after(columns[1], *ready)])
-    first, _ = collect_near(near, "sub", subs, SUB_DIRECT, ready)
+    terms = dict(enumerate(product("far_product", range(2, subs), columns[2:]), 2))
+    far = []
+    for step in range(subs - 2, 2, -2):
+        passed = swap(terms[step + 1], "sub", subs, 1)
+        both = (terms[step] + passed.astype(jnp.float32)).astype(jnp.bfloat16)
+        far.append(swap(both, "sub", subs, step))
+    near_shapes = [jax.ShapeDtypeStruct((high, width), kept(j, SUB_DIRECT)) for j in range(2)]
+    near_probe = [pltpu.VMEM((2 * high, width), jnp.bfloat16)]
+    near_cost = pl.CostEstimate(flops=8 * rows * width * high, bytes_accessed=4 * rows * width, transcendentals=0)
+    both, *near = pl.pallas_call(
+        merge_kernel,
+        out_shape=[jax.ShapeDtypeStruct((high, width), jnp.bfloat16)] + near_shapes,
+        in_specs=[VMEM] * 6,
+        out_specs=[VMEM] * 3,
+        scratch_shapes=near_probe,
+        compiler_params=params(24),
+        name="merge",
+    )(terms[2], swap(terms[3], "sub", subs, 1), jacobian, weighted, *columns[:2])
+    far.append(swap(both, "sub", subs, 2))
+    near = pl.pallas_call(
+        near_kernel,
+        out_shape=near_shapes,
+        in_specs=[VMEM] * 6,
+        out_specs=[VMEM] * 2,
+        scratch_shapes=near_probe,
+        input_output_aliases={0: 0, 1: 1},
+        compiler_params=params(24),
+        cost_estimate=near_cost,
+        name="near_product",
+    )(*near, jacobian, weighted, *columns[:2])
+    first, _ = collect_near(near, "sub", subs, SUB_DIRECT, ())
     partial = sum((term.astype(jnp.float32) for term in far), first[0])
     terms = place(info, partial, first[1])
     far, ready = collect_far(terms, "obs", obs_count, OBS_DIRECT)

time: 54 us -> 55.4 us (1.026)
  waiting for transfers between devices: 17.8 us -> 21.2 us
  starting transfers between devices: 23.2 us -> 21.2 us
    ppermute x20, waiting for transfers between devices: 17.8 us -> 21.2 us  [swap(): return lax.ppermute(value, axis, [(i, i ^ step) for i in range(count)])]
    pallas_call x0 -> x2, Pallas kernels: none -> 2.11 us  [the longest x1 2.06 us: local(): pl.pallas_call(near_kernel, out_shape=near_shapes, in_specs=[VMEM] * 6, o...]
    pallas_call x2 -> x1, Pallas kernels: 4.12 us -> 2.06 us  [product(): pl.pallas_call(product_kernel, out_shape=[jax.ShapeDtypeStruct((high, wid...]
    ppermute x20, starting transfers between devices: 23.2 us -> 21.2 us  [swap(): return lax.ppermute(value, axis, [(i, i ^ step) for i in range(count)])]
  transfers between devices with their start and end apart: 20 -> 20, of which waited for: 11 -> 12; matrix products, arithmetic and copies ran while one was open for 3% -> 3% of each run, Pallas kernels for 5% -> 9%
where the time goes in v10:
time: 55.4 us; the launch traced here: 55.2 us
  starting transfers between devices  21.2 us (38%)
  waiting for transfers between devices  21.2 us (38%)
  Pallas kernels  6.65 us (12%)
  local copies, waits for them, and re-layouts  3.16 us (6%)
  other arithmetic  2.18 us (4%)
  between operations  0.76 us (1%)
    ppermute x20, starting transfers between devices, swap(): return lax.ppermute(value, axis, [(i, i ^ step) for i in range(count)])  21.2 us
    ppermute x20, waiting for transfers between devices, swap(): return lax.ppermute(value, axis, [(i, i ^ step) for i in range(count)])  21.2 us
    unnamed x8, local copies, waits for them, and re-layouts  3.16 us
    pallas_call x1, Pallas kernels, local(): pl.pallas_call(near_kernel, out_shape=near_shapes, in_specs=[VMEM] * 6, o...  2.06 us
    pallas_call x1, Pallas kernels, product(): pl.pallas_call(product_kernel, out_shape=[jax.ShapeDtypeStruct((high, wid...  2.06 us
  transfers between devices with their start and end apart: 20, of which 12 were waited for; matrix products, arithmetic and copies ran while one was open for 3% of the time, Pallas kernels for 9%

profile of v10, /device:TPU:0, one launch (start us, length us, event | category | flops | bytes accessed | tf_op | source)
XLA Modules:
  0.0 55.2 jit_solution(5006499571753649559)
XLA Ops:
  0.0 1.0 %copy-done.3 = bf16[512,256]{1,0:T(8,128)(2,1)S(1)} copy-done((bf16[512,256]{1,0:T(8,128)(2,1)S(1)}, bf16[512,256]{1,0:T(8,128)(2,1)}, u32[]{:S(2)}) %copy-start.3) | copy-done | bytes 262168
  1.0 0.2 share_probe.1.refs_0_
  1.2 5.1 %collective-permute-start.5 = (bf16[64,512]{1,0:T(8,128)(2,1)S(1)}, bf16[64,512]{1,0:T(8,128)(2,1)S(1)}, u32[]{:S(2)}, u32[]{:S(2)}) collective-permute-start(bf16[64,512]{1,0:T(8,128)(2,1)S(1)} %share_probe.1.refs_0_), channel_id=1, source_target_pairs={{0,24},{4,28},{8,16},{12,20},{16,8},{20,12},{24,0},{28,4},{1,25},{... | collective-permute-start | bytes 196616 | tf_op jit(solution)/shard_map/ppermute | solution.py:22
  6.3 0.0 collective-permute-start.3
  6.3 0.6 %collective-permute-start.1 = (bf16[64,512]{1,0:T(8,128)(2,1)S(1)}, bf16[64,512]{1,0:T(8,128)(2,1)S(1)}, u32[]{:S(2)}, u32[]{:S(2)}) collective-permute-start(bf16[64,512]{1,0:T(8,128)(2,1)S(1)} %share_probe.1.refs_0_), channel_id=1, source_target_pairs={{0,8},{4,12},{8,0},{12,4},{16,24},{20,28},{24,16},{28,20},{1,9},{5... | collective-permute-start | bytes 196616 | tf_op jit(solution)/shard_map/ppermute | solution.py:22
  6.9 1.6 %collective-permute-start = (bf16[64,512]{1,0:T(8,128)(2,1)S(1)}, bf16[64,512]{1,0:T(8,128)(2,1)S(1)}, u32[]{:S(2)}, u32[]{:S(2)}) collective-permute-start(bf16[64,512]{1,0:T(8,128)(2,1)S(1)} %share_probe.1.refs_0_), channel_id=1, source_target_pairs={{0,4},{4,0},{8,12},{12,8},{16,20},{20,16},{24,28},{28,24},{1,5},{5... | collective-permute-start | bytes 196616 | tf_op jit(solution)/shard_map/ppermute | solution.py:22
  9.2 0.7 %select_bitcast_fusion.weight = f32[8,128]{1,0:T(8,128)S(1)} fusion(f32[1024]{0:T(1024)} %param.7, s32[]{:T(128)} %bitcast.7, s32[]{:T(128)S(6)} %mul.6), kind=kLoop, calls=%fused_computation.6 | loop fusion | flops 3072 | bytes 8200 | tf_op jit(solution)/shard_map/reshape | solution.py:188
  9.9 0.0 collective-permute-done.5.refs_6_
  9.9 0.8 %collective-permute-start.6 = (bf16[64,512]{1,0:T(8,128)(2,1)S(1)}, bf16[64,512]{1,0:T(8,128)(2,1)S(1)}, u32[]{:S(2)}, u32[]{:S(2)}) collective-permute-start(bf16[64,512]{1,0:T(8,128)(2,1)S(1)} %collective-permute-done.5.refs_6_), channel_id=1, source_target_pairs={{0,4},{4,0},{8,12},{12,8},{16,20},{20,16},{24,28},{28,24},{1,5},{5... | collective-permute-start | bytes 196616 | tf_op jit(solution)/shard_map/ppermute | solution.py:22
  10.7 1.2 %collective-permute-done.3.refs_4_ = bf16[64,512]{1,0:T(8,128)(2,1)S(1)} collective-permute-done((bf16[64,512]{1,0:T(8,128)(2,1)S(1)}, bf16[64,512]{1,0:T(8,128)(2,1)S(1)}, u32[]{:S(2)}, u32[]{:S(2)}) %collective-permute-start.3) | collective-permute-done | bytes 65568 | tf_op jit(solution)/shard_map/ppermute | solution.py:22
  11.9 1.5 %collective-permute-start.4 = (bf16[64,512]{1,0:T(8,128)(2,1)S(1)}, bf16[64,512]{1,0:T(8,128)(2,1)S(1)}, u32[]{:S(2)}, u32[]{:S(2)}) collective-permute-start(bf16[64,512]{1,0:T(8,128)(2,1)S(1)} %collective-permute-done.3.refs_4_), channel_id=1, source_target_pairs={{0,4},{4,0},{8,12},{12,8},{16,20},{20,16},{24,28},{28,24},{1,5},{5... | collective-permute-start | bytes 196616 | tf_op jit(solution)/shard_map/ppermute | solution.py:22
  13.4 0.0 collective-permute-done.1.refs_2_
  13.4 0.5 collective-permute-start.2
  13.9 0.7 %pad_add_fusion.info = s32[24]{0:T(128)S(1)} fusion(s32[16]{0:T(128)} %param.10, s32[8]{0:T(128)S(1)} %dynamic-slice_bitcast_fusion), kind=kLoop, calls=%fused_computation.8 | loop fusion | flops 24 | bytes 192 | tf_op jit(solution)/shard_map/concatenate | solution.py:163
  14.7 0.0 collective-permute-done.6.refs_7_
  14.7 2.1 %collective-permute-done.4.refs_5_ = bf16[64,512]{1,0:T(8,128)(2,1)S(1)} collective-permute-done((bf16[64,512]{1,0:T(8,128)(2,1)S(1)}, bf16[64,512]{1,0:T(8,128)(2,1)S(1)}, u32[]{:S(2)}, u32[]{:S(2)}) %collective-permute-start.4) | collective-permute-done | bytes 65568 | tf_op jit(solution)/shard_map/ppermute | solution.py:22
  16.8 0.9 %collective-permute-done.2.refs_3_ = bf16[64,512]{1,0:T(8,128)(2,1)S(1)} collective-permute-done((bf16[64,512]{1,0:T(8,128)(2,1)S(1)}, bf16[64,512]{1,0:T(8,128)(2,1)S(1)}, u32[]{:S(2)}, u32[]{:S(2)}) %collective-permute-start.2) | collective-permute-done | bytes 65568 | tf_op jit(solution)/shard_map/ppermute | solution.py:22
  17.6 0.8 %pick_listed.1.after.own = bf16[8,64,256]{2,1,0:T(8,128)(2,1)S(1)} custom-call(s32[24]{0:T(128)S(1)} %pad_add_fusion.info, bf16[64,512]{1,0:T(8,128)(2,1)S(1)} %share_probe.1.refs_0_, bf16[64,512]{1,0:T(8,128)(2,1)S(1)} %collective-permute-done.refs_1_, bf16[64,512]{1,0:T(8,128)(2,1)S(1)} %collective-permute-done.1.refs_2_, ...), custom_call_target="tpu_custom_call" | custom-call | tf_op jit(solution)/shard_map/pick_listed/pallas_call | solution.py:190
  18.5 1.6 %collective-permute-start.7 = (bf16[8,64,256]{2,1,0:T(8,128)(2,1)S(1)}, bf16[8,64,256]{2,1,0:T(8,128)(2,1)S(1)}, u32[]{:S(2)}, u32[]{:S(2)}) collective-permute-start(bf16[8,64,256]{2,1,0:T(8,128)(2,1)S(1)} %pick_listed.1.after.own), channel_id=1, source_target_pairs={{0,2},{1,3},{2,0},{3,1},{4,6},{5,7},{6,4},{7,5},{8,10},{9,11},{10,... | collective-permute-start | bytes 786440 | tf_op jit(solution)/shard_map/ppermute | solution.py:22
  20.1 2.2 %copy-done.1 = bf16[1024,2048]{1,0:T(8,128)(2,1)S(1)} copy-done((bf16[1024,2048]{1,0:T(8,128)(2,1)S(1)}, bf16[1024,2048]{1,0:T(8,128)(2,1)}, u32[]{:S(2)}) %copy-start.1) | copy-done | bytes 4194328
  22.2 0.7 %weigh.1.weighted = bf16[1024,2048]{1,0:T(8,128)(2,1)S(1)} custom-call(f32[8,128]{1,0:T(8,128)S(1)} %select_bitcast_fusion.weight, bf16[1024,2048]{1,0:T(8,128)(2,1)S(1)} %copy-done.1, bf16[8,64,256]{2,1,0:T(8,128)(2,1)S(1)} %pick_listed.1.after.own), custom_call_target="tpu_custom_call" | custom-call | flops 4194304 | bytes 8388608 | tf_op jit(solution)/shard_map/weigh/pallas_call | solution.py:191
  23.0 3.0 %collective-permute-done.7.refs_0_ = bf16[8,64,256]{2,1,0:T(8,128)(2,1)S(1)} collective-permute-done((bf16[8,64,256]{2,1,0:T(8,128)(2,1)S(1)}, bf16[8,64,256]{2,1,0:T(8,128)(2,1)S(1)}, u32[]{:S(2)}, u32[]{:S(2)}) %collective-permute-start.7) | collective-permute-done | bytes 262176 | tf_op jit(solution)/shard_map/ppermute | solution.py:22
  26.0 0.0 collective-permute-start.8
  26.0 0.5 collective-permute-start.10
  26.5 1.0 %collective-permute-done.8.refs_1_ = bf16[8,64,256]{2,1,0:T(8,128)(2,1)S(1)} collective-permute-done((bf16[8,64,256]{2,1,0:T(8,128)(2,1)S(1)}, bf16[8,64,256]{2,1,0:T(8,128)(2,1)S(1)}, u32[]{:S(2)}, u32[]{:S(2)}) %collective-permute-start.8) | collective-permute-done | bytes 262176 | tf_op jit(solution)/shard_map/ppermute | solution.py:22
  27.5 2.1 %far_product.1 = (f32[64,2048]{1,0:T(8,128)S(1)}, bf16[64,2048]{1,0:T(8,128)(2,1)S(1)}) custom-call(bf16[1024,2048]{1,0:T(8,128)(2,1)S(1)} %copy-done.2, bf16[1024,2048]{1,0:T(8,128)(2,1)S(1)} %weigh.1.weighted, bf16[8,64,256]{2,1,0:T(8,128)(2,1)S(1)} %collective-permute-done.7.refs_0_, bf16[8,64,256]{2,1,0:T(8,128)(2,1)S(1)} %collective-permute-done.8.refs_1_), custom_call_target="tpu_custom_call" | custom-call | flops 1073741824 | bytes 8388608 | tf_op jit(solution)/shard_map/far_product/pallas_call | solution.py:203
  29.6 0.2 collective-permute-start.9
  29.8 0.0 collective-permute-done.10.beside
  29.8 1.4 %collective-permute-done.9.passed = bf16[64,2048]{1,0:T(8,128)(2,1)S(1)} collective-permute-done((bf16[64,2048]{1,0:T(8,128)(2,1)S(1)}, bf16[64,2048]{1,0:T(8,128)(2,1)S(1)}, u32[]{:S(2)}, u32[]{:S(2)}) %collective-permute-start.9) | collective-permute-done | bytes 262176 | tf_op jit(solution)/shard_map/ppermute | solution.py:22
  31.2 1.6 %collective-permute-start.11 = (bf16[64,2048]{1,0:T(8,128)(2,1)S(1)}, bf16[64,2048]{1,0:T(8,128)(2,1)S(1)}, u32[]{:S(2)}, u32[]{:S(2)}) collective-permute-start(bf16[64,2048]{1,0:T(8,128)(2,1)S(1)} %get-tuple-element.32), channel_id=1, source_target_pairs={{0,2},{1,3},{2,0},{3,1},{4,6},{5,7},{6,4},{7,5},{8,10},{9,11},{10,... | collective-permute-start | bytes 786440 | tf_op jit(solution)/shard_map/ppermute | solution.py:22
  32.8 2.1 %near_product.1 = (f32[64,2048]{1,0:T(8,128)S(1)}, bf16[64,2048]{1,0:T(8,128)(2,1)S(1)}) custom-call(f32[64,2048]{1,0:T(8,128)S(1)} %get-tuple-element.29._, bf16[64,2048]{1,0:T(8,128)(2,1)S(1)} %get-tuple-element.30.__, bf16[1024,2048]{1,0:T(8,128)(2,1)S(1)} %copy-done.2, ...), custom_call_target="tpu_custom_call", output_to_operand_aliasing={{0}: (0, {}), {1}: (1, {})} | custom-call | flops 1073741824 | bytes 8388608 | tf_op jit(solution)/shard_map/near_product/pallas_call | solution.py:245
  34.9 0.1 collective-permute-start.12
  35.0 4.2 %collective-permute-done.11 = bf16[64,2048]{1,0:T(8,128)(2,1)S(1)} collective-permute-done((bf16[64,2048]{1,0:T(8,128)(2,1)S(1)}, bf16[64,2048]{1,0:T(8,128)(2,1)S(1)}, u32[]{:S(2)}, u32[]{:S(2)}) %collective-permute-start.11) | collective-permute-done | bytes 262176 | tf_op jit(solution)/shard_map/ppermute | solution.py:22
  39.3 0.0 collective-permute-done.12.refs_1_
  39.3 0.7 %place.1 = (f32[64,512]{1,0:T(8,128)S(1)}, bf16[64,512]{1,0:T(8,128)(2,1)S(1)}, bf16[64,512]{1,0:T(8,128)(2,1)S(1)}, bf16[64,512]{1,0:T(8,128)(2,1)S(1)}, f32[64...) custom-call(s32[24]{0:T(128)S(1)} %pad_add_fusion.info, ...), custom_call_target="tpu_custom_call" | custom-call | tf_op jit(solution)/shard_map/place/pallas_call | solution.py:258
  40.0 0.8 %collective-permute-start.15 = (bf16[64,512]{1,0:T(8,128)(2,1)S(1)}, bf16[64,512]{1,0:T(8,128)(2,1)S(1)}, u32[]{:S(2)}, u32[]{:S(2)}) collective-permute-start(bf16[64,512]{1,0:T(8,128)(2,1)S(1)} %get-tuple-element.38), channel_id=1, source_target_pairs={{0,4},{4,0},{8,12},{12,8},{16,20},{20,16},{24,28},{28,24},{1,5},{5... | collective-permute-start | bytes 196616 | tf_op jit(solution)/shard_map/ppermute | solution.py:22
  40.8 1.3 %collective-permute-start.13 = (bf16[64,512]{1,0:T(8,128)(2,1)S(1)}, bf16[64,512]{1,0:T(8,128)(2,1)S(1)}, u32[]{:S(2)}, u32[]{:S(2)}) collective-permute-start(bf16[64,512]{1,0:T(8,128)(2,1)S(1)} %get-tuple-element.35), channel_id=1, source_target_pairs={{0,4},{4,0},{8,12},{12,8},{16,20},{20,16},{24,28},{28,24},{1,5},{5... | collective-permute-start | bytes 196616 | tf_op jit(solution)/shard_map/ppermute | solution.py:22
  42.1 0.7 %collective-permute-start.17 = (bf16[64,512]{1,0:T(8,128)(2,1)S(1)}, bf16[64,512]{1,0:T(8,128)(2,1)S(1)}, u32[]{:S(2)}, u32[]{:S(2)}) collective-permute-start(bf16[64,512]{1,0:T(8,128)(2,1)S(1)} %get-tuple-element.40), channel_id=1, source_target_pairs={{0,4},{4,0},{8,12},{12,8},{16,20},{20,16},{24,28},{28,24},{1,5},{5... | collective-permute-start | bytes 196616 | tf_op jit(solution)/shard_map/ppermute | solution.py:22
  42.8 2.1 %collective-permute-done.15 = bf16[64,512]{1,0:T(8,128)(2,1)S(1)} collective-permute-done((bf16[64,512]{1,0:T(8,128)(2,1)S(1)}, bf16[64,512]{1,0:T(8,128)(2,1)S(1)}, u32[]{:S(2)}, u32[]{:S(2)}) %collective-permute-start.15) | collective-permute-done | bytes 65568 | tf_op jit(solution)/shard_map/ppermute | solution.py:22
  44.9 1.7 %collective-permute-start.16 = (bf16[64,512]{1,0:T(8,128)(2,1)S(1)}, bf16[64,512]{1,0:T(8,128)(2,1)S(1)}, u32[]{:S(2)}, u32[]{:S(2)}) collective-permute-start(bf16[64,512]{1,0:T(8,128)(2,1)S(1)} %add_convert_fusion.2), channel_id=1, source_target_pairs={{0,24},{4,28},{8,16},{12,20},{16,8},{20,12},{24,0},{28,4},{1,25},{... | collective-permute-start | bytes 196616 | tf_op jit(solution)/shard_map/ppermute | solution.py:22
  46.7 1.1 %collective-permute-done.17 = bf16[64,512]{1,0:T(8,128)(2,1)S(1)} collective-permute-done((bf16[64,512]{1,0:T(8,128)(2,1)S(1)}, bf16[64,512]{1,0:T(8,128)(2,1)S(1)}, u32[]{:S(2)}, u32[]{:S(2)}) %collective-permute-start.17) | collective-permute-done | bytes 65568 | tf_op jit(solution)/shard_map/ppermute | solution.py:22
  47.8 0.9 %collective-permute-start.18 = (bf16[64,512]{1,0:T(8,128)(2,1)S(1)}, bf16[64,512]{1,0:T(8,128)(2,1)S(1)}, u32[]{:S(2)}, u32[]{:S(2)}) collective-permute-start(bf16[64,512]{1,0:T(8,128)(2,1)S(1)} %add_convert_fusion.1), channel_id=1, source_target_pairs={{0,16},{4,20},{8,24},{12,28},{16,0},{20,4},{24,8},{28,12},{1,17},{... | collective-permute-start | bytes 196616 | tf_op jit(solution)/shard_map/ppermute | solution.py:22
  48.7 1.6 %collective-permute-start.19 = (bf16[64,512]{1,0:T(8,128)(2,1)S(1)}, bf16[64,512]{1,0:T(8,128)(2,1)S(1)}, u32[]{:S(2)}, u32[]{:S(2)}) collective-permute-start(bf16[64,512]{1,0:T(8,128)(2,1)S(1)} %get-tuple-element.42), channel_id=1, source_target_pairs={{0,12},{4,8},{8,4},{12,0},{16,28},{20,24},{24,20},{28,16},{1,13},{... | collective-permute-start | bytes 196616 | tf_op jit(solution)/shard_map/ppermute | solution.py:22
  50.3 0.0 collective-permute-done.14
  50.3 1.5 %collective-permute-done.16 = bf16[64,512]{1,0:T(8,128)(2,1)S(1)} collective-permute-done((bf16[64,512]{1,0:T(8,128)(2,1)S(1)}, bf16[64,512]{1,0:T(8,128)(2,1)S(1)}, u32[]{:S(2)}, u32[]{:S(2)}) %collective-permute-start.16) | collective-permute-done | bytes 65568 | tf_op jit(solution)/shard_map/ppermute | solution.py:22
  51.7 2.2 %collective-permute-done.18 = bf16[64,512]{1,0:T(8,128)(2,1)S(1)} collective-permute-done((bf16[64,512]{1,0:T(8,128)(2,1)S(1)}, bf16[64,512]{1,0:T(8,128)(2,1)S(1)}, u32[]{:S(2)}, u32[]{:S(2)}) %collective-permute-start.18) | collective-permute-done | bytes 65568 | tf_op jit(solution)/shard_map/ppermute | solution.py:22
  54.0 0.6 %collective-permute-done.19 = bf16[64,512]{1,0:T(8,128)(2,1)S(1)} collective-permute-done((bf16[64,512]{1,0:T(8,128)(2,1)S(1)}, bf16[64,512]{1,0:T(8,128)(2,1)S(1)}, u32[]{:S(2)}, u32[]{:S(2)}) %collective-permute-start.19) | collective-permute-done | bytes 65568 | tf_op jit(solution)/shard_map/ppermute | solution.py:22
  54.6 0.6 %fusion = bf16[512,64]{0,1:T(8,128)(2,1)} fusion(f32[64,512]{1,0:T(8,128)S(1)} %convert_add_fusion.1, bf16[64,512]{1,0:T(8,128)(2,1)S(1)} %collective-permute-done.19), kind=kLoop, calls=%fused_computation.5 | loop fusion | flops 98304 | bytes 262144 | tf_op jit(solution)/shard_map/convert_element_type | solution.py:263
  (15 shorter events, 0.2 us)
Async XLA Ops:
  0.0 9.9 %copy-start = (s32[8,8]{1,0:T(8,128)S(1)}, s32[8,8]{1,0:T(8,128)}, u32[]{:S(2)}) copy-start(s32[8,8]{1,0:T(8,128)} %param.9) | copy-start | bytes 772
  0.0 1.0 %copy-start.3 = (bf16[512,256]{1,0:T(8,128)(2,1)S(1)}, bf16[512,256]{1,0:T(8,128)(2,1)}, u32[]{:S(2)}) copy-start(bf16[512,256]{1,0:T(8,128)(2,1)} %probe.1) | copy-start | bytes 786436
  1.2 8.8 %collective-permute-start.5 = (bf16[64,512]{1,0:T(8,128)(2,1)S(1)}, bf16[64,512]{1,0:T(8,128)(2,1)S(1)}, u32[]{:S(2)}, u32[]{:S(2)}) collective-permute-start(bf16[64,512]{1,0:T(8,128)(2,1)S(1)} %share_probe.1.refs_0_), channel_id=1, source_target_pairs={{0,24},{4,28},{8,16},{12,20},{16,8},{20,12},{24,0},{28,4},{1,25},{... | collective-permute-start | bytes 196616 | tf_op jit(solution)/shard_map/ppermute | solution.py:22
  6.3 5.6 %collective-permute-start.3 = (bf16[64,512]{1,0:T(8,128)(2,1)S(1)}, bf16[64,512]{1,0:T(8,128)(2,1)S(1)}, u32[]{:S(2)}, u32[]{:S(2)}) collective-permute-start(bf16[64,512]{1,0:T(8,128)(2,1)S(1)} %share_probe.1.refs_0_), channel_id=1, source_target_pairs={{0,16},{4,20},{8,24},{12,28},{16,0},{20,4},{24,8},{28,12},{1,17},{... | collective-permute-start | bytes 196616 | tf_op jit(solution)/shard_map/ppermute | solution.py:22
  6.3 7.1 %collective-permute-start.1 = (bf16[64,512]{1,0:T(8,128)(2,1)S(1)}, bf16[64,512]{1,0:T(8,128)(2,1)S(1)}, u32[]{:S(2)}, u32[]{:S(2)}) collective-permute-start(bf16[64,512]{1,0:T(8,128)(2,1)S(1)} %share_probe.1.refs_0_), channel_id=1, source_target_pairs={{0,8},{4,12},{8,0},{12,4},{16,24},{20,28},{24,16},{28,20},{1,9},{5... | collective-permute-start | bytes 196616 | tf_op jit(solution)/shard_map/ppermute | solution.py:22
  6.9 7.7 %collective-permute-start = (bf16[64,512]{1,0:T(8,128)(2,1)S(1)}, bf16[64,512]{1,0:T(8,128)(2,1)S(1)}, u32[]{:S(2)}, u32[]{:S(2)}) collective-permute-start(bf16[64,512]{1,0:T(8,128)(2,1)S(1)} %share_probe.1.refs_0_), channel_id=1, source_target_pairs={{0,4},{4,0},{8,12},{12,8},{16,20},{20,16},{24,28},{28,24},{1,5},{5... | collective-permute-start | bytes 196616 | tf_op jit(solution)/shard_map/ppermute | solution.py:22
  9.9 4.7 %collective-permute-start.6 = (bf16[64,512]{1,0:T(8,128)(2,1)S(1)}, bf16[64,512]{1,0:T(8,128)(2,1)S(1)}, u32[]{:S(2)}, u32[]{:S(2)}) collective-permute-start(bf16[64,512]{1,0:T(8,128)(2,1)S(1)} %collective-permute-done.5.refs_6_), channel_id=1, source_target_pairs={{0,4},{4,0},{8,12},{12,8},{16,20},{20,16},{24,28},{28,24},{1,5},{5... | collective-permute-start | bytes 196616 | tf_op jit(solution)/shard_map/ppermute | solution.py:22
  11.9 4.9 %collective-permute-start.4 = (bf16[64,512]{1,0:T(8,128)(2,1)S(1)}, bf16[64,512]{1,0:T(8,128)(2,1)S(1)}, u32[]{:S(2)}, u32[]{:S(2)}) collective-permute-start(bf16[64,512]{1,0:T(8,128)(2,1)S(1)} %collective-permute-done.3.refs_4_), channel_id=1, source_target_pairs={{0,4},{4,0},{8,12},{12,8},{16,20},{20,16},{24,28},{28,24},{1,5},{5... | collective-permute-start | bytes 196616 | tf_op jit(solution)/shard_map/ppermute | solution.py:22
  13.4 4.3 %collective-permute-start.2 = (bf16[64,512]{1,0:T(8,128)(2,1)S(1)}, bf16[64,512]{1,0:T(8,128)(2,1)S(1)}, u32[]{:S(2)}, u32[]{:S(2)}) collective-permute-start(bf16[64,512]{1,0:T(8,128)(2,1)S(1)} %collective-permute-done.1.refs_2_), channel_id=1, source_target_pairs={{0,4},{4,0},{8,12},{12,8},{16,20},{20,16},{24,28},{28,24},{1,5},{5... | collective-permute-start | bytes 196616 | tf_op jit(solution)/shard_map/ppermute | solution.py:22
  18.5 7.5 %collective-permute-start.7 = (bf16[8,64,256]{2,1,0:T(8,128)(2,1)S(1)}, bf16[8,64,256]{2,1,0:T(8,128)(2,1)S(1)}, u32[]{:S(2)}, u32[]{:S(2)}) collective-permute-start(bf16[8,64,256]{2,1,0:T(8,128)(2,1)S(1)} %pick_listed.1.after.own), channel_id=1, source_target_pairs={{0,2},{1,3},{2,0},{3,1},{4,6},{5,7},{6,4},{7,5},{8,10},{9,11},{10,... | collective-permute-start | bytes 786440 | tf_op jit(solution)/shard_map/ppermute | solution.py:22
  20.1 2.2 %copy-start.1 = (bf16[1024,2048]{1,0:T(8,128)(2,1)S(1)}, bf16[1024,2048]{1,0:T(8,128)(2,1)}, u32[]{:S(2)}) copy-start(bf16[1024,2048]{1,0:T(8,128)(2,1)} %held.5) | copy-start | bytes 12582916
  22.2 5.3 %copy-start.2 = (bf16[1024,2048]{1,0:T(8,128)(2,1)S(1)}, bf16[1024,2048]{1,0:T(8,128)(2,1)}, u32[]{:S(2)}) copy-start(bf16[1024,2048]{1,0:T(8,128)(2,1)} %held.5) | copy-start | bytes 12582916
  26.0 1.5 %collective-permute-start.8 = (bf16[8,64,256]{2,1,0:T(8,128)(2,1)S(1)}, bf16[8,64,256]{2,1,0:T(8,128)(2,1)S(1)}, u32[]{:S(2)}, u32[]{:S(2)}) collective-permute-start(bf16[8,64,256]{2,1,0:T(8,128)(2,1)S(1)} %collective-permute-done.7.refs_0_), channel_id=1, source_target_pairs={{0,1},{1,0},{2,3},{3,2},{4,5},{5,4},{6,7},{7,6},{8,9},{9,8},{10,11... | collective-permute-start | bytes 786440 | tf_op jit(solution)/shard_map/ppermute | solution.py:22
  26.0 3.8 %collective-permute-start.10 = (bf16[8,64,256]{2,1,0:T(8,128)(2,1)S(1)}, bf16[8,64,256]{2,1,0:T(8,128)(2,1)S(1)}, u32[]{:S(2)}, u32[]{:S(2)}) collective-permute-start(bf16[8,64,256]{2,1,0:T(8,128)(2,1)S(1)} %pick_listed.1.after.own), channel_id=1, source_target_pairs={{0,1},{1,0},{2,3},{3,2},{4,5},{5,4},{6,7},{7,6},{8,9},{9,8},{10,11... | collective-permute-start | bytes 786440 | tf_op jit(solution)/shard_map/ppermute | solution.py:22
  29.6 1.6 %collective-permute-start.9 = (bf16[64,2048]{1,0:T(8,128)(2,1)S(1)}, bf16[64,2048]{1,0:T(8,128)(2,1)S(1)}, u32[]{:S(2)}, u32[]{:S(2)}) collective-permute-start(bf16[64,2048]{1,0:T(8,128)(2,1)S(1)} %get-tuple-element.28), channel_id=1, source_target_pairs={{0,1},{1,0},{2,3},{3,2},{4,5},{5,4},{6,7},{7,6},{8,9},{9,8},{10,11... | collective-permute-start | bytes 786440 | tf_op jit(solution)/shard_map/ppermute | solution.py:22
  31.2 8.0 %collective-permute-start.11 = (bf16[64,2048]{1,0:T(8,128)(2,1)S(1)}, bf16[64,2048]{1,0:T(8,128)(2,1)S(1)}, u32[]{:S(2)}, u32[]{:S(2)}) collective-permute-start(bf16[64,2048]{1,0:T(8,128)(2,1)S(1)} %get-tuple-element.32), channel_id=1, source_target_pairs={{0,2},{1,3},{2,0},{3,1},{4,6},{5,7},{6,4},{7,5},{8,10},{9,11},{10,... | collective-permute-start | bytes 786440 | tf_op jit(solution)/shard_map/ppermute | solution.py:22
  34.9 4.4 %collective-permute-start.12 = (bf16[64,2048]{1,0:T(8,128)(2,1)S(1)}, bf16[64,2048]{1,0:T(8,128)(2,1)S(1)}, u32[]{:S(2)}, u32[]{:S(2)}) collective-permute-start(bf16[64,2048]{1,0:T(8,128)(2,1)S(1)} %get-tuple-element.33), channel_id=1, source_target_pairs={{0,1},{1,0},{2,3},{3,2},{4,5},{5,4},{6,7},{7,6},{8,9},{9,8},{10,11... | collective-permute-start | bytes 786440 | tf_op jit(solution)/shard_map/ppermute | solution.py:22
  40.0 4.9 %collective-permute-start.15 = (bf16[64,512]{1,0:T(8,128)(2,1)S(1)}, bf16[64,512]{1,0:T(8,128)(2,1)S(1)}, u32[]{:S(2)}, u32[]{:S(2)}) collective-permute-start(bf16[64,512]{1,0:T(8,128)(2,1)S(1)} %get-tuple-element.38), channel_id=1, source_target_pairs={{0,4},{4,0},{8,12},{12,8},{16,20},{20,16},{24,28},{28,24},{1,5},{5... | collective-permute-start | bytes 196616 | tf_op jit(solution)/shard_map/ppermute | solution.py:22
  40.8 9.5 %collective-permute-start.13 = (bf16[64,512]{1,0:T(8,128)(2,1)S(1)}, bf16[64,512]{1,0:T(8,128)(2,1)S(1)}, u32[]{:S(2)}, u32[]{:S(2)}) collective-permute-start(bf16[64,512]{1,0:T(8,128)(2,1)S(1)} %get-tuple-element.35), channel_id=1, source_target_pairs={{0,4},{4,0},{8,12},{12,8},{16,20},{20,16},{24,28},{28,24},{1,5},{5... | collective-permute-start | bytes 196616 | tf_op jit(solution)/shard_map/ppermute | solution.py:22
  42.1 8.2 %collective-permute-start.14 = (bf16[64,512]{1,0:T(8,128)(2,1)S(1)}, bf16[64,512]{1,0:T(8,128)(2,1)S(1)}, u32[]{:S(2)}, u32[]{:S(2)}) collective-permute-start(bf16[64,512]{1,0:T(8,128)(2,1)S(1)} %get-tuple-element.36), channel_id=1, source_target_pairs={{0,8},{4,12},{8,0},{12,4},{16,24},{20,28},{24,16},{28,20},{1,9},{5... | collective-permute-start | bytes 196616 | tf_op jit(solution)/shard_map/ppermute | solution.py:22
  42.1 5.6 %collective-permute-start.17 = (bf16[64,512]{1,0:T(8,128)(2,1)S(1)}, bf16[64,512]{1,0:T(8,128)(2,1)S(1)}, u32[]{:S(2)}, u32[]{:S(2)}) collective-permute-start(bf16[64,512]{1,0:T(8,128)(2,1)S(1)} %get-tuple-element.40), channel_id=1, source_target_pairs={{0,4},{4,0},{8,12},{12,8},{16,20},{20,16},{24,28},{28,24},{1,5},{5... | collective-permute-start | bytes 196616 | tf_op jit(solution)/shard_map/ppermute | solution.py:22
  44.9 6.8 %collective-permute-start.16 = (bf16[64,512]{1,0:T(8,128)(2,1)S(1)}, bf16[64,512]{1,0:T(8,128)(2,1)S(1)}, u32[]{:S(2)}, u32[]{:S(2)}) collective-permute-start(bf16[64,512]{1,0:T(8,128)(2,1)S(1)} %add_convert_fusion.2), channel_id=1, source_target_pairs={{0,24},{4,28},{8,16},{12,20},{16,8},{20,12},{24,0},{28,4},{1,25},{... | collective-permute-start | bytes 196616 | tf_op jit(solution)/shard_map/ppermute | solution.py:22
  47.8 6.2 %collective-permute-start.18 = (bf16[64,512]{1,0:T(8,128)(2,1)S(1)}, bf16[64,512]{1,0:T(8,128)(2,1)S(1)}, u32[]{:S(2)}, u32[]{:S(2)}) collective-permute-start(bf16[64,512]{1,0:T(8,128)(2,1)S(1)} %add_convert_fusion.1), channel_id=1, source_target_pairs={{0,16},{4,20},{8,24},{12,28},{16,0},{20,4},{24,8},{28,12},{1,17},{... | collective-permute-start | bytes 196616 | tf_op jit(solution)/shard_map/ppermute | solution.py:22
  48.7 5.9 %collective-permute-start.19 = (bf16[64,512]{1,0:T(8,128)(2,1)S(1)}, bf16[64,512]{1,0:T(8,128)(2,1)S(1)}, u32[]{:S(2)}, u32[]{:S(2)}) collective-permute-start(bf16[64,512]{1,0:T(8,128)(2,1)S(1)} %get-tuple-element.42), channel_id=1, source_target_pairs={{0,12},{4,8},{8,4},{12,0},{16,28},{20,24},{24,20},{28,16},{1,13},{... | collective-permute-start | bytes 196616 | tf_op jit(solution)/shard_map/ppermute | solution.py:22

commit v11 on v9

--- a/solution.py
+++ b/solution.py
@@ -74,8 +74,8 @@
         weighted[span, :] = (jac[span, :].astype(jnp.float32) * scale).astype(jnp.bfloat16)
 
 
-def pick_kernel(unit, info, *refs):
-    pieces, out, position = refs[:-2], refs[-2], refs[-1]
+def pick_kernel(unit, steps, info, *refs):
+    pieces, out, position = refs[-2 - len(steps):-2], refs[-2], refs[-1]
     listed, _, tile = out.shape
     block = lax.axis_index("obs")
     units = pieces[0].shape[1] // unit
@@ -83,7 +83,7 @@
         position[a] = -1
     for k in range(listed):
         position[info[k]] = k
-    for step, piece in enumerate(pieces):
+    for step, piece in zip(steps, pieces):
         for u in range(units):
             row = ((block ^ step) * units + u) * unit
             at = position[row // tile]
@@ -159,21 +159,28 @@
         compiler_params=params(8),
         name="share_probe",
     )(probe_block)
-    pick = pl.pallas_call(
-        functools.partial(pick_kernel, unit),
-        out_shape=jax.ShapeDtypeStruct((listed, high, tile), jnp.bfloat16),
-        in_specs=[SMEM] + [VMEM] * obs_count,
-        out_specs=VMEM,
-        scratch_shapes=[pltpu.SMEM((tiles,), jnp.int32)],
-        compiler_params=params(8),
-        name="pick_listed",
-    )
+    def pick(name, steps, info, *before):
+        held = [pieces[step] for step in steps]
+        return pl.pallas_call(
+            functools.partial(pick_kernel, unit, steps),
+            out_shape=jax.ShapeDtypeStruct((listed, high, tile), jnp.bfloat16),
+            in_specs=[SMEM] + [VMEM] * (len(before) + len(held)),
+            out_specs=VMEM,
+            scratch_shapes=[pltpu.SMEM((tiles,), jnp.int32)],
+            input_output_aliases={1: 0} if before else {},
+            compiler_params=params(8),
+            name=name,
+        )(info, *before, *held)
+
     weight_lanes = min(128, rows)
     observation = lax.axis_index("sub") * rows + jnp.arange(rows, dtype=jnp.int32)
     weight = obs_weight * (observation < row_counts[0]).astype(jnp.float32)
     weight = weight.reshape(rows // weight_lanes, weight_lanes)
+    pieces = spread(share, "obs", obs_count, SPREAD_DIRECT)
+    last = obs_count // 2 + 1
+    picked = pick("pick_listed", [step for step in range(obs_count) if step != last], info)
     info, weight = lax.optimization_barrier((info, weight))
-    picked = pick(info, *spread(share, "obs", obs_count, SPREAD_DIRECT))
+    picked = pick("pick_last", [last], info, picked)
     weighted = pl.pallas_call(
         weigh_kernel,
         out_shape=jax.ShapeDtypeStruct((rows, width), jnp.bfloat16),

time: 54 us -> 53.2 us (0.985)
  waiting for transfers between devices: 17.8 us -> 16.2 us
  Pallas kernels: 6.6 us -> 7.15 us
    ppermute x20, waiting for transfers between devices: 17.8 us -> 16.2 us  [swap(): return lax.ppermute(value, axis, [(i, i ^ step) for i in range(count)])]
    pallas_call x1 -> x2, Pallas kernels: 0.81 us -> 1.37 us  [pick(): pl.pallas_call(functools.partial(pick_kernel, unit, steps), out_shape=jax...]
  transfers between devices with their start and end apart: 20 -> 20, of which waited for: 11 -> 10; matrix products, arithmetic and copies ran while one was open for 3% -> 3% of each run, Pallas kernels for 5% -> 7%
where the time goes in v11:
time: 53.2 us; the launch traced here: 53 us
  starting transfers between devices  23.5 us (44%)
  waiting for transfers between devices  16.2 us (30%)
  Pallas kernels  7.15 us (13%)
  local copies, waits for them, and re-layouts  3.16 us (6%)
  other arithmetic  2.23 us (4%)
  between operations  0.78 us (1%)
    ppermute x20, starting transfers between devices, swap(): return lax.ppermute(value, axis, [(i, i ^ step) for i in range(count)])  23.5 us
    ppermute x20, waiting for transfers between devices, swap(): return lax.ppermute(value, axis, [(i, i ^ step) for i in range(count)])  16.2 us
    pallas_call x2, Pallas kernels, product(): pl.pallas_call(product_kernel, out_shape=[jax.ShapeDtypeStruct((high, wid...  4.11 us
    unnamed x8, local copies, waits for them, and re-layouts  3.16 us
    pallas_call x2, Pallas kernels, pick(): pl.pallas_call(functools.partial(pick_kernel, unit, steps), out_shape=jax...  1.37 us
  transfers between devices with their start and end apart: 20, of which 10 were waited for; matrix products, arithmetic and copies ran while one was open for 3% of the time, Pallas kernels for 7%

profile of v11, /device:TPU:0, one launch (start us, length us, event | category | flops | bytes accessed | tf_op | source)
XLA Modules:
  0.0 53.0 jit_solution(4119514449707267070)
XLA Ops:
  0.0 1.0 %copy-done.3 = bf16[512,256]{1,0:T(8,128)(2,1)S(1)} copy-done((bf16[512,256]{1,0:T(8,128)(2,1)S(1)}, bf16[512,256]{1,0:T(8,128)(2,1)}, u32[]{:S(2)}) %copy-start.3) | copy-done | bytes 262168
  1.0 0.2 share_probe.1.refs_0_
  1.2 3.1 %collective-permute-start.1 = (bf16[64,512]{1,0:T(8,128)(2,1)S(1)}, bf16[64,512]{1,0:T(8,128)(2,1)S(1)}, u32[]{:S(2)}, u32[]{:S(2)}) collective-permute-start(bf16[64,512]{1,0:T(8,128)(2,1)S(1)} %share_probe.1.refs_0_), channel_id=1, source_target_pairs={{0,8},{4,12},{8,0},{12,4},{16,24},{20,28},{24,16},{28,20},{1,9},{5... | collective-permute-start | bytes 196616 | tf_op jit(solution)/shard_map/ppermute | solution.py:22
  4.3 2.5 %collective-permute-start.4 = (bf16[64,512]{1,0:T(8,128)(2,1)S(1)}, bf16[64,512]{1,0:T(8,128)(2,1)S(1)}, u32[]{:S(2)}, u32[]{:S(2)}) collective-permute-start(bf16[64,512]{1,0:T(8,128)(2,1)S(1)} %share_probe.1.refs_0_), channel_id=1, source_target_pairs={{0,24},{4,28},{8,16},{12,20},{16,8},{20,12},{24,0},{28,4},{1,25},{... | collective-permute-start | bytes 196616 | tf_op jit(solution)/shard_map/ppermute | solution.py:22
  6.7 0.1 collective-permute-start.3
  6.9 1.5 %collective-permute-start = (bf16[64,512]{1,0:T(8,128)(2,1)S(1)}, bf16[64,512]{1,0:T(8,128)(2,1)S(1)}, u32[]{:S(2)}, u32[]{:S(2)}) collective-permute-start(bf16[64,512]{1,0:T(8,128)(2,1)S(1)} %share_probe.1.refs_0_), channel_id=1, source_target_pairs={{0,4},{4,0},{8,12},{12,8},{16,20},{20,16},{24,28},{28,24},{1,5},{5... | collective-permute-start | bytes 196616 | tf_op jit(solution)/shard_map/ppermute | solution.py:22
  9.0 0.7 %select_bitcast_fusion.weight = f32[8,128]{1,0:T(8,128)S(1)} fusion(f32[1024]{0:T(1024)} %param.7, s32[]{:T(128)} %bitcast.7, s32[]{:T(128)S(6)} %mul.6), kind=kLoop, calls=%fused_computation.7 | loop fusion | flops 3072 | bytes 8200 | tf_op jit(solution)/shard_map/reshape | solution.py:178
  9.7 0.0 collective-permute-done.1.refs_2_
  9.7 0.6 %collective-permute-start.2 = (bf16[64,512]{1,0:T(8,128)(2,1)S(1)}, bf16[64,512]{1,0:T(8,128)(2,1)S(1)}, u32[]{:S(2)}, u32[]{:S(2)}) collective-permute-start(bf16[64,512]{1,0:T(8,128)(2,1)S(1)} %collective-permute-done.1.refs_2_), channel_id=1, source_target_pairs={{0,4},{4,0},{8,12},{12,8},{16,20},{20,16},{24,28},{28,24},{1,5},{5... | collective-permute-start | bytes 196616 | tf_op jit(solution)/shard_map/ppermute | solution.py:22
  10.3 0.8 %collective-permute-done.4.refs_5_ = bf16[64,512]{1,0:T(8,128)(2,1)S(1)} collective-permute-done((bf16[64,512]{1,0:T(8,128)(2,1)S(1)}, bf16[64,512]{1,0:T(8,128)(2,1)S(1)}, u32[]{:S(2)}, u32[]{:S(2)}) %collective-permute-start.4) | collective-permute-done | bytes 65568 | tf_op jit(solution)/shard_map/ppermute | solution.py:22
  11.1 1.5 %collective-permute-start.5 = (bf16[64,512]{1,0:T(8,128)(2,1)S(1)}, bf16[64,512]{1,0:T(8,128)(2,1)S(1)}, u32[]{:S(2)}, u32[]{:S(2)}) collective-permute-start(bf16[64,512]{1,0:T(8,128)(2,1)S(1)} %collective-permute-done.4.refs_5_), channel_id=1, source_target_pairs={{0,4},{4,0},{8,12},{12,8},{16,20},{20,16},{24,28},{28,24},{1,5},{5... | collective-permute-start | bytes 196616 | tf_op jit(solution)/shard_map/ppermute | solution.py:22
  12.6 0.6 %collective-permute-done.3.refs_4_ = bf16[64,512]{1,0:T(8,128)(2,1)S(1)} collective-permute-done((bf16[64,512]{1,0:T(8,128)(2,1)S(1)}, bf16[64,512]{1,0:T(8,128)(2,1)S(1)}, u32[]{:S(2)}, u32[]{:S(2)}) %collective-permute-start.3) | collective-permute-done | bytes 65568 | tf_op jit(solution)/shard_map/ppermute | solution.py:22
  13.2 1.5 %collective-permute-start.6 = (bf16[64,512]{1,0:T(8,128)(2,1)S(1)}, bf16[64,512]{1,0:T(8,128)(2,1)S(1)}, u32[]{:S(2)}, u32[]{:S(2)}) collective-permute-start(bf16[64,512]{1,0:T(8,128)(2,1)S(1)} %collective-permute-done.3.refs_4_), channel_id=1, source_target_pairs={{0,4},{4,0},{8,12},{12,8},{16,20},{20,16},{24,28},{28,24},{1,5},{5... | collective-permute-start | bytes 196616 | tf_op jit(solution)/shard_map/ppermute | solution.py:22
  14.7 0.7 %pad_add_fusion.info = s32[24]{0:T(128)S(1)} fusion(s32[16]{0:T(128)} %param.10, s32[8]{0:T(128)S(1)} %dynamic-slice_bitcast_fusion), kind=kLoop, calls=%fused_computation.9 | loop fusion | flops 24 | bytes 192 | tf_op jit(solution)/shard_map/concatenate | solution.py:149
  15.4 0.0 collective-permute-done.refs_1_
  15.4 0.0 collective-permute-done.2.refs_3_
  15.4 0.0 collective-permute-done.5.refs_6_
  15.4 0.8 %pick_listed.1.refs_0_ = bf16[8,64,256]{2,1,0:T(8,128)(2,1)S(1)} custom-call(s32[24]{0:T(128)S(1)} %pad_add_fusion.info, bf16[64,512]{1,0:T(8,128)(2,1)S(1)} %share_probe.1.refs_0_, bf16[64,512]{1,0:T(8,128)(2,1)S(1)} %collective-permute-done.refs_1_, bf16[64,512]{1,0:T(8,128)(2,1)S(1)} %collective-permute-done.1.refs_2_, ...), custom_call_target="tpu_custom_call" | custom-call | tf_op jit(solution)/shard_map/pick_listed/pallas_call | solution.py:164
  16.2 1.2 %collective-permute-done.6.refs_1_ = bf16[64,512]{1,0:T(8,128)(2,1)S(1)} collective-permute-done((bf16[64,512]{1,0:T(8,128)(2,1)S(1)}, bf16[64,512]{1,0:T(8,128)(2,1)S(1)}, u32[]{:S(2)}, u32[]{:S(2)}) %collective-permute-start.6) | collective-permute-done | bytes 65568 | tf_op jit(solution)/shard_map/ppermute | solution.py:22
  17.4 0.6 %pick_last.1.after.refs_0_ = bf16[8,64,256]{2,1,0:T(8,128)(2,1)S(1)} custom-call(s32[24]{0:T(128)S(1)} %pad_add_fusion.info, bf16[8,64,256]{2,1,0:T(8,128)(2,1)S(1)} %pick_listed.1.refs_0_, bf16[64,512]{1,0:T(8,128)(2,1)S(1)} %collective-permute-done.6.refs_1_), custom_call_target="tpu_custom_call", output_to_operand_aliasing={{}: (1, {})} | custom-call | tf_op jit(solution)/shard_map/pick_last/pallas_call | solution.py:164
  18.0 1.6 %collective-permute-start.8 = (bf16[8,64,256]{2,1,0:T(8,128)(2,1)S(1)}, bf16[8,64,256]{2,1,0:T(8,128)(2,1)S(1)}, u32[]{:S(2)}, u32[]{:S(2)}) collective-permute-start(bf16[8,64,256]{2,1,0:T(8,128)(2,1)S(1)} %pick_last.1.after.refs_0_), channel_id=1, source_target_pairs={{0,2},{1,3},{2,0},{3,1},{4,6},{5,7},{6,4},{7,5},{8,10},{9,11},{10,... | collective-permute-start | bytes 786440 | tf_op jit(solution)/shard_map/ppermute | solution.py:22
  19.6 2.2 %copy-done.1 = bf16[1024,2048]{1,0:T(8,128)(2,1)S(1)} copy-done((bf16[1024,2048]{1,0:T(8,128)(2,1)S(1)}, bf16[1024,2048]{1,0:T(8,128)(2,1)}, u32[]{:S(2)}) %copy-start.1) | copy-done | bytes 4194328
  21.8 0.7 %weigh.1.weighted = bf16[1024,2048]{1,0:T(8,128)(2,1)S(1)} custom-call(f32[8,128]{1,0:T(8,128)S(1)} %select_bitcast_fusion.weight, bf16[1024,2048]{1,0:T(8,128)(2,1)S(1)} %copy-done.1, bf16[8,64,256]{2,1,0:T(8,128)(2,1)S(1)} %pick_last.1.after.refs_0_), custom_call_target="tpu_custom_call" | custom-call | flops 4194304 | bytes 8388608 | tf_op jit(solution)/shard_map/weigh/pallas_call | solution.py:184
  22.6 2.6 %collective-permute-done.8.refs_0_ = bf16[8,64,256]{2,1,0:T(8,128)(2,1)S(1)} collective-permute-done((bf16[8,64,256]{2,1,0:T(8,128)(2,1)S(1)}, bf16[8,64,256]{2,1,0:T(8,128)(2,1)S(1)}, u32[]{:S(2)}, u32[]{:S(2)}) %collective-permute-start.8) | collective-permute-done | bytes 262176 | tf_op jit(solution)/shard_map/ppermute | solution.py:22
  25.1 0.0 collective-permute-start.9
  25.2 1.5 %collective-permute-done.9.refs_1_ = bf16[8,64,256]{2,1,0:T(8,128)(2,1)S(1)} collective-permute-done((bf16[8,64,256]{2,1,0:T(8,128)(2,1)S(1)}, bf16[8,64,256]{2,1,0:T(8,128)(2,1)S(1)}, u32[]{:S(2)}, u32[]{:S(2)}) %collective-permute-start.9) | collective-permute-done | bytes 262176 | tf_op jit(solution)/shard_map/ppermute | solution.py:22
  26.7 2.1 %far_product.1 = (f32[64,2048]{1,0:T(8,128)S(1)}, bf16[64,2048]{1,0:T(8,128)(2,1)S(1)}) custom-call(bf16[1024,2048]{1,0:T(8,128)(2,1)S(1)} %copy-done.2, bf16[1024,2048]{1,0:T(8,128)(2,1)S(1)} %weigh.1.weighted, bf16[8,64,256]{2,1,0:T(8,128)(2,1)S(1)} %collective-permute-done.8.refs_0_, bf16[8,64,256]{2,1,0:T(8,128)(2,1)S(1)} %collective-permute-done.9.refs_1_), custom_call_target="tpu_custom_call" | custom-call | flops 1073741824 | bytes 8388608 | tf_op jit(solution)/shard_map/far_product/pallas_call | solution.py:196
  28.8 0.2 collective-permute-start.10
  29.0 0.4 collective-permute-start.7
  29.3 1.0 %collective-permute-done.10 = bf16[64,2048]{1,0:T(8,128)(2,1)S(1)} collective-permute-done((bf16[64,2048]{1,0:T(8,128)(2,1)S(1)}, bf16[64,2048]{1,0:T(8,128)(2,1)S(1)}, u32[]{:S(2)}, u32[]{:S(2)}) %collective-permute-start.10) | collective-permute-done | bytes 262176 | tf_op jit(solution)/shard_map/ppermute | solution.py:22
  30.4 1.6 %collective-permute-start.11 = (bf16[64,2048]{1,0:T(8,128)(2,1)S(1)}, bf16[64,2048]{1,0:T(8,128)(2,1)S(1)}, u32[]{:S(2)}, u32[]{:S(2)}) collective-permute-start(bf16[64,2048]{1,0:T(8,128)(2,1)S(1)} %add_convert_fusion), channel_id=1, source_target_pairs={{0,2},{1,3},{2,0},{3,1},{4,6},{5,7},{6,4},{7,5},{8,10},{9,11},{10,... | collective-permute-start | bytes 786440 | tf_op jit(solution)/shard_map/ppermute | solution.py:22
  32.0 0.0 collective-permute-done.7.refs_1_
  32.0 2.1 %near_product.1 = (f32[64,2048]{1,0:T(8,128)S(1)}, bf16[64,2048]{1,0:T(8,128)(2,1)S(1)}) custom-call(bf16[1024,2048]{1,0:T(8,128)(2,1)S(1)} %copy-done.2, bf16[1024,2048]{1,0:T(8,128)(2,1)S(1)} %weigh.1.weighted, bf16[8,64,256]{2,1,0:T(8,128)(2,1)S(1)} %pick_last.1.after.refs_0_, bf16[8,64,256]{2,1,0:T(8,128)(2,1)S(1)} %collective-permute-done.7.refs_1_), custom_call_target="tpu_custom_call" | custom-call | flops 1073741824 | bytes 8388608 | tf_op jit(solution)/shard_map/near_product/pallas_call | solution.py:196
  34.1 0.1 collective-permute-start.12
  34.1 4.7 %collective-permute-done.11 = bf16[64,2048]{1,0:T(8,128)(2,1)S(1)} collective-permute-done((bf16[64,2048]{1,0:T(8,128)(2,1)S(1)}, bf16[64,2048]{1,0:T(8,128)(2,1)S(1)}, u32[]{:S(2)}, u32[]{:S(2)}) %collective-permute-start.11) | collective-permute-done | bytes 262176 | tf_op jit(solution)/shard_map/ppermute | solution.py:22
  38.9 0.0 collective-permute-done.12.refs_1_
  38.9 0.7 %place.1 = (f32[64,512]{1,0:T(8,128)S(1)}, bf16[64,512]{1,0:T(8,128)(2,1)S(1)}, bf16[64,512]{1,0:T(8,128)(2,1)S(1)}, bf16[64,512]{1,0:T(8,128)(2,1)S(1)}, f32[64...) custom-call(s32[24]{0:T(128)S(1)} %pad_add_fusion.info, ...), custom_call_target="tpu_custom_call" | custom-call | tf_op jit(solution)/shard_map/place/pallas_call | solution.py:226
  39.6 1.6 %collective-permute-start.15 = (bf16[64,512]{1,0:T(8,128)(2,1)S(1)}, bf16[64,512]{1,0:T(8,128)(2,1)S(1)}, u32[]{:S(2)}, u32[]{:S(2)}) collective-permute-start(bf16[64,512]{1,0:T(8,128)(2,1)S(1)} %get-tuple-element.34), channel_id=1, source_target_pairs={{0,4},{4,0},{8,12},{12,8},{16,20},{20,16},{24,28},{28,24},{1,5},{5... | collective-permute-start | bytes 196616 | tf_op jit(solution)/shard_map/ppermute | solution.py:22
  41.2 0.5 %collective-permute-start.17 = (bf16[64,512]{1,0:T(8,128)(2,1)S(1)}, bf16[64,512]{1,0:T(8,128)(2,1)S(1)}, u32[]{:S(2)}, u32[]{:S(2)}) collective-permute-start(bf16[64,512]{1,0:T(8,128)(2,1)S(1)} %get-tuple-element.36), channel_id=1, source_target_pairs={{0,4},{4,0},{8,12},{12,8},{16,20},{20,16},{24,28},{28,24},{1,5},{5... | collective-permute-start | bytes 196616 | tf_op jit(solution)/shard_map/ppermute | solution.py:22
  41.7 1.5 %collective-permute-start.13 = (bf16[64,512]{1,0:T(8,128)(2,1)S(1)}, bf16[64,512]{1,0:T(8,128)(2,1)S(1)}, u32[]{:S(2)}, u32[]{:S(2)}) collective-permute-start(bf16[64,512]{1,0:T(8,128)(2,1)S(1)} %get-tuple-element.31), channel_id=1, source_target_pairs={{0,4},{4,0},{8,12},{12,8},{16,20},{20,16},{24,28},{28,24},{1,5},{5... | collective-permute-start | bytes 196616 | tf_op jit(solution)/shard_map/ppermute | solution.py:22
  43.2 1.4 %collective-permute-done.15 = bf16[64,512]{1,0:T(8,128)(2,1)S(1)} collective-permute-done((bf16[64,512]{1,0:T(8,128)(2,1)S(1)}, bf16[64,512]{1,0:T(8,128)(2,1)S(1)}, u32[]{:S(2)}, u32[]{:S(2)}) %collective-permute-start.15) | collective-permute-done | bytes 65568 | tf_op jit(solution)/shard_map/ppermute | solution.py:22
  44.6 2.0 %collective-permute-start.16 = (bf16[64,512]{1,0:T(8,128)(2,1)S(1)}, bf16[64,512]{1,0:T(8,128)(2,1)S(1)}, u32[]{:S(2)}, u32[]{:S(2)}) collective-permute-start(bf16[64,512]{1,0:T(8,128)(2,1)S(1)} %add_convert_fusion.3), channel_id=1, source_target_pairs={{0,24},{4,28},{8,16},{12,20},{16,8},{20,12},{24,0},{28,4},{1,25},{... | collective-permute-start | bytes 196616 | tf_op jit(solution)/shard_map/ppermute | solution.py:22
  46.6 0.0 collective-permute-done.17
  46.6 0.3 collective-permute-start.18
  46.9 3.1 %collective-permute-start.19 = (bf16[64,512]{1,0:T(8,128)(2,1)S(1)}, bf16[64,512]{1,0:T(8,128)(2,1)S(1)}, u32[]{:S(2)}, u32[]{:S(2)}) collective-permute-start(bf16[64,512]{1,0:T(8,128)(2,1)S(1)} %get-tuple-element.38), channel_id=1, source_target_pairs={{0,12},{4,8},{8,4},{12,0},{16,28},{20,24},{24,20},{28,16},{1,13},{... | collective-permute-start | bytes 196616 | tf_op jit(solution)/shard_map/ppermute | solution.py:22
  50.0 0.8 %collective-permute-done.16 = bf16[64,512]{1,0:T(8,128)(2,1)S(1)} collective-permute-done((bf16[64,512]{1,0:T(8,128)(2,1)S(1)}, bf16[64,512]{1,0:T(8,128)(2,1)S(1)}, u32[]{:S(2)}, u32[]{:S(2)}) %collective-permute-start.16) | collective-permute-done | bytes 65568 | tf_op jit(solution)/shard_map/ppermute | solution.py:22
  50.8 1.5 %collective-permute-done.18 = bf16[64,512]{1,0:T(8,128)(2,1)S(1)} collective-permute-done((bf16[64,512]{1,0:T(8,128)(2,1)S(1)}, bf16[64,512]{1,0:T(8,128)(2,1)S(1)}, u32[]{:S(2)}, u32[]{:S(2)}) %collective-permute-start.18) | collective-permute-done | bytes 65568 | tf_op jit(solution)/shard_map/ppermute | solution.py:22
  52.3 0.6 %fusion = bf16[512,64]{0,1:T(8,128)(2,1)} fusion(f32[64,512]{1,0:T(8,128)S(1)} %convert_add_fusion.1, bf16[64,512]{1,0:T(8,128)(2,1)S(1)} %collective-permute-done.19), kind=kLoop, calls=%fused_computation.6 | loop fusion | flops 98304 | bytes 262144 | tf_op jit(solution)/shard_map/convert_element_type | solution.py:231
  (16 shorter events, 0.2 us)
Async XLA Ops:
  0.0 9.7 %copy-start = (s32[8,8]{1,0:T(8,128)S(1)}, s32[8,8]{1,0:T(8,128)}, u32[]{:S(2)}) copy-start(s32[8,8]{1,0:T(8,128)} %param.9) | copy-start | bytes 772
  0.0 1.0 %copy-start.3 = (bf16[512,256]{1,0:T(8,128)(2,1)S(1)}, bf16[512,256]{1,0:T(8,128)(2,1)}, u32[]{:S(2)}) copy-start(bf16[512,256]{1,0:T(8,128)(2,1)} %probe.1) | copy-start | bytes 786436
  1.2 8.5 %collective-permute-start.1 = (bf16[64,512]{1,0:T(8,128)(2,1)S(1)}, bf16[64,512]{1,0:T(8,128)(2,1)S(1)}, u32[]{:S(2)}, u32[]{:S(2)}) collective-permute-start(bf16[64,512]{1,0:T(8,128)(2,1)S(1)} %share_probe.1.refs_0_), channel_id=1, source_target_pairs={{0,8},{4,12},{8,0},{12,4},{16,24},{20,28},{24,16},{28,20},{1,9},{5... | collective-permute-start | bytes 196616 | tf_op jit(solution)/shard_map/ppermute | solution.py:22
  4.3 6.9 %collective-permute-start.4 = (bf16[64,512]{1,0:T(8,128)(2,1)S(1)}, bf16[64,512]{1,0:T(8,128)(2,1)S(1)}, u32[]{:S(2)}, u32[]{:S(2)}) collective-permute-start(bf16[64,512]{1,0:T(8,128)(2,1)S(1)} %share_probe.1.refs_0_), channel_id=1, source_target_pairs={{0,24},{4,28},{8,16},{12,20},{16,8},{20,12},{24,0},{28,4},{1,25},{... | collective-permute-start | bytes 196616 | tf_op jit(solution)/shard_map/ppermute | solution.py:22
  6.7 6.4 %collective-permute-start.3 = (bf16[64,512]{1,0:T(8,128)(2,1)S(1)}, bf16[64,512]{1,0:T(8,128)(2,1)S(1)}, u32[]{:S(2)}, u32[]{:S(2)}) collective-permute-start(bf16[64,512]{1,0:T(8,128)(2,1)S(1)} %share_probe.1.refs_0_), channel_id=1, source_target_pairs={{0,16},{4,20},{8,24},{12,28},{16,0},{20,4},{24,8},{28,12},{1,17},{... | collective-permute-start | bytes 196616 | tf_op jit(solution)/shard_map/ppermute | solution.py:22
  6.9 8.6 %collective-permute-start = (bf16[64,512]{1,0:T(8,128)(2,1)S(1)}, bf16[64,512]{1,0:T(8,128)(2,1)S(1)}, u32[]{:S(2)}, u32[]{:S(2)}) collective-permute-start(bf16[64,512]{1,0:T(8,128)(2,1)S(1)} %share_probe.1.refs_0_), channel_id=1, source_target_pairs={{0,4},{4,0},{8,12},{12,8},{16,20},{20,16},{24,28},{28,24},{1,5},{5... | collective-permute-start | bytes 196616 | tf_op jit(solution)/shard_map/ppermute | solution.py:22
  9.7 5.7 %collective-permute-start.2 = (bf16[64,512]{1,0:T(8,128)(2,1)S(1)}, bf16[64,512]{1,0:T(8,128)(2,1)S(1)}, u32[]{:S(2)}, u32[]{:S(2)}) collective-permute-start(bf16[64,512]{1,0:T(8,128)(2,1)S(1)} %collective-permute-done.1.refs_2_), channel_id=1, source_target_pairs={{0,4},{4,0},{8,12},{12,8},{16,20},{20,16},{24,28},{28,24},{1,5},{5... | collective-permute-start | bytes 196616 | tf_op jit(solution)/shard_map/ppermute | solution.py:22
  11.1 4.3 %collective-permute-start.5 = (bf16[64,512]{1,0:T(8,128)(2,1)S(1)}, bf16[64,512]{1,0:T(8,128)(2,1)S(1)}, u32[]{:S(2)}, u32[]{:S(2)}) collective-permute-start(bf16[64,512]{1,0:T(8,128)(2,1)S(1)} %collective-permute-done.4.refs_5_), channel_id=1, source_target_pairs={{0,4},{4,0},{8,12},{12,8},{16,20},{20,16},{24,28},{28,24},{1,5},{5... | collective-permute-start | bytes 196616 | tf_op jit(solution)/shard_map/ppermute | solution.py:22
  13.2 4.3 %collective-permute-start.6 = (bf16[64,512]{1,0:T(8,128)(2,1)S(1)}, bf16[64,512]{1,0:T(8,128)(2,1)S(1)}, u32[]{:S(2)}, u32[]{:S(2)}) collective-permute-start(bf16[64,512]{1,0:T(8,128)(2,1)S(1)} %collective-permute-done.3.refs_4_), channel_id=1, source_target_pairs={{0,4},{4,0},{8,12},{12,8},{16,20},{20,16},{24,28},{28,24},{1,5},{5... | collective-permute-start | bytes 196616 | tf_op jit(solution)/shard_map/ppermute | solution.py:22
  18.0 7.1 %collective-permute-start.8 = (bf16[8,64,256]{2,1,0:T(8,128)(2,1)S(1)}, bf16[8,64,256]{2,1,0:T(8,128)(2,1)S(1)}, u32[]{:S(2)}, u32[]{:S(2)}) collective-permute-start(bf16[8,64,256]{2,1,0:T(8,128)(2,1)S(1)} %pick_last.1.after.refs_0_), channel_id=1, source_target_pairs={{0,2},{1,3},{2,0},{3,1},{4,6},{5,7},{6,4},{7,5},{8,10},{9,11},{10,... | collective-permute-start | bytes 786440 | tf_op jit(solution)/shard_map/ppermute | solution.py:22
  19.6 2.2 %copy-start.1 = (bf16[1024,2048]{1,0:T(8,128)(2,1)S(1)}, bf16[1024,2048]{1,0:T(8,128)(2,1)}, u32[]{:S(2)}) copy-start(bf16[1024,2048]{1,0:T(8,128)(2,1)} %held.3) | copy-start | bytes 12582916
  21.8 4.9 %copy-start.2 = (bf16[1024,2048]{1,0:T(8,128)(2,1)S(1)}, bf16[1024,2048]{1,0:T(8,128)(2,1)}, u32[]{:S(2)}) copy-start(bf16[1024,2048]{1,0:T(8,128)(2,1)} %held.3) | copy-start | bytes 12582916
  25.1 1.5 %collective-permute-start.9 = (bf16[8,64,256]{2,1,0:T(8,128)(2,1)S(1)}, bf16[8,64,256]{2,1,0:T(8,128)(2,1)S(1)}, u32[]{:S(2)}, u32[]{:S(2)}) collective-permute-start(bf16[8,64,256]{2,1,0:T(8,128)(2,1)S(1)} %collective-permute-done.8.refs_0_), channel_id=1, source_target_pairs={{0,1},{1,0},{2,3},{3,2},{4,5},{5,4},{6,7},{7,6},{8,9},{9,8},{10,11... | collective-permute-start | bytes 786440 | tf_op jit(solution)/shard_map/ppermute | solution.py:22
  28.8 1.6 %collective-permute-start.10 = (bf16[64,2048]{1,0:T(8,128)(2,1)S(1)}, bf16[64,2048]{1,0:T(8,128)(2,1)S(1)}, u32[]{:S(2)}, u32[]{:S(2)}) collective-permute-start(bf16[64,2048]{1,0:T(8,128)(2,1)S(1)} %get-tuple-element.26), channel_id=1, source_target_pairs={{0,1},{1,0},{2,3},{3,2},{4,5},{5,4},{6,7},{7,6},{8,9},{9,8},{10,11... | collective-permute-start | bytes 786440 | tf_op jit(solution)/shard_map/ppermute | solution.py:22
  29.0 3.0 %collective-permute-start.7 = (bf16[8,64,256]{2,1,0:T(8,128)(2,1)S(1)}, bf16[8,64,256]{2,1,0:T(8,128)(2,1)S(1)}, u32[]{:S(2)}, u32[]{:S(2)}) collective-permute-start(bf16[8,64,256]{2,1,0:T(8,128)(2,1)S(1)} %pick_last.1.after.refs_0_), channel_id=1, source_target_pairs={{0,1},{1,0},{2,3},{3,2},{4,5},{5,4},{6,7},{7,6},{8,9},{9,8},{10,11... | collective-permute-start | bytes 786440 | tf_op jit(solution)/shard_map/ppermute | solution.py:22
  30.4 8.4 %collective-permute-start.11 = (bf16[64,2048]{1,0:T(8,128)(2,1)S(1)}, bf16[64,2048]{1,0:T(8,128)(2,1)S(1)}, u32[]{:S(2)}, u32[]{:S(2)}) collective-permute-start(bf16[64,2048]{1,0:T(8,128)(2,1)S(1)} %add_convert_fusion), channel_id=1, source_target_pairs={{0,2},{1,3},{2,0},{3,1},{4,6},{5,7},{6,4},{7,5},{8,10},{9,11},{10,... | collective-permute-start | bytes 786440 | tf_op jit(solution)/shard_map/ppermute | solution.py:22
  34.1 4.8 %collective-permute-start.12 = (bf16[64,2048]{1,0:T(8,128)(2,1)S(1)}, bf16[64,2048]{1,0:T(8,128)(2,1)S(1)}, u32[]{:S(2)}, u32[]{:S(2)}) collective-permute-start(bf16[64,2048]{1,0:T(8,128)(2,1)S(1)} %get-tuple-element.29), channel_id=1, source_target_pairs={{0,1},{1,0},{2,3},{3,2},{4,5},{5,4},{6,7},{7,6},{8,9},{9,8},{10,11... | collective-permute-start | bytes 786440 | tf_op jit(solution)/shard_map/ppermute | solution.py:22
  39.6 5.0 %collective-permute-start.15 = (bf16[64,512]{1,0:T(8,128)(2,1)S(1)}, bf16[64,512]{1,0:T(8,128)(2,1)S(1)}, u32[]{:S(2)}, u32[]{:S(2)}) collective-permute-start(bf16[64,512]{1,0:T(8,128)(2,1)S(1)} %get-tuple-element.34), channel_id=1, source_target_pairs={{0,4},{4,0},{8,12},{12,8},{16,20},{20,16},{24,28},{28,24},{1,5},{5... | collective-permute-start | bytes 196616 | tf_op jit(solution)/shard_map/ppermute | solution.py:22
  41.2 5.4 %collective-permute-start.17 = (bf16[64,512]{1,0:T(8,128)(2,1)S(1)}, bf16[64,512]{1,0:T(8,128)(2,1)S(1)}, u32[]{:S(2)}, u32[]{:S(2)}) collective-permute-start(bf16[64,512]{1,0:T(8,128)(2,1)S(1)} %get-tuple-element.36), channel_id=1, source_target_pairs={{0,4},{4,0},{8,12},{12,8},{16,20},{20,16},{24,28},{28,24},{1,5},{5... | collective-permute-start | bytes 196616 | tf_op jit(solution)/shard_map/ppermute | solution.py:22
  41.7 8.2 %collective-permute-start.13 = (bf16[64,512]{1,0:T(8,128)(2,1)S(1)}, bf16[64,512]{1,0:T(8,128)(2,1)S(1)}, u32[]{:S(2)}, u32[]{:S(2)}) collective-permute-start(bf16[64,512]{1,0:T(8,128)(2,1)S(1)} %get-tuple-element.31), channel_id=1, source_target_pairs={{0,4},{4,0},{8,12},{12,8},{16,20},{20,16},{24,28},{28,24},{1,5},{5... | collective-permute-start | bytes 196616 | tf_op jit(solution)/shard_map/ppermute | solution.py:22
  43.2 6.7 %collective-permute-start.14 = (bf16[64,512]{1,0:T(8,128)(2,1)S(1)}, bf16[64,512]{1,0:T(8,128)(2,1)S(1)}, u32[]{:S(2)}, u32[]{:S(2)}) collective-permute-start(bf16[64,512]{1,0:T(8,128)(2,1)S(1)} %get-tuple-element.32), channel_id=1, source_target_pairs={{0,8},{4,12},{8,0},{12,4},{16,24},{20,28},{24,16},{28,20},{1,9},{5... | collective-permute-start | bytes 196616 | tf_op jit(solution)/shard_map/ppermute | solution.py:22
  44.6 6.2 %collective-permute-start.16 = (bf16[64,512]{1,0:T(8,128)(2,1)S(1)}, bf16[64,512]{1,0:T(8,128)(2,1)S(1)}, u32[]{:S(2)}, u32[]{:S(2)}) collective-permute-start(bf16[64,512]{1,0:T(8,128)(2,1)S(1)} %add_convert_fusion.3), channel_id=1, source_target_pairs={{0,24},{4,28},{8,16},{12,20},{16,8},{20,12},{24,0},{28,4},{1,25},{... | collective-permute-start | bytes 196616 | tf_op jit(solution)/shard_map/ppermute | solution.py:22
  46.6 5.6 %collective-permute-start.18 = (bf16[64,512]{1,0:T(8,128)(2,1)S(1)}, bf16[64,512]{1,0:T(8,128)(2,1)S(1)}, u32[]{:S(2)}, u32[]{:S(2)}) collective-permute-start(bf16[64,512]{1,0:T(8,128)(2,1)S(1)} %add_convert_fusion.2), channel_id=1, source_target_pairs={{0,16},{4,20},{8,24},{12,28},{16,0},{20,4},{24,8},{28,12},{1,17},{... | collective-permute-start | bytes 196616 | tf_op jit(solution)/shard_map/ppermute | solution.py:22
  46.9 5.4 %collective-permute-start.19 = (bf16[64,512]{1,0:T(8,128)(2,1)S(1)}, bf16[64,512]{1,0:T(8,128)(2,1)S(1)}, u32[]{:S(2)}, u32[]{:S(2)}) collective-permute-start(bf16[64,512]{1,0:T(8,128)(2,1)S(1)} %get-tuple-element.38), channel_id=1, source_target_pairs={{0,12},{4,8},{8,4},{12,0},{16,28},{20,24},{24,20},{28,16},{1,13},{... | collective-permute-start | bytes 196616 | tf_op jit(solution)/shard_map/ppermute | solution.py:22
